TPU v7x, 128 devices: a whole 4x4x4 slice. The times are simulated.
128 devices in a mesh: blk: 16 (over x, z_lo, core), maps: 8 (over y, z_hi).
Axes of the slice: x: 4, y: 4, z: 4 (z_hi: 2, z_lo: 2; z = z_hi * 2 + z_lo), core: 2. Of those that a mesh axis runs over, the one named last changes fastest.
Arguments:
- inv_cov: float32 [24576, 24576], P('blk', 'maps'), as said below
- sim_maps: float32 [24576, 512], P(('maps', 'blk')), may hold values from -6 to 6
- templates: float32 [24576, 4608], P(('blk', 'maps')), may hold values from -0.009765625 to 0.009765625
- band_index: int32 [4608], P(('blk', 'maps')), may hold values from 0 to 47, as said below
Outputs:
- band_power: float32 [48, 512], replicated
- fisher_part: float32 [48, 48], replicated
Inputs may be any that keep to these rules, and one draw needn't show every extreme that they name: `band_index`: every band holds at least 48 columns. `inv_cov`: Symmetric.
All inputs are finite; a program needn't handle non-finite values.
Results may differ from a plain program's by a relative error of at most 0.00016.
Values sent between devices are 32-bit elements; how exact they have to be, the bound alone decides.
No kernel may reach another device: no remote copies, remote signals or barrier semaphores. Data moves between devices by JAX's collectives and lax.ppermute only.
A program may use at most 128 MiB of HBM per device.

v0:
```python
import jax
import jax.numpy as jnp
from jax import lax
from jax.sharding import PartitionSpec as P

NMODES = 4608
NBANDS = 48
NMAPS = 512


def per_device(inv_cov, sim_maps, templates, band_index):
    high = lax.Precision.HIGHEST
    partial_rows = jnp.dot(
        inv_cov,
        lax.all_gather(sim_maps, "blk", axis=0, tiled=True),
        precision=high,
        preferred_element_type=jnp.float32,
    )
    weighted = lax.psum_scatter(partial_rows, "maps", scatter_dimension=0, tiled=True)
    projected = lax.dot_general(
        templates,
        weighted,
        (((0,), (0,)), ((), ())),
        precision=high,
        preferred_element_type=jnp.float32,
    )
    labels = jnp.arange(NBANDS, dtype=jnp.int32)
    all_modes = lax.psum(projected, ("blk", "maps"))
    all_bands = lax.all_gather(band_index, ("blk", "maps"), axis=0, tiled=True)
    onehot = (all_bands[:, None] == labels[None, :]).astype(jnp.float32)
    band_sum = lax.dot_general(
        onehot,
        all_modes * all_modes,
        (((0,), (0,)), ((), ())),
        precision=high,
        preferred_element_type=jnp.float32,
    )
    count = jnp.sum(onehot, axis=0)
    band_power = band_sum / (2.0 * count[:, None])
    centered = band_power - jnp.mean(band_power, axis=1, keepdims=True)
    fisher_part = jnp.dot(
        centered, centered.T, precision=high, preferred_element_type=jnp.float32
    ) * (NMODES / NBANDS / NMAPS)
    return (band_power, fisher_part)


def solution(mesh):
    placed = (
        P("blk", "maps"),
        P(("maps", "blk"), None),
        P(("blk", "maps"), None),
        P(("blk", "maps")),
    )
    return jax.shard_map(
        per_device, mesh=mesh, in_specs=placed, out_specs=(P(), P()), check_vma=False
    )
```

profile of v0, /device:TPU:1, one launch (start us, length us, event | category | flops | bytes accessed | tf_op | source)
XLA Modules:
  0.0 362.2 jit_solution(17280869200549791872)
XLA Ops:
  7.2 0.0 copy-start
  7.2 0.0 all-gather.2.cloned.1.call-start
  7.2 0.7 all-gather.2.cloned.1.call-update
  7.9 0.0 reduce-scatter.2.cloned.1.call-start
  8.0 47.8 %all-gather.2.cloned.1.call-done = f32[3072,512]{1,0:T(8,128)} async-done(((f32[192,512]{1,0:T(8,128)}), f32[3072,512]{1,0:T(8,128)}) %all-gather.2.cloned.1.call-update) | async-done | bytes 6291472 | tf_op jit(solution)/shard_map/all_gather | solution.py:15
  55.7 35.3 %fusion.9 = f32[1536,512]{1,0:T(8,128)} fusion(f32[1536,3072]{1,0:T(8,128)} %param.4, f32[3072,512]{1,0:T(8,128)} %all-gather.2.cloned.1.call-done), kind=kOutput, calls=%fused_computation.13 | convolution fusion | flops 28991029248 | bytes 28311552 | tf_op jit(solution)/shard_map/dot_general | solution.py:13
  91.1 0.0 reduce-scatter.2.cloned.1.call-update
  91.1 0.0 copy-start.2
  91.1 0.0 all-reduce.3.cloned.1.call-start
  91.2 79.1 %reduce-scatter.2.cloned.1.call-done = f32[192,512]{1,0:T(8,128)} async-done(((f32[1536,512]{1,0:T(8,128)}), f32[192,512]{1,0:T(8,128)}) %reduce-scatter.2.cloned.1.call-update) | async-done | bytes 393232 | tf_op jit(solution)/shard_map/reduce_scatter | solution.py:19
  170.2 0.0 copy-done
  170.2 11.3 %convolution_bitcast_fusion = f32[4608,512]{0,1:T(8,128)} fusion(f32[192,512]{1,0:T(8,128)} %reduce-scatter.2.cloned.1.call-done, f32[192,4608]{1,0:T(8,128)S(1)} %copy-done), kind=kOutput, calls=%fused_computation.2 | convolution fusion | flops 5435817984 | bytes 13369344 | tf_op jit(solution)/shard_map/dot_general | solution.py:20
  181.5 0.0 all-reduce.3.cloned.1.call-update
  181.6 0.6 broadcast.12
  182.2 0.0 copy-done.2
  182.2 1.4 dynamic-update-slice
  183.6 66.3 %all-reduce = s32[4608]{0:T(1024)} all-reduce(s32[4608]{0:T(1024)} %dynamic-update-slice), channel_id=1, replica_groups=mesh['blk'=16,'maps'=8] {'blk','maps'}, use_global_device_ids=true, to_apply=%add | all-reduce | flops 4608 | bytes 36864
  249.9 0.9 convert_reduce_fusion
  250.8 94.9 %all-reduce.3.cloned.1.call-done = f32[4608,512]{0,1:T(8,128)} async-done(((f32[4608,512]{0,1:T(8,128)}), f32[4608,512]{0,1:T(8,128)}) %all-reduce.3.cloned.1.call-update) | async-done | bytes 9437200 | tf_op jit(solution)/shard_map/psum | solution.py:28
  345.8 8.9 %fusion.8 = (f32[48]{0:T(128)S(1)}, f32[48,512]{1,0:T(8,128)S(1)}) fusion(f32[48]{0:T(128)S(1)} %broadcast_multiply_fusion.1, f32[4608,512]{0,1:T(8,128)} %all-reduce.3.cloned.1.call-done, s32[4608]{0:T(1024)} %all-reduce), kind=kOutput, calls=%fused_computation.12 | convolution fusion | flops 1361584128 | bytes 9554304 | tf_op jit(solution)/shard_map/dot_general | solution.py:31
  354.7 0.0 copy-start.1
  354.7 0.9 convolution_multiply_fusion
  355.6 0.0 copy-done.1
  (2 shorter events, 0.0 us)
Async XLA Ops:
  7.2 163.1 %copy-start = (f32[192,4608]{1,0:T(8,128)S(1)}, f32[192,4608]{1,0:T(8,128)}, u32[]{:S(2)}) copy-start(f32[192,4608]{1,0:T(8,128)} %param.6) | copy-start | bytes 10616836
  7.2 48.6 %all-gather.2.cloned.1.call-start = ((), (), s32[]{:S(2)}) async-start(), calls=%async_computation.1 | async-start | bytes 6684672 | tf_op jit(solution)/shard_map/all_gather | solution.py:15
  7.9 162.3 %reduce-scatter.2.cloned.1.call-start = ((), (), s32[]{:S(2)}) async-start(), calls=%async_computation.2 | async-start | bytes 3538944 | tf_op jit(solution)/shard_map/reduce_scatter | solution.py:19
  91.1 91.1 %copy-start.2 = (s32[36]{0:T(128)S(1)}, s32[36]{0:T(128)}, u32[]{:S(2)}) copy-start(s32[36]{0:T(128)} %param.7) | copy-start | bytes 436
  91.1 254.7 %all-reduce.3.cloned.1.call-start = ((), (), s32[]{:S(2)}) async-start(), calls=%async_computation.3 | async-start | bytes 18874368 | tf_op jit(solution)/shard_map/psum | solution.py:28
  354.7 0.9 copy-start.1
Sparse Core Ops, SparseCore 0:
  9.7 45.9 all-gather.1
  91.2 78.9 reduce-scatter.1
  181.7 164.0 all-reduce.2
where the time goes:
time: 363 us; the launch traced here: 362 us
  waiting for transfers between devices  223 us (61%)
  blocking collectives  66.3 us (18%)
  matrix products  56.5 us (16%)
  between operations  13.8 us (4%)
    psum x1, waiting for transfers between devices, per_device(): all_modes = lax.psum(projected, ('blk', 'maps'))  94.9 us
    reduce_scatter x1, waiting for transfers between devices, per_device(): lax.psum_scatter(partial_rows, 'maps', scatter_dimension=0, tiled=True)  79.1 us
    unnamed x1, blocking collectives  66.3 us
    all_gather x1, waiting for transfers between devices, per_device(): lax.all_gather(sim_maps, 'blk', axis=0, tiled=True)  47.8 us
    dot_general x1, matrix products, per_device(): jnp.dot(inv_cov, lax.all_gather(sim_maps, 'blk', axis=0, tiled=True), pre...  35.3 us
    dot_general x1, matrix products, per_device(): lax.dot_general(templates, weighted, (((0,), (0,)), ((), ())), precision=...  11.3 us
    dot_general x1, matrix products, per_device(): lax.dot_general(onehot, all_modes * all_modes, (((0,), (0,)), ((), ())),...  8.9 us
  transfers between devices with their start and end apart: 3, of which 3 were waited for; matrix products, arithmetic and copies ran while one was open for 1% of the time, Pallas kernels for 0%

commit v1 on v0

v1 whole, which is shorter than its diff:
```python
import jax
import jax.numpy as jnp
from jax import lax
from jax.sharding import Mesh, PartitionSpec as P

NMODES = 4608
NBANDS = 48
NMAPS = 512
NY = 4
SPAN = NMODES // NY
HALF = NMAPS // 2
CHIPS = ("x", "zh", "zl")
EVERY = ("x", "zl", "c", "y", "zh")


def per_device(inv_cov, sim_maps, templates, band_index):
    high = lax.Precision.HIGH
    highest = lax.Precision.HIGHEST
    y = lax.axis_index("y")
    c = lax.axis_index("c")

    gathered = lax.all_gather(sim_maps, ("x", "zl", "c"), axis=0, tiled=True)

    spans = jnp.stack([templates[:, i * SPAN : (i + 1) * SPAN] for i in range(NY)])
    own = lax.all_to_all(spans, "y", 0, 0, tiled=True)
    other = lax.ppermute(own, "c", [(0, 1), (1, 0)])
    spread = jnp.stack([own, other], axis=1).reshape(1536, SPAN)

    bands = lax.all_to_all(
        jnp.broadcast_to(band_index[None, None, :], (128, 1, 36)), EVERY, 0, 0, tiled=True
    ).reshape(NMODES)

    partial = jnp.dot(inv_cov, gathered, precision=high, preferred_element_type=jnp.float32)
    partial = partial.reshape(8, 192, 2, HALF).transpose(2, 0, 1, 3).reshape(16, 192, HALF)
    partial, spread, bands = lax.optimization_barrier((partial, spread, bands))
    terms = lax.all_to_all(partial, ("c", "y", "zh"), 0, 0, tiled=True)
    rows = jnp.sum(terms.reshape(2, 8, 192, HALF), axis=1)
    rows = jnp.stack([rows[c], rows[1 - c]])
    weighted = lax.all_to_all(
        jnp.broadcast_to(rows[None], (NY, 2, 192, HALF)), "y", 0, 0, tiled=True
    ).reshape(1536, HALF)

    projected = lax.dot_general(
        weighted,
        spread,
        (((0,), (0,)), ((), ())),
        precision=high,
        preferred_element_type=jnp.float32,
    )
    pieces = lax.all_to_all(projected.reshape(16, 16, SPAN), CHIPS, 0, 0, tiled=True)
    modes = jnp.sum(pieces, axis=0)

    labels = jnp.arange(NBANDS, dtype=jnp.int32)
    count = jnp.sum((bands[None, :] == labels[:, None]).astype(jnp.float32), axis=1)
    mine = lax.dynamic_slice(bands, (y * SPAN,), (SPAN,))
    onehot = (mine[:, None] == labels[None, :]).astype(jnp.float32)
    sums = jnp.dot(modes * modes, onehot, precision=highest, preferred_element_type=jnp.float32)
    blocks = lax.all_to_all(
        jnp.broadcast_to(sums[None], (128, 16, NBANDS)), ("c",) + CHIPS + ("y",), 0, 0, tiled=True
    )
    band_sum = jnp.sum(blocks.reshape(32, NY, 16, NBANDS), axis=1).reshape(NMAPS, NBANDS).T
    band_power = band_sum / (2.0 * count[:, None])
    centered = band_power - jnp.mean(band_power, axis=1, keepdims=True)
    fisher_part = jnp.dot(
        centered, centered.T, precision=highest, preferred_element_type=jnp.float32
    ) * (NMODES / NBANDS / NMAPS)
    return (band_power, fisher_part)


def solution(mesh):
    split = Mesh(mesh.devices.reshape(4, 2, 2, 4, 2), EVERY)
    blk, maps = ("x", "zl", "c"), ("y", "zh")
    placed = (
        P(blk, maps),
        P(maps + blk, None),
        P(blk + maps, None),
        P(blk + maps),
    )
    return jax.shard_map(
        per_device, mesh=split, in_specs=placed, out_specs=(P(), P()), check_vma=False
    )
```

time: 363 us -> 243 us (0.67)
  waiting for transfers between devices: 223 us -> 72.7 us
  matrix products: 56.5 us -> 28.4 us
  blocking collectives: 66.3 us -> 85.9 us
  starting transfers between devices: 0.12 us -> 16.7 us
  local copies, waits for them, and re-layouts: 2.07 us -> 14.5 us
  other arithmetic: 0.93 us -> 10.2 us
    psum x1 -> x0, waiting for transfers between devices: 94.9 us -> none  [per_device(): all_modes = lax.psum(projected, ('blk', 'maps'))]
    all_to_all x0 -> x3, blocking collectives: none -> 85.9 us  [the longest x1 45.7 us: per_device(): own = lax.all_to_all(spans, 'y', 0, 0, tiled=True)]
    reduce_scatter x1 -> x0, waiting for transfers between devices: 79.1 us -> none  [per_device(): lax.psum_scatter(partial_rows, 'maps', scatter_dimension=0, tiled=True)]
    all_to_all x0 -> x3, waiting for transfers between devices: none -> 72.1 us  [the longest x1 44.3 us: per_device(): terms = lax.all_to_all(partial, ('c', 'y', 'zh'), 0, 0, tiled=True)]
    unnamed x1 -> x0, blocking collectives: 66.3 us -> none
    all_gather x1, waiting for transfers between devices: 47.8 us -> 0.01 us  [per_device(): gathered = lax.all_gather(sim_maps, ('x', 'zl', 'c'), axis=0, tiled=True)]
    dot_general x4, matrix products: 56.5 us -> 28.4 us  [the longest x1 20 us: per_device(): jnp.dot(inv_cov, gathered, precision=high, preferred_element_type=jnp.flo...]
    all_to_all x0 -> x3, starting transfers between devices: none -> 14.8 us  [the longest x1 6.82 us: per_device(): lax.all_to_all(jnp.broadcast_to(sums[None], (128, 16, NBANDS)), ('c',) +...]
  transfers between devices with their start and end apart: 3 -> 5, of which waited for: 3 -> 3; matrix products, arithmetic and copies ran while one was open for 1% -> 5% of each run, Pallas kernels for 0% -> 0%
where the time goes in v1:
time: 243 us
  blocking collectives  85.9 us (35%)
  waiting for transfers between devices  72.7 us (30%)
  matrix products  28.4 us (12%)
  starting transfers between devices  16.7 us (7%)
  local copies, waits for them, and re-layouts  14.5 us (6%)
  between operations  14.2 us (6%)
  other arithmetic  10.2 us (4%)
    all_to_all x1, blocking collectives, per_device(): own = lax.all_to_all(spans, 'y', 0, 0, tiled=True)  45.7 us
    all_to_all x1, waiting for transfers between devices, per_device(): terms = lax.all_to_all(partial, ('c', 'y', 'zh'), 0, 0, tiled=True)  44.3 us
    all_to_all x1, blocking collectives, per_device(): lax.all_to_all(jnp.broadcast_to(rows[None], (NY, 2, 192, HALF)), 'y', 0,...  22.1 us
    dot_general x1, matrix products, per_device(): jnp.dot(inv_cov, gathered, precision=high, preferred_element_type=jnp.flo...  20 us
    all_to_all x1, blocking collectives, per_device(): lax.all_to_all(jnp.broadcast_to(band_index[None, None, :], (128, 1, 36)),...  18.1 us
    all_to_all x1, waiting for transfers between devices, per_device(): lax.all_to_all(projected.reshape(16, 16, SPAN), CHIPS, 0, 0, tiled=True)  16 us
    all_to_all x1, waiting for transfers between devices, per_device(): lax.all_to_all(jnp.broadcast_to(sums[None], (128, 16, NBANDS)), ('c',) +...  11.8 us
    dot_general x1, matrix products, per_device(): lax.dot_general(weighted, spread, (((0,), (0,)), ((), ())), precision=hig...  6.86 us
  transfers between devices with their start and end apart: 5, of which 3 were waited for; matrix products, arithmetic and copies ran while one was open for 5% of the time, Pallas kernels for 0%

profile of v1, /device:TPU:1, one launch (start us, length us, event | category | flops | bytes accessed | tf_op | source)
XLA Modules:
  0.0 242.6 jit_solution(5749658368800581166)
XLA Ops:
  7.2 0.7 all-gather.2.cloned.1.call-update
  7.9 2.2 slice_bitcast_fusion.3
  10.4 45.7 %all_to_all.30 = f32[4,192,1152]{2,1,0:T(8,128)S(1)} all-to-all(f32[4,192,1152]{2,1,0:T(8,128)S(1)} %pad_maximum_fusion.1), channel_id=1, replica_groups=mesh['x'=4,'zl'=2,'c'=2,'y'=4,'zh'=2] {'y'}, dimensions={0} | all-to-all | bytes 7077888 | tf_op jit(solution)/shard_map/all_to_all | solution.py:25
  56.1 1.9 collective-permute-start
  58.0 18.1 %all_to_all.31 = s32[128,1,36]{2,1,0:T(1,128)} all-to-all(s32[128,1,36]{2,1,0:T(1,128)S(1)} %broadcast_in_dim.6), channel_id=1, replica_groups=mesh['x'=4,'zl'=2,'c'=2,'y'=4,'zh'=2] {'x','zl','c','y','zh'}, dimensions={0} | all-to-all | bytes 36864 | tf_op jit(solution)/shard_map/all_to_all | solution.py:29
  76.6 2.3 reduce.4
  78.9 1.5 reshape.48
  80.4 5.4 %pad_maximum_fusion = f32[4,2,192,1152]{3,2,1,0:T(8,128)} fusion(f32[4,1,192,1152]{3,2,1,0:T(8,128)} %bitcast.8, f32[4,1,192,1152]{3,2,1,0:T(8,128)S(1)} %bitcast.39), kind=kLoop, calls=%fused_computation | loop fusion | flops 1769472 | bytes 14155776 | tf_op jit(solution)/shard_map/stack | solution.py:27
  85.8 20.0 %fusion.9 = f32[1536,512]{1,0:T(8,128)} fusion(f32[1536,3072]{1,0:T(8,128)} %param.4, f32[3072,512]{1,0:T(8,128)} %all-gather.2.cloned.1.call-done), kind=kOutput, calls=%fused_computation.27 | convolution fusion | flops 14495514624 | bytes 28311552 | tf_op jit(solution)/shard_map/dot_general | solution.py:33
  105.8 3.8 %reshape.45 = f32[8,192,2,256]{3,2,1,0:T(2,128)S(1)} reshape(f32[1536,512]{1,0:T(8,128)} %fusion.9) | data formatting | bytes 6291456 | tf_op jit(solution)/shard_map/reshape | solution.py:34
  109.6 2.1 copy.17
  111.7 4.1 %all-to-all-start.2 = ((f32[16,192,256]{2,1,0:T(8,128)}), f32[16,192,256]{2,1,0:T(8,128)S(1)}, u32[]{:S(2)}, u32[]{:S(2)}) async-start(f32[16,192,256]{2,1,0:T(8,128)} %bitcast.40), calls=%async_computation.2 | async-start | bytes 6291456 | tf_op jit(solution)/shard_map/all_to_all | solution.py:36
  115.8 44.3 %all-to-all-done.2 = f32[16,192,256]{2,1,0:T(8,128)S(1)} async-done(((f32[16,192,256]{2,1,0:T(8,128)}), f32[16,192,256]{2,1,0:T(8,128)S(1)}, u32[]{:S(2)}, u32[]{:S(2)}) %all-to-all-start.2) | async-done | bytes 3145760 | tf_op jit(solution)/shard_map/all_to_all | solution.py:36
  160.5 22.1 %all_to_all.32 = f32[4,2,192,256]{3,2,1,0:T(8,128)S(1)} all-to-all(f32[4,2,192,256]{3,2,1,0:T(8,128)S(1)} %broadcast_in_dim.7), channel_id=1, replica_groups=mesh['x'=4,'zl'=2,'c'=2,'y'=4,'zh'=2] {'y'}, dimensions={0} | all-to-all | bytes 3145728 | tf_op jit(solution)/shard_map/all_to_all | solution.py:39
  183.0 6.9 %fusion = f32[16,16,1152]{2,1,0:T(8,128)} fusion(f32[16,16,1536]{2,1,0:T(8,128)S(1)} %bitcast.41, f32[1536,1152]{1,0:T(8,128)} %bitcast.38), kind=kOutput, calls=%fused_computation.1 | convolution fusion | flops 2717908992 | bytes 9830400 | tf_op jit(solution)/shard_map/dot_general | solution.py:43
  189.9 3.9 %all-to-all-start.4 = ((f32[16,16,1152]{2,1,0:T(8,128)}), f32[16,16,1152]{2,1,0:T(8,128)S(1)}, u32[]{:S(2)}, u32[]{:S(2)}) async-start(f32[16,16,1152]{2,1,0:T(8,128)} %fusion), calls=%async_computation.4 | async-start | bytes 2359296 | tf_op jit(solution)/shard_map/all_to_all | solution.py:50
  193.9 16.0 %all-to-all-done.4 = f32[16,16,1152]{2,1,0:T(8,128)S(1)} async-done(((f32[16,16,1152]{2,1,0:T(8,128)}), f32[16,16,1152]{2,1,0:T(8,128)S(1)}, u32[]{:S(2)}, u32[]{:S(2)}) %all-to-all-start.4) | async-done | bytes 1179680 | tf_op jit(solution)/shard_map/all_to_all | solution.py:50
  210.4 1.7 reshape.63
  212.2 6.8 %all-to-all-start.5 = ((f32[128,1,768]{2,1,0:T(1,128)}), f32[128,1,768]{2,1,0:T(1,128)S(1)}, u32[]{:S(2)}, u32[]{:S(2)}) async-start(f32[128,1,768]{2,1,0:T(1,128)} %reshape.63), calls=%async_computation.5 | async-start | bytes 786432 | tf_op jit(solution)/shard_map/all_to_all | solution.py:58
  219.2 11.8 %all-to-all-done.5 = f32[128,1,768]{2,1,0:T(1,128)S(1)} async-done(((f32[128,1,768]{2,1,0:T(1,128)}), f32[128,1,768]{2,1,0:T(1,128)S(1)}, u32[]{:S(2)}, u32[]{:S(2)}) %all-to-all-start.5) | async-done | bytes 393248 | tf_op jit(solution)/shard_map/all_to_all | solution.py:58
  231.5 1.6 reduce.5
  233.1 0.5 reshape.64
  233.8 1.2 convolution_multiply_fusion
  235.0 0.8 copy.20
  (25 shorter events, 3.2 us)
Async XLA Ops:
  7.2 78.7 %all-gather.2.cloned.1.call-start = ((), (), s32[]{:S(2)}) async-start(), calls=%async_computation.6 | async-start | bytes 6684672 | tf_op jit(solution)/shard_map/all_gather | solution.py:22
  10.4 47.6 %copy-start.1 = (s32[36]{0:T(128)S(1)}, s32[36]{0:T(128)}, u32[]{:S(2)}) copy-start(s32[36]{0:T(128)} %param.7) | copy-start | bytes 436
  56.1 24.4 %collective-permute-start = (f32[4,192,1152]{2,1,0:T(8,128)S(1)}, f32[4,192,1152]{2,1,0:T(8,128)}, u32[]{:S(2)}, u32[]{:S(2)}) collective-permute-start(f32[4,192,1152]{2,1,0:T(8,128)S(1)} %all_to_all.30), channel_id=1, source_target_pairs={{0,8},{8,0},{1,9},{9,1},{2,10},{10,2},{3,11},{11,3},{4,12},{12,4},... | collective-permute-start | bytes 10616840 | tf_op jit(solution)/shard_map/ppermute | solution.py:26
  111.7 48.4 %all-to-all-start.2 = ((f32[16,192,256]{2,1,0:T(8,128)}), f32[16,192,256]{2,1,0:T(8,128)S(1)}, u32[]{:S(2)}, u32[]{:S(2)}) async-start(f32[16,192,256]{2,1,0:T(8,128)} %bitcast.40), calls=%async_computation.2 | async-start | bytes 6291456 | tf_op jit(solution)/shard_map/all_to_all | solution.py:36
  183.0 10.8 %copy-start = (s32[4608]{0:T(1024)S(1)}, s32[4608]{0:T(1024)}, u32[]{:S(2)}) copy-start(s32[4608]{0:T(1024)} %reshape.48) | copy-start | bytes 55300
  189.9 20.0 %all-to-all-start.4 = ((f32[16,16,1152]{2,1,0:T(8,128)}), f32[16,16,1152]{2,1,0:T(8,128)S(1)}, u32[]{:S(2)}, u32[]{:S(2)}) async-start(f32[16,16,1152]{2,1,0:T(8,128)} %fusion), calls=%async_computation.4 | async-start | bytes 2359296 | tf_op jit(solution)/shard_map/all_to_all | solution.py:50
  212.2 18.8 %all-to-all-start.5 = ((f32[128,1,768]{2,1,0:T(1,128)}), f32[128,1,768]{2,1,0:T(1,128)S(1)}, u32[]{:S(2)}, u32[]{:S(2)}) async-start(f32[128,1,768]{2,1,0:T(1,128)} %reshape.63), calls=%async_computation.5 | async-start | bytes 786432 | tf_op jit(solution)/shard_map/all_to_all | solution.py:58
Sparse Core Ops, SparseCore 0:
  9.7 45.9 all-gather.1

commit v2 on v0

v2 whole, which is shorter than its diff:
```python
import jax
import jax.numpy as jnp
from jax import lax
from jax.experimental import pallas as pl
from jax.experimental.pallas import tpu as pltpu
from jax.sharding import Mesh, PartitionSpec as P

NMODES = 4608
NBANDS = 48
NMAPS = 512
NY = 4
SPAN = NMODES // NY
HALF = NMAPS // 2
ROWS = 192
BLK = ("x", "zl", "c")
RING = ("y", "zh")
CHIPS = ("x", "zh", "zl")
EVERY = BLK + RING
MIB = 2**20
F32 = jnp.float32
BF16 = jnp.bfloat16


def split(value):
    high = value.astype(BF16)
    return high, (value - high.astype(F32)).astype(BF16)


def dot(a, b):
    return jnp.dot(a, b, preferred_element_type=F32)


def limit(mib):
    return pltpu.CompilerParams(vmem_limit_bytes=mib * MIB)


def shift(value, dy, dz):
    pairs = [
        (y * 2 + z, ((y + dy) % NY) * 2 + (z + dz) % 2)
        for y in range(NY)
        for z in range(2)
    ]
    return lax.ppermute(value, RING, pairs)


def swap(value):
    return lax.ppermute(value, "c", [(0, 1), (1, 0)])


def split_body(a, high, low):
    high[...], low[...] = split(a[...])


def split_rows(a):
    rows, cols = a.shape
    step = 128
    block = pl.BlockSpec((step, cols), lambda i: (i, 0))
    return pl.pallas_call(
        split_body,
        grid=(rows // step,),
        in_specs=[block],
        out_specs=[block] * 2,
        out_shape=[jax.ShapeDtypeStruct(a.shape, BF16)] * 2,
        compiler_params=limit(58),
        cost_estimate=pl.CostEstimate(
            flops=2 * rows * cols, bytes_accessed=8 * rows * cols, transcendentals=0
        ),
    )(a)


def add_step(out, value):
    @pl.when(pl.program_id(0) == 0)
    def _():
        out[...] = value

    @pl.when(pl.program_id(0) > 0)
    def _():
        out[...] += value


def first_body(at, a_high, a_low, s, out, s_high, s_low):
    sh, sl = split(s[...])
    s_high[...] = sh
    s_low[...] = sl
    ah = a_high[...]
    add_step(out, dot(ah, sh) + dot(ah, sl) + dot(a_low[...], sh))


def next_body(at, a_high, a_low, s_high, s_low, out):
    ah = a_high[...]
    sh = s_high[...]
    add_step(out, dot(ah, sh) + dot(ah, s_low[...]) + dot(a_low[...], sh))


def rows_of(at, a_high, a_low, maps):
    inner, cols = maps[0].shape
    step = 1024
    tall = 2 * ROWS
    a_block = pl.BlockSpec((tall, step), lambda k, at: (at[0], k))
    s_block = pl.BlockSpec((step, cols), lambda k, at: (k, 0))
    o_block = pl.BlockSpec((tall, cols), lambda k, at: (0, 0))
    o_shape = jax.ShapeDtypeStruct((tall, cols), F32)
    parts = jax.ShapeDtypeStruct((inner, cols), BF16)
    first = len(maps) == 1
    return pl.pallas_call(
        first_body if first else next_body,
        grid_spec=pltpu.PrefetchScalarGridSpec(
            num_scalar_prefetch=1,
            grid=(inner // step,),
            in_specs=[a_block, a_block] + [s_block] * len(maps),
            out_specs=[o_block, s_block, s_block] if first else o_block,
        ),
        out_shape=[o_shape, parts, parts] if first else o_shape,
        compiler_params=limit(58),
        cost_estimate=pl.CostEstimate(
            flops=6 * tall * inner * cols,
            bytes_accessed=4 * inner * (tall + cols),
            transcendentals=0,
        ),
    )(jnp.reshape(at, (1,)).astype(jnp.int32), a_high, a_low, *maps)


def project_body(terms, begun, *refs):
    out = refs[-1]
    cols = 384
    left = []
    for t in range(terms):
        w = refs[3 * t]
        wh, wl = split(jnp.concatenate([w[0], w[1]], axis=0).T)
        left.append(jnp.concatenate([wh, wh, wl], axis=1))
    for n in range(0, SPAN, cols):
        total = None
        for t in range(terms):
            own, other = refs[3 * t + 1 : 3 * t + 3]
            th, tl = split(
                jnp.concatenate([own[:, n : n + cols], other[:, n : n + cols]], axis=0)
            )
            term = dot(left[t], jnp.concatenate([th, tl, th], axis=0))
            total = term if total is None else total + term
        for half in range(2):
            part = total[128 * half : 128 * half + 128].reshape(16, 8, cols)
            if begun:
                part += refs[3 * terms][:, half, :, n : n + cols]
            out[:, half, :, n : n + cols] = part


def project(groups, begun=None):
    operands = [v for g in groups for v in g] + ([] if begun is None else [begun])

    def body(*refs):
        project_body(len(groups), begun is not None, *refs)

    return pl.pallas_call(
        body,
        out_shape=jax.ShapeDtypeStruct((16, 2, 8, SPAN), F32),
        compiler_params=limit(32),
        cost_estimate=pl.CostEstimate(
            flops=len(groups) * 6 * 2 * ROWS * HALF * SPAN,
            bytes_accessed=4 * sum(v.size for v in operands),
            transcendentals=0,
        ),
    )(*operands)


def band_body(pieces, onehot, out):
    modes = jnp.sum(pieces[...], axis=0)
    squares = modes * modes
    sums = jnp.dot(
        squares.reshape(16, SPAN),
        onehot[...],
        precision=lax.Precision.HIGHEST,
        preferred_element_type=F32,
    )
    lane = lax.broadcasted_iota(jnp.int32, (8, 128), 1)
    both = jnp.where(lane < NBANDS, sums[:8], sums[8:])
    out[...] = jnp.broadcast_to(both[None], out.shape)


def final_body(blocks, count, power, fisher):
    total = jnp.sum(blocks[...].reshape(32, NY, 8, 128), axis=1).reshape(HALF, 128).T
    scale = 2.0 * count[...]
    for c in range(2):
        for half in range(2):
            at = HALF * c + 128 * half
            power[:, at : at + 128] = (
                total[NBANDS * half : NBANDS * half + NBANDS, 128 * c : 128 * c + 128] / scale
            )
    value = power[...]
    centered = value - jnp.mean(value, axis=1, keepdims=True)
    fisher[...] = lax.dot_general(
        centered,
        centered,
        (((1,), (1,)), ((), ())),
        precision=lax.Precision.HIGHEST,
        preferred_element_type=F32,
    ) * (NMODES / NBANDS / NMAPS)


def per_device(inv_cov, sim_maps, templates, band_index):
    y = lax.axis_index("y")
    zh = lax.axis_index("zh")
    c = lax.axis_index("c")

    gathered = lax.all_gather(sim_maps, BLK, axis=0, tiled=True)

    own = []
    for dy in range(NY):
        block = lax.dynamic_slice(templates, (0, lax.rem(y + dy, NY) * SPAN), (ROWS, SPAN))
        own.append(shift(block, dy, 0) if dy else block)

    bands = lax.all_to_all(
        jnp.broadcast_to(band_index[None, None, :], (128, 1, 36)), EVERY, 0, 0, tiled=True
    )
    a_high, a_low = split_rows(inv_cov)
    gathered, a_high, a_low, bands, *own = lax.optimization_barrier(
        (gathered, a_high, a_low, bands, *own)
    )

    maps = (gathered,)
    sent = []
    for dy in (2, 1, 3, 0):
        found = rows_of(lax.rem(y + dy, NY), a_high, a_low, maps)
        if len(maps) == 1:
            found, *maps = found
        far = lax.dynamic_slice(found, ((1 - zh) * ROWS, 0), (ROWS, NMAPS))
        near = lax.dynamic_slice(found, (zh * ROWS, 0), (ROWS, NMAPS))
        sent.append(shift(far, dy, 1))
        sent.append(shift(near, dy, 0) if dy else near)

    bands = bands.reshape(NMODES)
    labels = jnp.arange(NBANDS, dtype=jnp.int32)
    count = jnp.sum((bands[None, :] == labels[:, None]).astype(F32), axis=1, keepdims=True)
    mine = lax.dynamic_slice(bands, (y * SPAN,), (SPAN,))
    lane = jnp.arange(128, dtype=jnp.int32)
    names = jnp.where(lane < 2 * NBANDS, lane % NBANDS, -1)
    onehot = (mine[:, None] == names[None, :]).astype(F32)

    rows = sent[0]
    for value in sent[1:]:
        rows = rows + value
    rows, count, onehot, *own = lax.optimization_barrier((rows, count, onehot, *own))

    keep = lax.dynamic_slice(rows, (0, c * HALF), (ROWS, HALF))
    give = lax.dynamic_slice(rows, (0, (1 - c) * HALF), (ROWS, HALF))
    pair = jnp.stack([keep, swap(give)])
    around = [shift(pair, dy, 0) if dy else pair for dy in range(NY)]
    other = [swap(v) for v in own]
    projected = project([(around[0], own[0], other[0])])
    projected = project([(around[d], own[d], other[d]) for d in (1, 3)], projected)
    projected = project([(around[2], own[2], other[2])], projected)

    pieces = lax.all_to_all(projected, CHIPS, 0, 0, tiled=True)
    sums = pl.pallas_call(
        band_body,
        out_shape=jax.ShapeDtypeStruct((128, 8, 128), F32),
        compiler_params=limit(32),
    )(pieces, onehot)
    blocks = lax.all_to_all(sums, ("c",) + CHIPS + ("y",), 0, 0, tiled=True)
    return pl.pallas_call(
        final_body,
        out_shape=[
            jax.ShapeDtypeStruct((NBANDS, NMAPS), F32),
            jax.ShapeDtypeStruct((NBANDS, NBANDS), F32),
        ],
        compiler_params=limit(32),
    )(blocks, count)


def solution(mesh):
    parts = Mesh(mesh.devices.reshape(4, 2, 2, 4, 2), EVERY)
    placed = (P(BLK, RING), P(RING + BLK, None), P(BLK + RING, None), P(BLK + RING))
    body = jax.shard_map(
        per_device, mesh=parts, in_specs=placed, out_specs=(P(), P()), check_vma=False
    )
    return lambda *arrays: tuple(body(*arrays))
```

time: 363 us -> 225 us (0.62)
  waiting for transfers between devices: 223 us -> 61.4 us
  Pallas kernels: 0 us -> 57.7 us
  matrix products: 56.5 us -> 0 us
  starting transfers between devices: 0.12 us -> 52.5 us
  blocking collectives: 66.3 us -> 18.9 us
  local copies, waits for them, and re-layouts: 2.07 us -> 14.3 us
  other arithmetic: 0.93 us -> 5.39 us
    psum x1 -> x0, waiting for transfers between devices: 94.9 us -> none  [per_device(): all_modes = lax.psum(projected, ('blk', 'maps'))]
    reduce_scatter x1 -> x0, waiting for transfers between devices: 79.1 us -> none  [per_device(): lax.psum_scatter(partial_rows, 'maps', scatter_dimension=0, tiled=True)]
    unnamed x1 -> x0, blocking collectives: 66.3 us -> none
    pallas_call x0 -> x10, Pallas kernels: none -> 57.7 us  [the longest x4 33.8 us: rows_of(): pl.pallas_call(first_body if first else next_body, grid_spec=pltpu.Prefet...]
    dot_general x4 -> x0, matrix products: 56.5 us -> none  [the longest x1 35.3 us: per_device(): jnp.dot(inv_cov, lax.all_gather(sim_maps, 'blk', axis=0, tiled=True), pre...]
    all_gather x1, waiting for transfers between devices: 47.8 us -> 0.02 us  [per_device(): gathered = lax.all_gather(sim_maps, BLK, axis=0, tiled=True)]
    ppermute x0 -> x18, waiting for transfers between devices: none -> 32.6 us  [the longest x13 31 us: shift(): return lax.ppermute(value, RING, pairs)]
    all_to_all x0 -> x2, waiting for transfers between devices: none -> 28.1 us  [the longest x1 14.9 us: per_device(): lax.all_to_all(jnp.broadcast_to(band_index[None, None, :], (128, 1, 36)),...]
  transfers between devices with their start and end apart: 3 -> 21, of which waited for: 3 -> 7; matrix products, arithmetic and copies ran while one was open for 1% -> 7% of each run, Pallas kernels for 0% -> 16%
where the time goes in v2:
time: 225 us; the launch traced here: 224 us
  waiting for transfers between devices  61.4 us (27%)
  Pallas kernels  57.7 us (26%)
  starting transfers between devices  52.5 us (23%)
  blocking collectives  18.9 us (8%)
  local copies, waits for them, and re-layouts  14.3 us (6%)
  between operations  14.2 us (6%)
  other arithmetic  5.39 us (2%)
    pallas_call x4, Pallas kernels, rows_of(): pl.pallas_call(first_body if first else next_body, grid_spec=pltpu.Prefet...  33.8 us
    ppermute x13, waiting for transfers between devices, shift(): return lax.ppermute(value, RING, pairs)  31 us
    ppermute x13, starting transfers between devices, shift(): return lax.ppermute(value, RING, pairs)  21.9 us
    all_to_all x1, blocking collectives, per_device(): pieces = lax.all_to_all(projected, CHIPS, 0, 0, tiled=True)  18.9 us
    pallas_call x1, Pallas kernels, split_rows(): pl.pallas_call(split_body, grid=(rows // step,), in_specs=[block], out_sp...  17 us
    all_to_all x1, starting transfers between devices, per_device(): blocks = lax.all_to_all(sums, ('c',) + CHIPS + ('y',), 0, 0, tiled=True)  16.9 us
    all_to_all x1, waiting for transfers between devices, per_device(): lax.all_to_all(jnp.broadcast_to(band_index[None, None, :], (128, 1, 36)),...  14.9 us
    all_to_all x1, waiting for transfers between devices, per_device(): blocks = lax.all_to_all(sums, ('c',) + CHIPS + ('y',), 0, 0, tiled=True)  13.2 us
  transfers between devices with their start and end apart: 21, of which 7 were waited for; matrix products, arithmetic and copies ran while one was open for 7% of the time, Pallas kernels for 16%

profile of v2, /device:TPU:1, one launch (start us, length us, event | category | flops | bytes accessed | tf_op | source)
XLA Modules:
  0.0 224.4 jit_solution(11251406661291607685)
XLA Ops:
  7.9 3.6 %constant_dynamic-slice_fusion.8 = (f32[192,1152]{1,0:T(8,128)}, f32[192,1152]{1,0:T(8,128)}, f32[192,1152]{1,0:T(8,128)S(1)}, f32[192,1152]{1,0:T(8,128)}) fusion(f32[192,4608]{1,0:T(8,128)} %param.6, s32[]{:T(128)S(6)} %select_n.55, s32[]{:T(128)S(6)} %select_n.53, s32[]{:T(128)S(6)} %select_n.52, s32[]{:T(128)S(6)} %select_n.54), kind=kLoop, calls=%fused_computation.14 | loop fusion | bytes 7077904 | tf_op jit(solution)/shard_map/dynamic_slice | solution.py:208
  11.6 2.1 collective-permute-start
  13.7 2.6 %collective-permute-start.1 = (f32[192,1152]{1,0:T(8,128)}, f32[192,1152]{1,0:T(8,128)S(1)}, u32[]{:S(2)}, u32[]{:S(2)}) collective-permute-start(f32[192,1152]{1,0:T(8,128)} %get-tuple-element.45), channel_id=1, source_target_pairs={{0,4},{1,5},{2,6},{3,7},{4,0},{5,1},{6,2},{7,3},{8,12},{9,13},{10,... | collective-permute-start | bytes 2654216 | tf_op jit(solution)/shard_map/ppermute | solution.py:43
  18.1 9.4 %all-to-all-start = ((s32[128,1,36]{2,1,0:T(1,128)}), s32[128,1,36]{2,1,0:T(1,128)}, u32[]{:S(2)}, u32[]{:S(2)}) async-start(s32[128,1,36]{2,1,0:T(1,128)} %broadcast_in_dim.8), calls=%async_computation | async-start | bytes 131072 | tf_op jit(solution)/shard_map/all_to_all | solution.py:211
  27.5 17.0 %shard_map.59 = (bf16[1536,3072]{1,0:T(8,128)(2,1)}, bf16[1536,3072]{1,0:T(8,128)(2,1)}) custom-call(f32[1536,3072]{1,0:T(8,128)} %a.1), custom_call_target="tpu_custom_call" | custom-call | flops 9437184 | bytes 37748736 | tf_op jit(solution)/shard_map/pallas_call | solution.py:58
  44.5 14.9 %all-to-all-done = s32[128,1,36]{2,1,0:T(1,128)} async-done(((s32[128,1,36]{2,1,0:T(1,128)}), s32[128,1,36]{2,1,0:T(1,128)}, u32[]{:S(2)}, u32[]{:S(2)}) %all-to-all-start) | async-done | bytes 18464 | tf_op jit(solution)/shard_map/all_to_all | solution.py:211
  59.5 10.3 %shard_map.60 = (f32[384,512]{1,0:T(8,128)}, bf16[3072,512]{1,0:T(8,128)(2,1)}, bf16[3072,512]{1,0:T(8,128)(2,1)}) custom-call(s32[1]{0:T(128)} %bitcast.at, bf16[1536,3072]{1,0:T(8,128)(2,1)} %get-tuple-element.24.a_high, bf16[1536,3072]{1,0:T(8,128)(2,1)} %get-tuple-element.25.a_low, f32[3072,512]{1,0:T(8,128)} %all-gather.2.cloned.1.call-done.s), custom_call_target="tpu_custom_call" | custom-call | flops 3623878656 | bytes 11010048 | tf_op jit(solution)/shard_map/pallas_call | solution.py:105
  69.8 7.8 %shard_map.61 = f32[384,512]{1,0:T(8,128)} custom-call(s32[1]{0:T(128)} %bitcast.1.at, bf16[1536,3072]{1,0:T(8,128)(2,1)} %get-tuple-element.24.a_high, bf16[1536,3072]{1,0:T(8,128)(2,1)} %get-tuple-element.25.a_low, bf16[3072,512]{1,0:T(8,128)(2,1)} %get-tuple-element.28.s_high, bf16[3072,512]{1,0:T(8,128)(2,1)} %get-tuple-element.29.s_low), custom_call_target="tpu_custom_call" | custom-call | flops 3623878656 | bytes 11010048 | tf_op jit(solution)/shard_map/pallas_call | solution.py:105
  79.7 2.6 %collective-permute-start.5 = (f32[192,512]{1,0:T(8,128)}, f32[192,512]{1,0:T(8,128)}, u32[]{:S(2)}, u32[]{:S(2)}) collective-permute-start(f32[192,512]{1,0:T(8,128)} %get-tuple-element.48), channel_id=1, source_target_pairs={{0,3},{1,2},{2,5},{3,4},{4,7},{5,6},{6,1},{7,0},{8,11},{9,10},{10,... | collective-permute-start | bytes 1179656 | tf_op jit(solution)/shard_map/ppermute | solution.py:43
  82.6 7.8 %shard_map.62 = f32[384,512]{1,0:T(8,128)} custom-call(s32[1]{0:T(128)} %bitcast.2.at, bf16[1536,3072]{1,0:T(8,128)(2,1)} %get-tuple-element.24.a_high, bf16[1536,3072]{1,0:T(8,128)(2,1)} %get-tuple-element.25.a_low, bf16[3072,512]{1,0:T(8,128)(2,1)} %get-tuple-element.28.s_high, bf16[3072,512]{1,0:T(8,128)(2,1)} %get-tuple-element.29.s_low), custom_call_target="tpu_custom_call" | custom-call | flops 3623878656 | bytes 11010048 | tf_op jit(solution)/shard_map/pallas_call | solution.py:105
  92.5 3.9 %collective-permute-start.7 = (f32[192,512]{1,0:T(8,128)}, f32[192,512]{1,0:T(8,128)}, u32[]{:S(2)}, u32[]{:S(2)}) collective-permute-start(f32[192,512]{1,0:T(8,128)} %get-tuple-element.50), channel_id=1, source_target_pairs={{0,7},{1,6},{2,1},{3,0},{4,3},{5,2},{6,5},{7,4},{8,15},{9,14},{10,... | collective-permute-start | bytes 1179656 | tf_op jit(solution)/shard_map/ppermute | solution.py:43
  96.3 7.8 %shard_map.63 = f32[384,512]{1,0:T(8,128)} custom-call(s32[1]{0:T(128)} %bitcast.3.at, bf16[1536,3072]{1,0:T(8,128)(2,1)} %get-tuple-element.24.a_high, bf16[1536,3072]{1,0:T(8,128)(2,1)} %get-tuple-element.25.a_low, bf16[3072,512]{1,0:T(8,128)(2,1)} %get-tuple-element.28.s_high, bf16[3072,512]{1,0:T(8,128)(2,1)} %get-tuple-element.29.s_low), custom_call_target="tpu_custom_call" | custom-call | flops 3623878656 | bytes 11010048 | tf_op jit(solution)/shard_map/pallas_call | solution.py:105
  107.6 2.3 %reduce.3 = s32[128,36]{1,0:T(8,128)} reduce(s32[128,1,36]{2,1,0:T(1,128)} %all-to-all-done, s32[]{:T(128)} %broadcast.36), dimensions={1}, to_apply=%get-tuple-element.30.reduce_sub_computation.3 | reduce | bytes 36868 | tf_op jit(solution)/shard_map/optimization_barrier | solution.py:215
  114.3 2.5 %collective-permute-start.3 = (f32[192,512]{1,0:T(8,128)S(1)}, f32[192,512]{1,0:T(8,128)S(1)}, u32[]{:S(2)}, u32[]{:S(2)}) collective-permute-start(f32[192,512]{1,0:T(8,128)S(1)} %get-tuple-element.47), channel_id=1, source_target_pairs={{0,5},{1,4},{2,7},{3,6},{4,1},{5,0},{6,3},{7,2},{8,13},{9,12},{10,... | collective-permute-start | bytes 1179656 | tf_op jit(solution)/shard_map/ppermute | solution.py:43
  116.8 2.1 collective-permute-start.4
  119.2 7.8 %collective-permute-done.3 = f32[192,512]{1,0:T(8,128)S(1)} collective-permute-done((f32[192,512]{1,0:T(8,128)S(1)}, f32[192,512]{1,0:T(8,128)S(1)}, u32[]{:S(2)}, u32[]{:S(2)}) %collective-permute-start.3) | collective-permute-done | bytes 393248 | tf_op jit(solution)/shard_map/ppermute | solution.py:43
  127.0 7.6 %collective-permute-done.4 = f32[192,512]{1,0:T(8,128)S(1)} collective-permute-done((f32[192,512]{1,0:T(8,128)S(1)}, f32[192,512]{1,0:T(8,128)S(1)}, u32[]{:S(2)}, u32[]{:S(2)}) %collective-permute-start.4) | collective-permute-done | bytes 393248 | tf_op jit(solution)/shard_map/ppermute | solution.py:43
  136.5 2.9 %collective-permute-start.17 = (f32[192,1152]{1,0:T(8,128)S(1)}, f32[192,1152]{1,0:T(8,128)S(1)}, u32[]{:S(2)}, u32[]{:S(2)}) collective-permute-start(f32[192,1152]{1,0:T(8,128)S(1)} %get-tuple-element.39.refs_1_), channel_id=1, source_target_pairs={{0,8},{8,0},{1,9},{9,1},{2,10},{10,2},{3,11},{11,3},{4,12},{12,4},... | collective-permute-start | bytes 2654216 | tf_op jit(solution)/shard_map/ppermute | solution.py:47
  144.0 9.4 %collective-permute-done.13.refs_0_ = f32[2,192,256]{2,1,0:T(8,128)S(1)} collective-permute-done((f32[2,192,256]{2,1,0:T(8,128)S(1)}, f32[2,192,256]{2,1,0:T(8,128)S(1)}, u32[]{:S(2)}, u32[]{:S(2)}) %collective-permute-start.13) | collective-permute-done | bytes 393248 | tf_op jit(solution)/shard_map/ppermute | solution.py:43
  156.7 6.2 %collective-permute-done.15.refs_3_ = f32[2,192,256]{2,1,0:T(8,128)S(1)} collective-permute-done((f32[2,192,256]{2,1,0:T(8,128)S(1)}, f32[2,192,256]{2,1,0:T(8,128)S(1)}, u32[]{:S(2)}, u32[]{:S(2)}) %collective-permute-start.15) | collective-permute-done | bytes 393248 | tf_op jit(solution)/shard_map/ppermute | solution.py:43
  162.8 2.2 shard_map.65.refs_3_
  166.2 18.9 %all_to_all.15.pieces = f32[16,2,8,1152]{3,2,1,0:T(8,128)S(1)} all-to-all(f32[16,2,8,1152]{3,2,1,0:T(8,128)S(1)} %shard_map.66), channel_id=1, replica_groups=mesh['x'=4,'zl'=2,'c'=2,'y'=4,'zh'=2] {'x','zh','zl'}, dimensions={0} | all-to-all | bytes 2359296 | tf_op jit(solution)/shard_map/all_to_all | solution.py:252
  186.4 16.9 %all-to-all-start.2 = ((f32[128,8,128]{2,1,0:T(8,128)}), f32[128,8,128]{2,1,0:T(8,128)S(1)}, u32[]{:S(2)}, u32[]{:S(2)}) async-start(f32[128,8,128]{2,1,0:T(8,128)} %shard_map.67), calls=%async_computation.2 | async-start | bytes 1048576 | tf_op jit(solution)/shard_map/all_to_all | solution.py:258
  203.4 13.2 %all-to-all-done.2.blocks = f32[128,8,128]{2,1,0:T(8,128)S(1)} async-done(((f32[128,8,128]{2,1,0:T(8,128)}), f32[128,8,128]{2,1,0:T(8,128)S(1)}, u32[]{:S(2)}, u32[]{:S(2)}) %all-to-all-start.2) | async-done | bytes 524320 | tf_op jit(solution)/shard_map/all_to_all | solution.py:258
  (49 shorter events, 28.4 us)
Async XLA Ops:
  7.2 52.3 %all-gather.2.cloned.1.call-start = ((), (), s32[]{:S(2)}) async-start(), calls=%async_computation.3 | async-start | bytes 6684672 | tf_op jit(solution)/shard_map/all_gather | solution.py:204
  7.9 9.5 %copy-start = (s32[36]{0:T(128)S(1)}, s32[36]{0:T(128)}, u32[]{:S(2)}) copy-start(s32[36]{0:T(128)} %param.7) | copy-start | bytes 436
  11.6 47.9 %collective-permute-start = (f32[192,1152]{1,0:T(8,128)}, f32[192,1152]{1,0:T(8,128)S(1)}, u32[]{:S(2)}, u32[]{:S(2)}) collective-permute-start(f32[192,1152]{1,0:T(8,128)} %get-tuple-element.43), channel_id=1, source_target_pairs={{0,2},{1,3},{2,4},{3,5},{4,6},{5,7},{6,0},{7,1},{8,10},{9,11},{10,... | collective-permute-start | bytes 2654216 | tf_op jit(solution)/shard_map/ppermute | solution.py:43
  13.7 45.8 %collective-permute-start.1 = (f32[192,1152]{1,0:T(8,128)}, f32[192,1152]{1,0:T(8,128)S(1)}, u32[]{:S(2)}, u32[]{:S(2)}) collective-permute-start(f32[192,1152]{1,0:T(8,128)} %get-tuple-element.45), channel_id=1, source_target_pairs={{0,4},{1,5},{2,6},{3,7},{4,0},{5,1},{6,2},{7,3},{8,12},{9,13},{10,... | collective-permute-start | bytes 2654216 | tf_op jit(solution)/shard_map/ppermute | solution.py:43
  16.3 43.2 %collective-permute-start.2 = (f32[192,1152]{1,0:T(8,128)}, f32[192,1152]{1,0:T(8,128)S(1)}, u32[]{:S(2)}, u32[]{:S(2)}) collective-permute-start(f32[192,1152]{1,0:T(8,128)} %get-tuple-element.42), channel_id=1, source_target_pairs={{0,6},{1,7},{2,0},{3,1},{4,2},{5,3},{6,4},{7,5},{8,14},{9,15},{10,... | collective-permute-start | bytes 2654216 | tf_op jit(solution)/shard_map/ppermute | solution.py:43
  18.1 41.4 %all-to-all-start = ((s32[128,1,36]{2,1,0:T(1,128)}), s32[128,1,36]{2,1,0:T(1,128)}, u32[]{:S(2)}, u32[]{:S(2)}) async-start(s32[128,1,36]{2,1,0:T(1,128)} %broadcast_in_dim.8), calls=%async_computation | async-start | bytes 131072 | tf_op jit(solution)/shard_map/all_to_all | solution.py:211
  79.7 34.7 %collective-permute-start.5 = (f32[192,512]{1,0:T(8,128)}, f32[192,512]{1,0:T(8,128)}, u32[]{:S(2)}, u32[]{:S(2)}) collective-permute-start(f32[192,512]{1,0:T(8,128)} %get-tuple-element.48), channel_id=1, source_target_pairs={{0,3},{1,2},{2,5},{3,4},{4,7},{5,6},{6,1},{7,0},{8,11},{9,10},{10,... | collective-permute-start | bytes 1179656 | tf_op jit(solution)/shard_map/ppermute | solution.py:43
  82.3 34.5 %collective-permute-start.6 = (f32[192,512]{1,0:T(8,128)}, f32[192,512]{1,0:T(8,128)}, u32[]{:S(2)}, u32[]{:S(2)}) collective-permute-start(f32[192,512]{1,0:T(8,128)} %get-tuple-element.49), channel_id=1, source_target_pairs={{0,2},{1,3},{2,4},{3,5},{4,6},{5,7},{6,0},{7,1},{8,10},{9,11},{10,... | collective-permute-start | bytes 1179656 | tf_op jit(solution)/shard_map/ppermute | solution.py:43
  92.5 26.7 %collective-permute-start.7 = (f32[192,512]{1,0:T(8,128)}, f32[192,512]{1,0:T(8,128)}, u32[]{:S(2)}, u32[]{:S(2)}) collective-permute-start(f32[192,512]{1,0:T(8,128)} %get-tuple-element.50), channel_id=1, source_target_pairs={{0,7},{1,6},{2,1},{3,0},{4,3},{5,2},{6,5},{7,4},{8,15},{9,14},{10,... | collective-permute-start | bytes 1179656 | tf_op jit(solution)/shard_map/ppermute | solution.py:43
  96.3 22.8 %collective-permute-start.8 = (f32[192,512]{1,0:T(8,128)}, f32[192,512]{1,0:T(8,128)}, u32[]{:S(2)}, u32[]{:S(2)}) collective-permute-start(f32[192,512]{1,0:T(8,128)} %get-tuple-element.51), channel_id=1, source_target_pairs={{0,6},{1,7},{2,0},{3,1},{4,2},{5,3},{6,4},{7,5},{8,14},{9,15},{10,... | collective-permute-start | bytes 1179656 | tf_op jit(solution)/shard_map/ppermute | solution.py:43
  105.9 13.2 %collective-permute-start.9 = (f32[192,512]{1,0:T(8,128)}, f32[192,512]{1,0:T(8,128)}, u32[]{:S(2)}, u32[]{:S(2)}) collective-permute-start(f32[192,512]{1,0:T(8,128)} %constant_dynamic-slice_fusion.1), channel_id=1, source_target_pairs={{0,1},{1,0},{2,3},{3,2},{4,5},{5,4},{6,7},{7,6},{8,9},{9,8},{10,11... | collective-permute-start | bytes 1179656 | tf_op jit(solution)/shard_map/ppermute | solution.py:43
  114.3 12.6 %collective-permute-start.3 = (f32[192,512]{1,0:T(8,128)S(1)}, f32[192,512]{1,0:T(8,128)S(1)}, u32[]{:S(2)}, u32[]{:S(2)}) collective-permute-start(f32[192,512]{1,0:T(8,128)S(1)} %get-tuple-element.47), channel_id=1, source_target_pairs={{0,5},{1,4},{2,7},{3,6},{4,1},{5,0},{6,3},{7,2},{8,13},{9,12},{10,... | collective-permute-start | bytes 1179656 | tf_op jit(solution)/shard_map/ppermute | solution.py:43
  116.8 17.7 %collective-permute-start.4 = (f32[192,512]{1,0:T(8,128)S(1)}, f32[192,512]{1,0:T(8,128)S(1)}, u32[]{:S(2)}, u32[]{:S(2)}) collective-permute-start(f32[192,512]{1,0:T(8,128)S(1)} %get-tuple-element.46), channel_id=1, source_target_pairs={{0,4},{1,5},{2,6},{3,7},{4,0},{5,1},{6,2},{7,3},{8,12},{9,13},{10,... | collective-permute-start | bytes 1179656 | tf_op jit(solution)/shard_map/ppermute | solution.py:43
  136.5 16.9 %collective-permute-start.17 = (f32[192,1152]{1,0:T(8,128)S(1)}, f32[192,1152]{1,0:T(8,128)S(1)}, u32[]{:S(2)}, u32[]{:S(2)}) collective-permute-start(f32[192,1152]{1,0:T(8,128)S(1)} %get-tuple-element.39.refs_1_), channel_id=1, source_target_pairs={{0,8},{8,0},{1,9},{9,1},{2,10},{10,2},{3,11},{11,3},{4,12},{12,4},... | collective-permute-start | bytes 2654216 | tf_op jit(solution)/shard_map/ppermute | solution.py:47
  139.5 2.3 %collective-permute-start.10 = (f32[192,256]{1,0:T(8,128)S(1)}, f32[192,256]{1,0:T(8,128)S(1)}, u32[]{:S(2)}, u32[]{:S(2)}) collective-permute-start(f32[192,256]{1,0:T(8,128)S(1)} %get-tuple-element.53), channel_id=1, source_target_pairs={{0,8},{8,0},{1,9},{9,1},{2,10},{10,2},{3,11},{11,3},{4,12},{12,4},... | collective-permute-start | bytes 589832 | tf_op jit(solution)/shard_map/ppermute | solution.py:47
  139.6 23.2 %collective-permute-start.14 = (f32[192,1152]{1,0:T(8,128)S(1)}, f32[192,1152]{1,0:T(8,128)S(1)}, u32[]{:S(2)}, u32[]{:S(2)}) collective-permute-start(f32[192,1152]{1,0:T(8,128)S(1)} %collective-permute-done.refs_1_), channel_id=1, source_target_pairs={{0,8},{8,0},{1,9},{9,1},{2,10},{10,2},{3,11},{11,3},{4,12},{12,4},... | collective-permute-start | bytes 2654216 | tf_op jit(solution)/shard_map/ppermute | solution.py:47
  140.0 22.8 %collective-permute-start.16 = (f32[192,1152]{1,0:T(8,128)S(1)}, f32[192,1152]{1,0:T(8,128)S(1)}, u32[]{:S(2)}, u32[]{:S(2)}) collective-permute-start(f32[192,1152]{1,0:T(8,128)S(1)} %collective-permute-done.2.refs_4_), channel_id=1, source_target_pairs={{0,8},{8,0},{1,9},{9,1},{2,10},{10,2},{3,11},{11,3},{4,12},{12,4},... | collective-permute-start | bytes 2654216 | tf_op jit(solution)/shard_map/ppermute | solution.py:47
  141.8 11.6 %collective-permute-start.13 = (f32[2,192,256]{2,1,0:T(8,128)S(1)}, f32[2,192,256]{2,1,0:T(8,128)S(1)}, u32[]{:S(2)}, u32[]{:S(2)}) collective-permute-start(f32[2,192,256]{2,1,0:T(8,128)S(1)} %pad_maximum_fusion.refs_0_), channel_id=1, source_target_pairs={{0,2},{1,3},{2,4},{3,5},{4,6},{5,7},{6,0},{7,1},{8,10},{9,11},{10,... | collective-permute-start | bytes 1179656 | tf_op jit(solution)/shard_map/ppermute | solution.py:43
  143.3 21.7 %collective-permute-start.12 = (f32[192,1152]{1,0:T(8,128)S(1)}, f32[192,1152]{1,0:T(8,128)S(1)}, u32[]{:S(2)}, u32[]{:S(2)}) collective-permute-start(f32[192,1152]{1,0:T(8,128)S(1)} %collective-permute-done.1.refs_1_), channel_id=1, source_target_pairs={{0,8},{8,0},{1,9},{9,1},{2,10},{10,2},{3,11},{11,3},{4,12},{12,4},... | collective-permute-start | bytes 2654216 | tf_op jit(solution)/shard_map/ppermute | solution.py:47
  153.4 9.4 %collective-permute-start.15 = (f32[2,192,256]{2,1,0:T(8,128)S(1)}, f32[2,192,256]{2,1,0:T(8,128)S(1)}, u32[]{:S(2)}, u32[]{:S(2)}) collective-permute-start(f32[2,192,256]{2,1,0:T(8,128)S(1)} %pad_maximum_fusion.refs_0_), channel_id=1, source_target_pairs={{0,6},{1,7},{2,0},{3,1},{4,2},{5,3},{6,4},{7,5},{8,14},{9,15},{10,... | collective-permute-start | bytes 1179656 | tf_op jit(solution)/shard_map/ppermute | solution.py:43
  153.4 11.6 %collective-permute-start.11 = (f32[2,192,256]{2,1,0:T(8,128)S(1)}, f32[2,192,256]{2,1,0:T(8,128)S(1)}, u32[]{:S(2)}, u32[]{:S(2)}) collective-permute-start(f32[2,192,256]{2,1,0:T(8,128)S(1)} %pad_maximum_fusion.refs_0_), channel_id=1, source_target_pairs={{0,4},{1,5},{2,6},{3,7},{4,0},{5,1},{6,2},{7,3},{8,12},{9,13},{10,... | collective-permute-start | bytes 1179656 | tf_op jit(solution)/shard_map/ppermute | solution.py:43
  186.4 30.1 %all-to-all-start.2 = ((f32[128,8,128]{2,1,0:T(8,128)}), f32[128,8,128]{2,1,0:T(8,128)S(1)}, u32[]{:S(2)}, u32[]{:S(2)}) async-start(f32[128,8,128]{2,1,0:T(8,128)} %shard_map.67), calls=%async_computation.2 | async-start | bytes 1048576 | tf_op jit(solution)/shard_map/all_to_all | solution.py:258
Sparse Core Ops, SparseCore 0:
  9.7 46.6 all-gather.1

commit v3 on v2

--- a/solution.py
+++ b/solution.py
@@ -61,7 +61,7 @@
         in_specs=[block],
         out_specs=[block] * 2,
         out_shape=[jax.ShapeDtypeStruct(a.shape, BF16)] * 2,
-        compiler_params=limit(58),
+        compiler_params=limit(32),
         cost_estimate=pl.CostEstimate(
             flops=2 * rows * cols, bytes_accessed=8 * rows * cols, transcendentals=0
         ),
@@ -78,46 +78,52 @@
         out[...] += value
 
 
-def first_body(at, a_high, a_low, s, out, s_high, s_low):
-    sh, sl = split(s[...])
-    s_high[...] = sh
-    s_low[...] = sl
-    ah = a_high[...]
-    add_step(out, dot(ah, sh) + dot(ah, sl) + dot(a_low[...], sh))
-
-
-def next_body(at, a_high, a_low, s_high, s_low, out):
-    ah = a_high[...]
-    sh = s_high[...]
-    add_step(out, dot(ah, sh) + dot(ah, s_low[...]) + dot(a_low[...], sh))
+def row_body(blocks, first, at, *refs):
+    highs, lows, rest = refs[:blocks], refs[blocks : 2 * blocks], refs[2 * blocks :]
+    if first:
+        sh, sl = split(rest[0][...])
+        rest[-2][...] = sh
+        rest[-1][...] = sl
+        outs = rest[1:-2]
+    else:
+        sh, sl = rest[0][...], rest[1][...]
+        outs = rest[2:]
+    ah = jnp.concatenate([ref[...] for ref in highs], axis=0)
+    al = jnp.concatenate([ref[...] for ref in lows], axis=0)
+    found = dot(ah, sh) + dot(ah, sl) + dot(al, sh)
+    for n, out in enumerate(outs):
+        add_step(out, found[n * ROWS : n * ROWS + ROWS])
 
 
 def rows_of(at, a_high, a_low, maps):
     inner, cols = maps[0].shape
     step = 1024
-    tall = 2 * ROWS
-    a_block = pl.BlockSpec((tall, step), lambda k, at: (at[0], k))
+    blocks, first = len(at), len(maps) == 1
+    a_blocks = [pl.BlockSpec((ROWS, step), lambda k, at, n=n: (at[n], k)) for n in range(blocks)]
     s_block = pl.BlockSpec((step, cols), lambda k, at: (k, 0))
-    o_block = pl.BlockSpec((tall, cols), lambda k, at: (0, 0))
-    o_shape = jax.ShapeDtypeStruct((tall, cols), F32)
-    parts = jax.ShapeDtypeStruct((inner, cols), BF16)
-    first = len(maps) == 1
-    return pl.pallas_call(
-        first_body if first else next_body,
+    o_block = pl.BlockSpec((ROWS, cols), lambda k, at: (0, 0))
+    parts = [jax.ShapeDtypeStruct((inner, cols), BF16)] * 2 if first else []
+
+    def body(*refs):
+        row_body(blocks, first, *refs)
+
+    found = pl.pallas_call(
+        body,
         grid_spec=pltpu.PrefetchScalarGridSpec(
             num_scalar_prefetch=1,
             grid=(inner // step,),
-            in_specs=[a_block, a_block] + [s_block] * len(maps),
-            out_specs=[o_block, s_block, s_block] if first else o_block,
+            in_specs=a_blocks * 2 + [s_block] * len(maps),
+            out_specs=[o_block] * blocks + [s_block] * len(parts),
         ),
-        out_shape=[o_shape, parts, parts] if first else o_shape,
-        compiler_params=limit(58),
+        out_shape=[jax.ShapeDtypeStruct((ROWS, cols), F32)] * blocks + parts,
+        compiler_params=limit(32),
         cost_estimate=pl.CostEstimate(
-            flops=6 * tall * inner * cols,
-            bytes_accessed=4 * inner * (tall + cols),
+            flops=blocks * ROWS * cols,
+            bytes_accessed=blocks * ROWS * cols,
             transcendentals=0,
         ),
-    )(jnp.reshape(at, (1,)).astype(jnp.int32), a_high, a_low, *maps)
+    )(jnp.stack(at).astype(jnp.int32), *[a_high] * blocks, *[a_low] * blocks, *maps)
+    return found[:blocks], found[blocks:] or maps
 
 
 def project_body(terms, begun, *refs):
@@ -162,12 +168,30 @@
     )(*operands)
 
 
-def band_body(pieces, onehot, out):
+def names_row():
+    lane = lax.broadcasted_iota(jnp.int32, (1, 128), 1)
+    return jnp.where(
+        lane < NBANDS, lane, jnp.where(lane < 2 * NBANDS, lane - NBANDS, -1)
+    ).astype(F32)
+
+
+def band_body(y, pieces, bands, out):
+    devices, each = SPAN // 36, 36
+    held = bands[pl.ds(y[0] * devices, devices)].reshape(devices, each).astype(F32)
+    row = lax.broadcasted_iota(jnp.int32, (SPAN, devices), 0)
+    begin = lax.broadcasted_iota(jnp.int32, (SPAN, devices), 1) * each
+    source = ((row >= begin) & (row < begin + each)).astype(F32)
+    start = jnp.sum(source * begin.astype(F32), axis=1, keepdims=True)
+    at = lax.broadcasted_iota(jnp.int32, (SPAN, each), 0).astype(F32) - start
+    mask = at == lax.broadcasted_iota(jnp.int32, (SPAN, each), 1).astype(F32)
+    spread = jnp.dot(source, held, preferred_element_type=F32)
+    band = jnp.sum(jnp.where(mask, spread, 0.0), axis=1, keepdims=True)
+    onehot = (band == names_row()).astype(F32)
+
     modes = jnp.sum(pieces[...], axis=0)
-    squares = modes * modes
     sums = jnp.dot(
-        squares.reshape(16, SPAN),
-        onehot[...],
+        (modes * modes).reshape(16, SPAN),
+        onehot,
         precision=lax.Precision.HIGHEST,
         preferred_element_type=F32,
     )
@@ -176,15 +200,21 @@
     out[...] = jnp.broadcast_to(both[None], out.shape)
 
 
-def final_body(blocks, count, power, fisher):
-    total = jnp.sum(blocks[...].reshape(32, NY, 8, 128), axis=1).reshape(HALF, 128).T
-    scale = 2.0 * count[...]
+def final_body(blocks, bands, power, fisher):
+    held = bands[...].reshape(128, 36).astype(F32)
+    names = names_row()
+    found = jnp.zeros((128, 128), F32)
+    for k in range(36):
+        found += (held[:, k : k + 1] == names).astype(F32)
+    count = jnp.maximum(jnp.sum(found, axis=0, keepdims=True), 1.0)
+    total = jnp.sum(blocks[...].reshape(32, NY, 8, 128), axis=1).reshape(HALF, 128)
+    total = (total / (2.0 * count)).T
     for c in range(2):
         for half in range(2):
             at = HALF * c + 128 * half
-            power[:, at : at + 128] = (
-                total[NBANDS * half : NBANDS * half + NBANDS, 128 * c : 128 * c + 128] / scale
-            )
+            power[:, at : at + 128] = total[
+                NBANDS * half : NBANDS * half + NBANDS, 128 * c : 128 * c + 128
+            ]
     value = power[...]
     centered = value - jnp.mean(value, axis=1, keepdims=True)
     fisher[...] = lax.dot_general(
@@ -208,53 +238,48 @@
         block = lax.dynamic_slice(templates, (0, lax.rem(y + dy, NY) * SPAN), (ROWS, SPAN))
         own.append(shift(block, dy, 0) if dy else block)
 
-    bands = lax.all_to_all(
-        jnp.broadcast_to(band_index[None, None, :], (128, 1, 36)), EVERY, 0, 0, tiled=True
-    )
     a_high, a_low = split_rows(inv_cov)
-    gathered, a_high, a_low, bands, *own = lax.optimization_barrier(
-        (gathered, a_high, a_low, bands, *own)
-    )
-
-    maps = (gathered,)
+    gathered, a_high, a_low, *own = lax.optimization_barrier((gathered, a_high, a_low, *own))
+
+    maps = [gathered]
     sent = []
-    for dy in (2, 1, 3, 0):
-        found = rows_of(lax.rem(y + dy, NY), a_high, a_low, maps)
-        if len(maps) == 1:
-            found, *maps = found
-        far = lax.dynamic_slice(found, ((1 - zh) * ROWS, 0), (ROWS, NMAPS))
-        near = lax.dynamic_slice(found, (zh * ROWS, 0), (ROWS, NMAPS))
-        sent.append(shift(far, dy, 1))
-        sent.append(shift(near, dy, 0) if dy else near)
-
-    bands = bands.reshape(NMODES)
-    labels = jnp.arange(NBANDS, dtype=jnp.int32)
-    count = jnp.sum((bands[None, :] == labels[:, None]).astype(F32), axis=1, keepdims=True)
-    mine = lax.dynamic_slice(bands, (y * SPAN,), (SPAN,))
-    lane = jnp.arange(128, dtype=jnp.int32)
-    names = jnp.where(lane < 2 * NBANDS, lane % NBANDS, -1)
-    onehot = (mine[:, None] == names[None, :]).astype(F32)
-
+    for group in (((2, 1), (2, 0)), ((1, 1), (1, 0)), ((3, 1), (3, 0)), ((0, 1),), ((0, 0),)):
+        at = [lax.rem(y + dy, NY) * 2 + lax.rem(zh + dz, 2) for dy, dz in group]
+        found, maps = rows_of(at, a_high, a_low, maps)
+        found, maps = lax.optimization_barrier((found, maps))
+        for (dy, dz), block in zip(group, found):
+            sent.append(shift(block, dy, dz) if dy or dz else block)
+    sent[-1], *own = lax.optimization_barrier((sent[-1], *own))
+    other = [swap(v) for v in own]
     rows = sent[0]
     for value in sent[1:]:
         rows = rows + value
-    rows, count, onehot, *own = lax.optimization_barrier((rows, count, onehot, *own))
+    rows, band_index, *other = lax.optimization_barrier((rows, band_index, *other))
 
     keep = lax.dynamic_slice(rows, (0, c * HALF), (ROWS, HALF))
     give = lax.dynamic_slice(rows, (0, (1 - c) * HALF), (ROWS, HALF))
     pair = jnp.stack([keep, swap(give)])
     around = [shift(pair, dy, 0) if dy else pair for dy in range(NY)]
-    other = [swap(v) for v in own]
+    bands = lax.all_to_all(
+        jnp.broadcast_to(band_index[None, None, :], (128, 1, 36)), EVERY, 0, 0, tiled=True
+    )
     projected = project([(around[0], own[0], other[0])])
     projected = project([(around[d], own[d], other[d]) for d in (1, 3)], projected)
     projected = project([(around[2], own[2], other[2])], projected)
 
+    projected, bands = lax.optimization_barrier((projected, bands))
     pieces = lax.all_to_all(projected, CHIPS, 0, 0, tiled=True)
+
     sums = pl.pallas_call(
         band_body,
+        in_specs=[
+            pl.BlockSpec(memory_space=pltpu.SMEM),
+            pl.BlockSpec(memory_space=pltpu.VMEM),
+            pl.BlockSpec(memory_space=pltpu.VMEM),
+        ],
         out_shape=jax.ShapeDtypeStruct((128, 8, 128), F32),
         compiler_params=limit(32),
-    )(pieces, onehot)
+    )(jnp.reshape(y, (1,)).astype(jnp.int32), pieces, bands)
     blocks = lax.all_to_all(sums, ("c",) + CHIPS + ("y",), 0, 0, tiled=True)
     return pl.pallas_call(
         final_body,
@@ -263,7 +288,7 @@
             jax.ShapeDtypeStruct((NBANDS, NBANDS), F32),
         ],
         compiler_params=limit(32),
-    )(blocks, count)
+    )(blocks, bands)
 
 
 def solution(mesh):

time: 225 us -> 230 us (1.022)
  blocking collectives: 18.9 us -> 40.6 us
  waiting for transfers between devices: 61.4 us -> 47.8 us
  local copies, waits for them, and re-layouts: 14.3 us -> 23.2 us
  starting transfers between devices: 52.5 us -> 45.3 us
  other arithmetic: 5.39 us -> 2.11 us
    all_to_all x0 -> x1, blocking collectives: none -> 21.3 us  [per_device(): blocks = lax.all_to_all(sums, ('c',) + CHIPS + ('y',), 0, 0, tiled=True)]
    unnamed x2 -> x16, local copies, waits for them, and re-layouts: 0.01 us -> 19.3 us
    all_to_all x1 -> x0, starting transfers between devices: 16.9 us -> none  [per_device(): blocks = lax.all_to_all(sums, ('c',) + CHIPS + ('y',), 0, 0, tiled=True)]
    all_to_all x1, waiting for transfers between devices: 14.9 us -> 0.01 us  [per_device(): lax.all_to_all(jnp.broadcast_to(band_index[None, None, :], (128, 1, 36)),...]
    ppermute x13, waiting for transfers between devices: 31 us -> 44.3 us  [shift(): return lax.ppermute(value, RING, pairs)]
    all_to_all x1 -> x0, waiting for transfers between devices: 13.2 us -> none  [per_device(): blocks = lax.all_to_all(sums, ('c',) + CHIPS + ('y',), 0, 0, tiled=True)]
    ppermute x5, starting transfers between devices: 4.28 us -> 15.7 us  [swap(): return lax.ppermute(value, 'c', [(0, 1), (1, 0)])]
    dynamic_slice x5 -> x0, local copies, waits for them, and re-layouts: 7.83 us -> none  [the longest x3 5.88 us: per_device(): far = lax.dynamic_slice(found, ((1 - zh) * ROWS, 0), (ROWS, NMAPS))]
  transfers between devices with their start and end apart: 21 -> 20, of which waited for: 7 -> 7; matrix products, arithmetic and copies ran while one was open for 7% -> 3% of each run, Pallas kernels for 16% -> 10%
where the time goes in v3:
time: 230 us
  Pallas kernels  56.4 us (25%)
  waiting for transfers between devices  47.8 us (21%)
  starting transfers between devices  45.3 us (20%)
  blocking collectives  40.6 us (18%)
  local copies, waits for them, and re-layouts  23.2 us (10%)
  between operations  14.2 us (6%)
    ppermute x13, waiting for transfers between devices, shift(): return lax.ppermute(value, RING, pairs)  44.3 us
    pallas_call x5, Pallas kernels, rows_of(): pl.pallas_call(body, grid_spec=pltpu.PrefetchScalarGridSpec(num_scalar_pr...  29.6 us
    ppermute x13, starting transfers between devices, shift(): return lax.ppermute(value, RING, pairs)  22.7 us
    all_to_all x1, blocking collectives, per_device(): blocks = lax.all_to_all(sums, ('c',) + CHIPS + ('y',), 0, 0, tiled=True)  21.3 us
    unnamed x16, local copies, waits for them, and re-layouts  19.3 us
    all_to_all x1, blocking collectives, per_device(): pieces = lax.all_to_all(projected, CHIPS, 0, 0, tiled=True)  19.3 us
    ppermute x5, starting transfers between devices, swap(): return lax.ppermute(value, 'c', [(0, 1), (1, 0)])  15.7 us
    pallas_call x1, Pallas kernels, split_rows(): pl.pallas_call(split_body, grid=(rows // step,), in_specs=[block], out_sp...  10.8 us
  transfers between devices with their start and end apart: 20, of which 7 were waited for; matrix products, arithmetic and copies ran while one was open for 3% of the time, Pallas kernels for 10%

profile of v3, /device:TPU:1, one launch (start us, length us, event | category | flops | bytes accessed | tf_op | source)
XLA Modules:
  0.0 229.7 jit_solution(730540710001223186)
XLA Ops:
  7.9 3.2 %constant_dynamic-slice_fusion.1 = (f32[192,1152]{1,0:T(8,128)S(1)}, f32[192,1152]{1,0:T(8,128)S(1)}, f32[192,1152]{1,0:T(8,128)}, f32[192,1152]{1,0:T(8,128)S(1)}) fusion(f32[192,4608]{1,0:T(8,128)} %param.6, s32[]{:T(128)S(6)} %select_n.21, s32[]{:T(128)S(6)} %select_n.19, s32[]{:T(128)S(6)} %select_n.18, s32[]{:T(128)S(6)} %select_n.20), kind=kLoop, calls=%fused_computation.4 | loop fusion | bytes 7077904 | tf_op jit(solution)/shard_map/dynamic_slice | solution.py:238
  16.9 10.8 %shard_map.59 = (bf16[1536,3072]{1,0:T(8,128)(2,1)S(1)}, bf16[1536,3072]{1,0:T(8,128)(2,1)S(1)}) custom-call(f32[1536,3072]{1,0:T(8,128)} %a.1), custom_call_target="tpu_custom_call" | custom-call | flops 9437184 | bytes 37748736 | tf_op jit(solution)/shard_map/pallas_call | solution.py:58
  27.8 3.6 %copy-done = bf16[1536,3072]{1,0:T(8,128)(2,1)} copy-done((bf16[1536,3072]{1,0:T(8,128)(2,1)}, bf16[1536,3072]{1,0:T(8,128)(2,1)S(1)}, u32[]{:S(2)}) %copy-start) | copy-done | bytes 9437208
  31.4 3.7 %copy-done.3 = bf16[1536,3072]{1,0:T(8,128)(2,1)} copy-done((bf16[1536,3072]{1,0:T(8,128)(2,1)}, bf16[1536,3072]{1,0:T(8,128)(2,1)S(1)}, u32[]{:S(2)}) %copy-start.3) | copy-done | bytes 9437208
  35.2 18.8 %collective-permute-done.1.refs_1_ = f32[192,1152]{1,0:T(8,128)} collective-permute-done((f32[192,1152]{1,0:T(8,128)S(1)}, f32[192,1152]{1,0:T(8,128)}, u32[]{:S(2)}, u32[]{:S(2)}) %collective-permute-start.1) | collective-permute-done | bytes 884768 | tf_op jit(solution)/shard_map/ppermute | solution.py:43
  55.7 3.7 %copy-done.1 = bf16[1536,3072]{1,0:T(8,128)(2,1)S(1)} copy-done((bf16[1536,3072]{1,0:T(8,128)(2,1)S(1)}, bf16[1536,3072]{1,0:T(8,128)(2,1)}, u32[]{:S(2)}) %copy-start.1) | copy-done | bytes 9437208
  62.2 7.4 %shard_map.60 = (f32[192,512]{1,0:T(8,128)}, f32[192,512]{1,0:T(8,128)}, bf16[3072,512]{1,0:T(8,128)(2,1)S(1)}, bf16[3072,512]{1,0:T(8,128)(2,1)S(1)}) custom-call(s32[2]{0:T(128)S(1)} %get-tuple-element.92.refs_0_, bf16[1536,3072]{1,0:T(8,128)(2,1)S(1)} %copy-done.1, bf16[1536,3072]{1,0:T(8,128)(2,1)S(1)} %copy-done.1, bf16[1536,3072]{1,0:T(8,128)(2,1)} %copy-done.3, ...), custom_call_target="tpu_custom_call" | custom-call | flops 196608 | bytes 196608 | tf_op jit(solution)/shard_map/pallas_call | solution.py:110
  69.6 7.7 %shard_map.61 = (f32[192,512]{1,0:T(8,128)}, f32[192,512]{1,0:T(8,128)}) custom-call(s32[2]{0:T(128)S(1)} %get-tuple-element.93.refs_0_, bf16[1536,3072]{1,0:T(8,128)(2,1)S(1)} %copy-done.1, bf16[1536,3072]{1,0:T(8,128)(2,1)S(1)} %copy-done.1, bf16[1536,3072]{1,0:T(8,128)(2,1)} %copy-done.3, bf16[1536,3072]{1,0:T(8,128)(2,1)} %copy-done.3, ...), custom_call_target="tpu_custom_call" | custom-call | flops 196608 | bytes 196608 | tf_op jit(solution)/shard_map/pallas_call | solution.py:110
  77.2 7.2 %shard_map.62 = (f32[192,512]{1,0:T(8,128)}, f32[192,512]{1,0:T(8,128)}) custom-call(s32[2]{0:T(128)S(1)} %pad_add_fusion.2.refs_0_, bf16[1536,3072]{1,0:T(8,128)(2,1)S(1)} %copy-done.1, bf16[1536,3072]{1,0:T(8,128)(2,1)S(1)} %copy-done.1, bf16[1536,3072]{1,0:T(8,128)(2,1)} %copy-done.3, bf16[1536,3072]{1,0:T(8,128)(2,1)} %copy-done.3, ...), custom_call_target="tpu_custom_call" | custom-call | flops 196608 | bytes 196608 | tf_op jit(solution)/shard_map/pallas_call | solution.py:110
  84.4 3.7 %shard_map.63 = f32[192,512]{1,0:T(8,128)S(1)} custom-call(s32[1]{0:T(128)} %bitcast.7.refs_0_, bf16[1536,3072]{1,0:T(8,128)(2,1)S(1)} %copy-done.1, bf16[1536,3072]{1,0:T(8,128)(2,1)} %copy-done.3, bf16[3072,512]{1,0:T(8,128)(2,1)S(1)} %get-tuple-element.66.refs_5_.refs_3_, bf16[3072,512]{1,0:T(8,128)(2,1)S(1)} %get-tuple-element.67.refs_6_.refs_4_), custom_call_target="tpu_custom_call" | custom-call | flops 98304 | bytes 98304 | tf_op jit(solution)/shard_map/pallas_call | solution.py:110
  97.2 3.1 %collective-permute-done.9 = f32[192,512]{1,0:T(8,128)} collective-permute-done((f32[192,512]{1,0:T(8,128)S(1)}, f32[192,512]{1,0:T(8,128)}, u32[]{:S(2)}, u32[]{:S(2)}) %collective-permute-start.9) | collective-permute-done | bytes 393248 | tf_op jit(solution)/shard_map/ppermute | solution.py:43
  100.3 5.0 %collective-permute-start.3 = (f32[192,512]{1,0:T(8,128)}, f32[192,512]{1,0:T(8,128)}, u32[]{:S(2)}, u32[]{:S(2)}) collective-permute-start(f32[192,512]{1,0:T(8,128)} %get-tuple-element.49), channel_id=1, source_target_pairs={{0,5},{1,4},{2,7},{3,6},{4,1},{5,0},{6,3},{7,2},{8,13},{9,12},{10,... | collective-permute-start | bytes 1179656 | tf_op jit(solution)/shard_map/ppermute | solution.py:43
  105.3 3.7 %copy-done.2 = bf16[1536,3072]{1,0:T(8,128)(2,1)S(1)} copy-done((bf16[1536,3072]{1,0:T(8,128)(2,1)S(1)}, bf16[1536,3072]{1,0:T(8,128)(2,1)}, u32[]{:S(2)}) %copy-start.2) | copy-done | bytes 9437208
  110.9 3.7 %shard_map.64 = f32[192,512]{1,0:T(8,128)S(1)} custom-call(s32[1]{0:T(128)} %bitcast.8.refs_0_, bf16[1536,3072]{1,0:T(8,128)(2,1)S(1)} %copy-done.2, bf16[1536,3072]{1,0:T(8,128)(2,1)} %copy-done.3, bf16[3072,512]{1,0:T(8,128)(2,1)S(1)} %get-tuple-element.66.refs_5_.refs_3_, bf16[3072,512]{1,0:T(8,128)(2,1)S(1)} %copy-done.5), custom_call_target="tpu_custom_call" | custom-call | flops 98304 | bytes 98304 | tf_op jit(solution)/shard_map/pallas_call | solution.py:110
  116.1 10.6 %collective-permute-start.11 = (f32[192,1152]{1,0:T(8,128)}, f32[192,1152]{1,0:T(8,128)S(1)}, u32[]{:S(2)}, u32[]{:S(2)}) collective-permute-start(f32[192,1152]{1,0:T(8,128)} %collective-permute-done.refs_1_), channel_id=1, source_target_pairs={{0,8},{8,0},{1,9},{9,1},{2,10},{10,2},{3,11},{11,3},{4,12},{12,4},... | collective-permute-start | bytes 2654216 | tf_op jit(solution)/shard_map/ppermute | solution.py:47
  127.2 4.2 %collective-permute-done.3 = f32[192,512]{1,0:T(8,128)} collective-permute-done((f32[192,512]{1,0:T(8,128)}, f32[192,512]{1,0:T(8,128)}, u32[]{:S(2)}, u32[]{:S(2)}) %collective-permute-start.3) | collective-permute-done | bytes 393248 | tf_op jit(solution)/shard_map/ppermute | solution.py:43
  131.4 10.2 %collective-permute-done.4 = f32[192,512]{1,0:T(8,128)S(1)} collective-permute-done((f32[192,512]{1,0:T(8,128)}, f32[192,512]{1,0:T(8,128)S(1)}, u32[]{:S(2)}, u32[]{:S(2)}) %collective-permute-start.4) | collective-permute-done | bytes 393248 | tf_op jit(solution)/shard_map/ppermute | solution.py:43
  143.6 3.2 %collective-permute-start.14 = (f32[192,256]{1,0:T(8,128)S(1)}, f32[192,256]{1,0:T(8,128)S(1)}, u32[]{:S(2)}, u32[]{:S(2)}) collective-permute-start(f32[192,256]{1,0:T(8,128)S(1)} %get-tuple-element.91), channel_id=1, source_target_pairs={{0,8},{8,0},{1,9},{9,1},{2,10},{10,2},{3,11},{11,3},{4,12},{12,4},... | collective-permute-start | bytes 589832 | tf_op jit(solution)/shard_map/ppermute | solution.py:47
  151.3 6.9 %all-to-all-start = ((s32[128,1,36]{2,1,0:T(1,128)}), s32[128,1,36]{2,1,0:T(1,128)S(1)}, u32[]{:S(2)}, u32[]{:S(2)}) async-start(s32[128,1,36]{2,1,0:T(1,128)} %broadcast_in_dim.2), calls=%async_computation | async-start | bytes 131072 | tf_op jit(solution)/shard_map/all_to_all | solution.py:263
  160.6 8.0 %collective-permute-done.16.refs_0_ = f32[2,192,256]{2,1,0:T(8,128)} collective-permute-done((f32[2,192,256]{2,1,0:T(8,128)S(1)}, f32[2,192,256]{2,1,0:T(8,128)}, u32[]{:S(2)}, u32[]{:S(2)}) %collective-permute-start.16) | collective-permute-done | bytes 393248 | tf_op jit(solution)/shard_map/ppermute | solution.py:43
  168.6 3.8 %shard_map.66.refs_3_ = f32[16,2,8,1152]{3,2,1,0:T(8,128)S(1)} custom-call(f32[2,192,256]{2,1,0:T(8,128)} %collective-permute-done.16.refs_0_, f32[192,1152]{1,0:T(8,128)} %collective-permute-done.refs_1_, f32[192,1152]{1,0:T(8,128)S(1)} %collective-permute-done.11.refs_2_, f32[2,192,256]{2,1,0:T(8,128)} %collective-permute-done.17.refs_3_, ...), custom_call_target="tpu_custom_call" | custom-call | flops 1358954496 | bytes 5505024 | tf_op jit(solution)/shard_map/pallas_call | solution.py:159
  175.1 19.3 %all_to_all.15.pieces = f32[16,2,8,1152]{3,2,1,0:T(8,128)S(1)} all-to-all(f32[16,2,8,1152]{3,2,1,0:T(8,128)S(1)} %shard_map.67), channel_id=1, replica_groups=mesh['x'=4,'zl'=2,'c'=2,'y'=4,'zh'=2] {'x','zh','zl'}, dimensions={0} | all-to-all | bytes 2359296 | tf_op jit(solution)/shard_map/all_to_all | solution.py:271
  195.3 21.3 %all_to_all.16.blocks = f32[128,8,128]{2,1,0:T(8,128)S(1)} all-to-all(f32[128,8,128]{2,1,0:T(8,128)S(1)} %shard_map.68), channel_id=1, replica_groups=mesh['x'=4,'zl'=2,'c'=2,'y'=4,'zh'=2] {'c','x','zh','zl','y'}, dimensions={0} | all-to-all | bytes 1048576 | tf_op jit(solution)/shard_map/all_to_all | solution.py:283
  216.6 6.3 %shard_map.69 = (f32[48,512]{1,0:T(8,128)}, f32[48,48]{1,0:T(8,128)}) custom-call(f32[128,8,128]{2,1,0:T(8,128)S(1)} %all_to_all.16.blocks, s32[128,1,36]{2,1,0:T(1,128)S(1)} %all-to-all-done.bands), custom_call_target="tpu_custom_call" | custom-call | tf_op jit(solution)/shard_map/pallas_call | solution.py:284
  (53 shorter events, 36.6 us)
Async XLA Ops:
  7.2 48.6 %all-gather.2.cloned.1.call-start = ((), (), s32[]{:S(2)}) async-start(), calls=%async_computation.3 | async-start | bytes 6684672 | tf_op jit(solution)/shard_map/all_gather | solution.py:234
  11.1 24.1 %collective-permute-start = (f32[192,1152]{1,0:T(8,128)S(1)}, f32[192,1152]{1,0:T(8,128)}, u32[]{:S(2)}, u32[]{:S(2)}) collective-permute-start(f32[192,1152]{1,0:T(8,128)S(1)} %get-tuple-element.87), channel_id=1, source_target_pairs={{0,2},{1,3},{2,4},{3,5},{4,6},{5,7},{6,0},{7,1},{8,10},{9,11},{10,... | collective-permute-start | bytes 2654216 | tf_op jit(solution)/shard_map/ppermute | solution.py:43
  13.2 40.7 %collective-permute-start.1 = (f32[192,1152]{1,0:T(8,128)S(1)}, f32[192,1152]{1,0:T(8,128)}, u32[]{:S(2)}, u32[]{:S(2)}) collective-permute-start(f32[192,1152]{1,0:T(8,128)S(1)} %get-tuple-element.89), channel_id=1, source_target_pairs={{0,4},{1,5},{2,6},{3,7},{4,0},{5,1},{6,2},{7,3},{8,12},{9,13},{10,... | collective-permute-start | bytes 2654216 | tf_op jit(solution)/shard_map/ppermute | solution.py:43
  15.8 38.1 %collective-permute-start.2 = (f32[192,1152]{1,0:T(8,128)S(1)}, f32[192,1152]{1,0:T(8,128)}, u32[]{:S(2)}, u32[]{:S(2)}) collective-permute-start(f32[192,1152]{1,0:T(8,128)S(1)} %get-tuple-element.86), channel_id=1, source_target_pairs={{0,6},{1,7},{2,0},{3,1},{4,2},{5,3},{6,4},{7,5},{8,14},{9,15},{10,... | collective-permute-start | bytes 2654216 | tf_op jit(solution)/shard_map/ppermute | solution.py:43
  55.7 3.7 %copy-start.1 = (bf16[1536,3072]{1,0:T(8,128)(2,1)S(1)}, bf16[1536,3072]{1,0:T(8,128)(2,1)}, u32[]{:S(2)}) copy-start(bf16[1536,3072]{1,0:T(8,128)(2,1)} %copy-done) | copy-start | bytes 28311556
  69.6 14.8 %copy-start.4 = (bf16[3072,512]{1,0:T(8,128)(2,1)}, bf16[3072,512]{1,0:T(8,128)(2,1)S(1)}, u32[]{:S(2)}) copy-start(bf16[3072,512]{1,0:T(8,128)(2,1)S(1)} %get-tuple-element.67.refs_6_.refs_4_) | copy-start | bytes 9437188
  88.1 12.1 %collective-permute-start.9 = (f32[192,512]{1,0:T(8,128)S(1)}, f32[192,512]{1,0:T(8,128)}, u32[]{:S(2)}, u32[]{:S(2)}) collective-permute-start(f32[192,512]{1,0:T(8,128)S(1)} %shard_map.63), channel_id=1, source_target_pairs={{0,1},{1,0},{2,3},{3,2},{4,5},{5,4},{6,7},{7,6},{8,9},{9,8},{10,11... | collective-permute-start | bytes 1179656 | tf_op jit(solution)/shard_map/ppermute | solution.py:43
  90.9 23.8 %collective-permute-start.8 = (f32[192,512]{1,0:T(8,128)}, f32[192,512]{1,0:T(8,128)}, u32[]{:S(2)}, u32[]{:S(2)}) collective-permute-start(f32[192,512]{1,0:T(8,128)} %get-tuple-element.62), channel_id=1, source_target_pairs={{0,6},{1,7},{2,0},{3,1},{4,2},{5,3},{6,4},{7,5},{8,14},{9,15},{10,... | collective-permute-start | bytes 1179656 | tf_op jit(solution)/shard_map/ppermute | solution.py:43
  93.3 22.8 %collective-permute-start.7 = (f32[192,512]{1,0:T(8,128)}, f32[192,512]{1,0:T(8,128)}, u32[]{:S(2)}, u32[]{:S(2)}) collective-permute-start(f32[192,512]{1,0:T(8,128)} %get-tuple-element.61), channel_id=1, source_target_pairs={{0,7},{1,6},{2,1},{3,0},{4,3},{5,2},{6,5},{7,4},{8,15},{9,14},{10,... | collective-permute-start | bytes 1179656 | tf_op jit(solution)/shard_map/ppermute | solution.py:43
  93.9 32.8 %collective-permute-start.6 = (f32[192,512]{1,0:T(8,128)}, f32[192,512]{1,0:T(8,128)}, u32[]{:S(2)}, u32[]{:S(2)}) collective-permute-start(f32[192,512]{1,0:T(8,128)} %get-tuple-element.56), channel_id=1, source_target_pairs={{0,2},{1,3},{2,4},{3,5},{4,6},{5,7},{6,0},{7,1},{8,10},{9,11},{10,... | collective-permute-start | bytes 1179656 | tf_op jit(solution)/shard_map/ppermute | solution.py:43
  94.8 31.9 %collective-permute-start.5 = (f32[192,512]{1,0:T(8,128)}, f32[192,512]{1,0:T(8,128)}, u32[]{:S(2)}, u32[]{:S(2)}) collective-permute-start(f32[192,512]{1,0:T(8,128)} %get-tuple-element.55), channel_id=1, source_target_pairs={{0,3},{1,2},{2,5},{3,4},{4,7},{5,6},{6,1},{7,0},{8,11},{9,10},{10,... | collective-permute-start | bytes 1179656 | tf_op jit(solution)/shard_map/ppermute | solution.py:43
  100.3 31.1 %collective-permute-start.3 = (f32[192,512]{1,0:T(8,128)}, f32[192,512]{1,0:T(8,128)}, u32[]{:S(2)}, u32[]{:S(2)}) collective-permute-start(f32[192,512]{1,0:T(8,128)} %get-tuple-element.49), channel_id=1, source_target_pairs={{0,5},{1,4},{2,7},{3,6},{4,1},{5,0},{6,3},{7,2},{8,13},{9,12},{10,... | collective-permute-start | bytes 1179656 | tf_op jit(solution)/shard_map/ppermute | solution.py:43
  105.3 3.7 %copy-start.2 = (bf16[1536,3072]{1,0:T(8,128)(2,1)S(1)}, bf16[1536,3072]{1,0:T(8,128)(2,1)}, u32[]{:S(2)}) copy-start(bf16[1536,3072]{1,0:T(8,128)(2,1)} %copy-done) | copy-start | bytes 28311556
  114.6 36.0 %copy-start.7 = (s32[36]{0:T(128)S(1)}, s32[36]{0:T(128)}, u32[]{:S(2)}) copy-start(s32[36]{0:T(128)} %param.7) | copy-start | bytes 436
  114.6 28.9 %collective-permute-start.10 = (f32[192,1152]{1,0:T(8,128)}, f32[192,1152]{1,0:T(8,128)S(1)}, u32[]{:S(2)}, u32[]{:S(2)}) collective-permute-start(f32[192,1152]{1,0:T(8,128)} %get-tuple-element.74.refs_1_), channel_id=1, source_target_pairs={{0,8},{8,0},{1,9},{9,1},{2,10},{10,2},{3,11},{11,3},{4,12},{12,4},... | collective-permute-start | bytes 2654216 | tf_op jit(solution)/shard_map/ppermute | solution.py:47
  116.1 27.4 %collective-permute-start.11 = (f32[192,1152]{1,0:T(8,128)}, f32[192,1152]{1,0:T(8,128)S(1)}, u32[]{:S(2)}, u32[]{:S(2)}) collective-permute-start(f32[192,1152]{1,0:T(8,128)} %collective-permute-done.refs_1_), channel_id=1, source_target_pairs={{0,8},{8,0},{1,9},{9,1},{2,10},{10,2},{3,11},{11,3},{4,12},{12,4},... | collective-permute-start | bytes 2654216 | tf_op jit(solution)/shard_map/ppermute | solution.py:47
  126.7 16.8 %collective-permute-start.12 = (f32[192,1152]{1,0:T(8,128)}, f32[192,1152]{1,0:T(8,128)}, u32[]{:S(2)}, u32[]{:S(2)}) collective-permute-start(f32[192,1152]{1,0:T(8,128)} %collective-permute-done.1.refs_1_), channel_id=1, source_target_pairs={{0,8},{8,0},{1,9},{9,1},{2,10},{10,2},{3,11},{11,3},{4,12},{12,4},... | collective-permute-start | bytes 2654216 | tf_op jit(solution)/shard_map/ppermute | solution.py:47
  126.7 16.8 %collective-permute-start.13 = (f32[192,1152]{1,0:T(8,128)}, f32[192,1152]{1,0:T(8,128)S(1)}, u32[]{:S(2)}, u32[]{:S(2)}) collective-permute-start(f32[192,1152]{1,0:T(8,128)} %collective-permute-done.2.refs_4_), channel_id=1, source_target_pairs={{0,8},{8,0},{1,9},{9,1},{2,10},{10,2},{3,11},{11,3},{4,12},{12,4},... | collective-permute-start | bytes 2654216 | tf_op jit(solution)/shard_map/ppermute | solution.py:47
  131.4 10.2 %collective-permute-start.4 = (f32[192,512]{1,0:T(8,128)}, f32[192,512]{1,0:T(8,128)S(1)}, u32[]{:S(2)}, u32[]{:S(2)}) collective-permute-start(f32[192,512]{1,0:T(8,128)} %get-tuple-element.50), channel_id=1, source_target_pairs={{0,4},{1,5},{2,6},{3,7},{4,0},{5,1},{6,2},{7,3},{8,12},{9,13},{10,... | collective-permute-start | bytes 1179656 | tf_op jit(solution)/shard_map/ppermute | solution.py:43
  143.6 4.2 %collective-permute-start.14 = (f32[192,256]{1,0:T(8,128)S(1)}, f32[192,256]{1,0:T(8,128)S(1)}, u32[]{:S(2)}, u32[]{:S(2)}) collective-permute-start(f32[192,256]{1,0:T(8,128)S(1)} %get-tuple-element.91), channel_id=1, source_target_pairs={{0,8},{8,0},{1,9},{9,1},{2,10},{10,2},{3,11},{11,3},{4,12},{12,4},... | collective-permute-start | bytes 589832 | tf_op jit(solution)/shard_map/ppermute | solution.py:47
  147.8 20.8 %collective-permute-start.16 = (f32[2,192,256]{2,1,0:T(8,128)S(1)}, f32[2,192,256]{2,1,0:T(8,128)}, u32[]{:S(2)}, u32[]{:S(2)}) collective-permute-start(f32[2,192,256]{2,1,0:T(8,128)S(1)} %pad_maximum_fusion.refs_0_), channel_id=1, source_target_pairs={{0,2},{1,3},{2,4},{3,5},{4,6},{5,7},{6,0},{7,1},{8,10},{9,11},{10,... | collective-permute-start | bytes 1179656 | tf_op jit(solution)/shard_map/ppermute | solution.py:43
  147.9 20.7 %collective-permute-start.17 = (f32[2,192,256]{2,1,0:T(8,128)S(1)}, f32[2,192,256]{2,1,0:T(8,128)}, u32[]{:S(2)}, u32[]{:S(2)}) collective-permute-start(f32[2,192,256]{2,1,0:T(8,128)S(1)} %pad_maximum_fusion.refs_0_), channel_id=1, source_target_pairs={{0,6},{1,7},{2,0},{3,1},{4,2},{5,3},{6,4},{7,5},{8,14},{9,15},{10,... | collective-permute-start | bytes 1179656 | tf_op jit(solution)/shard_map/ppermute | solution.py:43
  150.6 21.9 %collective-permute-start.15 = (f32[2,192,256]{2,1,0:T(8,128)S(1)}, f32[2,192,256]{2,1,0:T(8,128)S(1)}, u32[]{:S(2)}, u32[]{:S(2)}) collective-permute-start(f32[2,192,256]{2,1,0:T(8,128)S(1)} %pad_maximum_fusion.refs_0_), channel_id=1, source_target_pairs={{0,4},{1,5},{2,6},{3,7},{4,0},{5,1},{6,2},{7,3},{8,12},{9,13},{10,... | collective-permute-start | bytes 1179656 | tf_op jit(solution)/shard_map/ppermute | solution.py:43
  151.3 23.9 %all-to-all-start = ((s32[128,1,36]{2,1,0:T(1,128)}), s32[128,1,36]{2,1,0:T(1,128)S(1)}, u32[]{:S(2)}, u32[]{:S(2)}) async-start(s32[128,1,36]{2,1,0:T(1,128)} %broadcast_in_dim.2), calls=%async_computation | async-start | bytes 131072 | tf_op jit(solution)/shard_map/all_to_all | solution.py:263
  (4 other events, 11.9 us)
Sparse Core Ops, SparseCore 0:
  9.7 45.9 all-gather.1

commit v4 on v2

--- a/solution.py
+++ b/solution.py
@@ -68,56 +68,39 @@
     )(a)
 
 
-def add_step(out, value):
-    @pl.when(pl.program_id(0) == 0)
-    def _():
-        out[...] = value
-
-    @pl.when(pl.program_id(0) > 0)
-    def _():
-        out[...] += value
-
-
-def first_body(at, a_high, a_low, s, out, s_high, s_low):
+def rows_body(a_high, a_low, s, out):
     sh, sl = split(s[...])
-    s_high[...] = sh
-    s_low[...] = sl
     ah = a_high[...]
-    add_step(out, dot(ah, sh) + dot(ah, sl) + dot(a_low[...], sh))
-
-
-def next_body(at, a_high, a_low, s_high, s_low, out):
-    ah = a_high[...]
-    sh = s_high[...]
-    add_step(out, dot(ah, sh) + dot(ah, s_low[...]) + dot(a_low[...], sh))
-
-
-def rows_of(at, a_high, a_low, maps):
-    inner, cols = maps[0].shape
-    step = 1024
-    tall = 2 * ROWS
-    a_block = pl.BlockSpec((tall, step), lambda k, at: (at[0], k))
-    s_block = pl.BlockSpec((step, cols), lambda k, at: (k, 0))
-    o_block = pl.BlockSpec((tall, cols), lambda k, at: (0, 0))
-    o_shape = jax.ShapeDtypeStruct((tall, cols), F32)
-    parts = jax.ShapeDtypeStruct((inner, cols), BF16)
-    first = len(maps) == 1
-    return pl.pallas_call(
-        first_body if first else next_body,
-        grid_spec=pltpu.PrefetchScalarGridSpec(
-            num_scalar_prefetch=1,
-            grid=(inner // step,),
-            in_specs=[a_block, a_block] + [s_block] * len(maps),
-            out_specs=[o_block, s_block, s_block] if first else o_block,
-        ),
-        out_shape=[o_shape, parts, parts] if first else o_shape,
+    found = dot(ah, sh) + dot(ah, sl) + dot(a_low[...], sh)
+
+    for core in range(2):
+        part = found[:, HALF * core : HALF * core + HALF].reshape(8, ROWS, HALF)
+        mine = pl.ds(8 * core, 8)
+
+        @pl.when(pl.program_id(0) == 0)
+        def _():
+            out[mine] = part
+
+        @pl.when(pl.program_id(0) > 0)
+        def _():
+            out[mine] += part
+
+
+def rows_of(a_high, a_low, maps):
+    tall, inner = a_high.shape
+    step = 512
+    a_block = pl.BlockSpec((tall, step), lambda k: (0, k))
+    return pl.pallas_call(
+        rows_body,
+        grid=(inner // step,),
+        in_specs=[a_block, a_block, pl.BlockSpec((step, NMAPS), lambda k: (k, 0))],
+        out_specs=pl.BlockSpec((16, ROWS, HALF), lambda k: (0, 0, 0)),
+        out_shape=jax.ShapeDtypeStruct((16, ROWS, HALF), F32),
         compiler_params=limit(58),
         cost_estimate=pl.CostEstimate(
-            flops=6 * tall * inner * cols,
-            bytes_accessed=4 * inner * (tall + cols),
-            transcendentals=0,
+            flops=tall * inner, bytes_accessed=tall * inner, transcendentals=0
         ),
-    )(jnp.reshape(at, (1,)).astype(jnp.int32), a_high, a_low, *maps)
+    )(a_high, a_low, maps)
 
 
 def project_body(terms, begun, *refs):
@@ -131,9 +114,9 @@
     for n in range(0, SPAN, cols):
         total = None
         for t in range(terms):
-            own, other = refs[3 * t + 1 : 3 * t + 3]
+            one, two = refs[3 * t + 1 : 3 * t + 3]
             th, tl = split(
-                jnp.concatenate([own[:, n : n + cols], other[:, n : n + cols]], axis=0)
+                jnp.concatenate([one[:, n : n + cols], two[:, n : n + cols]], axis=0)
             )
             term = dot(left[t], jnp.concatenate([th, tl, th], axis=0))
             total = term if total is None else total + term
@@ -198,34 +181,30 @@
 
 def per_device(inv_cov, sim_maps, templates, band_index):
     y = lax.axis_index("y")
-    zh = lax.axis_index("zh")
     c = lax.axis_index("c")
 
     gathered = lax.all_gather(sim_maps, BLK, axis=0, tiled=True)
+
+    bands = lax.all_to_all(
+        jnp.broadcast_to(band_index[None, None, :], (128, 1, 36)), EVERY, 0, 0, tiled=True
+    )
+    bands, templates = lax.optimization_barrier((bands, templates))
 
     own = []
     for dy in range(NY):
         block = lax.dynamic_slice(templates, (0, lax.rem(y + dy, NY) * SPAN), (ROWS, SPAN))
         own.append(shift(block, dy, 0) if dy else block)
 
-    bands = lax.all_to_all(
-        jnp.broadcast_to(band_index[None, None, :], (128, 1, 36)), EVERY, 0, 0, tiled=True
-    )
     a_high, a_low = split_rows(inv_cov)
-    gathered, a_high, a_low, bands, *own = lax.optimization_barrier(
-        (gathered, a_high, a_low, bands, *own)
-    )
-
-    maps = (gathered,)
-    sent = []
-    for dy in (2, 1, 3, 0):
-        found = rows_of(lax.rem(y + dy, NY), a_high, a_low, maps)
-        if len(maps) == 1:
-            found, *maps = found
-        far = lax.dynamic_slice(found, ((1 - zh) * ROWS, 0), (ROWS, NMAPS))
-        near = lax.dynamic_slice(found, (zh * ROWS, 0), (ROWS, NMAPS))
-        sent.append(shift(far, dy, 1))
-        sent.append(shift(near, dy, 0) if dy else near)
+    gathered, a_high, a_low = lax.optimization_barrier((gathered, a_high, a_low))
+    partial = rows_of(a_high, a_low, gathered)
+    partial, bands, *own = lax.optimization_barrier((partial, bands, *own))
+    terms = lax.all_to_all(partial, ("c",) + RING, 0, 0, tiled=True)
+
+    other = [swap(v) for v in own]
+    spread = [
+        (jnp.where(c == 0, a, b), jnp.where(c == 0, b, a)) for a, b in zip(own, other)
+    ]
 
     bands = bands.reshape(NMODES)
     labels = jnp.arange(NBANDS, dtype=jnp.int32)
@@ -234,20 +213,13 @@
     lane = jnp.arange(128, dtype=jnp.int32)
     names = jnp.where(lane < 2 * NBANDS, lane % NBANDS, -1)
     onehot = (mine[:, None] == names[None, :]).astype(F32)
-
-    rows = sent[0]
-    for value in sent[1:]:
-        rows = rows + value
-    rows, count, onehot, *own = lax.optimization_barrier((rows, count, onehot, *own))
-
-    keep = lax.dynamic_slice(rows, (0, c * HALF), (ROWS, HALF))
-    give = lax.dynamic_slice(rows, (0, (1 - c) * HALF), (ROWS, HALF))
-    pair = jnp.stack([keep, swap(give)])
-    around = [shift(pair, dy, 0) if dy else pair for dy in range(NY)]
-    other = [swap(v) for v in own]
-    projected = project([(around[0], own[0], other[0])])
-    projected = project([(around[d], own[d], other[d]) for d in (1, 3)], projected)
-    projected = project([(around[2], own[2], other[2])], projected)
+    terms, count, onehot, spread = lax.optimization_barrier((terms, count, onehot, spread))
+
+    rows = jnp.sum(terms.reshape(2, 8, ROWS, HALF), axis=1)
+    around = [shift(rows, dy, 0) if dy else rows for dy in range(NY)]
+    projected = project([(around[0], *spread[0])])
+    projected = project([(around[d], *spread[d]) for d in (1, 3)], projected)
+    projected = project([(around[2], *spread[2])], projected)
 
     pieces = lax.all_to_all(projected, CHIPS, 0, 0, tiled=True)
     sums = pl.pallas_call(

time: 225 us -> 202 us (0.90)
  starting transfers between devices: 52.5 us -> 35.2 us
  Pallas kernels: 57.7 us -> 45.4 us
  waiting for transfers between devices: 61.4 us -> 72.4 us
  local copies, waits for them, and re-layouts: 14.3 us -> 5.34 us
  other arithmetic: 5.39 us -> 11.6 us
    all_to_all x0 -> x1, waiting for transfers between devices: none -> 33 us  [per_device(): terms = lax.all_to_all(partial, ('c',) + RING, 0, 0, tiled=True)]
    ppermute x13 -> x6, waiting for transfers between devices: 31 us -> 13 us  [shift(): return lax.ppermute(value, RING, pairs)]
    ppermute x13 -> x6, starting transfers between devices: 21.9 us -> 5.71 us  [shift(): return lax.ppermute(value, RING, pairs)]
    pallas_call x4 -> x1, Pallas kernels: 33.8 us -> 21.6 us  [rows_of(): pl.pallas_call(rows_body, grid=(inner // step,), in_specs=[a_block, a_blo...]
    all_to_all x1, starting transfers between devices: 16.9 us -> 9.65 us  [per_device(): blocks = lax.all_to_all(sums, ('c',) + CHIPS + ('y',), 0, 0, tiled=True)]
    dynamic_slice x4 -> x0, local copies, waits for them, and re-layouts: 7.05 us -> none  [the longest x3 5.88 us: per_device(): far = lax.dynamic_slice(found, ((1 - zh) * ROWS, 0), (ROWS, NMAPS))]
    all_to_all x0 -> x1, starting transfers between devices: none -> 6.78 us  [per_device(): terms = lax.all_to_all(partial, ('c',) + RING, 0, 0, tiled=True)]
    select_n x0 -> x4, other arithmetic: none -> 6.46 us  [per_device(): jnp.where(c == 0, b, a)]
  transfers between devices with their start and end apart: 21 -> 14, of which waited for: 7 -> 7; matrix products, arithmetic and copies ran while one was open for 7% -> 7% of each run, Pallas kernels for 16% -> 21%
where the time goes in v4:
time: 202 us
  waiting for transfers between devices  72.4 us (36%)
  Pallas kernels  45.4 us (22%)
  starting transfers between devices  35.2 us (17%)
  blocking collectives  17.4 us (9%)
  between operations  14.2 us (7%)
  other arithmetic  11.6 us (6%)
  local copies, waits for them, and re-layouts  5.34 us (3%)
    all_to_all x1, waiting for transfers between devices, per_device(): terms = lax.all_to_all(partial, ('c',) + RING, 0, 0, tiled=True)  33 us
    pallas_call x1, Pallas kernels, rows_of(): pl.pallas_call(rows_body, grid=(inner // step,), in_specs=[a_block, a_blo...  21.6 us
    all_to_all x1, blocking collectives, per_device(): pieces = lax.all_to_all(projected, CHIPS, 0, 0, tiled=True)  17.4 us
    pallas_call x1, Pallas kernels, split_rows(): pl.pallas_call(split_body, grid=(rows // step,), in_specs=[block], out_sp...  17 us
    all_to_all x1, waiting for transfers between devices, per_device(): blocks = lax.all_to_all(sums, ('c',) + CHIPS + ('y',), 0, 0, tiled=True)  13.2 us
    ppermute x6, waiting for transfers between devices, shift(): return lax.ppermute(value, RING, pairs)  13 us
    all_to_all x1, starting transfers between devices, per_device(): lax.all_to_all(jnp.broadcast_to(band_index[None, None, :], (128, 1, 36)),...  12 us
    all_to_all x1, waiting for transfers between devices, per_device(): lax.all_to_all(jnp.broadcast_to(band_index[None, None, :], (128, 1, 36)),...  9.71 us
  transfers between devices with their start and end apart: 14, of which 7 were waited for; matrix products, arithmetic and copies ran while one was open for 7% of the time, Pallas kernels for 21%

profile of v4, /device:TPU:1, one launch (start us, length us, event | category | flops | bytes accessed | tf_op | source)
XLA Modules:
  0.0 201.6 jit_solution(15025847567475532222)
XLA Ops:
  7.9 1.3 broadcast_in_dim.8
  9.2 12.0 %all-to-all-start = ((s32[128,1,36]{2,1,0:T(1,128)}), s32[128,1,36]{2,1,0:T(1,128)}, u32[]{:S(2)}, u32[]{:S(2)}) async-start(s32[128,1,36]{2,1,0:T(1,128)} %broadcast_in_dim.8), calls=%async_computation | async-start | bytes 131072 | tf_op jit(solution)/shard_map/all_to_all | solution.py:188
  21.2 9.7 %all-to-all-done = s32[128,1,36]{2,1,0:T(1,128)} async-done(((s32[128,1,36]{2,1,0:T(1,128)}), s32[128,1,36]{2,1,0:T(1,128)}, u32[]{:S(2)}, u32[]{:S(2)}) %all-to-all-start) | async-done | bytes 18464 | tf_op jit(solution)/shard_map/all_to_all | solution.py:188
  30.9 3.2 %constant_dynamic-slice_fusion = (f32[192,1152]{1,0:T(8,128)S(1)}, f32[192,1152]{1,0:T(8,128)S(1)}, f32[192,1152]{1,0:T(8,128)}, f32[192,1152]{1,0:T(8,128)S(1)}) fusion(f32[192,4608]{1,0:T(8,128)} %param.6, s32[]{:T(128)S(6)} %select_n.73, s32[]{:T(128)S(6)} %select_n.72, s32[]{:T(128)S(6)} %select_n.71, s32[]{:T(128)S(6)} %select_n.70), kind=kLoop, calls=%fused_computation.14 | loop fusion | bytes 7077904 | tf_op jit(solution)/shard_map/dynamic_slice | solution.py:195
  34.5 1.3 collective-permute-start.1
  35.8 1.2 collective-permute-start.2
  37.0 17.0 %shard_map.59 = (bf16[1536,3072]{1,0:T(8,128)(2,1)}, bf16[1536,3072]{1,0:T(8,128)(2,1)}) custom-call(f32[1536,3072]{1,0:T(8,128)} %a.1), custom_call_target="tpu_custom_call" | custom-call | flops 9437184 | bytes 37748736 | tf_op jit(solution)/shard_map/pallas_call | solution.py:58
  54.0 2.3 %all-gather.2.cloned.1.call-done.s = f32[3072,512]{1,0:T(8,128)} async-done(((f32[192,512]{1,0:T(8,128)}), f32[3072,512]{1,0:T(8,128)}) %all-gather.2.cloned.1.call-update) | async-done | bytes 6291472 | tf_op jit(solution)/shard_map/all_gather | solution.py:186
  56.3 21.6 %shard_map.60 = f32[16,192,256]{2,1,0:T(8,128)} custom-call(bf16[1536,3072]{1,0:T(8,128)(2,1)} %get-tuple-element.28.a_high, bf16[1536,3072]{1,0:T(8,128)(2,1)} %get-tuple-element.29.a_low, f32[3072,512]{1,0:T(8,128)} %all-gather.2.cloned.1.call-done.s), custom_call_target="tpu_custom_call" | custom-call | flops 4718592 | bytes 4718592 | tf_op jit(solution)/shard_map/pallas_call | solution.py:93
  78.2 6.8 %all-to-all-start.1 = ((f32[16,192,256]{2,1,0:T(8,128)}), f32[16,192,256]{2,1,0:T(8,128)}, u32[]{:S(2)}, u32[]{:S(2)}) async-start(f32[16,192,256]{2,1,0:T(8,128)} %shard_map.60), calls=%async_computation.1 | async-start | bytes 6291456 | tf_op jit(solution)/shard_map/all_to_all | solution.py:202
  85.5 1.6 reduce.3
  89.4 1.3 broadcast_select_fusion.6
  91.3 2.5 %broadcast_select_fusion.2 = (f32[192,1152]{1,0:T(8,128)}, f32[192,1152]{1,0:T(8,128)}) fusion(f32[192,1152]{1,0:T(8,128)S(1)} %collective-permute-done.5, f32[192,1152]{1,0:T(8,128)} %collective-permute-done.1, pred[]{:T(512)S(6)} %eq.47), kind=kLoop, calls=%fused_computation.6 | loop fusion | flops 442368 | bytes 3538945 | tf_op jit(solution)/shard_map/jit(_where)/select_n | solution.py:206
  93.8 2.5 %broadcast_select_fusion = (f32[192,1152]{1,0:T(8,128)}, f32[192,1152]{1,0:T(8,128)}) fusion(f32[192,1152]{1,0:T(8,128)S(1)} %collective-permute-done.6, f32[192,1152]{1,0:T(8,128)} %collective-permute-done.2, pred[]{:T(512)S(6)} %eq.47), kind=kLoop, calls=%fused_computation.4 | loop fusion | flops 442368 | bytes 3538945 | tf_op jit(solution)/shard_map/jit(_where)/select_n | solution.py:206
  96.3 33.0 %all-to-all-done.1 = f32[16,192,256]{2,1,0:T(8,128)} async-done(((f32[16,192,256]{2,1,0:T(8,128)}), f32[16,192,256]{2,1,0:T(8,128)}, u32[]{:S(2)}, u32[]{:S(2)}) %all-to-all-start.1) | async-done | bytes 3145760 | tf_op jit(solution)/shard_map/all_to_all | solution.py:202
  129.3 2.3 %bitcast_reduce_fusion.refs_0_ = f32[2,192,256]{2,1,0:T(8,128)S(1)} fusion(f32[16,192,256]{2,1,0:T(8,128)} %all-to-all-done.1), kind=kLoop, calls=%fused_computation | loop fusion | flops 688128 | bytes 3538944 | tf_op jit(solution)/shard_map/reduce_sum | solution.py:218
  131.7 2.7 %collective-permute-start.9 = (f32[2,192,256]{2,1,0:T(8,128)S(1)}, f32[2,192,256]{2,1,0:T(8,128)S(1)}, u32[]{:S(2)}, u32[]{:S(2)}) collective-permute-start(f32[2,192,256]{2,1,0:T(8,128)S(1)} %bitcast_reduce_fusion.refs_0_), channel_id=1, source_target_pairs={{0,6},{1,7},{2,0},{3,1},{4,2},{5,3},{6,4},{7,5},{8,14},{9,15},{10,... | collective-permute-start | bytes 1179656 | tf_op jit(solution)/shard_map/ppermute | solution.py:43
  135.7 7.0 %collective-permute-done.8.refs_0_ = f32[2,192,256]{2,1,0:T(8,128)S(1)} collective-permute-done((f32[2,192,256]{2,1,0:T(8,128)S(1)}, f32[2,192,256]{2,1,0:T(8,128)S(1)}, u32[]{:S(2)}, u32[]{:S(2)}) %collective-permute-start.8) | collective-permute-done | bytes 393248 | tf_op jit(solution)/shard_map/ppermute | solution.py:43
  142.7 2.2 %shard_map.62.refs_3_ = f32[16,2,8,1152]{3,2,1,0:T(8,128)S(1)} custom-call(f32[2,192,256]{2,1,0:T(8,128)S(1)} %collective-permute-done.8.refs_0_, f32[192,1152]{1,0:T(8,128)S(1)} %get-tuple-element.42.refs_1_, f32[192,1152]{1,0:T(8,128)S(1)} %get-tuple-element.43.refs_2_, f32[2,192,256]{2,1,0:T(8,128)S(1)} %collective-permute-done.9.refs_3_, ...), custom_call_target="tpu_custom_call" | custom-call | flops 1358954496 | bytes 5505024 | tf_op jit(solution)/shard_map/pallas_call | solution.py:136
  144.9 6.0 %collective-permute-done.7.refs_0_ = f32[2,192,256]{2,1,0:T(8,128)S(1)} collective-permute-done((f32[2,192,256]{2,1,0:T(8,128)S(1)}, f32[2,192,256]{2,1,0:T(8,128)S(1)}, u32[]{:S(2)}, u32[]{:S(2)}) %collective-permute-start.7) | collective-permute-done | bytes 393248 | tf_op jit(solution)/shard_map/ppermute | solution.py:43
  152.1 17.4 %all_to_all.20.pieces = f32[16,2,8,1152]{3,2,1,0:T(8,128)S(1)} all-to-all(f32[16,2,8,1152]{3,2,1,0:T(8,128)S(1)} %shard_map.63), channel_id=1, replica_groups=mesh['x'=4,'zl'=2,'c'=2,'y'=4,'zh'=2] {'x','zh','zl'}, dimensions={0} | all-to-all | bytes 2359296 | tf_op jit(solution)/shard_map/all_to_all | solution.py:224
  169.5 1.3 shard_map.64
  170.8 9.6 %all-to-all-start.3 = ((f32[128,8,128]{2,1,0:T(8,128)}), f32[128,8,128]{2,1,0:T(8,128)S(1)}, u32[]{:S(2)}, u32[]{:S(2)}) async-start(f32[128,8,128]{2,1,0:T(8,128)} %shard_map.64), calls=%async_computation.3 | async-start | bytes 1048576 | tf_op jit(solution)/shard_map/all_to_all | solution.py:230
  180.5 13.2 %all-to-all-done.3.blocks = f32[128,8,128]{2,1,0:T(8,128)S(1)} async-done(((f32[128,8,128]{2,1,0:T(8,128)}), f32[128,8,128]{2,1,0:T(8,128)S(1)}, u32[]{:S(2)}, u32[]{:S(2)}) %all-to-all-start.3) | async-done | bytes 524320 | tf_op jit(solution)/shard_map/all_to_all | solution.py:230
  (42 shorter events, 8.5 us)
Async XLA Ops:
  7.2 49.1 %all-gather.2.cloned.1.call-start = ((), (), s32[]{:S(2)}) async-start(), calls=%async_computation.4 | async-start | bytes 6684672 | tf_op jit(solution)/shard_map/all_gather | solution.py:186
  9.2 21.7 %all-to-all-start = ((s32[128,1,36]{2,1,0:T(1,128)}), s32[128,1,36]{2,1,0:T(1,128)}, u32[]{:S(2)}, u32[]{:S(2)}) async-start(s32[128,1,36]{2,1,0:T(1,128)} %broadcast_in_dim.8), calls=%async_computation | async-start | bytes 131072 | tf_op jit(solution)/shard_map/all_to_all | solution.py:188
  34.1 43.7 %collective-permute-start = (f32[192,1152]{1,0:T(8,128)}, f32[192,1152]{1,0:T(8,128)S(1)}, u32[]{:S(2)}, u32[]{:S(2)}) collective-permute-start(f32[192,1152]{1,0:T(8,128)} %get-tuple-element.52), channel_id=1, source_target_pairs={{0,2},{1,3},{2,4},{3,5},{4,6},{5,7},{6,0},{7,1},{8,10},{9,11},{10,... | collective-permute-start | bytes 2654216 | tf_op jit(solution)/shard_map/ppermute | solution.py:43
  34.5 43.4 %collective-permute-start.1 = (f32[192,1152]{1,0:T(8,128)S(1)}, f32[192,1152]{1,0:T(8,128)}, u32[]{:S(2)}, u32[]{:S(2)}) collective-permute-start(f32[192,1152]{1,0:T(8,128)S(1)} %get-tuple-element.51), channel_id=1, source_target_pairs={{0,4},{1,5},{2,6},{3,7},{4,0},{5,1},{6,2},{7,3},{8,12},{9,13},{10,... | collective-permute-start | bytes 2654216 | tf_op jit(solution)/shard_map/ppermute | solution.py:43
  35.8 42.1 %collective-permute-start.2 = (f32[192,1152]{1,0:T(8,128)S(1)}, f32[192,1152]{1,0:T(8,128)}, u32[]{:S(2)}, u32[]{:S(2)}) collective-permute-start(f32[192,1152]{1,0:T(8,128)S(1)} %get-tuple-element.50), channel_id=1, source_target_pairs={{0,6},{1,7},{2,0},{3,1},{4,2},{5,3},{6,4},{7,5},{8,14},{9,15},{10,... | collective-permute-start | bytes 2654216 | tf_op jit(solution)/shard_map/ppermute | solution.py:43
  77.9 9.4 %copy-start.5 = (f32[192,1152]{1,0:T(8,128)}, f32[192,1152]{1,0:T(8,128)S(1)}, u32[]{:S(2)}) copy-start(f32[192,1152]{1,0:T(8,128)S(1)} %collective-permute-done) | copy-start | bytes 2654212
  77.9 11.5 %collective-permute-start.3 = (f32[192,1152]{1,0:T(8,128)S(1)}, f32[192,1152]{1,0:T(8,128)}, u32[]{:S(2)}, u32[]{:S(2)}) collective-permute-start(f32[192,1152]{1,0:T(8,128)S(1)} %get-tuple-element.35), channel_id=1, source_target_pairs={{0,8},{8,0},{1,9},{9,1},{2,10},{10,2},{3,11},{11,3},{4,12},{12,4},... | collective-permute-start | bytes 2654216 | tf_op jit(solution)/shard_map/ppermute | solution.py:47
  78.2 51.1 %all-to-all-start.1 = ((f32[16,192,256]{2,1,0:T(8,128)}), f32[16,192,256]{2,1,0:T(8,128)}, u32[]{:S(2)}, u32[]{:S(2)}) async-start(f32[16,192,256]{2,1,0:T(8,128)} %shard_map.60), calls=%async_computation.1 | async-start | bytes 6291456 | tf_op jit(solution)/shard_map/all_to_all | solution.py:202
  87.3 3.3 %collective-permute-start.4 = (f32[192,1152]{1,0:T(8,128)S(1)}, f32[192,1152]{1,0:T(8,128)S(1)}, u32[]{:S(2)}, u32[]{:S(2)}) collective-permute-start(f32[192,1152]{1,0:T(8,128)S(1)} %collective-permute-done), channel_id=1, source_target_pairs={{0,8},{8,0},{1,9},{9,1},{2,10},{10,2},{3,11},{11,3},{4,12},{12,4},... | collective-permute-start | bytes 2654216 | tf_op jit(solution)/shard_map/ppermute | solution.py:47
  87.5 3.1 %copy-start.6 = (f32[192,1152]{1,0:T(8,128)S(1)}, f32[192,1152]{1,0:T(8,128)}, u32[]{:S(2)}) copy-start(f32[192,1152]{1,0:T(8,128)} %copy-done.5) | copy-start | bytes 2654212
  87.5 3.8 %collective-permute-start.5 = (f32[192,1152]{1,0:T(8,128)}, f32[192,1152]{1,0:T(8,128)S(1)}, u32[]{:S(2)}, u32[]{:S(2)}) collective-permute-start(f32[192,1152]{1,0:T(8,128)} %collective-permute-done.1), channel_id=1, source_target_pairs={{0,8},{8,0},{1,9},{9,1},{2,10},{10,2},{3,11},{11,3},{4,12},{12,4},... | collective-permute-start | bytes 2654216 | tf_op jit(solution)/shard_map/ppermute | solution.py:47
  87.9 5.9 %collective-permute-start.6 = (f32[192,1152]{1,0:T(8,128)}, f32[192,1152]{1,0:T(8,128)S(1)}, u32[]{:S(2)}, u32[]{:S(2)}) collective-permute-start(f32[192,1152]{1,0:T(8,128)} %collective-permute-done.2), channel_id=1, source_target_pairs={{0,8},{8,0},{1,9},{9,1},{2,10},{10,2},{3,11},{11,3},{4,12},{12,4},... | collective-permute-start | bytes 2654216 | tf_op jit(solution)/shard_map/ppermute | solution.py:47
  129.3 13.4 %copy-start = (f32[192,1152]{1,0:T(8,128)S(1)}, f32[192,1152]{1,0:T(8,128)}, u32[]{:S(2)}) copy-start(f32[192,1152]{1,0:T(8,128)} %get-tuple-element.45.refs_5_) | copy-start | bytes 2654212
  129.3 13.4 %copy-start.1 = (f32[192,1152]{1,0:T(8,128)S(1)}, f32[192,1152]{1,0:T(8,128)}, u32[]{:S(2)}) copy-start(f32[192,1152]{1,0:T(8,128)} %get-tuple-element.44.refs_4_) | copy-start | bytes 2654212
  131.6 11.1 %collective-permute-start.8 = (f32[2,192,256]{2,1,0:T(8,128)S(1)}, f32[2,192,256]{2,1,0:T(8,128)S(1)}, u32[]{:S(2)}, u32[]{:S(2)}) collective-permute-start(f32[2,192,256]{2,1,0:T(8,128)S(1)} %bitcast_reduce_fusion.refs_0_), channel_id=1, source_target_pairs={{0,2},{1,3},{2,4},{3,5},{4,6},{5,7},{6,0},{7,1},{8,10},{9,11},{10,... | collective-permute-start | bytes 1179656 | tf_op jit(solution)/shard_map/ppermute | solution.py:43
  131.7 11.1 %collective-permute-start.9 = (f32[2,192,256]{2,1,0:T(8,128)S(1)}, f32[2,192,256]{2,1,0:T(8,128)S(1)}, u32[]{:S(2)}, u32[]{:S(2)}) collective-permute-start(f32[2,192,256]{2,1,0:T(8,128)S(1)} %bitcast_reduce_fusion.refs_0_), channel_id=1, source_target_pairs={{0,6},{1,7},{2,0},{3,1},{4,2},{5,3},{6,4},{7,5},{8,14},{9,15},{10,... | collective-permute-start | bytes 1179656 | tf_op jit(solution)/shard_map/ppermute | solution.py:43
  134.3 16.5 %collective-permute-start.7 = (f32[2,192,256]{2,1,0:T(8,128)S(1)}, f32[2,192,256]{2,1,0:T(8,128)S(1)}, u32[]{:S(2)}, u32[]{:S(2)}) collective-permute-start(f32[2,192,256]{2,1,0:T(8,128)S(1)} %bitcast_reduce_fusion.refs_0_), channel_id=1, source_target_pairs={{0,4},{1,5},{2,6},{3,7},{4,0},{5,1},{6,2},{7,3},{8,12},{9,13},{10,... | collective-permute-start | bytes 1179656 | tf_op jit(solution)/shard_map/ppermute | solution.py:43
  135.7 15.2 %copy-start.2 = (f32[192,1152]{1,0:T(8,128)S(1)}, f32[192,1152]{1,0:T(8,128)}, u32[]{:S(2)}) copy-start(f32[192,1152]{1,0:T(8,128)} %get-tuple-element.41.refs_2_) | copy-start | bytes 2654212
  135.7 15.2 %copy-start.3 = (f32[192,1152]{1,0:T(8,128)S(1)}, f32[192,1152]{1,0:T(8,128)}, u32[]{:S(2)}) copy-start(f32[192,1152]{1,0:T(8,128)} %get-tuple-element.40.refs_1_) | copy-start | bytes 2654212
  144.9 24.6 %copy-start.4 = (f32[1152,128]{1,0:T(8,128)S(1)}, f32[1152,128]{1,0:T(8,128)}, u32[]{:S(2)}) copy-start(f32[1152,128]{1,0:T(8,128)} %compare_convert_fusion.onehot) | copy-start | bytes 1769476
  170.8 22.9 %all-to-all-start.3 = ((f32[128,8,128]{2,1,0:T(8,128)}), f32[128,8,128]{2,1,0:T(8,128)S(1)}, u32[]{:S(2)}, u32[]{:S(2)}) async-start(f32[128,8,128]{2,1,0:T(8,128)} %shard_map.64), calls=%async_computation.3 | async-start | bytes 1048576 | tf_op jit(solution)/shard_map/all_to_all | solution.py:230
Sparse Core Ops, SparseCore 0:
  9.7 46.5 all-gather.1

commit v5 on v4

--- a/solution.py
+++ b/solution.py
@@ -8,13 +8,13 @@
 NMODES = 4608
 NBANDS = 48
 NMAPS = 512
-NY = 4
-SPAN = NMODES // NY
+NX = 4
+SPAN = NMODES // NX
 HALF = NMAPS // 2
 ROWS = 192
 BLK = ("x", "zl", "c")
 RING = ("y", "zh")
-CHIPS = ("x", "zh", "zl")
+CHIPS = ("y", "zh", "zl")
 EVERY = BLK + RING
 MIB = 2**20
 F32 = jnp.float32
@@ -34,13 +34,8 @@
     return pltpu.CompilerParams(vmem_limit_bytes=mib * MIB)
 
 
-def shift(value, dy, dz):
-    pairs = [
-        (y * 2 + z, ((y + dy) % NY) * 2 + (z + dz) % 2)
-        for y in range(NY)
-        for z in range(2)
-    ]
-    return lax.ppermute(value, RING, pairs)
+def shift(value, step):
+    return lax.ppermute(value, "x", [(n, (n + step) % NX) for n in range(NX)])
 
 
 def swap(value):
@@ -48,7 +43,15 @@
 
 
 def split_body(a, high, low):
-    high[...], low[...] = split(a[...])
+    for core in range(2):
+        for n in range(4):
+            at = 4 * n + core
+            value = jnp.concatenate(
+                [a[:, at * ROWS : (at + 1) * ROWS], a[:, (at + 2) * ROWS : (at + 3) * ROWS]],
+                axis=1,
+            )
+            to = pl.ds((core * 4 + n) * 2 * ROWS, 2 * ROWS)
+            high[:, to], low[:, to] = split(value)
 
 
 def split_rows(a):
@@ -68,39 +71,51 @@
     )(a)
 
 
-def rows_body(a_high, a_low, s, out):
+def rows_body(begun, core, a_high, a_low, s, *refs):
+    out = refs[-1]
     sh, sl = split(s[...])
     ah = a_high[...]
     found = dot(ah, sh) + dot(ah, sl) + dot(a_low[...], sh)
 
-    for core in range(2):
-        part = found[:, HALF * core : HALF * core + HALF].reshape(8, ROWS, HALF)
-        mine = pl.ds(8 * core, 8)
+    for half in range(2):
+        part = found[:, HALF * half : HALF * half + HALF].reshape(8, ROWS, HALF)
+        mine = pl.ds(8 * half, 8)
 
         @pl.when(pl.program_id(0) == 0)
         def _():
-            out[mine] = part
+            out[mine] = part + refs[0][mine] if begun else part
 
         @pl.when(pl.program_id(0) > 0)
         def _():
             out[mine] += part
 
 
-def rows_of(a_high, a_low, maps):
-    tall, inner = a_high.shape
+def rows_of(core, a_high, a_low, maps, begun=None):
+    tall, inner = a_high.shape[0], maps.shape[0]
     step = 512
-    a_block = pl.BlockSpec((tall, step), lambda k: (0, k))
-    return pl.pallas_call(
-        rows_body,
-        grid=(inner // step,),
-        in_specs=[a_block, a_block, pl.BlockSpec((step, NMAPS), lambda k: (k, 0))],
-        out_specs=pl.BlockSpec((16, ROWS, HALF), lambda k: (0, 0, 0)),
+    steps = inner // step
+    a_block = pl.BlockSpec((tall, step), lambda k, core: (0, core[0] * steps + k))
+    whole = pl.BlockSpec((16, ROWS, HALF), lambda k, core: (0, 0, 0))
+    more = [] if begun is None else [begun]
+
+    def body(*refs):
+        rows_body(len(more), *refs)
+
+    return pl.pallas_call(
+        body,
+        grid_spec=pltpu.PrefetchScalarGridSpec(
+            num_scalar_prefetch=1,
+            grid=(steps,),
+            in_specs=[a_block, a_block, pl.BlockSpec((step, NMAPS), lambda k, core: (k, 0))]
+            + [whole] * len(more),
+            out_specs=whole,
+        ),
         out_shape=jax.ShapeDtypeStruct((16, ROWS, HALF), F32),
         compiler_params=limit(58),
         cost_estimate=pl.CostEstimate(
             flops=tall * inner, bytes_accessed=tall * inner, transcendentals=0
         ),
-    )(a_high, a_low, maps)
+    )(jnp.reshape(core, (1,)).astype(jnp.int32), a_high, a_low, maps, *more)
 
 
 def project_body(terms, begun, *refs):
@@ -145,12 +160,30 @@
     )(*operands)
 
 
-def band_body(pieces, onehot, out):
+def names_row():
+    lane = lax.broadcasted_iota(jnp.int32, (1, 128), 1)
+    return jnp.where(
+        lane < NBANDS, lane, jnp.where(lane < 2 * NBANDS, lane - NBANDS, -1)
+    ).astype(F32)
+
+
+def band_body(x, pieces, bands, out):
+    devices, each = SPAN // 36, 36
+    held = bands[pl.ds(x[0] * devices, devices)].reshape(devices, each).astype(F32)
+    row = lax.broadcasted_iota(jnp.int32, (SPAN, devices), 0)
+    begin = lax.broadcasted_iota(jnp.int32, (SPAN, devices), 1) * each
+    source = ((row >= begin) & (row < begin + each)).astype(F32)
+    start = jnp.sum(source * begin.astype(F32), axis=1, keepdims=True)
+    at = lax.broadcasted_iota(jnp.int32, (SPAN, each), 0).astype(F32) - start
+    mask = at == lax.broadcasted_iota(jnp.int32, (SPAN, each), 1).astype(F32)
+    spread = jnp.dot(source, held, preferred_element_type=F32)
+    band = jnp.sum(jnp.where(mask, spread, 0.0), axis=1, keepdims=True)
+    onehot = (band == names_row()).astype(F32)
+
     modes = jnp.sum(pieces[...], axis=0)
-    squares = modes * modes
     sums = jnp.dot(
-        squares.reshape(16, SPAN),
-        onehot[...],
+        (modes * modes).reshape(16, SPAN),
+        onehot,
         precision=lax.Precision.HIGHEST,
         preferred_element_type=F32,
     )
@@ -159,9 +192,14 @@
     out[...] = jnp.broadcast_to(both[None], out.shape)
 
 
-def final_body(blocks, count, power, fisher):
-    total = jnp.sum(blocks[...].reshape(32, NY, 8, 128), axis=1).reshape(HALF, 128).T
-    scale = 2.0 * count[...]
+def final_body(blocks, bands, power, fisher):
+    held = bands[...].reshape(128, 36).astype(F32).T
+    label = lax.broadcasted_iota(jnp.int32, (NBANDS, 128), 0).astype(F32)
+    found = jnp.zeros((NBANDS, 128), F32)
+    for n in range(36):
+        found += (held[n : n + 1] == label).astype(F32)
+    scale = 2.0 * jnp.sum(found, axis=1, keepdims=True)
+    total = jnp.sum(blocks[...].reshape(32, NX, 8, 128), axis=1).reshape(HALF, 128).T
     for c in range(2):
         for half in range(2):
             at = HALF * c + 128 * half
@@ -180,25 +218,23 @@
 
 
 def per_device(inv_cov, sim_maps, templates, band_index):
-    y = lax.axis_index("y")
+    x = lax.axis_index("x")
     c = lax.axis_index("c")
 
-    gathered = lax.all_gather(sim_maps, BLK, axis=0, tiled=True)
-
-    bands = lax.all_to_all(
-        jnp.broadcast_to(band_index[None, None, :], (128, 1, 36)), EVERY, 0, 0, tiled=True
-    )
-    bands, templates = lax.optimization_barrier((bands, templates))
+    here = lax.all_to_all(
+        jnp.broadcast_to(sim_maps[None], (8, ROWS, NMAPS)), ("x", "zl"), 0, 0, tiled=True
+    ).reshape(8 * ROWS, NMAPS)
 
     own = []
-    for dy in range(NY):
-        block = lax.dynamic_slice(templates, (0, lax.rem(y + dy, NY) * SPAN), (ROWS, SPAN))
-        own.append(shift(block, dy, 0) if dy else block)
+    for step in range(NX):
+        block = lax.dynamic_slice(templates, (0, lax.rem(x + step, NX) * SPAN), (ROWS, SPAN))
+        own.append(shift(block, step) if step else block)
 
     a_high, a_low = split_rows(inv_cov)
-    gathered, a_high, a_low = lax.optimization_barrier((gathered, a_high, a_low))
-    partial = rows_of(a_high, a_low, gathered)
-    partial, bands, *own = lax.optimization_barrier((partial, bands, *own))
+    here, a_high, a_low = lax.optimization_barrier((here, a_high, a_low))
+    there = swap(here)
+    partial = rows_of(c, a_high, a_low, here)
+    partial = rows_of(1 - c, a_high, a_low, there, partial)
     terms = lax.all_to_all(partial, ("c",) + RING, 0, 0, tiled=True)
 
     other = [swap(v) for v in own]
@@ -206,28 +242,30 @@
         (jnp.where(c == 0, a, b), jnp.where(c == 0, b, a)) for a, b in zip(own, other)
     ]
 
-    bands = bands.reshape(NMODES)
-    labels = jnp.arange(NBANDS, dtype=jnp.int32)
-    count = jnp.sum((bands[None, :] == labels[:, None]).astype(F32), axis=1, keepdims=True)
-    mine = lax.dynamic_slice(bands, (y * SPAN,), (SPAN,))
-    lane = jnp.arange(128, dtype=jnp.int32)
-    names = jnp.where(lane < 2 * NBANDS, lane % NBANDS, -1)
-    onehot = (mine[:, None] == names[None, :]).astype(F32)
-    terms, count, onehot, spread = lax.optimization_barrier((terms, count, onehot, spread))
+    terms, band_index, spread = lax.optimization_barrier((terms, band_index, spread))
 
     rows = jnp.sum(terms.reshape(2, 8, ROWS, HALF), axis=1)
-    around = [shift(rows, dy, 0) if dy else rows for dy in range(NY)]
+    around = [shift(rows, step) if step else rows for step in range(NX)]
+    bands = lax.all_to_all(
+        jnp.broadcast_to(band_index[None, None, :], (128, 1, 36)), EVERY, 0, 0, tiled=True
+    )
     projected = project([(around[0], *spread[0])])
     projected = project([(around[d], *spread[d]) for d in (1, 3)], projected)
     projected = project([(around[2], *spread[2])], projected)
 
+    projected, bands = lax.optimization_barrier((projected, bands))
     pieces = lax.all_to_all(projected, CHIPS, 0, 0, tiled=True)
     sums = pl.pallas_call(
         band_body,
+        in_specs=[
+            pl.BlockSpec(memory_space=pltpu.SMEM),
+            pl.BlockSpec(memory_space=pltpu.VMEM),
+            pl.BlockSpec(memory_space=pltpu.VMEM),
+        ],
         out_shape=jax.ShapeDtypeStruct((128, 8, 128), F32),
         compiler_params=limit(32),
-    )(pieces, onehot)
-    blocks = lax.all_to_all(sums, ("c",) + CHIPS + ("y",), 0, 0, tiled=True)
+    )(jnp.reshape(x, (1,)).astype(jnp.int32), pieces, bands)
+    blocks = lax.all_to_all(sums, ("c",) + CHIPS + ("x",), 0, 0, tiled=True)
     return pl.pallas_call(
         final_body,
         out_shape=[
@@ -235,7 +273,7 @@
             jax.ShapeDtypeStruct((NBANDS, NBANDS), F32),
         ],
         compiler_params=limit(32),
-    )(blocks, count)
+    )(blocks, bands)
 
 
 def solution(mesh):

time: 202 us -> 217 us (1.074)
  blocking collectives: 17.4 us -> 43.2 us
  between operations: 14.2 us -> 0.76 us
  Pallas kernels: 45.4 us -> 56.9 us
  waiting for transfers between devices: 72.4 us -> 62 us
  local copies, waits for them, and re-layouts: 5.34 us -> 7.58 us
    all_to_all x0 -> x1, blocking collectives: none -> 21.9 us  [per_device(): blocks = lax.all_to_all(sums, ('c',) + CHIPS + ('x',), 0, 0, tiled=True)]
    all_to_all x1, waiting for transfers between devices: 13.2 us -> 26.6 us  [per_device(): lax.all_to_all(jnp.broadcast_to(sim_maps[None], (8, ROWS, NMAPS)), ('x',...]
    ppermute x6, waiting for transfers between devices: 13 us -> 3.19 us  [shift(): return lax.ppermute(value, 'x', [(n, (n + step) % NX) for n in range(NX)])]
    all_to_all x1, waiting for transfers between devices: 9.71 us -> 0.32 us  [per_device(): lax.all_to_all(jnp.broadcast_to(band_index[None, None, :], (128, 1, 36)),...]
    ppermute x4 -> x5, starting transfers between devices: 1.07 us -> 7.47 us  [swap(): return lax.ppermute(value, 'c', [(0, 1), (1, 0)])]
    pallas_call x2 -> x3, Pallas kernels: 22.8 us -> 28.7 us  [the longest x2 27 us: rows_of(): pl.pallas_call(body, grid_spec=pltpu.PrefetchScalarGridSpec(num_scalar_pr...]
    all_to_all x1, starting transfers between devices: 12 us -> 6.19 us  [per_device(): lax.all_to_all(jnp.broadcast_to(band_index[None, None, :], (128, 1, 36)),...]
    all_to_all x1, blocking collectives: 17.4 us -> 21.3 us  [per_device(): pieces = lax.all_to_all(projected, CHIPS, 0, 0, tiled=True)]
  transfers between devices with their start and end apart: 14 -> 14, of which waited for: 7 -> 5; matrix products, arithmetic and copies ran while one was open for 7% -> 6% of each run, Pallas kernels for 21% -> 25%
where the time goes in v5:
time: 217 us; the launch traced here: 216 us
  waiting for transfers between devices  62 us (29%)
  Pallas kernels  56.9 us (26%)
  blocking collectives  43.2 us (20%)
  starting transfers between devices  34.3 us (16%)
  other arithmetic  11.1 us (5%)
  local copies, waits for them, and re-layouts  7.58 us (3%)
    all_to_all x1, waiting for transfers between devices, per_device(): terms = lax.all_to_all(partial, ('c',) + RING, 0, 0, tiled=True)  30.5 us
    pallas_call x2, Pallas kernels, rows_of(): pl.pallas_call(body, grid_spec=pltpu.PrefetchScalarGridSpec(num_scalar_pr...  27 us
    all_to_all x1, waiting for transfers between devices, per_device(): lax.all_to_all(jnp.broadcast_to(sim_maps[None], (8, ROWS, NMAPS)), ('x',...  26.6 us
    all_to_all x1, blocking collectives, per_device(): blocks = lax.all_to_all(sums, ('c',) + CHIPS + ('x',), 0, 0, tiled=True)  21.9 us
    all_to_all x1, blocking collectives, per_device(): pieces = lax.all_to_all(projected, CHIPS, 0, 0, tiled=True)  21.3 us
    pallas_call x1, Pallas kernels, split_rows(): pl.pallas_call(split_body, grid=(rows // step,), in_specs=[block], out_sp...  18.2 us
    select_n x4, other arithmetic, per_device(): jnp.where(c == 0, b, a)  8.21 us
    pallas_call x3, Pallas kernels, project(): pl.pallas_call(body, out_shape=jax.ShapeDtypeStruct((16, 2, 8, SPAN), F32...  7.94 us
  transfers between devices with their start and end apart: 14, of which 5 were waited for; matrix products, arithmetic and copies ran while one was open for 6% of the time, Pallas kernels for 25%

profile of v5, /device:TPU:1, one launch (start us, length us, event | category | flops | bytes accessed | tf_op | source)
XLA Modules:
  0.0 215.8 jit_solution(6080194372796984202)
XLA Ops:
  0.6 3.1 %broadcast_in_dim.4 = f32[8,192,512]{2,1,0:T(8,128)} broadcast(f32[192,512]{1,0:T(8,128)} %param.5), dimensions={1,2} | broadcast | bytes 3538944 | tf_op jit(solution)/shard_map/broadcast_in_dim | solution.py:225
  3.7 6.2 %all-to-all-start = ((f32[8,192,512]{2,1,0:T(8,128)}), f32[8,192,512]{2,1,0:T(8,128)S(1)}, u32[]{:S(2)}, u32[]{:S(2)}) async-start(f32[8,192,512]{2,1,0:T(8,128)} %broadcast_in_dim.4), calls=%async_computation | async-start | bytes 6291456 | tf_op jit(solution)/shard_map/all_to_all | solution.py:224
  9.9 18.2 %shard_map.59 = (bf16[1536,3072]{1,0:T(8,128)(2,1)}, bf16[1536,3072]{1,0:T(8,128)(2,1)}) custom-call(f32[1536,3072]{1,0:T(8,128)} %a.1), custom_call_target="tpu_custom_call" | custom-call | flops 9437184 | bytes 37748736 | tf_op jit(solution)/shard_map/pallas_call | solution.py:61
  28.1 26.6 %all-to-all-done = f32[8,192,512]{2,1,0:T(8,128)S(1)} async-done(((f32[8,192,512]{2,1,0:T(8,128)}), f32[8,192,512]{2,1,0:T(8,128)S(1)}, u32[]{:S(2)}, u32[]{:S(2)}) %all-to-all-start) | async-done | bytes 3145760 | tf_op jit(solution)/shard_map/all_to_all | solution.py:224
  56.4 3.8 %constant_dynamic-slice_fusion = (f32[192,1152]{1,0:T(8,128)}, f32[192,1152]{1,0:T(8,128)}, f32[192,1152]{1,0:T(8,128)}, f32[192,1152]{1,0:T(8,128)}) fusion(f32[192,4608]{1,0:T(8,128)} %param.6, s32[]{:T(128)S(6)} %select_n.58, s32[]{:T(128)S(6)} %select_n.52, s32[]{:T(128)S(6)} %select_n.49, s32[]{:T(128)S(6)} %select_n.55), kind=kLoop, calls=%fused_computation.9 | loop fusion | bytes 7077904 | tf_op jit(solution)/shard_map/dynamic_slice | solution.py:230
  62.8 1.7 collective-permute-start.1
  64.5 12.7 %shard_map.60.refs_4_ = f32[16,192,256]{2,1,0:T(8,128)} custom-call(s32[1]{0:T(128)} %bitcast.3.refs_0_, bf16[1536,3072]{1,0:T(8,128)(2,1)} %get-tuple-element.21.refs_1_, bf16[1536,3072]{1,0:T(8,128)(2,1)} %get-tuple-element.22.refs_2_, f32[1536,512]{1,0:T(8,128)} %bitcast.7), custom_call_target="tpu_custom_call" | custom-call | flops 2359296 | bytes 2359296 | tf_op jit(solution)/shard_map/pallas_call | solution.py:104
  77.2 14.3 %shard_map.61 = f32[16,192,256]{2,1,0:T(8,128)} custom-call(s32[1]{0:T(128)} %bitcast.1.refs_0_, bf16[1536,3072]{1,0:T(8,128)(2,1)} %get-tuple-element.21.refs_1_, bf16[1536,3072]{1,0:T(8,128)(2,1)} %get-tuple-element.22.refs_2_, f32[1536,512]{1,0:T(8,128)} %collective-permute-done.refs_3_, f32[16,192,256]{2,1,0:T(8,128)} %shard_map.60.refs_4_), custom_call_target="tpu_custom_call" | custom-call | flops 2359296 | bytes 2359296 | tf_op jit(solution)/shard_map/pallas_call | solution.py:104
  91.5 7.6 %all-to-all-start.1 = ((f32[16,192,256]{2,1,0:T(8,128)}), f32[16,192,256]{2,1,0:T(8,128)}, u32[]{:S(2)}, u32[]{:S(2)}) async-start(f32[16,192,256]{2,1,0:T(8,128)} %shard_map.61), calls=%async_computation.1 | async-start | bytes 6291456 | tf_op jit(solution)/shard_map/all_to_all | solution.py:238
  99.2 3.5 %collective-permute-start.3 = (f32[192,1152]{1,0:T(8,128)}, f32[192,1152]{1,0:T(8,128)}, u32[]{:S(2)}, u32[]{:S(2)}) collective-permute-start(f32[192,1152]{1,0:T(8,128)} %collective-permute-done.2), channel_id=1, source_target_pairs={{0,8},{8,0},{1,9},{9,1},{2,10},{10,2},{3,11},{11,3},{4,12},{12,4},... | collective-permute-start | bytes 2654216 | tf_op jit(solution)/shard_map/ppermute | solution.py:42
  107.8 2.5 %broadcast_select_fusion.2 = (f32[192,1152]{1,0:T(8,128)}, f32[192,1152]{1,0:T(8,128)}) fusion(f32[192,1152]{1,0:T(8,128)S(1)} %collective-permute-done.5, f32[192,1152]{1,0:T(8,128)} %collective-permute-done.4, pred[]{:T(512)S(6)} %eq.2), kind=kLoop, calls=%fused_computation.3 | loop fusion | flops 442368 | bytes 3538945 | tf_op jit(solution)/shard_map/jit(_where)/select_n | solution.py:242
  110.4 2.6 %broadcast_select_fusion = (f32[192,1152]{1,0:T(8,128)}, f32[192,1152]{1,0:T(8,128)}) fusion(f32[192,1152]{1,0:T(8,128)S(1)} %collective-permute-done.7, f32[192,1152]{1,0:T(8,128)} %collective-permute-done.6, pred[]{:T(512)S(6)} %eq.2), kind=kLoop, calls=%fused_computation.1 | loop fusion | flops 442368 | bytes 3538945 | tf_op jit(solution)/shard_map/jit(_where)/select_n | solution.py:242
  112.9 30.5 %all-to-all-done.1 = f32[16,192,256]{2,1,0:T(8,128)} async-done(((f32[16,192,256]{2,1,0:T(8,128)}), f32[16,192,256]{2,1,0:T(8,128)}, u32[]{:S(2)}, u32[]{:S(2)}) %all-to-all-start.1) | async-done | bytes 3145760 | tf_op jit(solution)/shard_map/all_to_all | solution.py:238
  143.5 2.9 %bitcast_reduce_fusion.refs_0_ = f32[2,192,256]{2,1,0:T(8,128)} fusion(f32[16,192,256]{2,1,0:T(8,128)} %all-to-all-done.1), kind=kLoop, calls=%fused_computation | loop fusion | flops 688128 | bytes 3538944 | tf_op jit(solution)/shard_map/reduce_sum | solution.py:247
  146.9 2.1 collective-permute-start.10
  151.1 6.2 %all-to-all-start.2 = ((s32[128,1,36]{2,1,0:T(1,128)}), s32[128,1,36]{2,1,0:T(1,128)}, u32[]{:S(2)}, u32[]{:S(2)}) async-start(s32[128,1,36]{2,1,0:T(1,128)} %broadcast_in_dim.5), calls=%async_computation.2 | async-start | bytes 131072 | tf_op jit(solution)/shard_map/all_to_all | solution.py:249
  157.3 2.3 %shard_map.62.refs_6_ = f32[16,2,8,1152]{3,2,1,0:T(8,128)S(1)} custom-call(f32[2,192,256]{2,1,0:T(8,128)} %bitcast_reduce_fusion.refs_0_, f32[192,1152]{1,0:T(8,128)S(1)} %get-tuple-element.31.refs_1_, f32[192,1152]{1,0:T(8,128)S(1)} %get-tuple-element.32.refs_2_), custom_call_target="tpu_custom_call" | custom-call | flops 679477248 | bytes 2162688 | tf_op jit(solution)/shard_map/pallas_call | solution.py:151
  159.7 3.4 %shard_map.63.refs_3_ = f32[16,2,8,1152]{3,2,1,0:T(8,128)S(1)} custom-call(f32[2,192,256]{2,1,0:T(8,128)} %collective-permute-done.9.refs_0_, f32[192,1152]{1,0:T(8,128)S(1)} %get-tuple-element.27.refs_1_, f32[192,1152]{1,0:T(8,128)S(1)} %get-tuple-element.28.refs_2_, f32[2,192,256]{2,1,0:T(8,128)} %collective-permute-done.10.refs_3_, ...), custom_call_target="tpu_custom_call" | custom-call | flops 1358954496 | bytes 5505024 | tf_op jit(solution)/shard_map/pallas_call | solution.py:151
  163.1 3.2 %collective-permute-done.8.refs_0_ = f32[2,192,256]{2,1,0:T(8,128)} collective-permute-done((f32[2,192,256]{2,1,0:T(8,128)}, f32[2,192,256]{2,1,0:T(8,128)}, u32[]{:S(2)}, u32[]{:S(2)}) %collective-permute-start.8) | collective-permute-done | bytes 393248 | tf_op jit(solution)/shard_map/ppermute | solution.py:38
  166.3 2.2 %shard_map.64 = f32[16,2,8,1152]{3,2,1,0:T(8,128)S(1)} custom-call(f32[2,192,256]{2,1,0:T(8,128)} %collective-permute-done.8.refs_0_, f32[192,1152]{1,0:T(8,128)S(1)} %copy-done.3, f32[192,1152]{1,0:T(8,128)S(1)} %copy-done.2, f32[16,2,8,1152]{3,2,1,0:T(8,128)S(1)} %shard_map.63.refs_3_), custom_call_target="tpu_custom_call" | custom-call | flops 679477248 | bytes 3342336 | tf_op jit(solution)/shard_map/pallas_call | solution.py:151
  168.9 21.3 %all_to_all.25.pieces = f32[16,2,8,1152]{3,2,1,0:T(8,128)S(1)} all-to-all(f32[16,2,8,1152]{3,2,1,0:T(8,128)S(1)} %shard_map.64), channel_id=1, replica_groups=mesh['x'=4,'zl'=2,'c'=2,'y'=4,'zh'=2] {'y','zh','zl'}, dimensions={0} | all-to-all | bytes 2359296 | tf_op jit(solution)/shard_map/all_to_all | solution.py:257
  190.2 1.7 shard_map.65
  191.9 21.9 %all_to_all.26.blocks = f32[128,8,128]{2,1,0:T(8,128)S(1)} all-to-all(f32[128,8,128]{2,1,0:T(8,128)S(1)} %shard_map.65), channel_id=1, replica_groups=mesh['x'=4,'zl'=2,'c'=2,'y'=4,'zh'=2] {'c','y','zh','zl','x'}, dimensions={0} | all-to-all | bytes 1048576 | tf_op jit(solution)/shard_map/all_to_all | solution.py:268
  213.8 2.1 shard_map.66
  (34 shorter events, 12.5 us)
Async XLA Ops:
  3.7 51.0 %all-to-all-start = ((f32[8,192,512]{2,1,0:T(8,128)}), f32[8,192,512]{2,1,0:T(8,128)S(1)}, u32[]{:S(2)}, u32[]{:S(2)}) async-start(f32[8,192,512]{2,1,0:T(8,128)} %broadcast_in_dim.4), calls=%async_computation | async-start | bytes 6291456 | tf_op jit(solution)/shard_map/all_to_all | solution.py:224
  54.7 5.4 %copy-start.4 = (f32[8,192,512]{2,1,0:T(8,128)}, f32[8,192,512]{2,1,0:T(8,128)S(1)}, u32[]{:S(2)}) copy-start(f32[8,192,512]{2,1,0:T(8,128)S(1)} %all-to-all-done) | copy-start | bytes 9437188
  54.7 22.5 %collective-permute-start = (f32[1536,512]{1,0:T(8,128)S(1)}, f32[1536,512]{1,0:T(8,128)}, u32[]{:S(2)}, u32[]{:S(2)}) collective-permute-start(f32[1536,512]{1,0:T(8,128)S(1)} %bitcast.6), channel_id=1, source_target_pairs={{0,8},{8,0},{1,9},{9,1},{2,10},{10,2},{3,11},{11,3},{4,12},{12,4},... | collective-permute-start | bytes 9437192 | tf_op jit(solution)/shard_map/ppermute | solution.py:42
  60.1 39.0 %collective-permute-start.2 = (f32[192,1152]{1,0:T(8,128)}, f32[192,1152]{1,0:T(8,128)}, u32[]{:S(2)}, u32[]{:S(2)}) collective-permute-start(f32[192,1152]{1,0:T(8,128)} %get-tuple-element.37), channel_id=1, source_target_pairs={{0,32},{32,64},{64,96},{96,0},{1,33},{33,65},{65,97},{97,1},{2,34}... | collective-permute-start | bytes 2654216 | tf_op jit(solution)/shard_map/ppermute | solution.py:38
  60.1 42.5 %collective-permute-start.4 = (f32[192,1152]{1,0:T(8,128)}, f32[192,1152]{1,0:T(8,128)}, u32[]{:S(2)}, u32[]{:S(2)}) collective-permute-start(f32[192,1152]{1,0:T(8,128)} %get-tuple-element.39), channel_id=1, source_target_pairs={{0,64},{32,96},{64,0},{96,32},{1,65},{33,97},{65,1},{97,33},{2,66}... | collective-permute-start | bytes 2654216 | tf_op jit(solution)/shard_map/ppermute | solution.py:38
  61.7 41.0 %collective-permute-start.6 = (f32[192,1152]{1,0:T(8,128)}, f32[192,1152]{1,0:T(8,128)}, u32[]{:S(2)}, u32[]{:S(2)}) collective-permute-start(f32[192,1152]{1,0:T(8,128)} %get-tuple-element.36), channel_id=1, source_target_pairs={{0,96},{32,0},{64,32},{96,64},{1,97},{33,1},{65,33},{97,65},{2,98}... | collective-permute-start | bytes 2654216 | tf_op jit(solution)/shard_map/ppermute | solution.py:38
  62.8 40.5 %collective-permute-start.1 = (f32[192,1152]{1,0:T(8,128)}, f32[192,1152]{1,0:T(8,128)}, u32[]{:S(2)}, u32[]{:S(2)}) collective-permute-start(f32[192,1152]{1,0:T(8,128)} %get-tuple-element.38), channel_id=1, source_target_pairs={{0,8},{8,0},{1,9},{9,1},{2,10},{10,2},{3,11},{11,3},{4,12},{12,4},... | collective-permute-start | bytes 2654216 | tf_op jit(solution)/shard_map/ppermute | solution.py:42
  91.5 51.9 %all-to-all-start.1 = ((f32[16,192,256]{2,1,0:T(8,128)}), f32[16,192,256]{2,1,0:T(8,128)}, u32[]{:S(2)}, u32[]{:S(2)}) async-start(f32[16,192,256]{2,1,0:T(8,128)} %shard_map.61), calls=%async_computation.1 | async-start | bytes 6291456 | tf_op jit(solution)/shard_map/all_to_all | solution.py:238
  99.2 7.1 %collective-permute-start.3 = (f32[192,1152]{1,0:T(8,128)}, f32[192,1152]{1,0:T(8,128)}, u32[]{:S(2)}, u32[]{:S(2)}) collective-permute-start(f32[192,1152]{1,0:T(8,128)} %collective-permute-done.2), channel_id=1, source_target_pairs={{0,8},{8,0},{1,9},{9,1},{2,10},{10,2},{3,11},{11,3},{4,12},{12,4},... | collective-permute-start | bytes 2654216 | tf_op jit(solution)/shard_map/ppermute | solution.py:42
  102.7 5.1 %collective-permute-start.5 = (f32[192,1152]{1,0:T(8,128)}, f32[192,1152]{1,0:T(8,128)S(1)}, u32[]{:S(2)}, u32[]{:S(2)}) collective-permute-start(f32[192,1152]{1,0:T(8,128)} %collective-permute-done.4), channel_id=1, source_target_pairs={{0,8},{8,0},{1,9},{9,1},{2,10},{10,2},{3,11},{11,3},{4,12},{12,4},... | collective-permute-start | bytes 2654216 | tf_op jit(solution)/shard_map/ppermute | solution.py:42
  102.7 7.7 %collective-permute-start.7 = (f32[192,1152]{1,0:T(8,128)}, f32[192,1152]{1,0:T(8,128)S(1)}, u32[]{:S(2)}, u32[]{:S(2)}) collective-permute-start(f32[192,1152]{1,0:T(8,128)} %collective-permute-done.6), channel_id=1, source_target_pairs={{0,8},{8,0},{1,9},{9,1},{2,10},{10,2},{3,11},{11,3},{4,12},{12,4},... | collective-permute-start | bytes 2654216 | tf_op jit(solution)/shard_map/ppermute | solution.py:42
  110.4 40.1 %copy-start.5 = (s32[36]{0:T(128)S(1)}, s32[36]{0:T(128)}, u32[]{:S(2)}) copy-start(s32[36]{0:T(128)} %param.7) | copy-start | bytes 436
  146.3 13.4 %collective-permute-start.9 = (f32[2,192,256]{2,1,0:T(8,128)}, f32[2,192,256]{2,1,0:T(8,128)}, u32[]{:S(2)}, u32[]{:S(2)}) collective-permute-start(f32[2,192,256]{2,1,0:T(8,128)} %bitcast_reduce_fusion.refs_0_), channel_id=1, source_target_pairs={{0,32},{32,64},{64,96},{96,0},{1,33},{33,65},{65,97},{97,1},{2,34}... | collective-permute-start | bytes 1179656 | tf_op jit(solution)/shard_map/ppermute | solution.py:38
  146.9 12.8 %collective-permute-start.10 = (f32[2,192,256]{2,1,0:T(8,128)}, f32[2,192,256]{2,1,0:T(8,128)}, u32[]{:S(2)}, u32[]{:S(2)}) collective-permute-start(f32[2,192,256]{2,1,0:T(8,128)} %bitcast_reduce_fusion.refs_0_), channel_id=1, source_target_pairs={{0,96},{32,0},{64,32},{96,64},{1,97},{33,1},{65,33},{97,65},{2,98}... | collective-permute-start | bytes 1179656 | tf_op jit(solution)/shard_map/ppermute | solution.py:38
  149.0 17.3 %collective-permute-start.8 = (f32[2,192,256]{2,1,0:T(8,128)}, f32[2,192,256]{2,1,0:T(8,128)}, u32[]{:S(2)}, u32[]{:S(2)}) collective-permute-start(f32[2,192,256]{2,1,0:T(8,128)} %bitcast_reduce_fusion.refs_0_), channel_id=1, source_target_pairs={{0,64},{32,96},{64,0},{96,32},{1,65},{33,97},{65,1},{97,33},{2,66}... | collective-permute-start | bytes 1179656 | tf_op jit(solution)/shard_map/ppermute | solution.py:38
  151.1 17.7 %all-to-all-start.2 = ((s32[128,1,36]{2,1,0:T(1,128)}), s32[128,1,36]{2,1,0:T(1,128)}, u32[]{:S(2)}, u32[]{:S(2)}) async-start(s32[128,1,36]{2,1,0:T(1,128)} %broadcast_in_dim.5), calls=%async_computation.2 | async-start | bytes 131072 | tf_op jit(solution)/shard_map/all_to_all | solution.py:249
  157.3 2.4 %copy-start = (f32[192,1152]{1,0:T(8,128)S(1)}, f32[192,1152]{1,0:T(8,128)}, u32[]{:S(2)}) copy-start(f32[192,1152]{1,0:T(8,128)} %get-tuple-element.30.refs_5_) | copy-start | bytes 2654212
  157.3 2.4 %copy-start.1 = (f32[192,1152]{1,0:T(8,128)S(1)}, f32[192,1152]{1,0:T(8,128)}, u32[]{:S(2)}) copy-start(f32[192,1152]{1,0:T(8,128)} %get-tuple-element.29.refs_4_) | copy-start | bytes 2654212
  159.7 6.7 %copy-start.2 = (f32[192,1152]{1,0:T(8,128)S(1)}, f32[192,1152]{1,0:T(8,128)}, u32[]{:S(2)}) copy-start(f32[192,1152]{1,0:T(8,128)} %get-tuple-element.26.refs_2_) | copy-start | bytes 2654212
  159.7 6.7 %copy-start.3 = (f32[192,1152]{1,0:T(8,128)S(1)}, f32[192,1152]{1,0:T(8,128)}, u32[]{:S(2)}) copy-start(f32[192,1152]{1,0:T(8,128)} %get-tuple-element.25.refs_1_) | copy-start | bytes 2654212

commit v6 on v4

--- a/solution.py
+++ b/solution.py
@@ -11,6 +11,7 @@
 NY = 4
 SPAN = NMODES // NY
 HALF = NMAPS // 2
+PART = HALF // 2
 ROWS = 192
 BLK = ("x", "zl", "c")
 RING = ("y", "zh")
@@ -68,13 +69,13 @@
     )(a)
 
 
-def rows_body(a_high, a_low, s, out):
-    sh, sl = split(s[...])
+def rows_body(a_high, a_low, s0, s1, out):
+    sh, sl = split(jnp.concatenate([s0[...], s1[...]], axis=1))
     ah = a_high[...]
     found = dot(ah, sh) + dot(ah, sl) + dot(a_low[...], sh)
 
     for core in range(2):
-        part = found[:, HALF * core : HALF * core + HALF].reshape(8, ROWS, HALF)
+        part = found[:, PART * core : PART * core + PART].reshape(8, ROWS, PART)
         mine = pl.ds(8 * core, 8)
 
         @pl.when(pl.program_id(0) == 0)
@@ -86,24 +87,29 @@
             out[mine] += part
 
 
-def rows_of(a_high, a_low, maps):
+def rows_of(a_high, a_low, maps, half):
     tall, inner = a_high.shape
     step = 512
     a_block = pl.BlockSpec((tall, step), lambda k: (0, k))
     return pl.pallas_call(
         rows_body,
         grid=(inner // step,),
-        in_specs=[a_block, a_block, pl.BlockSpec((step, NMAPS), lambda k: (k, 0))],
-        out_specs=pl.BlockSpec((16, ROWS, HALF), lambda k: (0, 0, 0)),
-        out_shape=jax.ShapeDtypeStruct((16, ROWS, HALF), F32),
+        in_specs=[
+            a_block,
+            a_block,
+            pl.BlockSpec((step, PART), lambda k: (k, half)),
+            pl.BlockSpec((step, PART), lambda k: (k, 2 + half)),
+        ],
+        out_specs=pl.BlockSpec((16, ROWS, PART), lambda k: (0, 0, 0)),
+        out_shape=jax.ShapeDtypeStruct((16, ROWS, PART), F32),
         compiler_params=limit(58),
         cost_estimate=pl.CostEstimate(
             flops=tall * inner, bytes_accessed=tall * inner, transcendentals=0
         ),
-    )(a_high, a_low, maps)
-
-
-def project_body(terms, begun, *refs):
+    )(a_high, a_low, maps, maps)
+
+
+def project_body(terms, begun, earlier, *refs):
     out = refs[-1]
     cols = 384
     left = []
@@ -120,25 +126,30 @@
             )
             term = dot(left[t], jnp.concatenate([th, tl, th], axis=0))
             total = term if total is None else total + term
-        for half in range(2):
-            part = total[128 * half : 128 * half + 128].reshape(16, 8, cols)
-            if begun:
-                part += refs[3 * terms][:, half, :, n : n + cols]
-            out[:, half, :, n : n + cols] = part
-
-
-def project(groups, begun=None):
-    operands = [v for g in groups for v in g] + ([] if begun is None else [begun])
+        part = total.reshape(16, 8, cols)
+        if begun:
+            part += refs[3 * terms][:, :, n : n + cols]
+        if earlier:
+            out[:, 0, :, n : n + cols] = refs[3 * terms + 1][:, :, n : n + cols]
+            out[:, 1, :, n : n + cols] = part
+        else:
+            out[:, :, n : n + cols] = part
+
+
+def project(groups, begun=None, earlier=None):
+    more = [v for v in (begun, earlier) if v is not None]
+    operands = [v for g in groups for v in g] + more
 
     def body(*refs):
-        project_body(len(groups), begun is not None, *refs)
-
+        project_body(len(groups), begun is not None, earlier is not None, *refs)
+
+    shape = (16, 8, SPAN) if earlier is None else (16, 2, 8, SPAN)
     return pl.pallas_call(
         body,
-        out_shape=jax.ShapeDtypeStruct((16, 2, 8, SPAN), F32),
+        out_shape=jax.ShapeDtypeStruct(shape, F32),
         compiler_params=limit(32),
         cost_estimate=pl.CostEstimate(
-            flops=len(groups) * 6 * 2 * ROWS * HALF * SPAN,
+            flops=len(groups) * 6 * 2 * ROWS * PART * SPAN,
             bytes_accessed=4 * sum(v.size for v in operands),
             transcendentals=0,
         ),
@@ -197,9 +208,10 @@
 
     a_high, a_low = split_rows(inv_cov)
     gathered, a_high, a_low = lax.optimization_barrier((gathered, a_high, a_low))
-    partial = rows_of(a_high, a_low, gathered)
-    partial, bands, *own = lax.optimization_barrier((partial, bands, *own))
-    terms = lax.all_to_all(partial, ("c",) + RING, 0, 0, tiled=True)
+    early = rows_of(a_high, a_low, gathered, 0)
+    early, bands, *own = lax.optimization_barrier((early, bands, *own))
+    early = lax.all_to_all(early, ("c",) + RING, 0, 0, tiled=True)
+    late = rows_of(a_high, a_low, gathered, 1)
 
     other = [swap(v) for v in own]
     spread = [
@@ -213,13 +225,21 @@
     lane = jnp.arange(128, dtype=jnp.int32)
     names = jnp.where(lane < 2 * NBANDS, lane % NBANDS, -1)
     onehot = (mine[:, None] == names[None, :]).astype(F32)
-    terms, count, onehot, spread = lax.optimization_barrier((terms, count, onehot, spread))
-
-    rows = jnp.sum(terms.reshape(2, 8, ROWS, HALF), axis=1)
-    around = [shift(rows, dy, 0) if dy else rows for dy in range(NY)]
+    early, late, count, onehot, spread = lax.optimization_barrier(
+        (early, late, count, onehot, spread)
+    )
+    late = lax.all_to_all(late, ("c",) + RING, 0, 0, tiled=True)
+
+    def gather(terms):
+        rows = jnp.sum(terms.reshape(2, 8, ROWS, PART), axis=1)
+        return [shift(rows, dy, 0) if dy else rows for dy in range(NY)]
+
+    first = project([(w, *t) for w, t in zip(gather(early), spread)])
+    first, late = lax.optimization_barrier((first, late))
+    around = gather(late)
     projected = project([(around[0], *spread[0])])
     projected = project([(around[d], *spread[d]) for d in (1, 3)], projected)
-    projected = project([(around[2], *spread[2])], projected)
+    projected = project([(around[2], *spread[2])], projected, first)
 
     pieces = lax.all_to_all(projected, CHIPS, 0, 0, tiled=True)
     sums = pl.pallas_call(

time: 202 us -> 218 us (1.079)
  starting transfers between devices: 35.2 us -> 45.1 us
  waiting for transfers between devices: 72.4 us -> 64 us
  local copies, waits for them, and re-layouts: 5.34 us -> 12 us
  Pallas kernels: 45.4 us -> 51.5 us
    all_to_all x1 -> x2, waiting for transfers between devices: 33 us -> 0.01 us  [the longest x1 0.01 us: per_device(): early = lax.all_to_all(early, ('c',) + RING, 0, 0, tiled=True)]
    ppermute x6 -> x9, waiting for transfers between devices: 13 us -> 37.6 us  [shift(): return lax.ppermute(value, RING, pairs)]
    pallas_call x1 -> x2, Pallas kernels: 21.6 us -> 27.2 us  [rows_of(): pl.pallas_call(rows_body, grid=(inner // step,), in_specs=[a_block, a_blo...]
    ppermute x6 -> x9, starting transfers between devices: 5.71 us -> 10.4 us  [shift(): return lax.ppermute(value, RING, pairs)]
    all_to_all x1 -> x2, starting transfers between devices: 6.78 us -> 11.4 us  [the longest x1 7.15 us: per_device(): late = lax.all_to_all(late, ('c',) + RING, 0, 0, tiled=True)]
    unnamed x14 -> x30, local copies, waits for them, and re-layouts: 0.03 us -> 4.23 us
    select_n x4, other arithmetic: 6.46 us -> 4.13 us  [per_device(): jnp.where(c == 0, b, a)]
    pallas_call x3 -> x4, Pallas kernels: 4.61 us -> 4.97 us  [project(): pl.pallas_call(body, out_shape=jax.ShapeDtypeStruct(shape, F32), compiler...]
  transfers between devices with their start and end apart: 14 -> 18, of which waited for: 7 -> 10; matrix products, arithmetic and copies ran while one was open for 7% -> 8% of each run, Pallas kernels for 21% -> 22%
where the time goes in v6:
time: 218 us; the launch traced here: 217 us
  waiting for transfers between devices  64 us (29%)
  Pallas kernels  51.5 us (24%)
  starting transfers between devices  45.1 us (21%)
  blocking collectives  18.5 us (8%)
  between operations  14.2 us (7%)
  local copies, waits for them, and re-layouts  12 us (6%)
  other arithmetic  11.6 us (5%)
    ppermute x9, waiting for transfers between devices, shift(): return lax.ppermute(value, RING, pairs)  37.6 us
    pallas_call x2, Pallas kernels, rows_of(): pl.pallas_call(rows_body, grid=(inner // step,), in_specs=[a_block, a_blo...  27.2 us
    all_to_all x1, blocking collectives, per_device(): pieces = lax.all_to_all(projected, CHIPS, 0, 0, tiled=True)  18.5 us
    pallas_call x1, Pallas kernels, split_rows(): pl.pallas_call(split_body, grid=(rows // step,), in_specs=[block], out_sp...  17 us
    all_to_all x1, waiting for transfers between devices, per_device(): blocks = lax.all_to_all(sums, ('c',) + CHIPS + ('y',), 0, 0, tiled=True)  13.2 us
    all_to_all x1, starting transfers between devices, per_device(): lax.all_to_all(jnp.broadcast_to(band_index[None, None, :], (128, 1, 36)),...  12 us
    ppermute x9, starting transfers between devices, shift(): return lax.ppermute(value, RING, pairs)  10.4 us
    all_to_all x1, starting transfers between devices, per_device(): blocks = lax.all_to_all(sums, ('c',) + CHIPS + ('y',), 0, 0, tiled=True)  10.2 us
  transfers between devices with their start and end apart: 18, of which 10 were waited for; matrix products, arithmetic and copies ran while one was open for 8% of the time, Pallas kernels for 22%

profile of v6, /device:TPU:1, one launch (start us, length us, event | category | flops | bytes accessed | tf_op | source)
XLA Modules:
  0.0 216.9 jit_solution(13208771395314137326)
XLA Ops:
  9.2 12.0 %all-to-all-start = ((s32[128,1,36]{2,1,0:T(1,128)}), s32[128,1,36]{2,1,0:T(1,128)}, u32[]{:S(2)}, u32[]{:S(2)}) async-start(s32[128,1,36]{2,1,0:T(1,128)} %broadcast_in_dim.8), calls=%async_computation | async-start | bytes 131072 | tf_op jit(solution)/shard_map/all_to_all | solution.py:199
  21.2 9.7 %all-to-all-done = s32[128,1,36]{2,1,0:T(1,128)} async-done(((s32[128,1,36]{2,1,0:T(1,128)}), s32[128,1,36]{2,1,0:T(1,128)}, u32[]{:S(2)}, u32[]{:S(2)}) %all-to-all-start) | async-done | bytes 18464 | tf_op jit(solution)/shard_map/all_to_all | solution.py:199
  30.9 3.5 %constant_dynamic-slice_fusion = (f32[192,1152]{1,0:T(8,128)}, f32[192,1152]{1,0:T(8,128)}, f32[192,1152]{1,0:T(8,128)S(1)}, f32[192,1152]{1,0:T(8,128)S(1)}) fusion(f32[192,4608]{1,0:T(8,128)} %param.6, s32[]{:T(128)S(6)} %select_n.73, s32[]{:T(128)S(6)} %select_n.72, s32[]{:T(128)S(6)} %select_n.71, s32[]{:T(128)S(6)} %select_n.70), kind=kLoop, calls=%fused_computation.15 | loop fusion | bytes 7077904 | tf_op jit(solution)/shard_map/dynamic_slice | solution.py:206
  34.8 1.7 collective-permute-start.1
  36.5 17.0 %shard_map.59 = (bf16[1536,3072]{1,0:T(8,128)(2,1)}, bf16[1536,3072]{1,0:T(8,128)(2,1)}) custom-call(f32[1536,3072]{1,0:T(8,128)} %a.1), custom_call_target="tpu_custom_call" | custom-call | flops 9437184 | bytes 37748736 | tf_op jit(solution)/shard_map/pallas_call | solution.py:59
  53.5 2.7 %all-gather.2.cloned.1.call-done.s0.s1 = f32[3072,512]{1,0:T(8,128)} async-done(((f32[192,512]{1,0:T(8,128)}), f32[3072,512]{1,0:T(8,128)}) %all-gather.2.cloned.1.call-update) | async-done | bytes 6291472 | tf_op jit(solution)/shard_map/all_gather | solution.py:197
  56.3 13.6 %shard_map.60 = f32[16,192,128]{2,1,0:T(8,128)} custom-call(bf16[1536,3072]{1,0:T(8,128)(2,1)} %get-tuple-element.31.a_high, bf16[1536,3072]{1,0:T(8,128)(2,1)} %get-tuple-element.32.a_low, f32[3072,512]{1,0:T(8,128)} %all-gather.2.cloned.1.call-done.s0.s1, f32[3072,512]{1,0:T(8,128)} %all-gather.2.cloned.1.call-done.s0.s1), custom_call_target="tpu_custom_call" | custom-call | flops 4718592 | bytes 4718592 | tf_op jit(solution)/shard_map/pallas_call | solution.py:94
  69.9 7.2 %collective-permute-done = f32[192,1152]{1,0:T(8,128)S(1)} collective-permute-done((f32[192,1152]{1,0:T(8,128)S(1)}, f32[192,1152]{1,0:T(8,128)S(1)}, u32[]{:S(2)}, u32[]{:S(2)}) %collective-permute-start) | collective-permute-done | bytes 884768 | tf_op jit(solution)/shard_map/ppermute | solution.py:44
  77.6 4.3 %all-to-all-start.1 = ((f32[16,192,128]{2,1,0:T(8,128)}), f32[16,192,128]{2,1,0:T(8,128)}, u32[]{:S(2)}, u32[]{:S(2)}) async-start(f32[16,192,128]{2,1,0:T(8,128)} %shard_map.60), calls=%async_computation.1 | async-start | bytes 3145728 | tf_op jit(solution)/shard_map/all_to_all | solution.py:213
  82.4 2.3 %reduce.3 = s32[128,36]{1,0:T(8,128)} reduce(s32[128,1,36]{2,1,0:T(1,128)} %all-to-all-done, s32[]{:T(128)} %broadcast.36), dimensions={1}, to_apply=%get-tuple-element.37.reduce_sub_computation.3 | reduce | bytes 36868 | tf_op jit(solution)/shard_map/optimization_barrier | solution.py:212
  88.7 13.6 %shard_map.61 = f32[16,192,128]{2,1,0:T(8,128)} custom-call(bf16[1536,3072]{1,0:T(8,128)(2,1)} %get-tuple-element.31.a_high, bf16[1536,3072]{1,0:T(8,128)(2,1)} %get-tuple-element.32.a_low, f32[3072,512]{1,0:T(8,128)} %all-gather.2.cloned.1.call-done.s0.s1, f32[3072,512]{1,0:T(8,128)} %all-gather.2.cloned.1.call-done.s0.s1), custom_call_target="tpu_custom_call" | custom-call | flops 4718592 | bytes 4718592 | tf_op jit(solution)/shard_map/pallas_call | solution.py:94
  105.9 2.5 %broadcast_select_fusion = (f32[192,1152]{1,0:T(8,128)}, f32[192,1152]{1,0:T(8,128)}) fusion(f32[192,1152]{1,0:T(8,128)S(1)} %collective-permute-done.6, f32[192,1152]{1,0:T(8,128)} %collective-permute-done.2, pred[]{:T(512)S(6)} %eq.47), kind=kLoop, calls=%fused_computation.5 | loop fusion | flops 442368 | bytes 3538945 | tf_op jit(solution)/shard_map/jit(_where)/select_n | solution.py:218
  108.5 7.1 %all-to-all-start.2 = ((f32[16,192,128]{2,1,0:T(8,128)}), f32[16,192,128]{2,1,0:T(8,128)}, u32[]{:S(2)}, u32[]{:S(2)}) async-start(f32[16,192,128]{2,1,0:T(8,128)} %shard_map.61), calls=%async_computation.2 | async-start | bytes 3145728 | tf_op jit(solution)/shard_map/all_to_all | solution.py:231
  115.7 1.6 bitcast_reduce_fusion.1.refs_0_
  117.3 2.7 %collective-permute-start.9 = (f32[2,192,128]{2,1,0:T(8,128)S(1)}, f32[2,192,128]{2,1,0:T(8,128)S(1)}, u32[]{:S(2)}, u32[]{:S(2)}) collective-permute-start(f32[2,192,128]{2,1,0:T(8,128)S(1)} %bitcast_reduce_fusion.1.refs_0_), channel_id=1, source_target_pairs={{0,6},{1,7},{2,0},{3,1},{4,2},{5,3},{6,4},{7,5},{8,14},{9,15},{10,... | collective-permute-start | bytes 589832 | tf_op jit(solution)/shard_map/ppermute | solution.py:44
  121.1 20.5 %collective-permute-done.9.refs_9_ = f32[2,192,128]{2,1,0:T(8,128)S(1)} collective-permute-done((f32[2,192,128]{2,1,0:T(8,128)S(1)}, f32[2,192,128]{2,1,0:T(8,128)S(1)}, u32[]{:S(2)}, u32[]{:S(2)}) %collective-permute-start.9) | collective-permute-done | bytes 196640 | tf_op jit(solution)/shard_map/ppermute | solution.py:44
  141.8 3.4 %collective-permute-done.7.refs_3_ = f32[2,192,128]{2,1,0:T(8,128)S(1)} collective-permute-done((f32[2,192,128]{2,1,0:T(8,128)S(1)}, f32[2,192,128]{2,1,0:T(8,128)S(1)}, u32[]{:S(2)}, u32[]{:S(2)}) %collective-permute-start.7) | collective-permute-done | bytes 196640 | tf_op jit(solution)/shard_map/ppermute | solution.py:44
  147.6 2.3 %shard_map.62.refs_4_ = f32[16,8,1152]{2,1,0:T(8,128)S(1)} custom-call(f32[2,192,128]{2,1,0:T(8,128)S(1)} %bitcast_reduce_fusion.1.refs_0_, f32[192,1152]{1,0:T(8,128)S(1)} %copy-done.2, f32[192,1152]{1,0:T(8,128)S(1)} %copy-done, f32[2,192,128]{2,1,0:T(8,128)S(1)} %collective-permute-done.7.refs_3_, f32[192,1152]{1,0:T(8,128)S(1)} %get-tuple-element.45.refs_4_.refs_1_, ...), custom_call_target="tpu_custom_call" | custom-call | flops 1358954496 | bytes 7864320 | tf_op jit(solution)/shard_map/pallas_call | solution.py:147
  150.7 1.6 bitcast_reduce_fusion.refs_0_
  152.3 3.2 %collective-permute-start.12 = (f32[2,192,128]{2,1,0:T(8,128)S(1)}, f32[2,192,128]{2,1,0:T(8,128)S(1)}, u32[]{:S(2)}, u32[]{:S(2)}) collective-permute-start(f32[2,192,128]{2,1,0:T(8,128)S(1)} %bitcast_reduce_fusion.refs_0_), channel_id=1, source_target_pairs={{0,6},{1,7},{2,0},{3,1},{4,2},{5,3},{6,4},{7,5},{8,14},{9,15},{10,... | collective-permute-start | bytes 589832 | tf_op jit(solution)/shard_map/ppermute | solution.py:44
  158.9 4.4 %collective-permute-done.11.refs_0_ = f32[2,192,128]{2,1,0:T(8,128)S(1)} collective-permute-done((f32[2,192,128]{2,1,0:T(8,128)S(1)}, f32[2,192,128]{2,1,0:T(8,128)S(1)}, u32[]{:S(2)}, u32[]{:S(2)}) %collective-permute-start.11) | collective-permute-done | bytes 196640 | tf_op jit(solution)/shard_map/ppermute | solution.py:44
  165.9 18.5 %all_to_all.25.pieces = f32[16,2,8,1152]{3,2,1,0:T(8,128)S(1)} all-to-all(f32[16,2,8,1152]{3,2,1,0:T(8,128)S(1)} %shard_map.65), channel_id=1, replica_groups=mesh['x'=4,'zl'=2,'c'=2,'y'=4,'zh'=2] {'x','zh','zl'}, dimensions={0} | all-to-all | bytes 2359296 | tf_op jit(solution)/shard_map/all_to_all | solution.py:244
  185.6 10.2 %all-to-all-start.4 = ((f32[128,8,128]{2,1,0:T(8,128)}), f32[128,8,128]{2,1,0:T(8,128)S(1)}, u32[]{:S(2)}, u32[]{:S(2)}) async-start(f32[128,8,128]{2,1,0:T(8,128)} %shard_map.66), calls=%async_computation.4 | async-start | bytes 1048576 | tf_op jit(solution)/shard_map/all_to_all | solution.py:250
  195.9 13.2 %all-to-all-done.4.blocks = f32[128,8,128]{2,1,0:T(8,128)S(1)} async-done(((f32[128,8,128]{2,1,0:T(8,128)}), f32[128,8,128]{2,1,0:T(8,128)S(1)}, u32[]{:S(2)}, u32[]{:S(2)}) %all-to-all-start.4) | async-done | bytes 524320 | tf_op jit(solution)/shard_map/all_to_all | solution.py:250
  (69 shorter events, 23.9 us)
Async XLA Ops:
  7.2 49.1 %all-gather.2.cloned.1.call-start = ((), (), s32[]{:S(2)}) async-start(), calls=%async_computation.5 | async-start | bytes 6684672 | tf_op jit(solution)/shard_map/all_gather | solution.py:197
  9.2 21.7 %all-to-all-start = ((s32[128,1,36]{2,1,0:T(1,128)}), s32[128,1,36]{2,1,0:T(1,128)}, u32[]{:S(2)}, u32[]{:S(2)}) async-start(s32[128,1,36]{2,1,0:T(1,128)} %broadcast_in_dim.8), calls=%async_computation | async-start | bytes 131072 | tf_op jit(solution)/shard_map/all_to_all | solution.py:199
  34.4 35.5 %collective-permute-start.2 = (f32[192,1152]{1,0:T(8,128)}, f32[192,1152]{1,0:T(8,128)}, u32[]{:S(2)}, u32[]{:S(2)}) collective-permute-start(f32[192,1152]{1,0:T(8,128)} %get-tuple-element.56), channel_id=1, source_target_pairs={{0,6},{1,7},{2,0},{3,1},{4,2},{5,3},{6,4},{7,5},{8,14},{9,15},{10,... | collective-permute-start | bytes 2654216 | tf_op jit(solution)/shard_map/ppermute | solution.py:44
  34.8 35.1 %collective-permute-start.1 = (f32[192,1152]{1,0:T(8,128)}, f32[192,1152]{1,0:T(8,128)S(1)}, u32[]{:S(2)}, u32[]{:S(2)}) collective-permute-start(f32[192,1152]{1,0:T(8,128)} %get-tuple-element.57), channel_id=1, source_target_pairs={{0,4},{1,5},{2,6},{3,7},{4,0},{5,1},{6,2},{7,3},{8,12},{9,13},{10,... | collective-permute-start | bytes 2654216 | tf_op jit(solution)/shard_map/ppermute | solution.py:44
  36.5 40.5 %collective-permute-start = (f32[192,1152]{1,0:T(8,128)S(1)}, f32[192,1152]{1,0:T(8,128)S(1)}, u32[]{:S(2)}, u32[]{:S(2)}) collective-permute-start(f32[192,1152]{1,0:T(8,128)S(1)} %get-tuple-element.58), channel_id=1, source_target_pairs={{0,2},{1,3},{2,4},{3,5},{4,6},{5,7},{6,0},{7,1},{8,10},{9,11},{10,... | collective-permute-start | bytes 2654216 | tf_op jit(solution)/shard_map/ppermute | solution.py:44
  69.9 16.4 %copy-start.11 = (f32[192,1152]{1,0:T(8,128)}, f32[192,1152]{1,0:T(8,128)S(1)}, u32[]{:S(2)}) copy-start(f32[192,1152]{1,0:T(8,128)S(1)} %collective-permute-done.1) | copy-start | bytes 2654212
  77.1 26.2 %collective-permute-start.3 = (f32[192,1152]{1,0:T(8,128)S(1)}, f32[192,1152]{1,0:T(8,128)S(1)}, u32[]{:S(2)}, u32[]{:S(2)}) collective-permute-start(f32[192,1152]{1,0:T(8,128)S(1)} %get-tuple-element.38), channel_id=1, source_target_pairs={{0,8},{8,0},{1,9},{9,1},{2,10},{10,2},{3,11},{11,3},{4,12},{12,4},... | collective-permute-start | bytes 2654216 | tf_op jit(solution)/shard_map/ppermute | solution.py:48
  77.6 30.9 %all-to-all-start.1 = ((f32[16,192,128]{2,1,0:T(8,128)}), f32[16,192,128]{2,1,0:T(8,128)}, u32[]{:S(2)}, u32[]{:S(2)}) async-start(f32[16,192,128]{2,1,0:T(8,128)} %shard_map.60), calls=%async_computation.1 | async-start | bytes 3145728 | tf_op jit(solution)/shard_map/all_to_all | solution.py:213
  86.2 18.4 %collective-permute-start.4 = (f32[192,1152]{1,0:T(8,128)S(1)}, f32[192,1152]{1,0:T(8,128)S(1)}, u32[]{:S(2)}, u32[]{:S(2)}) collective-permute-start(f32[192,1152]{1,0:T(8,128)S(1)} %collective-permute-done), channel_id=1, source_target_pairs={{0,8},{8,0},{1,9},{9,1},{2,10},{10,2},{3,11},{11,3},{4,12},{12,4},... | collective-permute-start | bytes 2654216 | tf_op jit(solution)/shard_map/ppermute | solution.py:48
  86.4 18.5 %collective-permute-start.5 = (f32[192,1152]{1,0:T(8,128)S(1)}, f32[192,1152]{1,0:T(8,128)S(1)}, u32[]{:S(2)}, u32[]{:S(2)}) collective-permute-start(f32[192,1152]{1,0:T(8,128)S(1)} %collective-permute-done.1), channel_id=1, source_target_pairs={{0,8},{8,0},{1,9},{9,1},{2,10},{10,2},{3,11},{11,3},{4,12},{12,4},... | collective-permute-start | bytes 2654216 | tf_op jit(solution)/shard_map/ppermute | solution.py:48
  86.7 19.2 %collective-permute-start.6 = (f32[192,1152]{1,0:T(8,128)}, f32[192,1152]{1,0:T(8,128)S(1)}, u32[]{:S(2)}, u32[]{:S(2)}) collective-permute-start(f32[192,1152]{1,0:T(8,128)} %collective-permute-done.2), channel_id=1, source_target_pairs={{0,8},{8,0},{1,9},{9,1},{2,10},{10,2},{3,11},{11,3},{4,12},{12,4},... | collective-permute-start | bytes 2654216 | tf_op jit(solution)/shard_map/ppermute | solution.py:48
  108.5 42.2 %all-to-all-start.2 = ((f32[16,192,128]{2,1,0:T(8,128)}), f32[16,192,128]{2,1,0:T(8,128)}, u32[]{:S(2)}, u32[]{:S(2)}) async-start(f32[16,192,128]{2,1,0:T(8,128)} %shard_map.61), calls=%async_computation.2 | async-start | bytes 3145728 | tf_op jit(solution)/shard_map/all_to_all | solution.py:231
  115.6 29.6 %copy-start = (f32[192,1152]{1,0:T(8,128)S(1)}, f32[192,1152]{1,0:T(8,128)}, u32[]{:S(2)}) copy-start(f32[192,1152]{1,0:T(8,128)} %get-tuple-element.44.refs_2_) | copy-start | bytes 2654212
  115.6 29.6 %copy-start.2 = (f32[192,1152]{1,0:T(8,128)S(1)}, f32[192,1152]{1,0:T(8,128)}, u32[]{:S(2)}) copy-start(f32[192,1152]{1,0:T(8,128)} %get-tuple-element.43.refs_1_) | copy-start | bytes 2654212
  117.3 24.3 %collective-permute-start.9 = (f32[2,192,128]{2,1,0:T(8,128)S(1)}, f32[2,192,128]{2,1,0:T(8,128)S(1)}, u32[]{:S(2)}, u32[]{:S(2)}) collective-permute-start(f32[2,192,128]{2,1,0:T(8,128)S(1)} %bitcast_reduce_fusion.1.refs_0_), channel_id=1, source_target_pairs={{0,6},{1,7},{2,0},{3,1},{4,2},{5,3},{6,4},{7,5},{8,14},{9,15},{10,... | collective-permute-start | bytes 589832 | tf_op jit(solution)/shard_map/ppermute | solution.py:44
  120.0 21.9 %collective-permute-start.8 = (f32[2,192,128]{2,1,0:T(8,128)S(1)}, f32[2,192,128]{2,1,0:T(8,128)S(1)}, u32[]{:S(2)}, u32[]{:S(2)}) collective-permute-start(f32[2,192,128]{2,1,0:T(8,128)S(1)} %bitcast_reduce_fusion.1.refs_0_), channel_id=1, source_target_pairs={{0,4},{1,5},{2,6},{3,7},{4,0},{5,1},{6,2},{7,3},{8,12},{9,13},{10,... | collective-permute-start | bytes 589832 | tf_op jit(solution)/shard_map/ppermute | solution.py:44
  120.5 24.7 %collective-permute-start.7 = (f32[2,192,128]{2,1,0:T(8,128)S(1)}, f32[2,192,128]{2,1,0:T(8,128)S(1)}, u32[]{:S(2)}, u32[]{:S(2)}) collective-permute-start(f32[2,192,128]{2,1,0:T(8,128)S(1)} %bitcast_reduce_fusion.1.refs_0_), channel_id=1, source_target_pairs={{0,2},{1,3},{2,4},{3,5},{4,6},{5,7},{6,0},{7,1},{8,10},{9,11},{10,... | collective-permute-start | bytes 589832 | tf_op jit(solution)/shard_map/ppermute | solution.py:44
  152.3 11.0 %copy-start.5 = (f32[192,1152]{1,0:T(8,128)S(1)}, f32[192,1152]{1,0:T(8,128)}, u32[]{:S(2)}) copy-start(f32[192,1152]{1,0:T(8,128)} %get-tuple-element.50.refs_11_.refs_5_) | copy-start | bytes 2654212
  152.3 11.0 %copy-start.7 = (f32[192,1152]{1,0:T(8,128)S(1)}, f32[192,1152]{1,0:T(8,128)}, u32[]{:S(2)}) copy-start(f32[192,1152]{1,0:T(8,128)} %get-tuple-element.49.refs_10_.refs_4_) | copy-start | bytes 2654212
  152.3 6.5 %collective-permute-start.12 = (f32[2,192,128]{2,1,0:T(8,128)S(1)}, f32[2,192,128]{2,1,0:T(8,128)S(1)}, u32[]{:S(2)}, u32[]{:S(2)}) collective-permute-start(f32[2,192,128]{2,1,0:T(8,128)S(1)} %bitcast_reduce_fusion.refs_0_), channel_id=1, source_target_pairs={{0,6},{1,7},{2,0},{3,1},{4,2},{5,3},{6,4},{7,5},{8,14},{9,15},{10,... | collective-permute-start | bytes 589832 | tf_op jit(solution)/shard_map/ppermute | solution.py:44
  155.5 7.7 %collective-permute-start.11 = (f32[2,192,128]{2,1,0:T(8,128)S(1)}, f32[2,192,128]{2,1,0:T(8,128)S(1)}, u32[]{:S(2)}, u32[]{:S(2)}) collective-permute-start(f32[2,192,128]{2,1,0:T(8,128)S(1)} %bitcast_reduce_fusion.refs_0_), channel_id=1, source_target_pairs={{0,2},{1,3},{2,4},{3,5},{4,6},{5,7},{6,0},{7,1},{8,10},{9,11},{10,... | collective-permute-start | bytes 589832 | tf_op jit(solution)/shard_map/ppermute | solution.py:44
  155.5 9.6 %collective-permute-start.10 = (f32[2,192,128]{2,1,0:T(8,128)S(1)}, f32[2,192,128]{2,1,0:T(8,128)S(1)}, u32[]{:S(2)}, u32[]{:S(2)}) collective-permute-start(f32[2,192,128]{2,1,0:T(8,128)S(1)} %bitcast_reduce_fusion.refs_0_), channel_id=1, source_target_pairs={{0,4},{1,5},{2,6},{3,7},{4,0},{5,1},{6,2},{7,3},{8,12},{9,13},{10,... | collective-permute-start | bytes 589832 | tf_op jit(solution)/shard_map/ppermute | solution.py:44
  165.9 18.5 %copy-start.10 = (f32[1152,128]{1,0:T(8,128)S(1)}, f32[1152,128]{1,0:T(8,128)}, u32[]{:S(2)}) copy-start(f32[1152,128]{1,0:T(8,128)} %compare_convert_fusion.onehot) | copy-start | bytes 1769476
  185.6 23.4 %all-to-all-start.4 = ((f32[128,8,128]{2,1,0:T(8,128)}), f32[128,8,128]{2,1,0:T(8,128)S(1)}, u32[]{:S(2)}, u32[]{:S(2)}) async-start(f32[128,8,128]{2,1,0:T(8,128)} %shard_map.66), calls=%async_computation.4 | async-start | bytes 1048576 | tf_op jit(solution)/shard_map/all_to_all | solution.py:250
  (9 other events, 34.8 us)
Sparse Core Ops, SparseCore 0:
  9.7 46.5 all-gather.1

commit v7 on v3

--- a/solution.py
+++ b/solution.py
@@ -61,7 +61,7 @@
         in_specs=[block],
         out_specs=[block] * 2,
         out_shape=[jax.ShapeDtypeStruct(a.shape, BF16)] * 2,
-        compiler_params=limit(32),
+        compiler_params=limit(58),
         cost_estimate=pl.CostEstimate(
             flops=2 * rows * cols, bytes_accessed=8 * rows * cols, transcendentals=0
         ),
@@ -78,55 +78,39 @@
         out[...] += value
 
 
-def row_body(blocks, first, at, *refs):
-    highs, lows, rest = refs[:blocks], refs[blocks : 2 * blocks], refs[2 * blocks :]
-    if first:
-        sh, sl = split(rest[0][...])
-        rest[-2][...] = sh
-        rest[-1][...] = sl
-        outs = rest[1:-2]
-    else:
-        sh, sl = rest[0][...], rest[1][...]
-        outs = rest[2:]
-    ah = jnp.concatenate([ref[...] for ref in highs], axis=0)
-    al = jnp.concatenate([ref[...] for ref in lows], axis=0)
+def row_body(at, far_high, near_high, far_low, near_low, s, far, near):
+    sh, sl = split(s[...])
+    ah = jnp.concatenate([far_high[...], near_high[...]], axis=0)
+    al = jnp.concatenate([far_low[...], near_low[...]], axis=0)
     found = dot(ah, sh) + dot(ah, sl) + dot(al, sh)
-    for n, out in enumerate(outs):
-        add_step(out, found[n * ROWS : n * ROWS + ROWS])
-
-
-def rows_of(at, a_high, a_low, maps):
-    inner, cols = maps[0].shape
+    add_step(far, found[:ROWS])
+    add_step(near, found[ROWS:])
+
+
+def rows_of(far, near, a_high, a_low, maps):
+    inner, cols = maps.shape
     step = 1024
-    blocks, first = len(at), len(maps) == 1
-    a_blocks = [pl.BlockSpec((ROWS, step), lambda k, at, n=n: (at[n], k)) for n in range(blocks)]
-    s_block = pl.BlockSpec((step, cols), lambda k, at: (k, 0))
+    a_blocks = [pl.BlockSpec((ROWS, step), lambda k, at, n=n: (at[n], k)) for n in range(2)]
     o_block = pl.BlockSpec((ROWS, cols), lambda k, at: (0, 0))
-    parts = [jax.ShapeDtypeStruct((inner, cols), BF16)] * 2 if first else []
-
-    def body(*refs):
-        row_body(blocks, first, *refs)
-
-    found = pl.pallas_call(
-        body,
+    return pl.pallas_call(
+        row_body,
         grid_spec=pltpu.PrefetchScalarGridSpec(
             num_scalar_prefetch=1,
             grid=(inner // step,),
-            in_specs=a_blocks * 2 + [s_block] * len(maps),
-            out_specs=[o_block] * blocks + [s_block] * len(parts),
-        ),
-        out_shape=[jax.ShapeDtypeStruct((ROWS, cols), F32)] * blocks + parts,
-        compiler_params=limit(32),
+            in_specs=a_blocks * 2 + [pl.BlockSpec((step, cols), lambda k, at: (k, 0))],
+            out_specs=[o_block] * 2,
+        ),
+        out_shape=[jax.ShapeDtypeStruct((ROWS, cols), F32)] * 2,
+        compiler_params=limit(58),
         cost_estimate=pl.CostEstimate(
-            flops=blocks * ROWS * cols,
-            bytes_accessed=blocks * ROWS * cols,
+            flops=12 * ROWS * inner * cols,
+            bytes_accessed=4 * inner * (2 * ROWS + cols),
             transcendentals=0,
         ),
-    )(jnp.stack(at).astype(jnp.int32), *[a_high] * blocks, *[a_low] * blocks, *maps)
-    return found[:blocks], found[blocks:] or maps
-
-
-def project_body(terms, begun, *refs):
+    )(jnp.stack([far, near]).astype(jnp.int32), a_high, a_high, a_low, a_low, maps)
+
+
+def project_body(terms, begun, at, *refs):
     out = refs[-1]
     cols = 384
     left = []
@@ -139,7 +123,7 @@
         for t in range(terms):
             own, other = refs[3 * t + 1 : 3 * t + 3]
             th, tl = split(
-                jnp.concatenate([own[:, n : n + cols], other[:, n : n + cols]], axis=0)
+                jnp.concatenate([own[0, :, n : n + cols], other[0, :, n : n + cols]], axis=0)
             )
             term = dot(left[t], jnp.concatenate([th, tl, th], axis=0))
             total = term if total is None else total + term
@@ -150,22 +134,34 @@
             out[:, half, :, n : n + cols] = part
 
 
-def project(groups, begun=None):
-    operands = [v for g in groups for v in g] + ([] if begun is None else [begun])
+def project(at, weighted, own, other, begun=None):
+    terms = len(weighted)
+    operands = [v for w in weighted for v in (w, own, other)]
+    in_specs = []
+    for t in range(terms):
+        block = pl.BlockSpec((1, ROWS, SPAN), lambda i, at, t=t: (at[t], 0, 0))
+        in_specs += [pl.BlockSpec((2, ROWS, HALF), lambda i, at: (0, 0, 0)), block, block]
+    whole = pl.BlockSpec((16, 2, 8, SPAN), lambda i, at: (0, 0, 0, 0))
+    if begun is not None:
+        operands.append(begun)
+        in_specs.append(whole)
 
     def body(*refs):
-        project_body(len(groups), begun is not None, *refs)
+        project_body(terms, begun is not None, *refs)
 
     return pl.pallas_call(
         body,
+        grid_spec=pltpu.PrefetchScalarGridSpec(
+            num_scalar_prefetch=1, grid=(1,), in_specs=in_specs, out_specs=whole
+        ),
         out_shape=jax.ShapeDtypeStruct((16, 2, 8, SPAN), F32),
         compiler_params=limit(32),
         cost_estimate=pl.CostEstimate(
-            flops=len(groups) * 6 * 2 * ROWS * HALF * SPAN,
-            bytes_accessed=4 * sum(v.size for v in operands),
+            flops=terms * 6 * 2 * ROWS * HALF * SPAN,
+            bytes_accessed=8 * terms * ROWS * SPAN,
             transcendentals=0,
         ),
-    )(*operands)
+    )(jnp.stack(at).astype(jnp.int32), *operands)
 
 
 def names_row():
@@ -201,20 +197,19 @@
 
 
 def final_body(blocks, bands, power, fisher):
-    held = bands[...].reshape(128, 36).astype(F32)
-    names = names_row()
-    found = jnp.zeros((128, 128), F32)
-    for k in range(36):
-        found += (held[:, k : k + 1] == names).astype(F32)
-    count = jnp.maximum(jnp.sum(found, axis=0, keepdims=True), 1.0)
-    total = jnp.sum(blocks[...].reshape(32, NY, 8, 128), axis=1).reshape(HALF, 128)
-    total = (total / (2.0 * count)).T
+    held = bands[...].reshape(128, 36).astype(F32).T
+    label = lax.broadcasted_iota(jnp.int32, (NBANDS, 128), 0).astype(F32)
+    found = jnp.zeros((NBANDS, 128), F32)
+    for n in range(36):
+        found += (held[n : n + 1] == label).astype(F32)
+    scale = 2.0 * jnp.sum(found, axis=1, keepdims=True)
+    total = jnp.sum(blocks[...].reshape(32, NY, 8, 128), axis=1).reshape(HALF, 128).T
     for c in range(2):
         for half in range(2):
             at = HALF * c + 128 * half
-            power[:, at : at + 128] = total[
-                NBANDS * half : NBANDS * half + NBANDS, 128 * c : 128 * c + 128
-            ]
+            power[:, at : at + 128] = (
+                total[NBANDS * half : NBANDS * half + NBANDS, 128 * c : 128 * c + 128] / scale
+            )
     value = power[...]
     centered = value - jnp.mean(value, axis=1, keepdims=True)
     fisher[...] = lax.dot_general(
@@ -233,39 +228,38 @@
 
     gathered = lax.all_gather(sim_maps, BLK, axis=0, tiled=True)
 
-    own = []
-    for dy in range(NY):
-        block = lax.dynamic_slice(templates, (0, lax.rem(y + dy, NY) * SPAN), (ROWS, SPAN))
-        own.append(shift(block, dy, 0) if dy else block)
+    spans = jnp.stack([templates[:, n * SPAN : (n + 1) * SPAN] for n in range(NY)])
+    own = lax.all_to_all(spans, "y", 0, 0, tiled=True)
 
     a_high, a_low = split_rows(inv_cov)
-    gathered, a_high, a_low, *own = lax.optimization_barrier((gathered, a_high, a_low, *own))
-
-    maps = [gathered]
-    sent = []
-    for group in (((2, 1), (2, 0)), ((1, 1), (1, 0)), ((3, 1), (3, 0)), ((0, 1),), ((0, 0),)):
-        at = [lax.rem(y + dy, NY) * 2 + lax.rem(zh + dz, 2) for dy, dz in group]
-        found, maps = rows_of(at, a_high, a_low, maps)
-        found, maps = lax.optimization_barrier((found, maps))
-        for (dy, dz), block in zip(group, found):
-            sent.append(shift(block, dy, dz) if dy or dz else block)
-    sent[-1], *own = lax.optimization_barrier((sent[-1], *own))
-    other = [swap(v) for v in own]
+    gathered, a_high, a_low, own = lax.optimization_barrier((gathered, a_high, a_low, own))
+
+    got = {}
+    for dy in (2, 1, 3, 0):
+        to = lax.rem(y + dy, NY) * 2
+        far, near = rows_of(to + 1 - zh, to + zh, a_high, a_low, gathered)
+        if dy == 3:
+            far, near, *got[2] = lax.optimization_barrier((far, near, *got[2]))
+        got[dy] = [shift(far, dy, 1), shift(near, dy, 0) if dy else near]
+        gathered, a_high = lax.optimization_barrier((gathered, a_high, far))[:2]
+    sent = [value for dy in (2, 1, 3, 0) for value in got[dy]]
     rows = sent[0]
     for value in sent[1:]:
         rows = rows + value
-    rows, band_index, *other = lax.optimization_barrier((rows, band_index, *other))
 
     keep = lax.dynamic_slice(rows, (0, c * HALF), (ROWS, HALF))
     give = lax.dynamic_slice(rows, (0, (1 - c) * HALF), (ROWS, HALF))
     pair = jnp.stack([keep, swap(give)])
+    pair, own, band_index = lax.optimization_barrier((pair, own, band_index))
+    other = swap(own)
     around = [shift(pair, dy, 0) if dy else pair for dy in range(NY)]
     bands = lax.all_to_all(
         jnp.broadcast_to(band_index[None, None, :], (128, 1, 36)), EVERY, 0, 0, tiled=True
     )
-    projected = project([(around[0], own[0], other[0])])
-    projected = project([(around[d], own[d], other[d]) for d in (1, 3)], projected)
-    projected = project([(around[2], own[2], other[2])], projected)
+    held = [lax.rem(y + NY - dy, NY) for dy in range(NY)]
+    projected = project(held[:1], around[:1], own, other)
+    projected = project(held[1::2], around[1::2], own, other, projected)
+    projected = project(held[2:3], around[2:3], own, other, projected)
 
     projected, bands = lax.optimization_barrier((projected, bands))
     pieces = lax.all_to_all(projected, CHIPS, 0, 0, tiled=True)

time: 230 us -> 206 us (0.90)
  local copies, waits for them, and re-layouts: 23.2 us -> 3.93 us
  waiting for transfers between devices: 47.8 us -> 35.7 us
  starting transfers between devices: 45.3 us -> 35 us
  Pallas kernels: 56.4 us -> 65 us
  other arithmetic: 2.11 us -> 7.37 us
  blocking collectives: 40.6 us -> 44.4 us
    ppermute x13 -> x10, waiting for transfers between devices: 44.3 us -> 12.4 us  [shift(): return lax.ppermute(value, RING, pairs)]
    all_to_all x0 -> x1, waiting for transfers between devices: none -> 21.6 us  [per_device(): own = lax.all_to_all(spans, 'y', 0, 0, tiled=True)]
    unnamed x16 -> x8, local copies, waits for them, and re-layouts: 19.3 us -> 1.03 us
    ppermute x5 -> x2, starting transfers between devices: 15.7 us -> 4.64 us  [swap(): return lax.ppermute(value, 'c', [(0, 1), (1, 0)])]
    ppermute x13 -> x10, starting transfers between devices: 22.7 us -> 15.7 us  [shift(): return lax.ppermute(value, RING, pairs)]
    pallas_call x1, Pallas kernels: 10.8 us -> 16.9 us  [split_rows(): pl.pallas_call(split_body, grid=(rows // step,), in_specs=[block], out_sp...]
    pallas_call x8 -> x7, Pallas kernels: 38.5 us -> 44.3 us  [the longest x4 34.9 us: rows_of(): pl.pallas_call(row_body, grid_spec=pltpu.PrefetchScalarGridSpec(num_scala...]
    all_to_all x0 -> x1, starting transfers between devices: none -> 5.01 us  [per_device(): own = lax.all_to_all(spans, 'y', 0, 0, tiled=True)]
  transfers between devices with their start and end apart: 20 -> 15, of which waited for: 7 -> 5; matrix products, arithmetic and copies ran while one was open for 3% -> 4% of each run, Pallas kernels for 10% -> 26%
where the time goes in v7:
time: 206 us; the launch traced here: 205 us
  Pallas kernels  65 us (32%)
  blocking collectives  44.4 us (22%)
  waiting for transfers between devices  35.7 us (17%)
  starting transfers between devices  35 us (17%)
  between operations  14.2 us (7%)
  other arithmetic  7.37 us (4%)
  local copies, waits for them, and re-layouts  3.93 us (2%)
    pallas_call x4, Pallas kernels, rows_of(): pl.pallas_call(row_body, grid_spec=pltpu.PrefetchScalarGridSpec(num_scala...  34.9 us
    all_to_all x1, blocking collectives, per_device(): blocks = lax.all_to_all(sums, ('c',) + CHIPS + ('y',), 0, 0, tiled=True)  22.4 us
    all_to_all x1, blocking collectives, per_device(): pieces = lax.all_to_all(projected, CHIPS, 0, 0, tiled=True)  22 us
    all_to_all x1, waiting for transfers between devices, per_device(): own = lax.all_to_all(spans, 'y', 0, 0, tiled=True)  21.6 us
    pallas_call x1, Pallas kernels, split_rows(): pl.pallas_call(split_body, grid=(rows // step,), in_specs=[block], out_sp...  16.9 us
    ppermute x10, starting transfers between devices, shift(): return lax.ppermute(value, RING, pairs)  15.7 us
    ppermute x10, waiting for transfers between devices, shift(): return lax.ppermute(value, RING, pairs)  12.4 us
    all_to_all x1, starting transfers between devices, per_device(): lax.all_to_all(jnp.broadcast_to(band_index[None, None, :], (128, 1, 36)),...  9.55 us
  transfers between devices with their start and end apart: 15, of which 5 were waited for; matrix products, arithmetic and copies ran while one was open for 4% of the time, Pallas kernels for 26%

profile of v7, /device:TPU:1, one launch (start us, length us, event | category | flops | bytes accessed | tf_op | source)
XLA Modules:
  0.0 205.5 jit_solution(9034575455699988154)
XLA Ops:
  7.9 2.2 %slice_bitcast_fusion.3 = (f32[1,192,1152]{2,1,0:T(8,128)S(1)}, f32[1,192,1152]{2,1,0:T(8,128)S(1)}, f32[1,192,1152]{2,1,0:T(8,128)S(1)}, f32[1,192,1152]{2,1,0:T(8,128)S(1)}) fusion(f32[192,4608]{1,0:T(8,128)} %param.6), kind=kLoop, calls=%fused_computation.4 | loop fusion | bytes 7077888 | tf_op jit(solution)/shard_map/stack | solution.py:231
  12.1 5.0 %all-to-all-start = ((f32[4,192,1152]{2,1,0:T(8,128)}), f32[4,192,1152]{2,1,0:T(8,128)S(1)}, u32[]{:S(2)}, u32[]{:S(2)}) async-start(f32[4,192,1152]{2,1,0:T(8,128)} %pad_maximum_fusion), calls=%async_computation | async-start | bytes 7077888 | tf_op jit(solution)/shard_map/all_to_all | solution.py:232
  17.1 16.9 %shard_map.59 = (bf16[1536,3072]{1,0:T(8,128)(2,1)}, bf16[1536,3072]{1,0:T(8,128)(2,1)}) custom-call(f32[1536,3072]{1,0:T(8,128)} %a.1), custom_call_target="tpu_custom_call" | custom-call | flops 9437184 | bytes 37748736 | tf_op jit(solution)/shard_map/pallas_call | solution.py:58
  36.4 21.6 %all-to-all-done.refs_2_.refs_5_ = f32[4,192,1152]{2,1,0:T(8,128)S(1)} async-done(((f32[4,192,1152]{2,1,0:T(8,128)}), f32[4,192,1152]{2,1,0:T(8,128)S(1)}, u32[]{:S(2)}, u32[]{:S(2)}) %all-to-all-start) | async-done | bytes 3538976 | tf_op jit(solution)/shard_map/all_to_all | solution.py:232
  58.0 8.7 %shard_map.60 = (f32[192,512]{1,0:T(8,128)}, f32[192,512]{1,0:T(8,128)}) custom-call(s32[2]{0:T(128)} %pad_add_fusion.1.at, bf16[1536,3072]{1,0:T(8,128)(2,1)} %get-tuple-element.50.far_high.near_high, bf16[1536,3072]{1,0:T(8,128)(2,1)} %get-tuple-element.50.far_high.near_high, bf16[1536,3072]{1,0:T(8,128)(2,1)} %get-tuple-element.35.far_low.near_low, ...), custom_call_target="tpu_custom_call" | custom-call | flops 3623878656 | bytes 11010048 | tf_op jit(solution)/shard_map/pallas_call | solution.py:95
  66.7 3.7 %collective-permute-start = (f32[192,512]{1,0:T(8,128)}, f32[192,512]{1,0:T(8,128)S(1)}, u32[]{:S(2)}, u32[]{:S(2)}) collective-permute-start(f32[192,512]{1,0:T(8,128)} %get-tuple-element.36), channel_id=1, source_target_pairs={{0,5},{1,4},{2,7},{3,6},{4,1},{5,0},{6,3},{7,2},{8,13},{9,12},{10,... | collective-permute-start | bytes 1179656 | tf_op jit(solution)/shard_map/ppermute | solution.py:43
  70.4 2.6 %collective-permute-start.1 = (f32[192,512]{1,0:T(8,128)}, f32[192,512]{1,0:T(8,128)S(1)}, u32[]{:S(2)}, u32[]{:S(2)}) collective-permute-start(f32[192,512]{1,0:T(8,128)} %get-tuple-element.44), channel_id=1, source_target_pairs={{0,4},{1,5},{2,6},{3,7},{4,0},{5,1},{6,2},{7,3},{8,12},{9,13},{10,... | collective-permute-start | bytes 1179656 | tf_op jit(solution)/shard_map/ppermute | solution.py:43
  73.0 8.7 %shard_map.61 = (f32[192,512]{1,0:T(8,128)}, f32[192,512]{1,0:T(8,128)}) custom-call(s32[2]{0:T(128)} %pad_add_fusion.2.at, bf16[1536,3072]{1,0:T(8,128)(2,1)} %get-tuple-element.50.far_high.near_high, bf16[1536,3072]{1,0:T(8,128)(2,1)} %get-tuple-element.50.far_high.near_high, bf16[1536,3072]{1,0:T(8,128)(2,1)} %get-tuple-element.35.far_low.near_low, ...), custom_call_target="tpu_custom_call" | custom-call | flops 3623878656 | bytes 11010048 | tf_op jit(solution)/shard_map/pallas_call | solution.py:95
  82.0 8.7 %shard_map.62 = (f32[192,512]{1,0:T(8,128)}, f32[192,512]{1,0:T(8,128)}) custom-call(s32[2]{0:T(128)} %pad_add_fusion.at, bf16[1536,3072]{1,0:T(8,128)(2,1)} %get-tuple-element.50.far_high.near_high, bf16[1536,3072]{1,0:T(8,128)(2,1)} %get-tuple-element.50.far_high.near_high, bf16[1536,3072]{1,0:T(8,128)(2,1)} %get-tuple-element.35.far_low.near_low, ...), custom_call_target="tpu_custom_call" | custom-call | flops 3623878656 | bytes 11010048 | tf_op jit(solution)/shard_map/pallas_call | solution.py:95
  90.7 5.1 %collective-permute-start.4 = (f32[192,512]{1,0:T(8,128)}, f32[192,512]{1,0:T(8,128)}, u32[]{:S(2)}, u32[]{:S(2)}) collective-permute-start(f32[192,512]{1,0:T(8,128)} %get-tuple-element.48), channel_id=1, source_target_pairs={{0,7},{1,6},{2,1},{3,0},{4,3},{5,2},{6,5},{7,4},{8,15},{9,14},{10,... | collective-permute-start | bytes 1179656 | tf_op jit(solution)/shard_map/ppermute | solution.py:43
  95.9 8.8 %shard_map.63 = (f32[192,512]{1,0:T(8,128)}, f32[192,512]{1,0:T(8,128)}) custom-call(s32[2]{0:T(128)} %pad_add_fusion.3.at, bf16[1536,3072]{1,0:T(8,128)(2,1)} %get-tuple-element.50.far_high.near_high, bf16[1536,3072]{1,0:T(8,128)(2,1)} %get-tuple-element.50.far_high.near_high, bf16[1536,3072]{1,0:T(8,128)(2,1)} %get-tuple-element.35.far_low.near_low, ...), custom_call_target="tpu_custom_call" | custom-call | flops 3623878656 | bytes 11010048 | tf_op jit(solution)/shard_map/pallas_call | solution.py:95
  106.0 3.2 %collective-permute-done.3 = f32[192,512]{1,0:T(8,128)} collective-permute-done((f32[192,512]{1,0:T(8,128)}, f32[192,512]{1,0:T(8,128)}, u32[]{:S(2)}, u32[]{:S(2)}) %collective-permute-start.3) | collective-permute-done | bytes 393248 | tf_op jit(solution)/shard_map/ppermute | solution.py:43
  109.2 4.7 %collective-permute-done.6 = f32[192,512]{1,0:T(8,128)} collective-permute-done((f32[192,512]{1,0:T(8,128)}, f32[192,512]{1,0:T(8,128)}, u32[]{:S(2)}, u32[]{:S(2)}) %collective-permute-start.6) | collective-permute-done | bytes 393248 | tf_op jit(solution)/shard_map/ppermute | solution.py:43
  113.9 2.2 %add_add_fusion = f32[192,512]{1,0:T(8,128)S(1)} fusion(f32[192,512]{1,0:T(8,128)} %get-tuple-element.53, f32[192,512]{1,0:T(8,128)} %collective-permute-done.6, f32[192,512]{1,0:T(8,128)} %collective-permute-done.5, f32[192,512]{1,0:T(8,128)} %collective-permute-done.4, f32[192,512]{1,0:T(8,128)} %collective-permute-done.3, ...), kind=kLoop, calls=%fused_computation.6 | loop fusion | flops 688128 | bytes 3538944 | tf_op jit(solution)/shard_map/add | solution.py:248
  116.1 4.3 %collective-permute-start.7 = (f32[192,256]{1,0:T(8,128)S(1)}, f32[192,256]{1,0:T(8,128)S(1)}, u32[]{:S(2)}, u32[]{:S(2)}) collective-permute-start(f32[192,256]{1,0:T(8,128)S(1)} %get-tuple-element.65), channel_id=1, source_target_pairs={{0,8},{8,0},{1,9},{9,1},{2,10},{10,2},{3,11},{11,3},{4,12},{12,4},... | collective-permute-start | bytes 589832 | tf_op jit(solution)/shard_map/ppermute | solution.py:47
  122.6 2.7 %collective-permute-start.11 = (f32[2,192,256]{2,1,0:T(8,128)}, f32[2,192,256]{2,1,0:T(8,128)}, u32[]{:S(2)}, u32[]{:S(2)}) collective-permute-start(f32[2,192,256]{2,1,0:T(8,128)} %pad_maximum_fusion.1.refs_1_), channel_id=1, source_target_pairs={{0,6},{1,7},{2,0},{3,1},{4,2},{5,3},{6,4},{7,5},{8,14},{9,15},{10,... | collective-permute-start | bytes 1179656 | tf_op jit(solution)/shard_map/ppermute | solution.py:43
  126.0 9.5 %all-to-all-start.1 = ((s32[128,1,36]{2,1,0:T(1,128)}), s32[128,1,36]{2,1,0:T(1,128)}, u32[]{:S(2)}, u32[]{:S(2)}) async-start(s32[128,1,36]{2,1,0:T(1,128)} %broadcast_in_dim.2), calls=%async_computation.1 | async-start | bytes 131072 | tf_op jit(solution)/shard_map/all_to_all | solution.py:256
  135.6 2.5 %shard_map.64.refs_7_ = f32[16,2,8,1152]{3,2,1,0:T(8,128)S(1)} custom-call(s32[1]{0:T(128)} %bitcast.18.refs_0_, f32[2,192,256]{2,1,0:T(8,128)} %pad_maximum_fusion.1.refs_1_, f32[4,192,1152]{2,1,0:T(8,128)S(1)} %all-to-all-done.refs_2_.refs_5_, f32[4,192,1152]{2,1,0:T(8,128)} %collective-permute-done.9.refs_3_.refs_6_), custom_call_target="tpu_custom_call" | custom-call | flops 679477248 | bytes 1769472 | tf_op jit(solution)/shard_map/pallas_call | solution.py:152
  138.1 4.5 %collective-permute-done.11.refs_4_ = f32[2,192,256]{2,1,0:T(8,128)} collective-permute-done((f32[2,192,256]{2,1,0:T(8,128)}, f32[2,192,256]{2,1,0:T(8,128)}, u32[]{:S(2)}, u32[]{:S(2)}) %collective-permute-start.11) | collective-permute-done | bytes 393248 | tf_op jit(solution)/shard_map/ppermute | solution.py:43
  142.6 4.4 %shard_map.65.refs_4_ = f32[16,2,8,1152]{3,2,1,0:T(8,128)S(1)} custom-call(s32[2]{0:T(128)S(1)} %pad_add_fusion.4.refs_0_, f32[2,192,256]{2,1,0:T(8,128)} %collective-permute-done.10.refs_1_, f32[4,192,1152]{2,1,0:T(8,128)S(1)} %all-to-all-done.refs_2_.refs_5_, f32[4,192,1152]{2,1,0:T(8,128)} %collective-permute-done.9.refs_3_.refs_6_, ...), custom_call_target="tpu_custom_call" | custom-call | flops 1358954496 | bytes 3538944 | tf_op jit(solution)/shard_map/pallas_call | solution.py:152
  147.0 2.5 %shard_map.66 = f32[16,2,8,1152]{3,2,1,0:T(8,128)S(1)} custom-call(s32[1]{0:T(128)} %bitcast.1.refs_0_, f32[2,192,256]{2,1,0:T(8,128)} %collective-permute-done.8.refs_1_, f32[4,192,1152]{2,1,0:T(8,128)S(1)} %all-to-all-done.refs_2_.refs_5_, f32[4,192,1152]{2,1,0:T(8,128)} %collective-permute-done.9.refs_3_.refs_6_, f32[16,2,8,1152]{3,2,1,0:T(8,128)S(1)} %shard_map.65.refs_4_), custom_call_target="tpu_custom_call" | custom-call | flops 679477248 | bytes 1769472 | tf_op jit(solution)/shard_map/pallas_call | solution.py:152
  150.5 22.0 %all_to_all.20.pieces = f32[16,2,8,1152]{3,2,1,0:T(8,128)S(1)} all-to-all(f32[16,2,8,1152]{3,2,1,0:T(8,128)} %copy-done), channel_id=1, replica_groups=mesh['x'=4,'zl'=2,'c'=2,'y'=4,'zh'=2] {'x','zh','zl'}, dimensions={0} | all-to-all | bytes 2359296 | tf_op jit(solution)/shard_map/all_to_all | solution.py:265
  174.2 22.4 %all_to_all.21.blocks = f32[128,8,128]{2,1,0:T(8,128)S(1)} all-to-all(f32[128,8,128]{2,1,0:T(8,128)S(1)} %shard_map.67), channel_id=1, replica_groups=mesh['x'=4,'zl'=2,'c'=2,'y'=4,'zh'=2] {'c','x','zh','zl','y'}, dimensions={0} | all-to-all | bytes 1048576 | tf_op jit(solution)/shard_map/all_to_all | solution.py:277
  196.6 2.1 shard_map.68
  (38 shorter events, 12.4 us)
Async XLA Ops:
  7.2 50.8 %all-gather.2.cloned.1.call-start = ((), (), s32[]{:S(2)}) async-start(), calls=%async_computation.4 | async-start | bytes 6684672 | tf_op jit(solution)/shard_map/all_gather | solution.py:229
  12.1 45.9 %all-to-all-start = ((f32[4,192,1152]{2,1,0:T(8,128)}), f32[4,192,1152]{2,1,0:T(8,128)S(1)}, u32[]{:S(2)}, u32[]{:S(2)}) async-start(f32[4,192,1152]{2,1,0:T(8,128)} %pad_maximum_fusion), calls=%async_computation | async-start | bytes 7077888 | tf_op jit(solution)/shard_map/all_to_all | solution.py:232
  66.7 24.0 %collective-permute-start = (f32[192,512]{1,0:T(8,128)}, f32[192,512]{1,0:T(8,128)S(1)}, u32[]{:S(2)}, u32[]{:S(2)}) collective-permute-start(f32[192,512]{1,0:T(8,128)} %get-tuple-element.36), channel_id=1, source_target_pairs={{0,5},{1,4},{2,7},{3,6},{4,1},{5,0},{6,3},{7,2},{8,13},{9,12},{10,... | collective-permute-start | bytes 1179656 | tf_op jit(solution)/shard_map/ppermute | solution.py:43
  70.4 20.4 %collective-permute-start.1 = (f32[192,512]{1,0:T(8,128)}, f32[192,512]{1,0:T(8,128)S(1)}, u32[]{:S(2)}, u32[]{:S(2)}) collective-permute-start(f32[192,512]{1,0:T(8,128)} %get-tuple-element.44), channel_id=1, source_target_pairs={{0,4},{1,5},{2,6},{3,7},{4,0},{5,1},{6,2},{7,3},{8,12},{9,13},{10,... | collective-permute-start | bytes 1179656 | tf_op jit(solution)/shard_map/ppermute | solution.py:43
  81.7 24.3 %collective-permute-start.2 = (f32[192,512]{1,0:T(8,128)}, f32[192,512]{1,0:T(8,128)}, u32[]{:S(2)}, u32[]{:S(2)}) collective-permute-start(f32[192,512]{1,0:T(8,128)} %get-tuple-element.39), channel_id=1, source_target_pairs={{0,3},{1,2},{2,5},{3,4},{4,7},{5,6},{6,1},{7,0},{8,11},{9,10},{10,... | collective-permute-start | bytes 1179656 | tf_op jit(solution)/shard_map/ppermute | solution.py:43
  81.7 27.5 %collective-permute-start.3 = (f32[192,512]{1,0:T(8,128)}, f32[192,512]{1,0:T(8,128)}, u32[]{:S(2)}, u32[]{:S(2)}) collective-permute-start(f32[192,512]{1,0:T(8,128)} %get-tuple-element.47), channel_id=1, source_target_pairs={{0,2},{1,3},{2,4},{3,5},{4,6},{5,7},{6,0},{7,1},{8,10},{9,11},{10,... | collective-permute-start | bytes 1179656 | tf_op jit(solution)/shard_map/ppermute | solution.py:43
  90.7 13.9 %copy-start.1 = (f32[192,512]{1,0:T(8,128)}, f32[192,512]{1,0:T(8,128)S(1)}, u32[]{:S(2)}) copy-start(f32[192,512]{1,0:T(8,128)S(1)} %collective-permute-done) | copy-start | bytes 1179652
  90.7 13.9 %copy-start.2 = (f32[192,512]{1,0:T(8,128)}, f32[192,512]{1,0:T(8,128)S(1)}, u32[]{:S(2)}) copy-start(f32[192,512]{1,0:T(8,128)S(1)} %collective-permute-done.1) | copy-start | bytes 1179652
  90.7 23.2 %collective-permute-start.4 = (f32[192,512]{1,0:T(8,128)}, f32[192,512]{1,0:T(8,128)}, u32[]{:S(2)}, u32[]{:S(2)}) collective-permute-start(f32[192,512]{1,0:T(8,128)} %get-tuple-element.48), channel_id=1, source_target_pairs={{0,7},{1,6},{2,1},{3,0},{4,3},{5,2},{6,5},{7,4},{8,15},{9,14},{10,... | collective-permute-start | bytes 1179656 | tf_op jit(solution)/shard_map/ppermute | solution.py:43
  104.7 20.7 %copy-start.3 = (s32[36]{0:T(128)S(1)}, s32[36]{0:T(128)}, u32[]{:S(2)}) copy-start(s32[36]{0:T(128)} %param.7) | copy-start | bytes 436
  104.7 9.2 %collective-permute-start.6 = (f32[192,512]{1,0:T(8,128)}, f32[192,512]{1,0:T(8,128)}, u32[]{:S(2)}, u32[]{:S(2)}) collective-permute-start(f32[192,512]{1,0:T(8,128)} %get-tuple-element.52), channel_id=1, source_target_pairs={{0,1},{1,0},{2,3},{3,2},{4,5},{5,4},{6,7},{7,6},{8,9},{9,8},{10,11... | collective-permute-start | bytes 1179656 | tf_op jit(solution)/shard_map/ppermute | solution.py:43
  104.8 9.2 %collective-permute-start.5 = (f32[192,512]{1,0:T(8,128)}, f32[192,512]{1,0:T(8,128)}, u32[]{:S(2)}, u32[]{:S(2)}) collective-permute-start(f32[192,512]{1,0:T(8,128)} %get-tuple-element.49), channel_id=1, source_target_pairs={{0,6},{1,7},{2,0},{3,1},{4,2},{5,3},{6,4},{7,5},{8,14},{9,15},{10,... | collective-permute-start | bytes 1179656 | tf_op jit(solution)/shard_map/ppermute | solution.py:43
  116.1 5.3 %collective-permute-start.7 = (f32[192,256]{1,0:T(8,128)S(1)}, f32[192,256]{1,0:T(8,128)S(1)}, u32[]{:S(2)}, u32[]{:S(2)}) collective-permute-start(f32[192,256]{1,0:T(8,128)S(1)} %get-tuple-element.65), channel_id=1, source_target_pairs={{0,8},{8,0},{1,9},{9,1},{2,10},{10,2},{3,11},{11,3},{4,12},{12,4},... | collective-permute-start | bytes 589832 | tf_op jit(solution)/shard_map/ppermute | solution.py:47
  122.2 13.4 %collective-permute-start.9 = (f32[4,192,1152]{2,1,0:T(8,128)S(1)}, f32[4,192,1152]{2,1,0:T(8,128)}, u32[]{:S(2)}, u32[]{:S(2)}) collective-permute-start(f32[4,192,1152]{2,1,0:T(8,128)S(1)} %all-to-all-done.refs_2_.refs_5_), channel_id=1, source_target_pairs={{0,8},{8,0},{1,9},{9,1},{2,10},{10,2},{3,11},{11,3},{4,12},{12,4},... | collective-permute-start | bytes 10616840 | tf_op jit(solution)/shard_map/ppermute | solution.py:47
  122.6 15.5 %collective-permute-start.10 = (f32[2,192,256]{2,1,0:T(8,128)}, f32[2,192,256]{2,1,0:T(8,128)}, u32[]{:S(2)}, u32[]{:S(2)}) collective-permute-start(f32[2,192,256]{2,1,0:T(8,128)} %pad_maximum_fusion.1.refs_1_), channel_id=1, source_target_pairs={{0,2},{1,3},{2,4},{3,5},{4,6},{5,7},{6,0},{7,1},{8,10},{9,11},{10,... | collective-permute-start | bytes 1179656 | tf_op jit(solution)/shard_map/ppermute | solution.py:43
  122.6 19.9 %collective-permute-start.11 = (f32[2,192,256]{2,1,0:T(8,128)}, f32[2,192,256]{2,1,0:T(8,128)}, u32[]{:S(2)}, u32[]{:S(2)}) collective-permute-start(f32[2,192,256]{2,1,0:T(8,128)} %pad_maximum_fusion.1.refs_1_), channel_id=1, source_target_pairs={{0,6},{1,7},{2,0},{3,1},{4,2},{5,3},{6,4},{7,5},{8,14},{9,15},{10,... | collective-permute-start | bytes 1179656 | tf_op jit(solution)/shard_map/ppermute | solution.py:43
  125.3 21.7 %collective-permute-start.8 = (f32[2,192,256]{2,1,0:T(8,128)}, f32[2,192,256]{2,1,0:T(8,128)}, u32[]{:S(2)}, u32[]{:S(2)}) collective-permute-start(f32[2,192,256]{2,1,0:T(8,128)} %pad_maximum_fusion.1.refs_1_), channel_id=1, source_target_pairs={{0,4},{1,5},{2,6},{3,7},{4,0},{5,1},{6,2},{7,3},{8,12},{9,13},{10,... | collective-permute-start | bytes 1179656 | tf_op jit(solution)/shard_map/ppermute | solution.py:43
  126.0 24.5 %all-to-all-start.1 = ((s32[128,1,36]{2,1,0:T(1,128)}), s32[128,1,36]{2,1,0:T(1,128)}, u32[]{:S(2)}, u32[]{:S(2)}) async-start(s32[128,1,36]{2,1,0:T(1,128)} %broadcast_in_dim.2), calls=%async_computation.1 | async-start | bytes 131072 | tf_op jit(solution)/shard_map/all_to_all | solution.py:256
  149.5 1.0 copy-start
Sparse Core Ops, SparseCore 0:
  9.7 45.9 all-gather.1

commit v8 on v7

--- a/solution.py
+++ b/solution.py
@@ -41,6 +41,10 @@
         for z in range(2)
     ]
     return lax.ppermute(value, RING, pairs)
+
+
+def ring(dy):
+    return [(n, (n + dy) % NY) for n in range(NY)]
 
 
 def swap(value):
@@ -110,7 +114,7 @@
     )(jnp.stack([far, near]).astype(jnp.int32), a_high, a_high, a_low, a_low, maps)
 
 
-def project_body(terms, begun, at, *refs):
+def project_body(terms, begun, *refs):
     out = refs[-1]
     cols = 384
     left = []
@@ -139,9 +143,9 @@
     operands = [v for w in weighted for v in (w, own, other)]
     in_specs = []
     for t in range(terms):
-        block = pl.BlockSpec((1, ROWS, SPAN), lambda i, at, t=t: (at[t], 0, 0))
-        in_specs += [pl.BlockSpec((2, ROWS, HALF), lambda i, at: (0, 0, 0)), block, block]
-    whole = pl.BlockSpec((16, 2, 8, SPAN), lambda i, at: (0, 0, 0, 0))
+        block = pl.BlockSpec((1, ROWS, SPAN), lambda i, t=t: (at[t], 0, 0))
+        in_specs += [pl.BlockSpec((2, ROWS, HALF), lambda i: (0, 0, 0)), block, block]
+    whole = pl.BlockSpec((16, 2, 8, SPAN), lambda i: (0, 0, 0, 0))
     if begun is not None:
         operands.append(begun)
         in_specs.append(whole)
@@ -151,9 +155,9 @@
 
     return pl.pallas_call(
         body,
-        grid_spec=pltpu.PrefetchScalarGridSpec(
-            num_scalar_prefetch=1, grid=(1,), in_specs=in_specs, out_specs=whole
-        ),
+        grid=(1,),
+        in_specs=in_specs,
+        out_specs=whole,
         out_shape=jax.ShapeDtypeStruct((16, 2, 8, SPAN), F32),
         compiler_params=limit(32),
         cost_estimate=pl.CostEstimate(
@@ -161,7 +165,7 @@
             bytes_accessed=8 * terms * ROWS * SPAN,
             transcendentals=0,
         ),
-    )(jnp.stack(at).astype(jnp.int32), *operands)
+    )(*operands)
 
 
 def names_row():
@@ -228,11 +232,18 @@
 
     gathered = lax.all_gather(sim_maps, BLK, axis=0, tiled=True)
 
-    spans = jnp.stack([templates[:, n * SPAN : (n + 1) * SPAN] for n in range(NY)])
-    own = lax.all_to_all(spans, "y", 0, 0, tiled=True)
-
+    columns = []
+    for dy in range(NY):
+        block = lax.dynamic_slice(templates, (0, lax.rem(y + dy, NY) * SPAN), (ROWS, SPAN))
+        columns.append(lax.ppermute(block, "y", ring(dy)) if dy else block)
+
+    bands = lax.all_to_all(
+        jnp.broadcast_to(band_index[None, None, :], (128, 1, 36)), EVERY, 0, 0, tiled=True
+    )
     a_high, a_low = split_rows(inv_cov)
-    gathered, a_high, a_low, own = lax.optimization_barrier((gathered, a_high, a_low, own))
+    gathered, a_high, a_low, bands, *columns = lax.optimization_barrier(
+        (gathered, a_high, a_low, bands, *columns)
+    )
 
     got = {}
     for dy in (2, 1, 3, 0):
@@ -243,6 +254,9 @@
         got[dy] = [shift(far, dy, 1), shift(near, dy, 0) if dy else near]
         gathered, a_high = lax.optimization_barrier((gathered, a_high, far))[:2]
     sent = [value for dy in (2, 1, 3, 0) for value in got[dy]]
+    sent[-1], *columns = lax.optimization_barrier((sent[-1], *columns))
+    own = jnp.stack(columns)
+    *sent, own = lax.optimization_barrier((*sent, own))
     rows = sent[0]
     for value in sent[1:]:
         rows = rows + value
@@ -250,18 +264,13 @@
     keep = lax.dynamic_slice(rows, (0, c * HALF), (ROWS, HALF))
     give = lax.dynamic_slice(rows, (0, (1 - c) * HALF), (ROWS, HALF))
     pair = jnp.stack([keep, swap(give)])
-    pair, own, band_index = lax.optimization_barrier((pair, own, band_index))
+    pair, own = lax.optimization_barrier((pair, own))
     other = swap(own)
     around = [shift(pair, dy, 0) if dy else pair for dy in range(NY)]
-    bands = lax.all_to_all(
-        jnp.broadcast_to(band_index[None, None, :], (128, 1, 36)), EVERY, 0, 0, tiled=True
-    )
-    held = [lax.rem(y + NY - dy, NY) for dy in range(NY)]
-    projected = project(held[:1], around[:1], own, other)
-    projected = project(held[1::2], around[1::2], own, other, projected)
-    projected = project(held[2:3], around[2:3], own, other, projected)
-
-    projected, bands = lax.optimization_barrier((projected, bands))
+    projected = project((0,), around[:1], own, other)
+    projected = project((1, 3), around[1::2], own, other, projected)
+    projected = project((2,), around[2:3], own, other, projected)
+
     pieces = lax.all_to_all(projected, CHIPS, 0, 0, tiled=True)
 
     sums = pl.pallas_call(

time: 206 us -> 198 us (0.961)
  Pallas kernels: 65 us -> 58.6 us
  other arithmetic: 7.37 us -> 4.56 us
  waiting for transfers between devices: 35.7 us -> 38.2 us
    all_to_all x1 -> x0, waiting for transfers between devices: 21.6 us -> none  [per_device(): own = lax.all_to_all(spans, 'y', 0, 0, tiled=True)]
    all_to_all x1, waiting for transfers between devices: 0.01 us -> 14.1 us  [per_device(): lax.all_to_all(jnp.broadcast_to(band_index[None, None, :], (128, 1, 36)),...]
    ppermute x10, waiting for transfers between devices: 12.4 us -> 19.1 us  [shift(): return lax.ppermute(value, RING, pairs)]
    ppermute x0 -> x3, starting transfers between devices: none -> 5.81 us  [per_device(): columns.append(lax.ppermute(block, 'y', ring(dy)) if dy else block)]
    all_to_all x1 -> x0, starting transfers between devices: 5.01 us -> none  [per_device(): own = lax.all_to_all(spans, 'y', 0, 0, tiled=True)]
    pallas_call x3, Pallas kernels: 9.39 us -> 4.61 us  [project(): pl.pallas_call(body, grid=(1,), in_specs=in_specs, out_specs=whole, out_s...]
    dynamic_slice x0 -> x1, local copies, waits for them, and re-layouts: none -> 3.51 us  [per_device(): lax.dynamic_slice(templates, (0, lax.rem(y + dy, NY) * SPAN), (ROWS, SPAN))]
    ppermute x2, waiting for transfers between devices: 1.07 us -> 4.21 us  [swap(): return lax.ppermute(value, 'c', [(0, 1), (1, 0)])]
  transfers between devices with their start and end apart: 15 -> 17, of which waited for: 5 -> 6; matrix products, arithmetic and copies ran while one was open for 4% -> 3% of each run, Pallas kernels for 26% -> 24%
where the time goes in v8:
time: 198 us; the launch traced here: 197 us
  Pallas kernels  58.6 us (30%)
  blocking collectives  43.9 us (22%)
  waiting for transfers between devices  38.2 us (19%)
  starting transfers between devices  33.8 us (17%)
  between operations  14.2 us (7%)
  other arithmetic  4.56 us (2%)
  local copies, waits for them, and re-layouts  4.22 us (2%)
    pallas_call x4, Pallas kernels, rows_of(): pl.pallas_call(row_body, grid_spec=pltpu.PrefetchScalarGridSpec(num_scala...  34.9 us
    all_to_all x1, blocking collectives, per_device(): pieces = lax.all_to_all(projected, CHIPS, 0, 0, tiled=True)  23 us
    all_to_all x1, blocking collectives, per_device(): blocks = lax.all_to_all(sums, ('c',) + CHIPS + ('y',), 0, 0, tiled=True)  20.9 us
    ppermute x10, waiting for transfers between devices, shift(): return lax.ppermute(value, RING, pairs)  19.1 us
    pallas_call x1, Pallas kernels, split_rows(): pl.pallas_call(split_body, grid=(rows // step,), in_specs=[block], out_sp...  17 us
    ppermute x10, starting transfers between devices, shift(): return lax.ppermute(value, RING, pairs)  15.2 us
    all_to_all x1, waiting for transfers between devices, per_device(): lax.all_to_all(jnp.broadcast_to(band_index[None, None, :], (128, 1, 36)),...  14.1 us
    all_to_all x1, starting transfers between devices, per_device(): lax.all_to_all(jnp.broadcast_to(band_index[None, None, :], (128, 1, 36)),...  8.99 us
  transfers between devices with their start and end apart: 17, of which 6 were waited for; matrix products, arithmetic and copies ran while one was open for 3% of the time, Pallas kernels for 24%

profile of v8, /device:TPU:1, one launch (start us, length us, event | category | flops | bytes accessed | tf_op | source)
XLA Modules:
  0.0 197.5 jit_solution(9807261191592501201)
XLA Ops:
  7.9 3.5 %constant_dynamic-slice_fusion.1 = (f32[192,1152]{1,0:T(8,128)}, f32[192,1152]{1,0:T(8,128)}, f32[192,1152]{1,0:T(8,128)S(1)}, f32[192,1152]{1,0:T(8,128)}) fusion(f32[192,4608]{1,0:T(8,128)} %param.6, s32[]{:T(128)S(6)} %select_n.21, s32[]{:T(128)S(6)} %select_n.19, s32[]{:T(128)S(6)} %select_n.18, s32[]{:T(128)S(6)} %select_n.20), kind=kLoop, calls=%fused_computation.5 | loop fusion | bytes 7077904 | tf_op jit(solution)/shard_map/dynamic_slice | solution.py:237
  11.4 2.1 %collective-permute-start = (f32[192,1152]{1,0:T(8,128)}, f32[192,1152]{1,0:T(8,128)S(1)}, u32[]{:S(2)}, u32[]{:S(2)}) collective-permute-start(f32[192,1152]{1,0:T(8,128)} %get-tuple-element.91), channel_id=1, source_target_pairs={{0,2},{2,4},{4,6},{6,0},{1,3},{3,5},{5,7},{7,1},{8,10},{10,12},{12... | collective-permute-start | bytes 2654216 | tf_op jit(solution)/shard_map/ppermute | solution.py:238
  13.6 2.6 %collective-permute-start.1 = (f32[192,1152]{1,0:T(8,128)}, f32[192,1152]{1,0:T(8,128)S(1)}, u32[]{:S(2)}, u32[]{:S(2)}) collective-permute-start(f32[192,1152]{1,0:T(8,128)} %get-tuple-element.93), channel_id=1, source_target_pairs={{0,4},{2,6},{4,0},{6,2},{1,5},{3,7},{5,1},{7,3},{8,12},{10,14},{12... | collective-permute-start | bytes 2654216 | tf_op jit(solution)/shard_map/ppermute | solution.py:238
  17.9 9.0 %all-to-all-start = ((s32[128,1,36]{2,1,0:T(1,128)}), s32[128,1,36]{2,1,0:T(1,128)S(1)}, u32[]{:S(2)}, u32[]{:S(2)}) async-start(s32[128,1,36]{2,1,0:T(1,128)} %broadcast_in_dim.2), calls=%async_computation | async-start | bytes 131072 | tf_op jit(solution)/shard_map/all_to_all | solution.py:240
  28.2 17.0 %shard_map.59 = (bf16[1536,3072]{1,0:T(8,128)(2,1)}, bf16[1536,3072]{1,0:T(8,128)(2,1)}) custom-call(f32[1536,3072]{1,0:T(8,128)} %a.1), custom_call_target="tpu_custom_call" | custom-call | flops 9437184 | bytes 37748736 | tf_op jit(solution)/shard_map/pallas_call | solution.py:62
  45.3 14.1 %all-to-all-done.bands = s32[128,1,36]{2,1,0:T(1,128)S(1)} async-done(((s32[128,1,36]{2,1,0:T(1,128)}), s32[128,1,36]{2,1,0:T(1,128)S(1)}, u32[]{:S(2)}, u32[]{:S(2)}) %all-to-all-start) | async-done | bytes 18464 | tf_op jit(solution)/shard_map/all_to_all | solution.py:240
  59.4 8.7 %shard_map.60 = (f32[192,512]{1,0:T(8,128)}, f32[192,512]{1,0:T(8,128)}) custom-call(s32[2]{0:T(128)} %get-tuple-element.97.at, bf16[1536,3072]{1,0:T(8,128)(2,1)} %get-tuple-element.65.far_high.near_high, bf16[1536,3072]{1,0:T(8,128)(2,1)} %get-tuple-element.65.far_high.near_high, bf16[1536,3072]{1,0:T(8,128)(2,1)} %get-tuple-element.50.far_low.near_low, ...), custom_call_target="tpu_custom_call" | custom-call | flops 3623878656 | bytes 11010048 | tf_op jit(solution)/shard_map/pallas_call | solution.py:99
  68.2 3.2 %collective-permute-start.3 = (f32[192,512]{1,0:T(8,128)}, f32[192,512]{1,0:T(8,128)S(1)}, u32[]{:S(2)}, u32[]{:S(2)}) collective-permute-start(f32[192,512]{1,0:T(8,128)} %get-tuple-element.51), channel_id=1, source_target_pairs={{0,5},{1,4},{2,7},{3,6},{4,1},{5,0},{6,3},{7,2},{8,13},{9,12},{10,... | collective-permute-start | bytes 1179656 | tf_op jit(solution)/shard_map/ppermute | solution.py:43
  72.1 8.7 %shard_map.61 = (f32[192,512]{1,0:T(8,128)}, f32[192,512]{1,0:T(8,128)}) custom-call(s32[2]{0:T(128)} %get-tuple-element.98.at, bf16[1536,3072]{1,0:T(8,128)(2,1)} %get-tuple-element.65.far_high.near_high, bf16[1536,3072]{1,0:T(8,128)(2,1)} %get-tuple-element.65.far_high.near_high, bf16[1536,3072]{1,0:T(8,128)(2,1)} %get-tuple-element.50.far_low.near_low, ...), custom_call_target="tpu_custom_call" | custom-call | flops 3623878656 | bytes 11010048 | tf_op jit(solution)/shard_map/pallas_call | solution.py:99
  80.8 3.2 %collective-permute-start.5 = (f32[192,512]{1,0:T(8,128)}, f32[192,512]{1,0:T(8,128)}, u32[]{:S(2)}, u32[]{:S(2)}) collective-permute-start(f32[192,512]{1,0:T(8,128)} %get-tuple-element.54), channel_id=1, source_target_pairs={{0,3},{1,2},{2,5},{3,4},{4,7},{5,6},{6,1},{7,0},{8,11},{9,10},{10,... | collective-permute-start | bytes 1179656 | tf_op jit(solution)/shard_map/ppermute | solution.py:43
  84.3 8.7 %shard_map.62 = (f32[192,512]{1,0:T(8,128)}, f32[192,512]{1,0:T(8,128)}) custom-call(s32[2]{0:T(128)} %get-tuple-element.96.at, bf16[1536,3072]{1,0:T(8,128)(2,1)} %get-tuple-element.65.far_high.near_high, bf16[1536,3072]{1,0:T(8,128)(2,1)} %get-tuple-element.65.far_high.near_high, bf16[1536,3072]{1,0:T(8,128)(2,1)} %get-tuple-element.50.far_low.near_low, ...), custom_call_target="tpu_custom_call" | custom-call | flops 3623878656 | bytes 11010048 | tf_op jit(solution)/shard_map/pallas_call | solution.py:99
  93.0 3.4 %collective-permute-start.7 = (f32[192,512]{1,0:T(8,128)}, f32[192,512]{1,0:T(8,128)}, u32[]{:S(2)}, u32[]{:S(2)}) collective-permute-start(f32[192,512]{1,0:T(8,128)} %get-tuple-element.63), channel_id=1, source_target_pairs={{0,7},{1,6},{2,1},{3,0},{4,3},{5,2},{6,5},{7,4},{8,15},{9,14},{10,... | collective-permute-start | bytes 1179656 | tf_op jit(solution)/shard_map/ppermute | solution.py:43
  96.3 8.7 %shard_map.63 = (f32[192,512]{1,0:T(8,128)}, f32[192,512]{1,0:T(8,128)}) custom-call(s32[2]{0:T(128)} %get-tuple-element.99.at, bf16[1536,3072]{1,0:T(8,128)(2,1)} %get-tuple-element.65.far_high.near_high, bf16[1536,3072]{1,0:T(8,128)(2,1)} %get-tuple-element.65.far_high.near_high, bf16[1536,3072]{1,0:T(8,128)(2,1)} %get-tuple-element.50.far_low.near_low, ...), custom_call_target="tpu_custom_call" | custom-call | flops 3623878656 | bytes 11010048 | tf_op jit(solution)/shard_map/pallas_call | solution.py:99
  105.1 1.8 collective-permute-start.9
  108.3 7.1 %collective-permute-done.9 = f32[192,512]{1,0:T(8,128)} collective-permute-done((f32[192,512]{1,0:T(8,128)}, f32[192,512]{1,0:T(8,128)}, u32[]{:S(2)}, u32[]{:S(2)}) %collective-permute-start.9) | collective-permute-done | bytes 393248 | tf_op jit(solution)/shard_map/ppermute | solution.py:43
  115.5 1.8 add_add_fusion
  117.3 3.3 %collective-permute-start.10 = (f32[192,256]{1,0:T(8,128)S(1)}, f32[192,256]{1,0:T(8,128)S(1)}, u32[]{:S(2)}, u32[]{:S(2)}) collective-permute-start(f32[192,256]{1,0:T(8,128)S(1)} %get-tuple-element.95), channel_id=1, source_target_pairs={{0,8},{8,0},{1,9},{9,1},{2,10},{10,2},{3,11},{11,3},{4,12},{12,4},... | collective-permute-start | bytes 589832 | tf_op jit(solution)/shard_map/ppermute | solution.py:51
  122.2 2.7 %collective-permute-start.14 = (f32[2,192,256]{2,1,0:T(8,128)S(1)}, f32[2,192,256]{2,1,0:T(8,128)S(1)}, u32[]{:S(2)}, u32[]{:S(2)}) collective-permute-start(f32[2,192,256]{2,1,0:T(8,128)S(1)} %pad_maximum_fusion.1.refs_0_), channel_id=1, source_target_pairs={{0,6},{1,7},{2,0},{3,1},{4,2},{5,3},{6,4},{7,5},{8,14},{9,15},{10,... | collective-permute-start | bytes 1179656 | tf_op jit(solution)/shard_map/ppermute | solution.py:43
  124.9 3.1 %collective-permute-done.12.refs_2_.refs_5_ = f32[4,192,1152]{2,1,0:T(8,128)S(1)} collective-permute-done((f32[4,192,1152]{2,1,0:T(8,128)S(1)}, f32[4,192,1152]{2,1,0:T(8,128)S(1)}, u32[]{:S(2)}, u32[]{:S(2)}) %collective-permute-start.12) | collective-permute-done | bytes 3538976 | tf_op jit(solution)/shard_map/ppermute | solution.py:51
  129.3 5.0 %collective-permute-done.13.refs_0_ = f32[2,192,256]{2,1,0:T(8,128)S(1)} collective-permute-done((f32[2,192,256]{2,1,0:T(8,128)S(1)}, f32[2,192,256]{2,1,0:T(8,128)S(1)}, u32[]{:S(2)}, u32[]{:S(2)}) %collective-permute-start.13) | collective-permute-done | bytes 393248 | tf_op jit(solution)/shard_map/ppermute | solution.py:43
  134.3 7.0 %collective-permute-done.14.refs_3_ = f32[2,192,256]{2,1,0:T(8,128)S(1)} collective-permute-done((f32[2,192,256]{2,1,0:T(8,128)S(1)}, f32[2,192,256]{2,1,0:T(8,128)S(1)}, u32[]{:S(2)}, u32[]{:S(2)}) %collective-permute-start.14) | collective-permute-done | bytes 393248 | tf_op jit(solution)/shard_map/ppermute | solution.py:43
  141.2 2.2 %shard_map.65.refs_3_ = f32[16,2,8,1152]{3,2,1,0:T(8,128)S(1)} custom-call(f32[2,192,256]{2,1,0:T(8,128)S(1)} %collective-permute-done.13.refs_0_, f32[4,192,1152]{2,1,0:T(8,128)S(1)} %pad_maximum_fusion.refs_1_.refs_4_, f32[4,192,1152]{2,1,0:T(8,128)S(1)} %collective-permute-done.12.refs_2_.refs_5_, f32[2,192,256]{2,1,0:T(8,128)S(1)} %collective-permute-done.14.refs_3_, ...), custom_call_target="tpu_custom_call" | custom-call | flops 1358954496 | bytes 3538944 | tf_op jit(solution)/shard_map/pallas_call | solution.py:156
  144.7 23.0 %all_to_all.15.pieces = f32[16,2,8,1152]{3,2,1,0:T(8,128)S(1)} all-to-all(f32[16,2,8,1152]{3,2,1,0:T(8,128)S(1)} %shard_map.66), channel_id=1, replica_groups=mesh['x'=4,'zl'=2,'c'=2,'y'=4,'zh'=2] {'x','zh','zl'}, dimensions={0} | all-to-all | bytes 2359296 | tf_op jit(solution)/shard_map/all_to_all | solution.py:274
  168.6 20.9 %all_to_all.16.blocks = f32[128,8,128]{2,1,0:T(8,128)S(1)} all-to-all(f32[128,8,128]{2,1,0:T(8,128)S(1)} %shard_map.67), channel_id=1, replica_groups=mesh['x'=4,'zl'=2,'c'=2,'y'=4,'zh'=2] {'c','x','zh','zl','y'}, dimensions={0} | all-to-all | bytes 1048576 | tf_op jit(solution)/shard_map/all_to_all | solution.py:286
  (35 shorter events, 12.3 us)
Async XLA Ops:
  7.2 52.3 %all-gather.2.cloned.1.call-start = ((), (), s32[]{:S(2)}) async-start(), calls=%async_computation.3 | async-start | bytes 6684672 | tf_op jit(solution)/shard_map/all_gather | solution.py:233
  7.9 9.3 %copy-start.1 = (s32[36]{0:T(128)S(1)}, s32[36]{0:T(128)}, u32[]{:S(2)}) copy-start(s32[36]{0:T(128)} %param.7) | copy-start | bytes 436
  11.4 47.9 %collective-permute-start = (f32[192,1152]{1,0:T(8,128)}, f32[192,1152]{1,0:T(8,128)S(1)}, u32[]{:S(2)}, u32[]{:S(2)}) collective-permute-start(f32[192,1152]{1,0:T(8,128)} %get-tuple-element.91), channel_id=1, source_target_pairs={{0,2},{2,4},{4,6},{6,0},{1,3},{3,5},{5,7},{7,1},{8,10},{10,12},{12... | collective-permute-start | bytes 2654216 | tf_op jit(solution)/shard_map/ppermute | solution.py:238
  13.6 45.8 %collective-permute-start.1 = (f32[192,1152]{1,0:T(8,128)}, f32[192,1152]{1,0:T(8,128)S(1)}, u32[]{:S(2)}, u32[]{:S(2)}) collective-permute-start(f32[192,1152]{1,0:T(8,128)} %get-tuple-element.93), channel_id=1, source_target_pairs={{0,4},{2,6},{4,0},{6,2},{1,5},{3,7},{5,1},{7,3},{8,12},{10,14},{12... | collective-permute-start | bytes 2654216 | tf_op jit(solution)/shard_map/ppermute | solution.py:238
  16.2 43.2 %collective-permute-start.2 = (f32[192,1152]{1,0:T(8,128)}, f32[192,1152]{1,0:T(8,128)}, u32[]{:S(2)}, u32[]{:S(2)}) collective-permute-start(f32[192,1152]{1,0:T(8,128)} %get-tuple-element.90), channel_id=1, source_target_pairs={{0,6},{2,0},{4,2},{6,4},{1,7},{3,1},{5,3},{7,5},{8,14},{10,8},{12,... | collective-permute-start | bytes 2654216 | tf_op jit(solution)/shard_map/ppermute | solution.py:238
  17.9 41.5 %all-to-all-start = ((s32[128,1,36]{2,1,0:T(1,128)}), s32[128,1,36]{2,1,0:T(1,128)S(1)}, u32[]{:S(2)}, u32[]{:S(2)}) async-start(s32[128,1,36]{2,1,0:T(1,128)} %broadcast_in_dim.2), calls=%async_computation | async-start | bytes 131072 | tf_op jit(solution)/shard_map/all_to_all | solution.py:240
  68.2 24.8 %collective-permute-start.3 = (f32[192,512]{1,0:T(8,128)}, f32[192,512]{1,0:T(8,128)S(1)}, u32[]{:S(2)}, u32[]{:S(2)}) collective-permute-start(f32[192,512]{1,0:T(8,128)} %get-tuple-element.51), channel_id=1, source_target_pairs={{0,5},{1,4},{2,7},{3,6},{4,1},{5,0},{6,3},{7,2},{8,13},{9,12},{10,... | collective-permute-start | bytes 1179656 | tf_op jit(solution)/shard_map/ppermute | solution.py:43
  71.4 21.6 %collective-permute-start.4 = (f32[192,512]{1,0:T(8,128)}, f32[192,512]{1,0:T(8,128)S(1)}, u32[]{:S(2)}, u32[]{:S(2)}) collective-permute-start(f32[192,512]{1,0:T(8,128)} %get-tuple-element.59), channel_id=1, source_target_pairs={{0,4},{1,5},{2,6},{3,7},{4,0},{5,1},{6,2},{7,3},{8,12},{9,13},{10,... | collective-permute-start | bytes 1179656 | tf_op jit(solution)/shard_map/ppermute | solution.py:43
  80.8 27.5 %collective-permute-start.5 = (f32[192,512]{1,0:T(8,128)}, f32[192,512]{1,0:T(8,128)}, u32[]{:S(2)}, u32[]{:S(2)}) collective-permute-start(f32[192,512]{1,0:T(8,128)} %get-tuple-element.54), channel_id=1, source_target_pairs={{0,3},{1,2},{2,5},{3,4},{4,7},{5,6},{6,1},{7,0},{8,11},{9,10},{10,... | collective-permute-start | bytes 1179656 | tf_op jit(solution)/shard_map/ppermute | solution.py:43
  84.0 24.4 %collective-permute-start.6 = (f32[192,512]{1,0:T(8,128)}, f32[192,512]{1,0:T(8,128)}, u32[]{:S(2)}, u32[]{:S(2)}) collective-permute-start(f32[192,512]{1,0:T(8,128)} %get-tuple-element.62), channel_id=1, source_target_pairs={{0,2},{1,3},{2,4},{3,5},{4,6},{5,7},{6,0},{7,1},{8,10},{9,11},{10,... | collective-permute-start | bytes 1179656 | tf_op jit(solution)/shard_map/ppermute | solution.py:43
  93.0 22.5 %collective-permute-start.7 = (f32[192,512]{1,0:T(8,128)}, f32[192,512]{1,0:T(8,128)}, u32[]{:S(2)}, u32[]{:S(2)}) collective-permute-start(f32[192,512]{1,0:T(8,128)} %get-tuple-element.63), channel_id=1, source_target_pairs={{0,7},{1,6},{2,1},{3,0},{4,3},{5,2},{6,5},{7,4},{8,15},{9,14},{10,... | collective-permute-start | bytes 1179656 | tf_op jit(solution)/shard_map/ppermute | solution.py:43
  105.1 10.4 %collective-permute-start.9 = (f32[192,512]{1,0:T(8,128)}, f32[192,512]{1,0:T(8,128)}, u32[]{:S(2)}, u32[]{:S(2)}) collective-permute-start(f32[192,512]{1,0:T(8,128)} %get-tuple-element.67), channel_id=1, source_target_pairs={{0,1},{1,0},{2,3},{3,2},{4,5},{5,4},{6,7},{7,6},{8,9},{9,8},{10,11... | collective-permute-start | bytes 1179656 | tf_op jit(solution)/shard_map/ppermute | solution.py:43
  106.9 8.6 %collective-permute-start.8 = (f32[192,512]{1,0:T(8,128)}, f32[192,512]{1,0:T(8,128)}, u32[]{:S(2)}, u32[]{:S(2)}) collective-permute-start(f32[192,512]{1,0:T(8,128)} %get-tuple-element.64), channel_id=1, source_target_pairs={{0,6},{1,7},{2,0},{3,1},{4,2},{5,3},{6,4},{7,5},{8,14},{9,15},{10,... | collective-permute-start | bytes 1179656 | tf_op jit(solution)/shard_map/ppermute | solution.py:43
  106.9 8.6 %copy-start = (f32[192,512]{1,0:T(8,128)S(1)}, f32[192,512]{1,0:T(8,128)}, u32[]{:S(2)}) copy-start(f32[192,512]{1,0:T(8,128)} %get-tuple-element.85) | copy-start | bytes 1179652
  117.3 4.4 %collective-permute-start.10 = (f32[192,256]{1,0:T(8,128)S(1)}, f32[192,256]{1,0:T(8,128)S(1)}, u32[]{:S(2)}, u32[]{:S(2)}) collective-permute-start(f32[192,256]{1,0:T(8,128)S(1)} %get-tuple-element.95), channel_id=1, source_target_pairs={{0,8},{8,0},{1,9},{9,1},{2,10},{10,2},{3,11},{11,3},{4,12},{12,4},... | collective-permute-start | bytes 589832 | tf_op jit(solution)/shard_map/ppermute | solution.py:51
  121.8 6.3 %collective-permute-start.12 = (f32[4,192,1152]{2,1,0:T(8,128)S(1)}, f32[4,192,1152]{2,1,0:T(8,128)S(1)}, u32[]{:S(2)}, u32[]{:S(2)}) collective-permute-start(f32[4,192,1152]{2,1,0:T(8,128)S(1)} %pad_maximum_fusion.refs_1_.refs_4_), channel_id=1, source_target_pairs={{0,8},{8,0},{1,9},{9,1},{2,10},{10,2},{3,11},{11,3},{4,12},{12,4},... | collective-permute-start | bytes 10616840 | tf_op jit(solution)/shard_map/ppermute | solution.py:51
  122.2 12.1 %collective-permute-start.13 = (f32[2,192,256]{2,1,0:T(8,128)S(1)}, f32[2,192,256]{2,1,0:T(8,128)S(1)}, u32[]{:S(2)}, u32[]{:S(2)}) collective-permute-start(f32[2,192,256]{2,1,0:T(8,128)S(1)} %pad_maximum_fusion.1.refs_0_), channel_id=1, source_target_pairs={{0,2},{1,3},{2,4},{3,5},{4,6},{5,7},{6,0},{7,1},{8,10},{9,11},{10,... | collective-permute-start | bytes 1179656 | tf_op jit(solution)/shard_map/ppermute | solution.py:43
  122.2 19.0 %collective-permute-start.14 = (f32[2,192,256]{2,1,0:T(8,128)S(1)}, f32[2,192,256]{2,1,0:T(8,128)S(1)}, u32[]{:S(2)}, u32[]{:S(2)}) collective-permute-start(f32[2,192,256]{2,1,0:T(8,128)S(1)} %pad_maximum_fusion.1.refs_0_), channel_id=1, source_target_pairs={{0,6},{1,7},{2,0},{3,1},{4,2},{5,3},{6,4},{7,5},{8,14},{9,15},{10,... | collective-permute-start | bytes 1179656 | tf_op jit(solution)/shard_map/ppermute | solution.py:43
  124.9 18.5 %collective-permute-start.11 = (f32[2,192,256]{2,1,0:T(8,128)S(1)}, f32[2,192,256]{2,1,0:T(8,128)S(1)}, u32[]{:S(2)}, u32[]{:S(2)}) collective-permute-start(f32[2,192,256]{2,1,0:T(8,128)S(1)} %pad_maximum_fusion.1.refs_0_), channel_id=1, source_target_pairs={{0,4},{1,5},{2,6},{3,7},{4,0},{5,1},{6,2},{7,3},{8,12},{9,13},{10,... | collective-permute-start | bytes 1179656 | tf_op jit(solution)/shard_map/ppermute | solution.py:43
Sparse Core Ops, SparseCore 0:
  9.7 46.6 all-gather.1

commit v9 on v8

--- a/solution.py
+++ b/solution.py
@@ -65,7 +65,7 @@
         in_specs=[block],
         out_specs=[block] * 2,
         out_shape=[jax.ShapeDtypeStruct(a.shape, BF16)] * 2,
-        compiler_params=limit(58),
+        compiler_params=limit(20),
         cost_estimate=pl.CostEstimate(
             flops=2 * rows * cols, bytes_accessed=8 * rows * cols, transcendentals=0
         ),
@@ -82,36 +82,37 @@
         out[...] += value
 
 
-def row_body(at, far_high, near_high, far_low, near_low, s, far, near):
+def row_body(at, a_high, a_low, s, far, near):
     sh, sl = split(s[...])
-    ah = jnp.concatenate([far_high[...], near_high[...]], axis=0)
-    al = jnp.concatenate([far_low[...], near_low[...]], axis=0)
-    found = dot(ah, sh) + dot(ah, sl) + dot(al, sh)
-    add_step(far, found[:ROWS])
-    add_step(near, found[ROWS:])
-
-
-def rows_of(far, near, a_high, a_low, maps):
+    ah = a_high[...]
+    found = dot(ah, sh) + dot(ah, sl) + dot(a_low[...], sh)
+    first, second = found[:ROWS], found[ROWS:]
+    swapped = at[1] == 0
+    add_step(far, jnp.where(swapped, second, first))
+    add_step(near, jnp.where(swapped, first, second))
+
+
+def rows_of(to, zh, a_high, a_low, maps):
     inner, cols = maps.shape
     step = 1024
-    a_blocks = [pl.BlockSpec((ROWS, step), lambda k, at, n=n: (at[n], k)) for n in range(2)]
+    a_block = pl.BlockSpec((2 * ROWS, step), lambda k, at: (at[0], k))
     o_block = pl.BlockSpec((ROWS, cols), lambda k, at: (0, 0))
     return pl.pallas_call(
         row_body,
         grid_spec=pltpu.PrefetchScalarGridSpec(
             num_scalar_prefetch=1,
             grid=(inner // step,),
-            in_specs=a_blocks * 2 + [pl.BlockSpec((step, cols), lambda k, at: (k, 0))],
+            in_specs=[a_block, a_block, pl.BlockSpec((step, cols), lambda k, at: (k, 0))],
             out_specs=[o_block] * 2,
         ),
         out_shape=[jax.ShapeDtypeStruct((ROWS, cols), F32)] * 2,
-        compiler_params=limit(58),
+        compiler_params=limit(20),
         cost_estimate=pl.CostEstimate(
             flops=12 * ROWS * inner * cols,
             bytes_accessed=4 * inner * (2 * ROWS + cols),
             transcendentals=0,
         ),
-    )(jnp.stack([far, near]).astype(jnp.int32), a_high, a_high, a_low, a_low, maps)
+    )(jnp.stack([to, zh]).astype(jnp.int32), a_high, a_low, maps)
 
 
 def project_body(terms, begun, *refs):
@@ -241,18 +242,15 @@
         jnp.broadcast_to(band_index[None, None, :], (128, 1, 36)), EVERY, 0, 0, tiled=True
     )
     a_high, a_low = split_rows(inv_cov)
-    gathered, a_high, a_low, bands, *columns = lax.optimization_barrier(
-        (gathered, a_high, a_low, bands, *columns)
-    )
+    gathered, bands, *columns = lax.optimization_barrier((gathered, bands, *columns))
 
     got = {}
     for dy in (2, 1, 3, 0):
-        to = lax.rem(y + dy, NY) * 2
-        far, near = rows_of(to + 1 - zh, to + zh, a_high, a_low, gathered)
+        far, near = rows_of(lax.rem(y + dy, NY), zh, a_high, a_low, gathered)
         if dy == 3:
             far, near, *got[2] = lax.optimization_barrier((far, near, *got[2]))
         got[dy] = [shift(far, dy, 1), shift(near, dy, 0) if dy else near]
-        gathered, a_high = lax.optimization_barrier((gathered, a_high, far))[:2]
+        gathered, far = lax.optimization_barrier((gathered, far))
     sent = [value for dy in (2, 1, 3, 0) for value in got[dy]]
     sent[-1], *columns = lax.optimization_barrier((sent[-1], *columns))
     own = jnp.stack(columns)

time: 198 us -> 201 us (1.015)
  Pallas kernels: 58.6 us -> 39.8 us
  local copies, waits for them, and re-layouts: 4.22 us -> 22 us
  waiting for transfers between devices: 38.2 us -> 46 us
    unnamed x4 -> x26, local copies, waits for them, and re-layouts: 0.01 us -> 17.7 us
    pallas_call x4, Pallas kernels: 34.9 us -> 22 us  [rows_of(): pl.pallas_call(row_body, grid_spec=pltpu.PrefetchScalarGridSpec(num_scala...]
    ppermute x10, waiting for transfers between devices: 19.1 us -> 28.3 us  [shift(): return lax.ppermute(value, RING, pairs)]
    pallas_call x1, Pallas kernels: 17 us -> 11.1 us  [split_rows(): pl.pallas_call(split_body, grid=(rows // step,), in_specs=[block], out_sp...]
    all_to_all x1, blocking collectives: 23 us -> 19.5 us  [per_device(): pieces = lax.all_to_all(projected, CHIPS, 0, 0, tiled=True)]
    ppermute x2, starting transfers between devices: 3.77 us -> 1.02 us  [swap(): return lax.ppermute(value, 'c', [(0, 1), (1, 0)])]
  transfers between devices with their start and end apart: 17 -> 17, of which waited for: 6 -> 9; matrix products, arithmetic and copies ran while one was open for 3% -> 3% of each run, Pallas kernels for 24% -> 15%
where the time goes in v9:
time: 201 us
  waiting for transfers between devices  46 us (23%)
  blocking collectives  41.9 us (21%)
  Pallas kernels  39.8 us (20%)
  starting transfers between devices  32.5 us (16%)
  local copies, waits for them, and re-layouts  22 us (11%)
  between operations  14.3 us (7%)
  other arithmetic  4.01 us (2%)
    ppermute x10, waiting for transfers between devices, shift(): return lax.ppermute(value, RING, pairs)  28.3 us
    all_to_all x1, blocking collectives, per_device(): blocks = lax.all_to_all(sums, ('c',) + CHIPS + ('y',), 0, 0, tiled=True)  22.3 us
    pallas_call x4, Pallas kernels, rows_of(): pl.pallas_call(row_body, grid_spec=pltpu.PrefetchScalarGridSpec(num_scala...  22 us
    all_to_all x1, blocking collectives, per_device(): pieces = lax.all_to_all(projected, CHIPS, 0, 0, tiled=True)  19.5 us
    unnamed x26, local copies, waits for them, and re-layouts  17.7 us
    ppermute x10, starting transfers between devices, shift(): return lax.ppermute(value, RING, pairs)  16.6 us
    all_to_all x1, waiting for transfers between devices, per_device(): lax.all_to_all(jnp.broadcast_to(band_index[None, None, :], (128, 1, 36)),...  13.9 us
    pallas_call x1, Pallas kernels, split_rows(): pl.pallas_call(split_body, grid=(rows // step,), in_specs=[block], out_sp...  11.1 us
  transfers between devices with their start and end apart: 17, of which 9 were waited for; matrix products, arithmetic and copies ran while one was open for 3% of the time, Pallas kernels for 15%

profile of v9, /device:TPU:1, one launch (start us, length us, event | category | flops | bytes accessed | tf_op | source)
XLA Modules:
  0.0 200.5 jit_solution(1480797879722659938)
XLA Ops:
  7.9 3.6 %constant_dynamic-slice_fusion.1 = (f32[192,1152]{1,0:T(8,128)}, f32[192,1152]{1,0:T(8,128)}, f32[192,1152]{1,0:T(8,128)S(1)}, f32[192,1152]{1,0:T(8,128)}) fusion(f32[192,4608]{1,0:T(8,128)} %param.6, s32[]{:T(128)S(6)} %select_n.21, s32[]{:T(128)S(6)} %select_n.19, s32[]{:T(128)S(6)} %select_n.18, s32[]{:T(128)S(6)} %select_n.20), kind=kLoop, calls=%fused_computation.5 | loop fusion | bytes 7077904 | tf_op jit(solution)/shard_map/dynamic_slice | solution.py:238
  13.7 2.6 %collective-permute-start.1 = (f32[192,1152]{1,0:T(8,128)}, f32[192,1152]{1,0:T(8,128)}, u32[]{:S(2)}, u32[]{:S(2)}) collective-permute-start(f32[192,1152]{1,0:T(8,128)} %get-tuple-element.83), channel_id=1, source_target_pairs={{0,4},{2,6},{4,0},{6,2},{1,5},{3,7},{5,1},{7,3},{8,12},{10,14},{12... | collective-permute-start | bytes 2654216 | tf_op jit(solution)/shard_map/ppermute | solution.py:239
  18.1 9.0 %all-to-all-start = ((s32[128,1,36]{2,1,0:T(1,128)}), s32[128,1,36]{2,1,0:T(1,128)S(1)}, u32[]{:S(2)}, u32[]{:S(2)}) async-start(s32[128,1,36]{2,1,0:T(1,128)} %broadcast_in_dim.2), calls=%async_computation | async-start | bytes 131072 | tf_op jit(solution)/shard_map/all_to_all | solution.py:241
  27.2 11.1 %shard_map.59 = (bf16[1536,3072]{1,0:T(8,128)(2,1)S(1)}, bf16[1536,3072]{1,0:T(8,128)(2,1)S(1)}) custom-call(f32[1536,3072]{1,0:T(8,128)} %a.1), custom_call_target="tpu_custom_call" | custom-call | flops 9437184 | bytes 37748736 | tf_op jit(solution)/shard_map/pallas_call | solution.py:62
  38.4 3.6 %copy-done = bf16[1536,3072]{1,0:T(8,128)(2,1)} copy-done((bf16[1536,3072]{1,0:T(8,128)(2,1)}, bf16[1536,3072]{1,0:T(8,128)(2,1)S(1)}, u32[]{:S(2)}) %copy-start) | copy-done | bytes 9437208
  42.0 3.6 %copy-done.2 = bf16[1536,3072]{1,0:T(8,128)(2,1)} copy-done((bf16[1536,3072]{1,0:T(8,128)(2,1)}, bf16[1536,3072]{1,0:T(8,128)(2,1)S(1)}, u32[]{:S(2)}) %copy-start.2) | copy-done | bytes 9437208
  45.6 13.9 %all-to-all-done.bands = s32[128,1,36]{2,1,0:T(1,128)S(1)} async-done(((s32[128,1,36]{2,1,0:T(1,128)}), s32[128,1,36]{2,1,0:T(1,128)S(1)}, u32[]{:S(2)}, u32[]{:S(2)}) %all-to-all-start) | async-done | bytes 18464 | tf_op jit(solution)/shard_map/all_to_all | solution.py:241
  59.6 4.0 %copy-done.1 = bf16[1536,3072]{1,0:T(8,128)(2,1)S(1)} copy-done((bf16[1536,3072]{1,0:T(8,128)(2,1)S(1)}, bf16[1536,3072]{1,0:T(8,128)(2,1)}, u32[]{:S(2)}) %copy-start.1) | copy-done | bytes 9437208
  63.5 3.7 %copy-done.3 = bf16[1536,3072]{1,0:T(8,128)(2,1)S(1)} copy-done((bf16[1536,3072]{1,0:T(8,128)(2,1)S(1)}, bf16[1536,3072]{1,0:T(8,128)(2,1)}, u32[]{:S(2)}) %copy-start.3) | copy-done | bytes 9437208
  67.2 2.8 %copy-done.4 = f32[3072,512]{1,0:T(8,128)S(1)} copy-done((f32[3072,512]{1,0:T(8,128)S(1)}, f32[3072,512]{1,0:T(8,128)}, u32[]{:S(2)}) %copy-start.4) | copy-done | bytes 6291480
  70.0 5.5 %shard_map.60 = (f32[192,512]{1,0:T(8,128)S(1)}, f32[192,512]{1,0:T(8,128)S(1)}) custom-call(s32[2]{0:T(128)S(1)} %get-tuple-element.87.at, bf16[1536,3072]{1,0:T(8,128)(2,1)S(1)} %copy-done.1, bf16[1536,3072]{1,0:T(8,128)(2,1)S(1)} %copy-done.3, f32[3072,512]{1,0:T(8,128)S(1)} %copy-done.4), custom_call_target="tpu_custom_call" | custom-call | flops 3623878656 | bytes 11010048 | tf_op jit(solution)/shard_map/pallas_call | solution.py:100
  75.5 3.3 %collective-permute-start.3 = (f32[192,512]{1,0:T(8,128)S(1)}, f32[192,512]{1,0:T(8,128)S(1)}, u32[]{:S(2)}, u32[]{:S(2)}) collective-permute-start(f32[192,512]{1,0:T(8,128)S(1)} %get-tuple-element.44), channel_id=1, source_target_pairs={{0,5},{1,4},{2,7},{3,6},{4,1},{5,0},{6,3},{7,2},{8,13},{9,12},{10,... | collective-permute-start | bytes 1179656 | tf_op jit(solution)/shard_map/ppermute | solution.py:43
  79.5 5.5 %shard_map.61 = (f32[192,512]{1,0:T(8,128)S(1)}, f32[192,512]{1,0:T(8,128)S(1)}) custom-call(s32[2]{0:T(128)S(1)} %get-tuple-element.88.at, bf16[1536,3072]{1,0:T(8,128)(2,1)S(1)} %copy-done.1, bf16[1536,3072]{1,0:T(8,128)(2,1)S(1)} %copy-done.3, f32[3072,512]{1,0:T(8,128)S(1)} %copy-done.4), custom_call_target="tpu_custom_call" | custom-call | flops 3623878656 | bytes 11010048 | tf_op jit(solution)/shard_map/pallas_call | solution.py:100
  85.0 3.3 %collective-permute-start.5 = (f32[192,512]{1,0:T(8,128)S(1)}, f32[192,512]{1,0:T(8,128)}, u32[]{:S(2)}, u32[]{:S(2)}) collective-permute-start(f32[192,512]{1,0:T(8,128)S(1)} %get-tuple-element.46), channel_id=1, source_target_pairs={{0,3},{1,2},{2,5},{3,4},{4,7},{5,6},{6,1},{7,0},{8,11},{9,10},{10,... | collective-permute-start | bytes 1179656 | tf_op jit(solution)/shard_map/ppermute | solution.py:43
  88.5 5.5 %shard_map.62 = (f32[192,512]{1,0:T(8,128)S(1)}, f32[192,512]{1,0:T(8,128)S(1)}) custom-call(s32[2]{0:T(128)S(1)} %get-tuple-element.86.at, bf16[1536,3072]{1,0:T(8,128)(2,1)S(1)} %copy-done.1, bf16[1536,3072]{1,0:T(8,128)(2,1)S(1)} %copy-done.3, f32[3072,512]{1,0:T(8,128)S(1)} %copy-done.4), custom_call_target="tpu_custom_call" | custom-call | flops 3623878656 | bytes 11010048 | tf_op jit(solution)/shard_map/pallas_call | solution.py:100
  94.0 2.5 %collective-permute-done.4 = f32[192,512]{1,0:T(8,128)S(1)} collective-permute-done((f32[192,512]{1,0:T(8,128)S(1)}, f32[192,512]{1,0:T(8,128)S(1)}, u32[]{:S(2)}, u32[]{:S(2)}) %collective-permute-start.4) | collective-permute-done | bytes 393248 | tf_op jit(solution)/shard_map/ppermute | solution.py:43
  96.5 3.2 %collective-permute-start.7 = (f32[192,512]{1,0:T(8,128)S(1)}, f32[192,512]{1,0:T(8,128)}, u32[]{:S(2)}, u32[]{:S(2)}) collective-permute-start(f32[192,512]{1,0:T(8,128)S(1)} %get-tuple-element.54), channel_id=1, source_target_pairs={{0,7},{1,6},{2,1},{3,0},{4,3},{5,2},{6,5},{7,4},{8,15},{9,14},{10,... | collective-permute-start | bytes 1179656 | tf_op jit(solution)/shard_map/ppermute | solution.py:43
  99.7 5.5 %shard_map.63 = (f32[192,512]{1,0:T(8,128)S(1)}, f32[192,512]{1,0:T(8,128)S(1)}) custom-call(s32[2]{0:T(128)S(1)} %get-tuple-element.89.at, bf16[1536,3072]{1,0:T(8,128)(2,1)S(1)} %copy-done.1, bf16[1536,3072]{1,0:T(8,128)(2,1)S(1)} %copy-done.3, f32[3072,512]{1,0:T(8,128)S(1)} %bitcast.14), custom_call_target="tpu_custom_call" | custom-call | flops 3623878656 | bytes 11010048 | tf_op jit(solution)/shard_map/pallas_call | solution.py:100
  111.3 5.3 %collective-permute-done.6 = f32[192,512]{1,0:T(8,128)} collective-permute-done((f32[192,512]{1,0:T(8,128)S(1)}, f32[192,512]{1,0:T(8,128)}, u32[]{:S(2)}, u32[]{:S(2)}) %collective-permute-start.6) | collective-permute-done | bytes 393248 | tf_op jit(solution)/shard_map/ppermute | solution.py:43
  116.6 7.7 %collective-permute-done.9 = f32[192,512]{1,0:T(8,128)} collective-permute-done((f32[192,512]{1,0:T(8,128)S(1)}, f32[192,512]{1,0:T(8,128)}, u32[]{:S(2)}, u32[]{:S(2)}) %collective-permute-start.9) | collective-permute-done | bytes 393248 | tf_op jit(solution)/shard_map/ppermute | solution.py:43
  135.4 4.9 %collective-permute-done.13.refs_0_ = f32[2,192,256]{2,1,0:T(8,128)S(1)} collective-permute-done((f32[2,192,256]{2,1,0:T(8,128)S(1)}, f32[2,192,256]{2,1,0:T(8,128)S(1)}, u32[]{:S(2)}, u32[]{:S(2)}) %collective-permute-start.13) | collective-permute-done | bytes 393248 | tf_op jit(solution)/shard_map/ppermute | solution.py:43
  142.5 6.0 %collective-permute-done.11.refs_0_ = f32[2,192,256]{2,1,0:T(8,128)S(1)} collective-permute-done((f32[2,192,256]{2,1,0:T(8,128)S(1)}, f32[2,192,256]{2,1,0:T(8,128)S(1)}, u32[]{:S(2)}, u32[]{:S(2)}) %collective-permute-start.11) | collective-permute-done | bytes 393248 | tf_op jit(solution)/shard_map/ppermute | solution.py:43
  149.7 19.5 %all_to_all.15.pieces = f32[16,2,8,1152]{3,2,1,0:T(8,128)S(1)} all-to-all(f32[16,2,8,1152]{3,2,1,0:T(8,128)S(1)} %shard_map.66), channel_id=1, replica_groups=mesh['x'=4,'zl'=2,'c'=2,'y'=4,'zh'=2] {'x','zh','zl'}, dimensions={0} | all-to-all | bytes 2359296 | tf_op jit(solution)/shard_map/all_to_all | solution.py:272
  170.1 22.3 %all_to_all.16.blocks = f32[128,8,128]{2,1,0:T(8,128)S(1)} all-to-all(f32[128,8,128]{2,1,0:T(8,128)S(1)} %shard_map.67), channel_id=1, replica_groups=mesh['x'=4,'zl'=2,'c'=2,'y'=4,'zh'=2] {'c','x','zh','zl','y'}, dimensions={0} | all-to-all | bytes 1048576 | tf_op jit(solution)/shard_map/all_to_all | solution.py:284
  (58 shorter events, 28.4 us)
Async XLA Ops:
  7.2 52.4 %all-gather.2.cloned.1.call-start = ((), (), s32[]{:S(2)}) async-start(), calls=%async_computation.3 | async-start | bytes 6684672 | tf_op jit(solution)/shard_map/all_gather | solution.py:234
  7.9 9.5 %copy-start.10 = (s32[36]{0:T(128)S(1)}, s32[36]{0:T(128)}, u32[]{:S(2)}) copy-start(s32[36]{0:T(128)} %param.7) | copy-start | bytes 436
  11.6 47.9 %collective-permute-start = (f32[192,1152]{1,0:T(8,128)}, f32[192,1152]{1,0:T(8,128)S(1)}, u32[]{:S(2)}, u32[]{:S(2)}) collective-permute-start(f32[192,1152]{1,0:T(8,128)} %get-tuple-element.81), channel_id=1, source_target_pairs={{0,2},{2,4},{4,6},{6,0},{1,3},{3,5},{5,7},{7,1},{8,10},{10,12},{12... | collective-permute-start | bytes 2654216 | tf_op jit(solution)/shard_map/ppermute | solution.py:239
  13.7 45.8 %collective-permute-start.1 = (f32[192,1152]{1,0:T(8,128)}, f32[192,1152]{1,0:T(8,128)}, u32[]{:S(2)}, u32[]{:S(2)}) collective-permute-start(f32[192,1152]{1,0:T(8,128)} %get-tuple-element.83), channel_id=1, source_target_pairs={{0,4},{2,6},{4,0},{6,2},{1,5},{3,7},{5,1},{7,3},{8,12},{10,14},{12... | collective-permute-start | bytes 2654216 | tf_op jit(solution)/shard_map/ppermute | solution.py:239
  16.3 43.2 %collective-permute-start.2 = (f32[192,1152]{1,0:T(8,128)}, f32[192,1152]{1,0:T(8,128)}, u32[]{:S(2)}, u32[]{:S(2)}) collective-permute-start(f32[192,1152]{1,0:T(8,128)} %get-tuple-element.80), channel_id=1, source_target_pairs={{0,6},{2,0},{4,2},{6,4},{1,7},{3,1},{5,3},{7,5},{8,14},{10,8},{12,... | collective-permute-start | bytes 2654216 | tf_op jit(solution)/shard_map/ppermute | solution.py:239
  18.1 41.5 %all-to-all-start = ((s32[128,1,36]{2,1,0:T(1,128)}), s32[128,1,36]{2,1,0:T(1,128)S(1)}, u32[]{:S(2)}, u32[]{:S(2)}) async-start(s32[128,1,36]{2,1,0:T(1,128)} %broadcast_in_dim.2), calls=%async_computation | async-start | bytes 131072 | tf_op jit(solution)/shard_map/all_to_all | solution.py:241
  59.5 16.0 %copy-start.5 = (f32[192,1152]{1,0:T(8,128)}, f32[192,1152]{1,0:T(8,128)S(1)}, u32[]{:S(2)}) copy-start(f32[192,1152]{1,0:T(8,128)S(1)} %collective-permute-done) | copy-start | bytes 2654212
  75.5 18.5 %collective-permute-start.3 = (f32[192,512]{1,0:T(8,128)S(1)}, f32[192,512]{1,0:T(8,128)S(1)}, u32[]{:S(2)}, u32[]{:S(2)}) collective-permute-start(f32[192,512]{1,0:T(8,128)S(1)} %get-tuple-element.44), channel_id=1, source_target_pairs={{0,5},{1,4},{2,7},{3,6},{4,1},{5,0},{6,3},{7,2},{8,13},{9,12},{10,... | collective-permute-start | bytes 1179656 | tf_op jit(solution)/shard_map/ppermute | solution.py:43
  78.8 17.7 %collective-permute-start.4 = (f32[192,512]{1,0:T(8,128)S(1)}, f32[192,512]{1,0:T(8,128)S(1)}, u32[]{:S(2)}, u32[]{:S(2)}) collective-permute-start(f32[192,512]{1,0:T(8,128)S(1)} %get-tuple-element.50), channel_id=1, source_target_pairs={{0,4},{1,5},{2,6},{3,7},{4,0},{5,1},{6,2},{7,3},{8,12},{9,13},{10,... | collective-permute-start | bytes 1179656 | tf_op jit(solution)/shard_map/ppermute | solution.py:43
  85.0 26.4 %collective-permute-start.5 = (f32[192,512]{1,0:T(8,128)S(1)}, f32[192,512]{1,0:T(8,128)}, u32[]{:S(2)}, u32[]{:S(2)}) collective-permute-start(f32[192,512]{1,0:T(8,128)S(1)} %get-tuple-element.46), channel_id=1, source_target_pairs={{0,3},{1,2},{2,5},{3,4},{4,7},{5,6},{6,1},{7,0},{8,11},{9,10},{10,... | collective-permute-start | bytes 1179656 | tf_op jit(solution)/shard_map/ppermute | solution.py:43
  88.2 28.4 %collective-permute-start.6 = (f32[192,512]{1,0:T(8,128)S(1)}, f32[192,512]{1,0:T(8,128)}, u32[]{:S(2)}, u32[]{:S(2)}) collective-permute-start(f32[192,512]{1,0:T(8,128)S(1)} %get-tuple-element.53), channel_id=1, source_target_pairs={{0,2},{1,3},{2,4},{3,5},{4,6},{5,7},{6,0},{7,1},{8,10},{9,11},{10,... | collective-permute-start | bytes 1179656 | tf_op jit(solution)/shard_map/ppermute | solution.py:43
  88.5 11.2 %slice-start = ((s8[6291456]{0:T(1024)(128)(4,1)}), s8[4194304]{0:T(1024)(128)(4,1)S(1)}, s32[]{:S(2)}) async-start(s8[6291456]{0:T(1024)(128)(4,1)} %bitcast.13), calls=%async_computation.4 | async-start | bytes 8388608
  88.5 11.2 %slice-start.1 = ((s8[6291456]{0:T(1024)(128)(4,1)}), s8[2097152]{0:T(1024)(128)(4,1)S(1)}, s32[]{:S(2)}) async-start(s8[6291456]{0:T(1024)(128)(4,1)} %bitcast.13), calls=%async_computation.5 | async-start | bytes 4194304
  94.0 11.2 %copy-start.6 = (f32[192,512]{1,0:T(8,128)}, f32[192,512]{1,0:T(8,128)S(1)}, u32[]{:S(2)}) copy-start(f32[192,512]{1,0:T(8,128)S(1)} %collective-permute-done.3) | copy-start | bytes 1179652
  96.5 27.8 %collective-permute-start.7 = (f32[192,512]{1,0:T(8,128)S(1)}, f32[192,512]{1,0:T(8,128)}, u32[]{:S(2)}, u32[]{:S(2)}) collective-permute-start(f32[192,512]{1,0:T(8,128)S(1)} %get-tuple-element.54), channel_id=1, source_target_pairs={{0,7},{1,6},{2,1},{3,0},{4,3},{5,2},{6,5},{7,4},{8,15},{9,14},{10,... | collective-permute-start | bytes 1179656 | tf_op jit(solution)/shard_map/ppermute | solution.py:43
  105.2 19.1 %collective-permute-start.9 = (f32[192,512]{1,0:T(8,128)S(1)}, f32[192,512]{1,0:T(8,128)}, u32[]{:S(2)}, u32[]{:S(2)}) collective-permute-start(f32[192,512]{1,0:T(8,128)S(1)} %get-tuple-element.57), channel_id=1, source_target_pairs={{0,1},{1,0},{2,3},{3,2},{4,5},{5,4},{6,7},{7,6},{8,9},{9,8},{10,11... | collective-permute-start | bytes 1179656 | tf_op jit(solution)/shard_map/ppermute | solution.py:43
  106.5 17.9 %collective-permute-start.8 = (f32[192,512]{1,0:T(8,128)S(1)}, f32[192,512]{1,0:T(8,128)}, u32[]{:S(2)}, u32[]{:S(2)}) collective-permute-start(f32[192,512]{1,0:T(8,128)S(1)} %get-tuple-element.55), channel_id=1, source_target_pairs={{0,6},{1,7},{2,0},{3,1},{4,2},{5,3},{6,4},{7,5},{8,14},{9,15},{10,... | collective-permute-start | bytes 1179656 | tf_op jit(solution)/shard_map/ppermute | solution.py:43
  107.4 17.0 %copy-start.7 = (f32[192,512]{1,0:T(8,128)S(1)}, f32[192,512]{1,0:T(8,128)}, u32[]{:S(2)}) copy-start(f32[192,512]{1,0:T(8,128)} %copy-done.6) | copy-start | bytes 1179652
  107.4 17.0 %copy-start.9 = (f32[192,512]{1,0:T(8,128)S(1)}, f32[192,512]{1,0:T(8,128)}, u32[]{:S(2)}) copy-start(f32[192,512]{1,0:T(8,128)} %copy-done.8) | copy-start | bytes 1179652
  126.3 1.6 collective-permute-start.10
  127.9 6.3 %collective-permute-start.12 = (f32[4,192,1152]{2,1,0:T(8,128)S(1)}, f32[4,192,1152]{2,1,0:T(8,128)S(1)}, u32[]{:S(2)}, u32[]{:S(2)}) collective-permute-start(f32[4,192,1152]{2,1,0:T(8,128)S(1)} %pad_maximum_fusion.refs_1_.refs_4_), channel_id=1, source_target_pairs={{0,8},{8,0},{1,9},{9,1},{2,10},{10,2},{3,11},{11,3},{4,12},{12,4},... | collective-permute-start | bytes 10616840 | tf_op jit(solution)/shard_map/ppermute | solution.py:51
  128.4 11.9 %collective-permute-start.13 = (f32[2,192,256]{2,1,0:T(8,128)S(1)}, f32[2,192,256]{2,1,0:T(8,128)S(1)}, u32[]{:S(2)}, u32[]{:S(2)}) collective-permute-start(f32[2,192,256]{2,1,0:T(8,128)S(1)} %pad_maximum_fusion.1.refs_0_), channel_id=1, source_target_pairs={{0,2},{1,3},{2,4},{3,5},{4,6},{5,7},{6,0},{7,1},{8,10},{9,11},{10,... | collective-permute-start | bytes 1179656 | tf_op jit(solution)/shard_map/ppermute | solution.py:43
  129.2 11.1 %collective-permute-start.14 = (f32[2,192,256]{2,1,0:T(8,128)S(1)}, f32[2,192,256]{2,1,0:T(8,128)S(1)}, u32[]{:S(2)}, u32[]{:S(2)}) collective-permute-start(f32[2,192,256]{2,1,0:T(8,128)S(1)} %pad_maximum_fusion.1.refs_0_), channel_id=1, source_target_pairs={{0,6},{1,7},{2,0},{3,1},{4,2},{5,3},{6,4},{7,5},{8,14},{9,15},{10,... | collective-permute-start | bytes 1179656 | tf_op jit(solution)/shard_map/ppermute | solution.py:43
  131.1 17.4 %collective-permute-start.11 = (f32[2,192,256]{2,1,0:T(8,128)S(1)}, f32[2,192,256]{2,1,0:T(8,128)S(1)}, u32[]{:S(2)}, u32[]{:S(2)}) collective-permute-start(f32[2,192,256]{2,1,0:T(8,128)S(1)} %pad_maximum_fusion.1.refs_0_), channel_id=1, source_target_pairs={{0,4},{1,5},{2,6},{3,7},{4,0},{5,1},{6,2},{7,3},{8,12},{9,13},{10,... | collective-permute-start | bytes 1179656 | tf_op jit(solution)/shard_map/ppermute | solution.py:43
  (6 other events, 26.4 us)
Sparse Core Ops, SparseCore 0:
  9.7 46.6 all-gather.1

commit v10 on v9

--- a/solution.py
+++ b/solution.py
@@ -65,7 +65,7 @@
         in_specs=[block],
         out_specs=[block] * 2,
         out_shape=[jax.ShapeDtypeStruct(a.shape, BF16)] * 2,
-        compiler_params=limit(20),
+        compiler_params=limit(58),
         cost_estimate=pl.CostEstimate(
             flops=2 * rows * cols, bytes_accessed=8 * rows * cols, transcendentals=0
         ),
@@ -94,7 +94,7 @@
 
 def rows_of(to, zh, a_high, a_low, maps):
     inner, cols = maps.shape
-    step = 1024
+    step = 1536
     a_block = pl.BlockSpec((2 * ROWS, step), lambda k, at: (at[0], k))
     o_block = pl.BlockSpec((ROWS, cols), lambda k, at: (0, 0))
     return pl.pallas_call(
@@ -106,7 +106,7 @@
             out_specs=[o_block] * 2,
         ),
         out_shape=[jax.ShapeDtypeStruct((ROWS, cols), F32)] * 2,
-        compiler_params=limit(20),
+        compiler_params=limit(58),
         cost_estimate=pl.CostEstimate(
             flops=12 * ROWS * inner * cols,
             bytes_accessed=4 * inner * (2 * ROWS + cols),
@@ -242,15 +242,17 @@
         jnp.broadcast_to(band_index[None, None, :], (128, 1, 36)), EVERY, 0, 0, tiled=True
     )
     a_high, a_low = split_rows(inv_cov)
-    gathered, bands, *columns = lax.optimization_barrier((gathered, bands, *columns))
+    gathered, a_high, a_low = lax.optimization_barrier((gathered, a_high, a_low))
 
     got = {}
     for dy in (2, 1, 3, 0):
         far, near = rows_of(lax.rem(y + dy, NY), zh, a_high, a_low, gathered)
+        if dy == 2:
+            far, near, bands, *columns = lax.optimization_barrier((far, near, bands, *columns))
         if dy == 3:
             far, near, *got[2] = lax.optimization_barrier((far, near, *got[2]))
         got[dy] = [shift(far, dy, 1), shift(near, dy, 0) if dy else near]
-        gathered, far = lax.optimization_barrier((gathered, far))
+        gathered, a_high = lax.optimization_barrier((gathered, a_high, far))[:2]
     sent = [value for dy in (2, 1, 3, 0) for value in got[dy]]
     sent[-1], *columns = lax.optimization_barrier((sent[-1], *columns))
     own = jnp.stack(columns)

time: 201 us -> 193 us (0.960)
  local copies, waits for them, and re-layouts: 22 us -> 4.22 us
  Pallas kernels: 39.8 us -> 57.4 us
  waiting for transfers between devices: 46 us -> 37.4 us
    unnamed x26 -> x4, local copies, waits for them, and re-layouts: 17.7 us -> 0.01 us
    all_to_all x1, waiting for transfers between devices: 13.9 us -> 0.01 us  [per_device(): lax.all_to_all(jnp.broadcast_to(band_index[None, None, :], (128, 1, 36)),...]
    pallas_call x4, Pallas kernels: 22 us -> 33.7 us  [rows_of(): pl.pallas_call(row_body, grid_spec=pltpu.PrefetchScalarGridSpec(num_scala...]
    all_gather x1, waiting for transfers between devices: 0.02 us -> 11.3 us  [per_device(): gathered = lax.all_gather(sim_maps, BLK, axis=0, tiled=True)]
    ppermute x10, waiting for transfers between devices: 28.3 us -> 21.9 us  [shift(): return lax.ppermute(value, RING, pairs)]
    pallas_call x1, Pallas kernels: 11.1 us -> 17 us  [split_rows(): pl.pallas_call(split_body, grid=(rows // step,), in_specs=[block], out_sp...]
    ppermute x2, starting transfers between devices: 1.02 us -> 3.31 us  [swap(): return lax.ppermute(value, 'c', [(0, 1), (1, 0)])]
  transfers between devices with their start and end apart: 17 -> 17, of which waited for: 9 -> 6; matrix products, arithmetic and copies ran while one was open for 3% -> 4% of each run, Pallas kernels for 15% -> 28%
where the time goes in v10:
time: 193 us
  Pallas kernels  57.4 us (30%)
  blocking collectives  41.1 us (21%)
  waiting for transfers between devices  37.4 us (19%)
  starting transfers between devices  33.8 us (18%)
  between operations  14.2 us (7%)
  other arithmetic  4.55 us (2%)
  local copies, waits for them, and re-layouts  4.22 us (2%)
    pallas_call x4, Pallas kernels, rows_of(): pl.pallas_call(row_body, grid_spec=pltpu.PrefetchScalarGridSpec(num_scala...  33.7 us
    ppermute x10, waiting for transfers between devices, shift(): return lax.ppermute(value, RING, pairs)  21.9 us
    all_to_all x1, blocking collectives, per_device(): blocks = lax.all_to_all(sums, ('c',) + CHIPS + ('y',), 0, 0, tiled=True)  20.8 us
    all_to_all x1, blocking collectives, per_device(): pieces = lax.all_to_all(projected, CHIPS, 0, 0, tiled=True)  20.3 us
    pallas_call x1, Pallas kernels, split_rows(): pl.pallas_call(split_body, grid=(rows // step,), in_specs=[block], out_sp...  17 us
    ppermute x10, starting transfers between devices, shift(): return lax.ppermute(value, RING, pairs)  15.7 us
    all_gather x1, waiting for transfers between devices, per_device(): gathered = lax.all_gather(sim_maps, BLK, axis=0, tiled=True)  11.3 us
    all_to_all x1, starting transfers between devices, per_device(): lax.all_to_all(jnp.broadcast_to(band_index[None, None, :], (128, 1, 36)),...  8.99 us
  transfers between devices with their start and end apart: 17, of which 6 were waited for; matrix products, arithmetic and copies ran while one was open for 4% of the time, Pallas kernels for 28%

profile of v10, /device:TPU:1, one launch (start us, length us, event | category | flops | bytes accessed | tf_op | source)
XLA Modules:
  0.0 192.7 jit_solution(4167905231536131046)
XLA Ops:
  7.9 3.5 %constant_dynamic-slice_fusion.1 = (f32[192,1152]{1,0:T(8,128)}, f32[192,1152]{1,0:T(8,128)}, f32[192,1152]{1,0:T(8,128)S(1)}, f32[192,1152]{1,0:T(8,128)}) fusion(f32[192,4608]{1,0:T(8,128)} %param.6, s32[]{:T(128)S(6)} %select_n.21, s32[]{:T(128)S(6)} %select_n.19, s32[]{:T(128)S(6)} %select_n.18, s32[]{:T(128)S(6)} %select_n.20), kind=kLoop, calls=%fused_computation.5 | loop fusion | bytes 7077904 | tf_op jit(solution)/shard_map/dynamic_slice | solution.py:238
  11.4 2.1 %collective-permute-start = (f32[192,1152]{1,0:T(8,128)}, f32[192,1152]{1,0:T(8,128)S(1)}, u32[]{:S(2)}, u32[]{:S(2)}) collective-permute-start(f32[192,1152]{1,0:T(8,128)} %get-tuple-element.95), channel_id=1, source_target_pairs={{0,2},{2,4},{4,6},{6,0},{1,3},{3,5},{5,7},{7,1},{8,10},{10,12},{12... | collective-permute-start | bytes 2654216 | tf_op jit(solution)/shard_map/ppermute | solution.py:239
  13.6 2.6 %collective-permute-start.1 = (f32[192,1152]{1,0:T(8,128)}, f32[192,1152]{1,0:T(8,128)S(1)}, u32[]{:S(2)}, u32[]{:S(2)}) collective-permute-start(f32[192,1152]{1,0:T(8,128)} %get-tuple-element.97), channel_id=1, source_target_pairs={{0,4},{2,6},{4,0},{6,2},{1,5},{3,7},{5,1},{7,3},{8,12},{10,14},{12... | collective-permute-start | bytes 2654216 | tf_op jit(solution)/shard_map/ppermute | solution.py:239
  17.9 9.0 %all-to-all-start = ((s32[128,1,36]{2,1,0:T(1,128)}), s32[128,1,36]{2,1,0:T(1,128)S(1)}, u32[]{:S(2)}, u32[]{:S(2)}) async-start(s32[128,1,36]{2,1,0:T(1,128)} %broadcast_in_dim.2), calls=%async_computation | async-start | bytes 131072 | tf_op jit(solution)/shard_map/all_to_all | solution.py:241
  26.9 17.0 %shard_map.59 = (bf16[1536,3072]{1,0:T(8,128)(2,1)}, bf16[1536,3072]{1,0:T(8,128)(2,1)}) custom-call(f32[1536,3072]{1,0:T(8,128)} %a.1), custom_call_target="tpu_custom_call" | custom-call | flops 9437184 | bytes 37748736 | tf_op jit(solution)/shard_map/pallas_call | solution.py:62
  45.2 11.3 %all-gather.2.cloned.1.call-done.s = f32[3072,512]{1,0:T(8,128)} async-done(((f32[192,512]{1,0:T(8,128)}), f32[3072,512]{1,0:T(8,128)}) %all-gather.2.cloned.1.call-update) | async-done | bytes 6291472 | tf_op jit(solution)/shard_map/all_gather | solution.py:234
  56.4 8.5 %shard_map.60 = (f32[192,512]{1,0:T(8,128)}, f32[192,512]{1,0:T(8,128)}) custom-call(s32[2]{0:T(128)} %get-tuple-element.101.at, bf16[1536,3072]{1,0:T(8,128)(2,1)} %get-tuple-element.69.a_high, bf16[1536,3072]{1,0:T(8,128)(2,1)} %get-tuple-element.52.a_low, f32[3072,512]{1,0:T(8,128)} %all-gather.2.cloned.1.call-done.s), custom_call_target="tpu_custom_call" | custom-call | flops 3623878656 | bytes 11010048 | tf_op jit(solution)/shard_map/pallas_call | solution.py:100
  64.9 5.2 %collective-permute-start.3 = (f32[192,512]{1,0:T(8,128)}, f32[192,512]{1,0:T(8,128)S(1)}, u32[]{:S(2)}, u32[]{:S(2)}) collective-permute-start(f32[192,512]{1,0:T(8,128)} %get-tuple-element.55), channel_id=1, source_target_pairs={{0,5},{1,4},{2,7},{3,6},{4,1},{5,0},{6,3},{7,2},{8,13},{9,12},{10,... | collective-permute-start | bytes 1179656 | tf_op jit(solution)/shard_map/ppermute | solution.py:43
  70.3 8.4 %shard_map.61 = (f32[192,512]{1,0:T(8,128)}, f32[192,512]{1,0:T(8,128)}) custom-call(s32[2]{0:T(128)} %get-tuple-element.102.at, bf16[1536,3072]{1,0:T(8,128)(2,1)} %get-tuple-element.69.a_high, bf16[1536,3072]{1,0:T(8,128)(2,1)} %get-tuple-element.52.a_low, f32[3072,512]{1,0:T(8,128)} %all-gather.2.cloned.1.call-done.s), custom_call_target="tpu_custom_call" | custom-call | flops 3623878656 | bytes 11010048 | tf_op jit(solution)/shard_map/pallas_call | solution.py:100
  78.8 1.3 collective-permute-start.5
  81.2 8.4 %shard_map.62 = (f32[192,512]{1,0:T(8,128)}, f32[192,512]{1,0:T(8,128)}) custom-call(s32[2]{0:T(128)} %get-tuple-element.100.at, bf16[1536,3072]{1,0:T(8,128)(2,1)} %get-tuple-element.69.a_high, bf16[1536,3072]{1,0:T(8,128)(2,1)} %get-tuple-element.52.a_low, f32[3072,512]{1,0:T(8,128)} %all-gather.2.cloned.1.call-done.s), custom_call_target="tpu_custom_call" | custom-call | flops 3623878656 | bytes 11010048 | tf_op jit(solution)/shard_map/pallas_call | solution.py:100
  89.6 3.9 %collective-permute-start.7 = (f32[192,512]{1,0:T(8,128)}, f32[192,512]{1,0:T(8,128)}, u32[]{:S(2)}, u32[]{:S(2)}) collective-permute-start(f32[192,512]{1,0:T(8,128)} %get-tuple-element.67), channel_id=1, source_target_pairs={{0,7},{1,6},{2,1},{3,0},{4,3},{5,2},{6,5},{7,4},{8,15},{9,14},{10,... | collective-permute-start | bytes 1179656 | tf_op jit(solution)/shard_map/ppermute | solution.py:43
  93.5 8.4 %shard_map.63 = (f32[192,512]{1,0:T(8,128)}, f32[192,512]{1,0:T(8,128)}) custom-call(s32[2]{0:T(128)} %get-tuple-element.103.at, bf16[1536,3072]{1,0:T(8,128)(2,1)} %get-tuple-element.69.a_high, bf16[1536,3072]{1,0:T(8,128)(2,1)} %get-tuple-element.52.a_low, f32[3072,512]{1,0:T(8,128)} %all-gather.2.cloned.1.call-done.s), custom_call_target="tpu_custom_call" | custom-call | flops 3623878656 | bytes 11010048 | tf_op jit(solution)/shard_map/pallas_call | solution.py:100
  102.6 1.4 pad_maximum_fusion.refs_1_.refs_4_
  104.0 1.5 collective-permute-done.6
  105.5 7.2 %collective-permute-done.9 = f32[192,512]{1,0:T(8,128)} collective-permute-done((f32[192,512]{1,0:T(8,128)}, f32[192,512]{1,0:T(8,128)}, u32[]{:S(2)}, u32[]{:S(2)}) %collective-permute-start.9) | collective-permute-done | bytes 393248 | tf_op jit(solution)/shard_map/ppermute | solution.py:43
  112.7 1.8 add_add_fusion
  114.6 2.9 %collective-permute-start.10 = (f32[192,256]{1,0:T(8,128)S(1)}, f32[192,256]{1,0:T(8,128)S(1)}, u32[]{:S(2)}, u32[]{:S(2)}) collective-permute-start(f32[192,256]{1,0:T(8,128)S(1)} %get-tuple-element.99), channel_id=1, source_target_pairs={{0,8},{8,0},{1,9},{9,1},{2,10},{10,2},{3,11},{11,3},{4,12},{12,4},... | collective-permute-start | bytes 589832 | tf_op jit(solution)/shard_map/ppermute | solution.py:51
  119.4 2.3 %collective-permute-start.14 = (f32[2,192,256]{2,1,0:T(8,128)S(1)}, f32[2,192,256]{2,1,0:T(8,128)S(1)}, u32[]{:S(2)}, u32[]{:S(2)}) collective-permute-start(f32[2,192,256]{2,1,0:T(8,128)S(1)} %pad_maximum_fusion.1.refs_0_), channel_id=1, source_target_pairs={{0,6},{1,7},{2,0},{3,1},{4,2},{5,3},{6,4},{7,5},{8,14},{9,15},{10,... | collective-permute-start | bytes 1179656 | tf_op jit(solution)/shard_map/ppermute | solution.py:43
  122.4 2.5 %collective-permute-done.12.refs_2_.refs_5_ = f32[4,192,1152]{2,1,0:T(8,128)S(1)} collective-permute-done((f32[4,192,1152]{2,1,0:T(8,128)S(1)}, f32[4,192,1152]{2,1,0:T(8,128)S(1)}, u32[]{:S(2)}, u32[]{:S(2)}) %collective-permute-start.12) | collective-permute-done | bytes 3538976 | tf_op jit(solution)/shard_map/ppermute | solution.py:51
  126.1 13.2 %collective-permute-done.13.refs_0_ = f32[2,192,256]{2,1,0:T(8,128)S(1)} collective-permute-done((f32[2,192,256]{2,1,0:T(8,128)S(1)}, f32[2,192,256]{2,1,0:T(8,128)S(1)}, u32[]{:S(2)}, u32[]{:S(2)}) %collective-permute-start.13) | collective-permute-done | bytes 393248 | tf_op jit(solution)/shard_map/ppermute | solution.py:43
  139.2 2.2 %shard_map.65.refs_3_ = f32[16,2,8,1152]{3,2,1,0:T(8,128)S(1)} custom-call(f32[2,192,256]{2,1,0:T(8,128)S(1)} %collective-permute-done.13.refs_0_, f32[4,192,1152]{2,1,0:T(8,128)S(1)} %pad_maximum_fusion.refs_1_.refs_4_, f32[4,192,1152]{2,1,0:T(8,128)S(1)} %collective-permute-done.12.refs_2_.refs_5_, f32[2,192,256]{2,1,0:T(8,128)S(1)} %collective-permute-done.14.refs_3_, ...), custom_call_target="tpu_custom_call" | custom-call | flops 1358954496 | bytes 3538944 | tf_op jit(solution)/shard_map/pallas_call | solution.py:157
  142.7 20.3 %all_to_all.15.pieces = f32[16,2,8,1152]{3,2,1,0:T(8,128)S(1)} all-to-all(f32[16,2,8,1152]{3,2,1,0:T(8,128)S(1)} %shard_map.66), channel_id=1, replica_groups=mesh['x'=4,'zl'=2,'c'=2,'y'=4,'zh'=2] {'x','zh','zl'}, dimensions={0} | all-to-all | bytes 2359296 | tf_op jit(solution)/shard_map/all_to_all | solution.py:274
  163.8 20.8 %all_to_all.16.blocks = f32[128,8,128]{2,1,0:T(8,128)S(1)} all-to-all(f32[128,8,128]{2,1,0:T(8,128)S(1)} %shard_map.67), channel_id=1, replica_groups=mesh['x'=4,'zl'=2,'c'=2,'y'=4,'zh'=2] {'c','x','zh','zl','y'}, dimensions={0} | all-to-all | bytes 1048576 | tf_op jit(solution)/shard_map/all_to_all | solution.py:286
  (35 shorter events, 12.9 us)
Async XLA Ops:
  7.2 49.3 %all-gather.2.cloned.1.call-start = ((), (), s32[]{:S(2)}) async-start(), calls=%async_computation.3 | async-start | bytes 6684672 | tf_op jit(solution)/shard_map/all_gather | solution.py:234
  7.9 9.3 %copy-start.1 = (s32[36]{0:T(128)S(1)}, s32[36]{0:T(128)}, u32[]{:S(2)}) copy-start(s32[36]{0:T(128)} %param.7) | copy-start | bytes 436
  11.4 53.4 %collective-permute-start = (f32[192,1152]{1,0:T(8,128)}, f32[192,1152]{1,0:T(8,128)S(1)}, u32[]{:S(2)}, u32[]{:S(2)}) collective-permute-start(f32[192,1152]{1,0:T(8,128)} %get-tuple-element.95), channel_id=1, source_target_pairs={{0,2},{2,4},{4,6},{6,0},{1,3},{3,5},{5,7},{7,1},{8,10},{10,12},{12... | collective-permute-start | bytes 2654216 | tf_op jit(solution)/shard_map/ppermute | solution.py:239
  13.6 51.3 %collective-permute-start.1 = (f32[192,1152]{1,0:T(8,128)}, f32[192,1152]{1,0:T(8,128)S(1)}, u32[]{:S(2)}, u32[]{:S(2)}) collective-permute-start(f32[192,1152]{1,0:T(8,128)} %get-tuple-element.97), channel_id=1, source_target_pairs={{0,4},{2,6},{4,0},{6,2},{1,5},{3,7},{5,1},{7,3},{8,12},{10,14},{12... | collective-permute-start | bytes 2654216 | tf_op jit(solution)/shard_map/ppermute | solution.py:239
  16.2 48.7 %collective-permute-start.2 = (f32[192,1152]{1,0:T(8,128)}, f32[192,1152]{1,0:T(8,128)}, u32[]{:S(2)}, u32[]{:S(2)}) collective-permute-start(f32[192,1152]{1,0:T(8,128)} %get-tuple-element.94), channel_id=1, source_target_pairs={{0,6},{2,0},{4,2},{6,4},{1,7},{3,1},{5,3},{7,5},{8,14},{10,8},{12,... | collective-permute-start | bytes 2654216 | tf_op jit(solution)/shard_map/ppermute | solution.py:239
  17.9 47.0 %all-to-all-start = ((s32[128,1,36]{2,1,0:T(1,128)}), s32[128,1,36]{2,1,0:T(1,128)S(1)}, u32[]{:S(2)}, u32[]{:S(2)}) async-start(s32[128,1,36]{2,1,0:T(1,128)} %broadcast_in_dim.2), calls=%async_computation | async-start | bytes 131072 | tf_op jit(solution)/shard_map/all_to_all | solution.py:241
  64.9 24.7 %collective-permute-start.3 = (f32[192,512]{1,0:T(8,128)}, f32[192,512]{1,0:T(8,128)S(1)}, u32[]{:S(2)}, u32[]{:S(2)}) collective-permute-start(f32[192,512]{1,0:T(8,128)} %get-tuple-element.55), channel_id=1, source_target_pairs={{0,5},{1,4},{2,7},{3,6},{4,1},{5,0},{6,3},{7,2},{8,13},{9,12},{10,... | collective-permute-start | bytes 1179656 | tf_op jit(solution)/shard_map/ppermute | solution.py:43
  70.1 19.5 %collective-permute-start.4 = (f32[192,512]{1,0:T(8,128)}, f32[192,512]{1,0:T(8,128)S(1)}, u32[]{:S(2)}, u32[]{:S(2)}) collective-permute-start(f32[192,512]{1,0:T(8,128)} %get-tuple-element.63), channel_id=1, source_target_pairs={{0,4},{1,5},{2,6},{3,7},{4,0},{5,1},{6,2},{7,3},{8,12},{9,13},{10,... | collective-permute-start | bytes 1179656 | tf_op jit(solution)/shard_map/ppermute | solution.py:43
  78.8 25.3 %collective-permute-start.5 = (f32[192,512]{1,0:T(8,128)}, f32[192,512]{1,0:T(8,128)}, u32[]{:S(2)}, u32[]{:S(2)}) collective-permute-start(f32[192,512]{1,0:T(8,128)} %get-tuple-element.58), channel_id=1, source_target_pairs={{0,3},{1,2},{2,5},{3,4},{4,7},{5,6},{6,1},{7,0},{8,11},{9,10},{10,... | collective-permute-start | bytes 1179656 | tf_op jit(solution)/shard_map/ppermute | solution.py:43
  80.0 25.5 %collective-permute-start.6 = (f32[192,512]{1,0:T(8,128)}, f32[192,512]{1,0:T(8,128)}, u32[]{:S(2)}, u32[]{:S(2)}) collective-permute-start(f32[192,512]{1,0:T(8,128)} %get-tuple-element.66), channel_id=1, source_target_pairs={{0,2},{1,3},{2,4},{3,5},{4,6},{5,7},{6,0},{7,1},{8,10},{9,11},{10,... | collective-permute-start | bytes 1179656 | tf_op jit(solution)/shard_map/ppermute | solution.py:43
  89.6 23.1 %collective-permute-start.7 = (f32[192,512]{1,0:T(8,128)}, f32[192,512]{1,0:T(8,128)}, u32[]{:S(2)}, u32[]{:S(2)}) collective-permute-start(f32[192,512]{1,0:T(8,128)} %get-tuple-element.67), channel_id=1, source_target_pairs={{0,7},{1,6},{2,1},{3,0},{4,3},{5,2},{6,5},{7,4},{8,15},{9,14},{10,... | collective-permute-start | bytes 1179656 | tf_op jit(solution)/shard_map/ppermute | solution.py:43
  102.0 10.8 %collective-permute-start.9 = (f32[192,512]{1,0:T(8,128)}, f32[192,512]{1,0:T(8,128)}, u32[]{:S(2)}, u32[]{:S(2)}) collective-permute-start(f32[192,512]{1,0:T(8,128)} %get-tuple-element.71), channel_id=1, source_target_pairs={{0,1},{1,0},{2,3},{3,2},{4,5},{5,4},{6,7},{7,6},{8,9},{9,8},{10,11... | collective-permute-start | bytes 1179656 | tf_op jit(solution)/shard_map/ppermute | solution.py:43
  102.3 10.4 %collective-permute-start.8 = (f32[192,512]{1,0:T(8,128)}, f32[192,512]{1,0:T(8,128)}, u32[]{:S(2)}, u32[]{:S(2)}) collective-permute-start(f32[192,512]{1,0:T(8,128)} %get-tuple-element.68), channel_id=1, source_target_pairs={{0,6},{1,7},{2,0},{3,1},{4,2},{5,3},{6,4},{7,5},{8,14},{9,15},{10,... | collective-permute-start | bytes 1179656 | tf_op jit(solution)/shard_map/ppermute | solution.py:43
  102.6 10.2 %copy-start = (f32[192,512]{1,0:T(8,128)S(1)}, f32[192,512]{1,0:T(8,128)}, u32[]{:S(2)}) copy-start(f32[192,512]{1,0:T(8,128)} %get-tuple-element.89) | copy-start | bytes 1179652
  114.6 3.9 %collective-permute-start.10 = (f32[192,256]{1,0:T(8,128)S(1)}, f32[192,256]{1,0:T(8,128)S(1)}, u32[]{:S(2)}, u32[]{:S(2)}) collective-permute-start(f32[192,256]{1,0:T(8,128)S(1)} %get-tuple-element.99), channel_id=1, source_target_pairs={{0,8},{8,0},{1,9},{9,1},{2,10},{10,2},{3,11},{11,3},{4,12},{12,4},... | collective-permute-start | bytes 589832 | tf_op jit(solution)/shard_map/ppermute | solution.py:51
  118.6 6.3 %collective-permute-start.12 = (f32[4,192,1152]{2,1,0:T(8,128)S(1)}, f32[4,192,1152]{2,1,0:T(8,128)S(1)}, u32[]{:S(2)}, u32[]{:S(2)}) collective-permute-start(f32[4,192,1152]{2,1,0:T(8,128)S(1)} %pad_maximum_fusion.refs_1_.refs_4_), channel_id=1, source_target_pairs={{0,8},{8,0},{1,9},{9,1},{2,10},{10,2},{3,11},{11,3},{4,12},{12,4},... | collective-permute-start | bytes 10616840 | tf_op jit(solution)/shard_map/ppermute | solution.py:51
  119.0 20.2 %collective-permute-start.13 = (f32[2,192,256]{2,1,0:T(8,128)S(1)}, f32[2,192,256]{2,1,0:T(8,128)S(1)}, u32[]{:S(2)}, u32[]{:S(2)}) collective-permute-start(f32[2,192,256]{2,1,0:T(8,128)S(1)} %pad_maximum_fusion.1.refs_0_), channel_id=1, source_target_pairs={{0,2},{1,3},{2,4},{3,5},{4,6},{5,7},{6,0},{7,1},{8,10},{9,11},{10,... | collective-permute-start | bytes 1179656 | tf_op jit(solution)/shard_map/ppermute | solution.py:43
  119.4 19.8 %collective-permute-start.14 = (f32[2,192,256]{2,1,0:T(8,128)S(1)}, f32[2,192,256]{2,1,0:T(8,128)S(1)}, u32[]{:S(2)}, u32[]{:S(2)}) collective-permute-start(f32[2,192,256]{2,1,0:T(8,128)S(1)} %pad_maximum_fusion.1.refs_0_), channel_id=1, source_target_pairs={{0,6},{1,7},{2,0},{3,1},{4,2},{5,3},{6,4},{7,5},{8,14},{9,15},{10,... | collective-permute-start | bytes 1179656 | tf_op jit(solution)/shard_map/ppermute | solution.py:43
  121.7 19.7 %collective-permute-start.11 = (f32[2,192,256]{2,1,0:T(8,128)S(1)}, f32[2,192,256]{2,1,0:T(8,128)S(1)}, u32[]{:S(2)}, u32[]{:S(2)}) collective-permute-start(f32[2,192,256]{2,1,0:T(8,128)S(1)} %pad_maximum_fusion.1.refs_0_), channel_id=1, source_target_pairs={{0,4},{1,5},{2,6},{3,7},{4,0},{5,1},{6,2},{7,3},{8,12},{9,13},{10,... | collective-permute-start | bytes 1179656 | tf_op jit(solution)/shard_map/ppermute | solution.py:43
Sparse Core Ops, SparseCore 0:
  9.7 46.6 all-gather.1

commit v11 on v10

--- a/solution.py
+++ b/solution.py
@@ -113,6 +113,34 @@
             transcendentals=0,
         ),
     )(jnp.stack([to, zh]).astype(jnp.int32), a_high, a_low, maps)
+
+
+def block_body(at, a_high, a_low, s, out):
+    sh, sl = split(s[...])
+    ah = a_high[...]
+    add_step(out, dot(ah, sh) + dot(ah, sl) + dot(a_low[...], sh))
+
+
+def block_of(at, a_high, a_low, maps):
+    inner, cols = maps.shape
+    step = 1536
+    a_block = pl.BlockSpec((ROWS, step), lambda k, at: (at[0], k))
+    return pl.pallas_call(
+        block_body,
+        grid_spec=pltpu.PrefetchScalarGridSpec(
+            num_scalar_prefetch=1,
+            grid=(inner // step,),
+            in_specs=[a_block, a_block, pl.BlockSpec((step, cols), lambda k, at: (k, 0))],
+            out_specs=pl.BlockSpec((ROWS, cols), lambda k, at: (0, 0)),
+        ),
+        out_shape=jax.ShapeDtypeStruct((ROWS, cols), F32),
+        compiler_params=limit(58),
+        cost_estimate=pl.CostEstimate(
+            flops=6 * ROWS * inner * cols,
+            bytes_accessed=4 * inner * (ROWS + cols),
+            transcendentals=0,
+        ),
+    )(jnp.reshape(at, (1,)).astype(jnp.int32), a_high, a_low, maps)
 
 
 def project_body(terms, begun, *refs):
@@ -246,7 +274,12 @@
 
     got = {}
     for dy in (2, 1, 3, 0):
-        far, near = rows_of(lax.rem(y + dy, NY), zh, a_high, a_low, gathered)
+        if dy:
+            far, near = rows_of(lax.rem(y + dy, NY), zh, a_high, a_low, gathered)
+        else:
+            far = block_of(2 * y + 1 - zh, a_high, a_low, gathered)
+            gathered, far = lax.optimization_barrier((gathered, far))
+            near = block_of(2 * y + zh, a_high, a_low, gathered)
         if dy == 2:
             far, near, bands, *columns = lax.optimization_barrier((far, near, bands, *columns))
         if dy == 3:

time: 193 us -> 191 us (0.990)
  waiting for transfers between devices: 37.4 us -> 32.8 us
  Pallas kernels: 57.4 us -> 59.9 us
  blocking collectives: 41.1 us -> 43.1 us
    pallas_call x0 -> x2, Pallas kernels: none -> 11 us  [block_of(): pl.pallas_call(block_body, grid_spec=pltpu.PrefetchScalarGridSpec(num_sca...]
    pallas_call x4 -> x3, Pallas kernels: 33.7 us -> 25.3 us  [rows_of(): pl.pallas_call(row_body, grid_spec=pltpu.PrefetchScalarGridSpec(num_scala...]
    ppermute x10, waiting for transfers between devices: 21.9 us -> 18.1 us  [shift(): return lax.ppermute(value, RING, pairs)]
    all_to_all x1, blocking collectives: 20.3 us -> 23.2 us  [per_device(): pieces = lax.all_to_all(projected, CHIPS, 0, 0, tiled=True)]
  transfers between devices with their start and end apart: 17 -> 17, of which waited for: 6 -> 6; matrix products, arithmetic and copies ran while one was open for 4% -> 4% of each run, Pallas kernels for 28% -> 30%
where the time goes in v11:
time: 191 us; the launch traced here: 190 us
  Pallas kernels  59.9 us (31%)
  blocking collectives  43.1 us (23%)
  starting transfers between devices  32.9 us (17%)
  waiting for transfers between devices  32.8 us (17%)
  between operations  14.2 us (7%)
  local copies, waits for them, and re-layouts  4.21 us (2%)
  other arithmetic  3.04 us (2%)
    pallas_call x3, Pallas kernels, rows_of(): pl.pallas_call(row_body, grid_spec=pltpu.PrefetchScalarGridSpec(num_scala...  25.3 us
    all_to_all x1, blocking collectives, per_device(): pieces = lax.all_to_all(projected, CHIPS, 0, 0, tiled=True)  23.2 us
    all_to_all x1, blocking collectives, per_device(): blocks = lax.all_to_all(sums, ('c',) + CHIPS + ('y',), 0, 0, tiled=True)  19.8 us
    ppermute x10, waiting for transfers between devices, shift(): return lax.ppermute(value, RING, pairs)  18.1 us
    pallas_call x1, Pallas kernels, split_rows(): pl.pallas_call(split_body, grid=(rows // step,), in_specs=[block], out_sp...  17 us
    ppermute x10, starting transfers between devices, shift(): return lax.ppermute(value, RING, pairs)  16.6 us
    all_gather x1, waiting for transfers between devices, per_device(): gathered = lax.all_gather(sim_maps, BLK, axis=0, tiled=True)  11.3 us
    pallas_call x2, Pallas kernels, block_of(): pl.pallas_call(block_body, grid_spec=pltpu.PrefetchScalarGridSpec(num_sca...  11 us
  transfers between devices with their start and end apart: 17, of which 6 were waited for; matrix products, arithmetic and copies ran while one was open for 4% of the time, Pallas kernels for 30%

profile of v11, /device:TPU:1, one launch (start us, length us, event | category | flops | bytes accessed | tf_op | source)
XLA Modules:
  0.0 190.1 jit_solution(3578912965686340154)
XLA Ops:
  7.9 3.5 %constant_dynamic-slice_fusion.1 = (f32[192,1152]{1,0:T(8,128)}, f32[192,1152]{1,0:T(8,128)}, f32[192,1152]{1,0:T(8,128)S(1)}, f32[192,1152]{1,0:T(8,128)}) fusion(f32[192,4608]{1,0:T(8,128)} %param.6, s32[]{:T(128)S(6)} %select_n.21, s32[]{:T(128)S(6)} %select_n.19, s32[]{:T(128)S(6)} %select_n.18, s32[]{:T(128)S(6)} %select_n.20), kind=kLoop, calls=%fused_computation.5 | loop fusion | bytes 7077904 | tf_op jit(solution)/shard_map/dynamic_slice | solution.py:266
  11.4 2.1 %collective-permute-start = (f32[192,1152]{1,0:T(8,128)}, f32[192,1152]{1,0:T(8,128)S(1)}, u32[]{:S(2)}, u32[]{:S(2)}) collective-permute-start(f32[192,1152]{1,0:T(8,128)} %get-tuple-element.95), channel_id=1, source_target_pairs={{0,2},{2,4},{4,6},{6,0},{1,3},{3,5},{5,7},{7,1},{8,10},{10,12},{12... | collective-permute-start | bytes 2654216 | tf_op jit(solution)/shard_map/ppermute | solution.py:267
  13.6 2.6 %collective-permute-start.1 = (f32[192,1152]{1,0:T(8,128)}, f32[192,1152]{1,0:T(8,128)S(1)}, u32[]{:S(2)}, u32[]{:S(2)}) collective-permute-start(f32[192,1152]{1,0:T(8,128)} %get-tuple-element.97), channel_id=1, source_target_pairs={{0,4},{2,6},{4,0},{6,2},{1,5},{3,7},{5,1},{7,3},{8,12},{10,14},{12... | collective-permute-start | bytes 2654216 | tf_op jit(solution)/shard_map/ppermute | solution.py:267
  17.9 9.0 %all-to-all-start = ((s32[128,1,36]{2,1,0:T(1,128)}), s32[128,1,36]{2,1,0:T(1,128)S(1)}, u32[]{:S(2)}, u32[]{:S(2)}) async-start(s32[128,1,36]{2,1,0:T(1,128)} %broadcast_in_dim.2), calls=%async_computation | async-start | bytes 131072 | tf_op jit(solution)/shard_map/all_to_all | solution.py:269
  26.9 17.0 %shard_map.59 = (bf16[1536,3072]{1,0:T(8,128)(2,1)}, bf16[1536,3072]{1,0:T(8,128)(2,1)}) custom-call(f32[1536,3072]{1,0:T(8,128)} %a.1), custom_call_target="tpu_custom_call" | custom-call | flops 9437184 | bytes 37748736 | tf_op jit(solution)/shard_map/pallas_call | solution.py:62
  45.1 11.3 %all-gather.2.cloned.1.call-done.s = f32[3072,512]{1,0:T(8,128)} async-done(((f32[192,512]{1,0:T(8,128)}), f32[3072,512]{1,0:T(8,128)}) %all-gather.2.cloned.1.call-update) | async-done | bytes 6291472 | tf_op jit(solution)/shard_map/all_gather | solution.py:262
  56.4 8.5 %shard_map.60 = (f32[192,512]{1,0:T(8,128)}, f32[192,512]{1,0:T(8,128)}) custom-call(s32[2]{0:T(128)} %get-tuple-element.101.at, bf16[1536,3072]{1,0:T(8,128)(2,1)} %get-tuple-element.70.a_high, bf16[1536,3072]{1,0:T(8,128)(2,1)} %get-tuple-element.52.a_low, f32[3072,512]{1,0:T(8,128)} %all-gather.2.cloned.1.call-done.s), custom_call_target="tpu_custom_call" | custom-call | flops 3623878656 | bytes 11010048 | tf_op jit(solution)/shard_map/pallas_call | solution.py:100
  64.9 5.2 %collective-permute-start.3 = (f32[192,512]{1,0:T(8,128)}, f32[192,512]{1,0:T(8,128)S(1)}, u32[]{:S(2)}, u32[]{:S(2)}) collective-permute-start(f32[192,512]{1,0:T(8,128)} %get-tuple-element.55), channel_id=1, source_target_pairs={{0,5},{1,4},{2,7},{3,6},{4,1},{5,0},{6,3},{7,2},{8,13},{9,12},{10,... | collective-permute-start | bytes 1179656 | tf_op jit(solution)/shard_map/ppermute | solution.py:43
  70.3 8.4 %shard_map.61 = (f32[192,512]{1,0:T(8,128)}, f32[192,512]{1,0:T(8,128)}) custom-call(s32[2]{0:T(128)} %pad_add_fusion.2.at, bf16[1536,3072]{1,0:T(8,128)(2,1)} %get-tuple-element.70.a_high, bf16[1536,3072]{1,0:T(8,128)(2,1)} %get-tuple-element.52.a_low, f32[3072,512]{1,0:T(8,128)} %all-gather.2.cloned.1.call-done.s), custom_call_target="tpu_custom_call" | custom-call | flops 3623878656 | bytes 11010048 | tf_op jit(solution)/shard_map/pallas_call | solution.py:100
  81.2 8.4 %shard_map.62 = (f32[192,512]{1,0:T(8,128)}, f32[192,512]{1,0:T(8,128)}) custom-call(s32[2]{0:T(128)} %get-tuple-element.100.at, bf16[1536,3072]{1,0:T(8,128)(2,1)} %get-tuple-element.70.a_high, bf16[1536,3072]{1,0:T(8,128)(2,1)} %get-tuple-element.52.a_low, f32[3072,512]{1,0:T(8,128)} %all-gather.2.cloned.1.call-done.s), custom_call_target="tpu_custom_call" | custom-call | flops 3623878656 | bytes 11010048 | tf_op jit(solution)/shard_map/pallas_call | solution.py:100
  89.6 3.9 %collective-permute-start.7 = (f32[192,512]{1,0:T(8,128)}, f32[192,512]{1,0:T(8,128)S(1)}, u32[]{:S(2)}, u32[]{:S(2)}) collective-permute-start(f32[192,512]{1,0:T(8,128)} %get-tuple-element.67), channel_id=1, source_target_pairs={{0,7},{1,6},{2,1},{3,0},{4,3},{5,2},{6,5},{7,4},{8,15},{9,14},{10,... | collective-permute-start | bytes 1179656 | tf_op jit(solution)/shard_map/ppermute | solution.py:43
  93.5 5.5 %shard_map.63 = f32[192,512]{1,0:T(8,128)} custom-call(s32[1]{0:T(128)} %bitcast.5.at, bf16[1536,3072]{1,0:T(8,128)(2,1)} %get-tuple-element.70.a_high, bf16[1536,3072]{1,0:T(8,128)(2,1)} %get-tuple-element.52.a_low, f32[3072,512]{1,0:T(8,128)} %all-gather.2.cloned.1.call-done.s), custom_call_target="tpu_custom_call" | custom-call | flops 1811939328 | bytes 8650752 | tf_op jit(solution)/shard_map/pallas_call | solution.py:128
  99.6 5.5 %shard_map.64 = f32[192,512]{1,0:T(8,128)} custom-call(s32[1]{0:T(128)} %bitcast.6.at, bf16[1536,3072]{1,0:T(8,128)(2,1)} %get-tuple-element.70.a_high, bf16[1536,3072]{1,0:T(8,128)(2,1)} %get-tuple-element.52.a_low, f32[3072,512]{1,0:T(8,128)} %all-gather.2.cloned.1.call-done.s), custom_call_target="tpu_custom_call" | custom-call | flops 1811939328 | bytes 8650752 | tf_op jit(solution)/shard_map/pallas_call | solution.py:128
  105.1 1.4 pad_maximum_fusion.refs_1_.refs_4_
  106.5 6.8 %collective-permute-done.9 = f32[192,512]{1,0:T(8,128)S(1)} collective-permute-done((f32[192,512]{1,0:T(8,128)}, f32[192,512]{1,0:T(8,128)S(1)}, u32[]{:S(2)}, u32[]{:S(2)}) %collective-permute-start.9) | collective-permute-done | bytes 393248 | tf_op jit(solution)/shard_map/ppermute | solution.py:43
  116.4 1.3 collective-permute-start.13
  117.7 1.4 collective-permute-start.14
  119.1 1.5 collective-permute-start.11
  120.6 1.6 collective-permute-done.12.refs_2_.refs_5_
  123.5 4.7 %collective-permute-done.13.refs_0_ = f32[2,192,256]{2,1,0:T(8,128)S(1)} collective-permute-done((f32[2,192,256]{2,1,0:T(8,128)S(1)}, f32[2,192,256]{2,1,0:T(8,128)S(1)}, u32[]{:S(2)}, u32[]{:S(2)}) %collective-permute-start.13) | collective-permute-done | bytes 393248 | tf_op jit(solution)/shard_map/ppermute | solution.py:43
  128.2 2.2 %shard_map.66.refs_3_ = f32[16,2,8,1152]{3,2,1,0:T(8,128)S(1)} custom-call(f32[2,192,256]{2,1,0:T(8,128)S(1)} %collective-permute-done.13.refs_0_, f32[4,192,1152]{2,1,0:T(8,128)S(1)} %pad_maximum_fusion.refs_1_.refs_4_, f32[4,192,1152]{2,1,0:T(8,128)S(1)} %collective-permute-done.12.refs_2_.refs_5_, f32[2,192,256]{2,1,0:T(8,128)S(1)} %collective-permute-done.14.refs_3_, ...), custom_call_target="tpu_custom_call" | custom-call | flops 1358954496 | bytes 3538944 | tf_op jit(solution)/shard_map/pallas_call | solution.py:185
  130.4 6.5 %collective-permute-done.11.refs_0_ = f32[2,192,256]{2,1,0:T(8,128)S(1)} collective-permute-done((f32[2,192,256]{2,1,0:T(8,128)S(1)}, f32[2,192,256]{2,1,0:T(8,128)S(1)}, u32[]{:S(2)}, u32[]{:S(2)}) %collective-permute-start.11) | collective-permute-done | bytes 393248 | tf_op jit(solution)/shard_map/ppermute | solution.py:43
  138.1 23.2 %all_to_all.15.pieces = f32[16,2,8,1152]{3,2,1,0:T(8,128)S(1)} all-to-all(f32[16,2,8,1152]{3,2,1,0:T(8,128)S(1)} %shard_map.67), channel_id=1, replica_groups=mesh['x'=4,'zl'=2,'c'=2,'y'=4,'zh'=2] {'x','zh','zl'}, dimensions={0} | all-to-all | bytes 2359296 | tf_op jit(solution)/shard_map/all_to_all | solution.py:307
  162.2 19.8 %all_to_all.16.blocks = f32[128,8,128]{2,1,0:T(8,128)S(1)} all-to-all(f32[128,8,128]{2,1,0:T(8,128)S(1)} %shard_map.68), channel_id=1, replica_groups=mesh['x'=4,'zl'=2,'c'=2,'y'=4,'zh'=2] {'c','x','zh','zl','y'}, dimensions={0} | all-to-all | bytes 1048576 | tf_op jit(solution)/shard_map/all_to_all | solution.py:319
  (38 shorter events, 14.5 us)
Async XLA Ops:
  7.2 49.3 %all-gather.2.cloned.1.call-start = ((), (), s32[]{:S(2)}) async-start(), calls=%async_computation.3 | async-start | bytes 6684672 | tf_op jit(solution)/shard_map/all_gather | solution.py:262
  7.9 9.3 %copy-start.1 = (s32[36]{0:T(128)S(1)}, s32[36]{0:T(128)}, u32[]{:S(2)}) copy-start(s32[36]{0:T(128)} %param.7) | copy-start | bytes 436
  11.4 53.4 %collective-permute-start = (f32[192,1152]{1,0:T(8,128)}, f32[192,1152]{1,0:T(8,128)S(1)}, u32[]{:S(2)}, u32[]{:S(2)}) collective-permute-start(f32[192,1152]{1,0:T(8,128)} %get-tuple-element.95), channel_id=1, source_target_pairs={{0,2},{2,4},{4,6},{6,0},{1,3},{3,5},{5,7},{7,1},{8,10},{10,12},{12... | collective-permute-start | bytes 2654216 | tf_op jit(solution)/shard_map/ppermute | solution.py:267
  13.6 51.3 %collective-permute-start.1 = (f32[192,1152]{1,0:T(8,128)}, f32[192,1152]{1,0:T(8,128)S(1)}, u32[]{:S(2)}, u32[]{:S(2)}) collective-permute-start(f32[192,1152]{1,0:T(8,128)} %get-tuple-element.97), channel_id=1, source_target_pairs={{0,4},{2,6},{4,0},{6,2},{1,5},{3,7},{5,1},{7,3},{8,12},{10,14},{12... | collective-permute-start | bytes 2654216 | tf_op jit(solution)/shard_map/ppermute | solution.py:267
  16.2 48.7 %collective-permute-start.2 = (f32[192,1152]{1,0:T(8,128)}, f32[192,1152]{1,0:T(8,128)}, u32[]{:S(2)}, u32[]{:S(2)}) collective-permute-start(f32[192,1152]{1,0:T(8,128)} %get-tuple-element.94), channel_id=1, source_target_pairs={{0,6},{2,0},{4,2},{6,4},{1,7},{3,1},{5,3},{7,5},{8,14},{10,8},{12,... | collective-permute-start | bytes 2654216 | tf_op jit(solution)/shard_map/ppermute | solution.py:267
  17.9 47.0 %all-to-all-start = ((s32[128,1,36]{2,1,0:T(1,128)}), s32[128,1,36]{2,1,0:T(1,128)S(1)}, u32[]{:S(2)}, u32[]{:S(2)}) async-start(s32[128,1,36]{2,1,0:T(1,128)} %broadcast_in_dim.2), calls=%async_computation | async-start | bytes 131072 | tf_op jit(solution)/shard_map/all_to_all | solution.py:269
  64.9 24.7 %collective-permute-start.3 = (f32[192,512]{1,0:T(8,128)}, f32[192,512]{1,0:T(8,128)S(1)}, u32[]{:S(2)}, u32[]{:S(2)}) collective-permute-start(f32[192,512]{1,0:T(8,128)} %get-tuple-element.55), channel_id=1, source_target_pairs={{0,5},{1,4},{2,7},{3,6},{4,1},{5,0},{6,3},{7,2},{8,13},{9,12},{10,... | collective-permute-start | bytes 1179656 | tf_op jit(solution)/shard_map/ppermute | solution.py:43
  70.1 19.5 %collective-permute-start.4 = (f32[192,512]{1,0:T(8,128)}, f32[192,512]{1,0:T(8,128)S(1)}, u32[]{:S(2)}, u32[]{:S(2)}) collective-permute-start(f32[192,512]{1,0:T(8,128)} %get-tuple-element.63), channel_id=1, source_target_pairs={{0,4},{1,5},{2,6},{3,7},{4,0},{5,1},{6,2},{7,3},{8,12},{9,13},{10,... | collective-permute-start | bytes 1179656 | tf_op jit(solution)/shard_map/ppermute | solution.py:43
  78.7 27.8 %collective-permute-start.5 = (f32[192,512]{1,0:T(8,128)}, f32[192,512]{1,0:T(8,128)S(1)}, u32[]{:S(2)}, u32[]{:S(2)}) collective-permute-start(f32[192,512]{1,0:T(8,128)} %get-tuple-element.58), channel_id=1, source_target_pairs={{0,3},{1,2},{2,5},{3,4},{4,7},{5,6},{6,1},{7,0},{8,11},{9,10},{10,... | collective-permute-start | bytes 1179656 | tf_op jit(solution)/shard_map/ppermute | solution.py:43
  80.0 26.6 %collective-permute-start.6 = (f32[192,512]{1,0:T(8,128)}, f32[192,512]{1,0:T(8,128)S(1)}, u32[]{:S(2)}, u32[]{:S(2)}) collective-permute-start(f32[192,512]{1,0:T(8,128)} %get-tuple-element.66), channel_id=1, source_target_pairs={{0,2},{1,3},{2,4},{3,5},{4,6},{5,7},{6,0},{7,1},{8,10},{9,11},{10,... | collective-permute-start | bytes 1179656 | tf_op jit(solution)/shard_map/ppermute | solution.py:43
  89.6 23.7 %collective-permute-start.7 = (f32[192,512]{1,0:T(8,128)}, f32[192,512]{1,0:T(8,128)S(1)}, u32[]{:S(2)}, u32[]{:S(2)}) collective-permute-start(f32[192,512]{1,0:T(8,128)} %get-tuple-element.67), channel_id=1, source_target_pairs={{0,7},{1,6},{2,1},{3,0},{4,3},{5,2},{6,5},{7,4},{8,15},{9,14},{10,... | collective-permute-start | bytes 1179656 | tf_op jit(solution)/shard_map/ppermute | solution.py:43
  93.5 5.8 %copy-start.2 = (f32[192,512]{1,0:T(8,128)S(1)}, f32[192,512]{1,0:T(8,128)}, u32[]{:S(2)}) copy-start(f32[192,512]{1,0:T(8,128)} %get-tuple-element.68) | copy-start | bytes 1179652
  99.0 14.3 %collective-permute-start.9 = (f32[192,512]{1,0:T(8,128)}, f32[192,512]{1,0:T(8,128)S(1)}, u32[]{:S(2)}, u32[]{:S(2)}) collective-permute-start(f32[192,512]{1,0:T(8,128)} %shard_map.63), channel_id=1, source_target_pairs={{0,1},{1,0},{2,3},{3,2},{4,5},{5,4},{6,7},{7,6},{8,9},{9,8},{10,11... | collective-permute-start | bytes 1179656 | tf_op jit(solution)/shard_map/ppermute | solution.py:43
  99.4 14.0 %collective-permute-start.8 = (f32[192,512]{1,0:T(8,128)S(1)}, f32[192,512]{1,0:T(8,128)S(1)}, u32[]{:S(2)}, u32[]{:S(2)}) collective-permute-start(f32[192,512]{1,0:T(8,128)S(1)} %copy-done.2), channel_id=1, source_target_pairs={{0,6},{1,7},{2,0},{3,1},{4,2},{5,3},{6,4},{7,5},{8,14},{9,15},{10,... | collective-permute-start | bytes 1179656 | tf_op jit(solution)/shard_map/ppermute | solution.py:43
  105.1 8.3 %copy-start = (f32[192,512]{1,0:T(8,128)S(1)}, f32[192,512]{1,0:T(8,128)}, u32[]{:S(2)}) copy-start(f32[192,512]{1,0:T(8,128)} %shard_map.64) | copy-start | bytes 1179652
  113.8 2.1 %collective-permute-start.10 = (f32[192,256]{1,0:T(8,128)S(1)}, f32[192,256]{1,0:T(8,128)S(1)}, u32[]{:S(2)}, u32[]{:S(2)}) collective-permute-start(f32[192,256]{1,0:T(8,128)S(1)} %get-tuple-element.99), channel_id=1, source_target_pairs={{0,8},{8,0},{1,9},{9,1},{2,10},{10,2},{3,11},{11,3},{4,12},{12,4},... | collective-permute-start | bytes 589832 | tf_op jit(solution)/shard_map/ppermute | solution.py:51
  115.9 6.3 %collective-permute-start.12 = (f32[4,192,1152]{2,1,0:T(8,128)S(1)}, f32[4,192,1152]{2,1,0:T(8,128)S(1)}, u32[]{:S(2)}, u32[]{:S(2)}) collective-permute-start(f32[4,192,1152]{2,1,0:T(8,128)S(1)} %pad_maximum_fusion.refs_1_.refs_4_), channel_id=1, source_target_pairs={{0,8},{8,0},{1,9},{9,1},{2,10},{10,2},{3,11},{11,3},{4,12},{12,4},... | collective-permute-start | bytes 10616840 | tf_op jit(solution)/shard_map/ppermute | solution.py:51
  116.4 11.8 %collective-permute-start.13 = (f32[2,192,256]{2,1,0:T(8,128)S(1)}, f32[2,192,256]{2,1,0:T(8,128)S(1)}, u32[]{:S(2)}, u32[]{:S(2)}) collective-permute-start(f32[2,192,256]{2,1,0:T(8,128)S(1)} %pad_maximum_fusion.1.refs_0_), channel_id=1, source_target_pairs={{0,2},{1,3},{2,4},{3,5},{4,6},{5,7},{6,0},{7,1},{8,10},{9,11},{10,... | collective-permute-start | bytes 1179656 | tf_op jit(solution)/shard_map/ppermute | solution.py:43
  117.7 10.5 %collective-permute-start.14 = (f32[2,192,256]{2,1,0:T(8,128)S(1)}, f32[2,192,256]{2,1,0:T(8,128)S(1)}, u32[]{:S(2)}, u32[]{:S(2)}) collective-permute-start(f32[2,192,256]{2,1,0:T(8,128)S(1)} %pad_maximum_fusion.1.refs_0_), channel_id=1, source_target_pairs={{0,6},{1,7},{2,0},{3,1},{4,2},{5,3},{6,4},{7,5},{8,14},{9,15},{10,... | collective-permute-start | bytes 1179656 | tf_op jit(solution)/shard_map/ppermute | solution.py:43
  119.1 17.8 %collective-permute-start.11 = (f32[2,192,256]{2,1,0:T(8,128)S(1)}, f32[2,192,256]{2,1,0:T(8,128)S(1)}, u32[]{:S(2)}, u32[]{:S(2)}) collective-permute-start(f32[2,192,256]{2,1,0:T(8,128)S(1)} %pad_maximum_fusion.1.refs_0_), channel_id=1, source_target_pairs={{0,4},{1,5},{2,6},{3,7},{4,0},{5,1},{6,2},{7,3},{8,12},{9,13},{10,... | collective-permute-start | bytes 1179656 | tf_op jit(solution)/shard_map/ppermute | solution.py:43
Sparse Core Ops, SparseCore 0:
  9.7 46.6 all-gather.1

commit v12 on v11

--- a/solution.py
+++ b/solution.py
@@ -273,20 +273,20 @@
     gathered, a_high, a_low = lax.optimization_barrier((gathered, a_high, a_low))
 
     got = {}
-    for dy in (2, 1, 3, 0):
+    for dy in (1, 3, 2, 0):
         if dy:
             far, near = rows_of(lax.rem(y + dy, NY), zh, a_high, a_low, gathered)
         else:
             far = block_of(2 * y + 1 - zh, a_high, a_low, gathered)
             gathered, far = lax.optimization_barrier((gathered, far))
             near = block_of(2 * y + zh, a_high, a_low, gathered)
+        if dy == 1:
+            far, near, bands, *columns = lax.optimization_barrier((far, near, bands, *columns))
         if dy == 2:
-            far, near, bands, *columns = lax.optimization_barrier((far, near, bands, *columns))
-        if dy == 3:
-            far, near, *got[2] = lax.optimization_barrier((far, near, *got[2]))
+            far, near, *got[1] = lax.optimization_barrier((far, near, *got[1]))
         got[dy] = [shift(far, dy, 1), shift(near, dy, 0) if dy else near]
         gathered, a_high = lax.optimization_barrier((gathered, a_high, far))[:2]
-    sent = [value for dy in (2, 1, 3, 0) for value in got[dy]]
+    sent = [value for dy in (1, 3, 2, 0) for value in got[dy]]
     sent[-1], *columns = lax.optimization_barrier((sent[-1], *columns))
     own = jnp.stack(columns)
     *sent, own = lax.optimization_barrier((*sent, own))

time: 191 us -> 192 us (level)
  starting transfers between devices: 32.9 us -> 37.6 us
  blocking collectives: 43.1 us -> 40.2 us
    ppermute x10, starting transfers between devices: 16.6 us -> 21.1 us  [shift(): return lax.ppermute(value, RING, pairs)]
    all_to_all x1, blocking collectives: 23.2 us -> 20.8 us  [per_device(): pieces = lax.all_to_all(projected, CHIPS, 0, 0, tiled=True)]
  transfers between devices with their start and end apart: 17 -> 17, of which waited for: 6 -> 5; matrix products, arithmetic and copies ran while one was open for 4% -> 4% of each run, Pallas kernels for 30% -> 30%
where the time goes in v12:
time: 192 us; the launch traced here: 191 us
  Pallas kernels  59.9 us (31%)
  blocking collectives  40.2 us (21%)
  starting transfers between devices  37.6 us (20%)
  waiting for transfers between devices  32 us (17%)
  between operations  14.2 us (7%)
  local copies, waits for them, and re-layouts  4.21 us (2%)
  other arithmetic  3.04 us (2%)
    pallas_call x3, Pallas kernels, rows_of(): pl.pallas_call(row_body, grid_spec=pltpu.PrefetchScalarGridSpec(num_scala...  25.3 us
    ppermute x10, starting transfers between devices, shift(): return lax.ppermute(value, RING, pairs)  21.1 us
    all_to_all x1, blocking collectives, per_device(): pieces = lax.all_to_all(projected, CHIPS, 0, 0, tiled=True)  20.8 us
    all_to_all x1, blocking collectives, per_device(): blocks = lax.all_to_all(sums, ('c',) + CHIPS + ('y',), 0, 0, tiled=True)  19.4 us
    ppermute x10, waiting for transfers between devices, shift(): return lax.ppermute(value, RING, pairs)  19 us
    pallas_call x1, Pallas kernels, split_rows(): pl.pallas_call(split_body, grid=(rows // step,), in_specs=[block], out_sp...  17 us
    all_gather x1, waiting for transfers between devices, per_device(): gathered = lax.all_gather(sim_maps, BLK, axis=0, tiled=True)  11.3 us
    pallas_call x2, Pallas kernels, block_of(): pl.pallas_call(block_body, grid_spec=pltpu.PrefetchScalarGridSpec(num_sca...  11 us
  transfers between devices with their start and end apart: 17, of which 5 were waited for; matrix products, arithmetic and copies ran while one was open for 4% of the time, Pallas kernels for 30%

profile of v12, /device:TPU:1, one launch (start us, length us, event | category | flops | bytes accessed | tf_op | source)
XLA Modules:
  0.0 191.2 jit_solution(12067459761545833751)
XLA Ops:
  7.9 3.5 %constant_dynamic-slice_fusion.1 = (f32[192,1152]{1,0:T(8,128)}, f32[192,1152]{1,0:T(8,128)}, f32[192,1152]{1,0:T(8,128)S(1)}, f32[192,1152]{1,0:T(8,128)}) fusion(f32[192,4608]{1,0:T(8,128)} %param.6, s32[]{:T(128)S(6)} %select_n.21, s32[]{:T(128)S(6)} %select_n.19, s32[]{:T(128)S(6)} %select_n.18, s32[]{:T(128)S(6)} %select_n.20), kind=kLoop, calls=%fused_computation.5 | loop fusion | bytes 7077904 | tf_op jit(solution)/shard_map/dynamic_slice | solution.py:266
  11.4 2.1 %collective-permute-start = (f32[192,1152]{1,0:T(8,128)}, f32[192,1152]{1,0:T(8,128)S(1)}, u32[]{:S(2)}, u32[]{:S(2)}) collective-permute-start(f32[192,1152]{1,0:T(8,128)} %get-tuple-element.95), channel_id=1, source_target_pairs={{0,2},{2,4},{4,6},{6,0},{1,3},{3,5},{5,7},{7,1},{8,10},{10,12},{12... | collective-permute-start | bytes 2654216 | tf_op jit(solution)/shard_map/ppermute | solution.py:267
  13.6 2.6 %collective-permute-start.1 = (f32[192,1152]{1,0:T(8,128)}, f32[192,1152]{1,0:T(8,128)S(1)}, u32[]{:S(2)}, u32[]{:S(2)}) collective-permute-start(f32[192,1152]{1,0:T(8,128)} %get-tuple-element.97), channel_id=1, source_target_pairs={{0,4},{2,6},{4,0},{6,2},{1,5},{3,7},{5,1},{7,3},{8,12},{10,14},{12... | collective-permute-start | bytes 2654216 | tf_op jit(solution)/shard_map/ppermute | solution.py:267
  17.9 9.0 %all-to-all-start = ((s32[128,1,36]{2,1,0:T(1,128)}), s32[128,1,36]{2,1,0:T(1,128)S(1)}, u32[]{:S(2)}, u32[]{:S(2)}) async-start(s32[128,1,36]{2,1,0:T(1,128)} %broadcast_in_dim.2), calls=%async_computation | async-start | bytes 131072 | tf_op jit(solution)/shard_map/all_to_all | solution.py:269
  26.9 17.0 %shard_map.59 = (bf16[1536,3072]{1,0:T(8,128)(2,1)}, bf16[1536,3072]{1,0:T(8,128)(2,1)}) custom-call(f32[1536,3072]{1,0:T(8,128)} %a.1), custom_call_target="tpu_custom_call" | custom-call | flops 9437184 | bytes 37748736 | tf_op jit(solution)/shard_map/pallas_call | solution.py:62
  45.1 11.3 %all-gather.2.cloned.1.call-done.s = f32[3072,512]{1,0:T(8,128)} async-done(((f32[192,512]{1,0:T(8,128)}), f32[3072,512]{1,0:T(8,128)}) %all-gather.2.cloned.1.call-update) | async-done | bytes 6291472 | tf_op jit(solution)/shard_map/all_gather | solution.py:262
  56.4 8.5 %shard_map.60 = (f32[192,512]{1,0:T(8,128)}, f32[192,512]{1,0:T(8,128)}) custom-call(s32[2]{0:T(128)} %get-tuple-element.101.at, bf16[1536,3072]{1,0:T(8,128)(2,1)} %get-tuple-element.70.a_high, bf16[1536,3072]{1,0:T(8,128)(2,1)} %get-tuple-element.52.a_low, f32[3072,512]{1,0:T(8,128)} %all-gather.2.cloned.1.call-done.s), custom_call_target="tpu_custom_call" | custom-call | flops 3623878656 | bytes 11010048 | tf_op jit(solution)/shard_map/pallas_call | solution.py:100
  64.9 3.6 %collective-permute-start.3 = (f32[192,512]{1,0:T(8,128)}, f32[192,512]{1,0:T(8,128)S(1)}, u32[]{:S(2)}, u32[]{:S(2)}) collective-permute-start(f32[192,512]{1,0:T(8,128)} %get-tuple-element.55), channel_id=1, source_target_pairs={{0,3},{1,2},{2,5},{3,4},{4,7},{5,6},{6,1},{7,0},{8,11},{9,10},{10,... | collective-permute-start | bytes 1179656 | tf_op jit(solution)/shard_map/ppermute | solution.py:43
  69.8 8.4 %shard_map.61 = (f32[192,512]{1,0:T(8,128)}, f32[192,512]{1,0:T(8,128)}) custom-call(s32[2]{0:T(128)} %pad_add_fusion.2.at, bf16[1536,3072]{1,0:T(8,128)(2,1)} %get-tuple-element.70.a_high, bf16[1536,3072]{1,0:T(8,128)(2,1)} %get-tuple-element.52.a_low, f32[3072,512]{1,0:T(8,128)} %all-gather.2.cloned.1.call-done.s), custom_call_target="tpu_custom_call" | custom-call | flops 3623878656 | bytes 11010048 | tf_op jit(solution)/shard_map/pallas_call | solution.py:100
  78.2 1.5 collective-permute-start.5
  79.9 8.4 %shard_map.62 = (f32[192,512]{1,0:T(8,128)}, f32[192,512]{1,0:T(8,128)}) custom-call(s32[2]{0:T(128)} %get-tuple-element.100.at, bf16[1536,3072]{1,0:T(8,128)(2,1)} %get-tuple-element.70.a_high, bf16[1536,3072]{1,0:T(8,128)(2,1)} %get-tuple-element.52.a_low, f32[3072,512]{1,0:T(8,128)} %all-gather.2.cloned.1.call-done.s), custom_call_target="tpu_custom_call" | custom-call | flops 3623878656 | bytes 11010048 | tf_op jit(solution)/shard_map/pallas_call | solution.py:100
  88.4 4.0 %collective-permute-start.7 = (f32[192,512]{1,0:T(8,128)}, f32[192,512]{1,0:T(8,128)S(1)}, u32[]{:S(2)}, u32[]{:S(2)}) collective-permute-start(f32[192,512]{1,0:T(8,128)} %get-tuple-element.67), channel_id=1, source_target_pairs={{0,5},{1,4},{2,7},{3,6},{4,1},{5,0},{6,3},{7,2},{8,13},{9,12},{10,... | collective-permute-start | bytes 1179656 | tf_op jit(solution)/shard_map/ppermute | solution.py:43
  92.3 5.5 %shard_map.63 = f32[192,512]{1,0:T(8,128)} custom-call(s32[1]{0:T(128)} %bitcast.5.at, bf16[1536,3072]{1,0:T(8,128)(2,1)} %get-tuple-element.70.a_high, bf16[1536,3072]{1,0:T(8,128)(2,1)} %get-tuple-element.52.a_low, f32[3072,512]{1,0:T(8,128)} %all-gather.2.cloned.1.call-done.s), custom_call_target="tpu_custom_call" | custom-call | flops 1811939328 | bytes 8650752 | tf_op jit(solution)/shard_map/pallas_call | solution.py:128
  98.2 1.4 collective-permute-start.8
  99.6 5.5 %shard_map.64 = f32[192,512]{1,0:T(8,128)} custom-call(s32[1]{0:T(128)} %bitcast.6.at, bf16[1536,3072]{1,0:T(8,128)(2,1)} %get-tuple-element.70.a_high, bf16[1536,3072]{1,0:T(8,128)(2,1)} %get-tuple-element.52.a_low, f32[3072,512]{1,0:T(8,128)} %all-gather.2.cloned.1.call-done.s), custom_call_target="tpu_custom_call" | custom-call | flops 1811939328 | bytes 8650752 | tf_op jit(solution)/shard_map/pallas_call | solution.py:128
  105.1 1.4 pad_maximum_fusion.refs_1_.refs_4_
  106.5 4.8 %collective-permute-done.9 = f32[192,512]{1,0:T(8,128)S(1)} collective-permute-done((f32[192,512]{1,0:T(8,128)}, f32[192,512]{1,0:T(8,128)S(1)}, u32[]{:S(2)}, u32[]{:S(2)}) %collective-permute-start.9) | collective-permute-done | bytes 393248 | tf_op jit(solution)/shard_map/ppermute | solution.py:43
  114.6 6.0 %collective-permute-start.13 = (f32[2,192,256]{2,1,0:T(8,128)S(1)}, f32[2,192,256]{2,1,0:T(8,128)S(1)}, u32[]{:S(2)}, u32[]{:S(2)}) collective-permute-start(f32[2,192,256]{2,1,0:T(8,128)S(1)} %pad_maximum_fusion.1.refs_0_), channel_id=1, source_target_pairs={{0,2},{1,3},{2,4},{3,5},{4,6},{5,7},{6,0},{7,1},{8,10},{9,11},{10,... | collective-permute-start | bytes 1179656 | tf_op jit(solution)/shard_map/ppermute | solution.py:43
  120.5 1.6 collective-permute-start.14
  124.5 6.9 %collective-permute-done.13.refs_0_ = f32[2,192,256]{2,1,0:T(8,128)S(1)} collective-permute-done((f32[2,192,256]{2,1,0:T(8,128)S(1)}, f32[2,192,256]{2,1,0:T(8,128)S(1)}, u32[]{:S(2)}, u32[]{:S(2)}) %collective-permute-start.13) | collective-permute-done | bytes 393248 | tf_op jit(solution)/shard_map/ppermute | solution.py:43
  131.5 2.2 %shard_map.66.refs_3_ = f32[16,2,8,1152]{3,2,1,0:T(8,128)S(1)} custom-call(f32[2,192,256]{2,1,0:T(8,128)S(1)} %collective-permute-done.13.refs_0_, f32[4,192,1152]{2,1,0:T(8,128)S(1)} %pad_maximum_fusion.refs_1_.refs_4_, f32[4,192,1152]{2,1,0:T(8,128)S(1)} %collective-permute-done.12.refs_2_.refs_5_, f32[2,192,256]{2,1,0:T(8,128)S(1)} %collective-permute-done.14.refs_3_, ...), custom_call_target="tpu_custom_call" | custom-call | flops 1358954496 | bytes 3538944 | tf_op jit(solution)/shard_map/pallas_call | solution.py:185
  133.7 7.2 %collective-permute-done.11.refs_0_ = f32[2,192,256]{2,1,0:T(8,128)S(1)} collective-permute-done((f32[2,192,256]{2,1,0:T(8,128)S(1)}, f32[2,192,256]{2,1,0:T(8,128)S(1)}, u32[]{:S(2)}, u32[]{:S(2)}) %collective-permute-start.11) | collective-permute-done | bytes 393248 | tf_op jit(solution)/shard_map/ppermute | solution.py:43
  142.1 20.8 %all_to_all.15.pieces = f32[16,2,8,1152]{3,2,1,0:T(8,128)S(1)} all-to-all(f32[16,2,8,1152]{3,2,1,0:T(8,128)S(1)} %shard_map.67), channel_id=1, replica_groups=mesh['x'=4,'zl'=2,'c'=2,'y'=4,'zh'=2] {'x','zh','zl'}, dimensions={0} | all-to-all | bytes 2359296 | tf_op jit(solution)/shard_map/all_to_all | solution.py:307
  163.8 19.4 %all_to_all.16.blocks = f32[128,8,128]{2,1,0:T(8,128)S(1)} all-to-all(f32[128,8,128]{2,1,0:T(8,128)S(1)} %shard_map.68), channel_id=1, replica_groups=mesh['x'=4,'zl'=2,'c'=2,'y'=4,'zh'=2] {'c','x','zh','zl','y'}, dimensions={0} | all-to-all | bytes 1048576 | tf_op jit(solution)/shard_map/all_to_all | solution.py:319
  (38 shorter events, 14.4 us)
Async XLA Ops:
  7.2 49.3 %all-gather.2.cloned.1.call-start = ((), (), s32[]{:S(2)}) async-start(), calls=%async_computation.3 | async-start | bytes 6684672 | tf_op jit(solution)/shard_map/all_gather | solution.py:262
  7.9 9.3 %copy-start.1 = (s32[36]{0:T(128)S(1)}, s32[36]{0:T(128)}, u32[]{:S(2)}) copy-start(s32[36]{0:T(128)} %param.7) | copy-start | bytes 436
  11.4 53.4 %collective-permute-start = (f32[192,1152]{1,0:T(8,128)}, f32[192,1152]{1,0:T(8,128)S(1)}, u32[]{:S(2)}, u32[]{:S(2)}) collective-permute-start(f32[192,1152]{1,0:T(8,128)} %get-tuple-element.95), channel_id=1, source_target_pairs={{0,2},{2,4},{4,6},{6,0},{1,3},{3,5},{5,7},{7,1},{8,10},{10,12},{12... | collective-permute-start | bytes 2654216 | tf_op jit(solution)/shard_map/ppermute | solution.py:267
  13.6 51.3 %collective-permute-start.1 = (f32[192,1152]{1,0:T(8,128)}, f32[192,1152]{1,0:T(8,128)S(1)}, u32[]{:S(2)}, u32[]{:S(2)}) collective-permute-start(f32[192,1152]{1,0:T(8,128)} %get-tuple-element.97), channel_id=1, source_target_pairs={{0,4},{2,6},{4,0},{6,2},{1,5},{3,7},{5,1},{7,3},{8,12},{10,14},{12... | collective-permute-start | bytes 2654216 | tf_op jit(solution)/shard_map/ppermute | solution.py:267
  16.2 48.7 %collective-permute-start.2 = (f32[192,1152]{1,0:T(8,128)}, f32[192,1152]{1,0:T(8,128)}, u32[]{:S(2)}, u32[]{:S(2)}) collective-permute-start(f32[192,1152]{1,0:T(8,128)} %get-tuple-element.94), channel_id=1, source_target_pairs={{0,6},{2,0},{4,2},{6,4},{1,7},{3,1},{5,3},{7,5},{8,14},{10,8},{12,... | collective-permute-start | bytes 2654216 | tf_op jit(solution)/shard_map/ppermute | solution.py:267
  17.9 47.0 %all-to-all-start = ((s32[128,1,36]{2,1,0:T(1,128)}), s32[128,1,36]{2,1,0:T(1,128)S(1)}, u32[]{:S(2)}, u32[]{:S(2)}) async-start(s32[128,1,36]{2,1,0:T(1,128)} %broadcast_in_dim.2), calls=%async_computation | async-start | bytes 131072 | tf_op jit(solution)/shard_map/all_to_all | solution.py:269
  64.9 23.5 %collective-permute-start.3 = (f32[192,512]{1,0:T(8,128)}, f32[192,512]{1,0:T(8,128)S(1)}, u32[]{:S(2)}, u32[]{:S(2)}) collective-permute-start(f32[192,512]{1,0:T(8,128)} %get-tuple-element.55), channel_id=1, source_target_pairs={{0,3},{1,2},{2,5},{3,4},{4,7},{5,6},{6,1},{7,0},{8,11},{9,10},{10,... | collective-permute-start | bytes 1179656 | tf_op jit(solution)/shard_map/ppermute | solution.py:43
  68.6 19.8 %collective-permute-start.4 = (f32[192,512]{1,0:T(8,128)}, f32[192,512]{1,0:T(8,128)S(1)}, u32[]{:S(2)}, u32[]{:S(2)}) collective-permute-start(f32[192,512]{1,0:T(8,128)} %get-tuple-element.63), channel_id=1, source_target_pairs={{0,2},{1,3},{2,4},{3,5},{4,6},{5,7},{6,0},{7,1},{8,10},{9,11},{10,... | collective-permute-start | bytes 1179656 | tf_op jit(solution)/shard_map/ppermute | solution.py:43
  78.2 28.4 %collective-permute-start.5 = (f32[192,512]{1,0:T(8,128)}, f32[192,512]{1,0:T(8,128)S(1)}, u32[]{:S(2)}, u32[]{:S(2)}) collective-permute-start(f32[192,512]{1,0:T(8,128)} %get-tuple-element.58), channel_id=1, source_target_pairs={{0,7},{1,6},{2,1},{3,0},{4,3},{5,2},{6,5},{7,4},{8,15},{9,14},{10,... | collective-permute-start | bytes 1179656 | tf_op jit(solution)/shard_map/ppermute | solution.py:43
  79.7 26.9 %collective-permute-start.6 = (f32[192,512]{1,0:T(8,128)}, f32[192,512]{1,0:T(8,128)S(1)}, u32[]{:S(2)}, u32[]{:S(2)}) collective-permute-start(f32[192,512]{1,0:T(8,128)} %get-tuple-element.66), channel_id=1, source_target_pairs={{0,6},{1,7},{2,0},{3,1},{4,2},{5,3},{6,4},{7,5},{8,14},{9,15},{10,... | collective-permute-start | bytes 1179656 | tf_op jit(solution)/shard_map/ppermute | solution.py:43
  88.4 23.0 %collective-permute-start.7 = (f32[192,512]{1,0:T(8,128)}, f32[192,512]{1,0:T(8,128)S(1)}, u32[]{:S(2)}, u32[]{:S(2)}) collective-permute-start(f32[192,512]{1,0:T(8,128)} %get-tuple-element.67), channel_id=1, source_target_pairs={{0,5},{1,4},{2,7},{3,6},{4,1},{5,0},{6,3},{7,2},{8,13},{9,12},{10,... | collective-permute-start | bytes 1179656 | tf_op jit(solution)/shard_map/ppermute | solution.py:43
  92.3 5.8 %copy-start.2 = (f32[192,512]{1,0:T(8,128)S(1)}, f32[192,512]{1,0:T(8,128)}, u32[]{:S(2)}) copy-start(f32[192,512]{1,0:T(8,128)} %get-tuple-element.68) | copy-start | bytes 1179652
  97.8 13.5 %collective-permute-start.9 = (f32[192,512]{1,0:T(8,128)}, f32[192,512]{1,0:T(8,128)S(1)}, u32[]{:S(2)}, u32[]{:S(2)}) collective-permute-start(f32[192,512]{1,0:T(8,128)} %shard_map.63), channel_id=1, source_target_pairs={{0,1},{1,0},{2,3},{3,2},{4,5},{5,4},{6,7},{7,6},{8,9},{9,8},{10,11... | collective-permute-start | bytes 1179656 | tf_op jit(solution)/shard_map/ppermute | solution.py:43
  98.2 13.2 %collective-permute-start.8 = (f32[192,512]{1,0:T(8,128)S(1)}, f32[192,512]{1,0:T(8,128)S(1)}, u32[]{:S(2)}, u32[]{:S(2)}) collective-permute-start(f32[192,512]{1,0:T(8,128)S(1)} %copy-done.2), channel_id=1, source_target_pairs={{0,4},{1,5},{2,6},{3,7},{4,0},{5,1},{6,2},{7,3},{8,12},{9,13},{10,... | collective-permute-start | bytes 1179656 | tf_op jit(solution)/shard_map/ppermute | solution.py:43
  105.1 6.3 %copy-start = (f32[192,512]{1,0:T(8,128)S(1)}, f32[192,512]{1,0:T(8,128)}, u32[]{:S(2)}) copy-start(f32[192,512]{1,0:T(8,128)} %shard_map.64) | copy-start | bytes 1179652
  111.8 2.3 %collective-permute-start.10 = (f32[192,256]{1,0:T(8,128)S(1)}, f32[192,256]{1,0:T(8,128)S(1)}, u32[]{:S(2)}, u32[]{:S(2)}) collective-permute-start(f32[192,256]{1,0:T(8,128)S(1)} %get-tuple-element.99), channel_id=1, source_target_pairs={{0,8},{8,0},{1,9},{9,1},{2,10},{10,2},{3,11},{11,3},{4,12},{12,4},... | collective-permute-start | bytes 589832 | tf_op jit(solution)/shard_map/ppermute | solution.py:51
  114.1 9.2 %collective-permute-start.12 = (f32[4,192,1152]{2,1,0:T(8,128)S(1)}, f32[4,192,1152]{2,1,0:T(8,128)S(1)}, u32[]{:S(2)}, u32[]{:S(2)}) collective-permute-start(f32[4,192,1152]{2,1,0:T(8,128)S(1)} %pad_maximum_fusion.refs_1_.refs_4_), channel_id=1, source_target_pairs={{0,8},{8,0},{1,9},{9,1},{2,10},{10,2},{3,11},{11,3},{4,12},{12,4},... | collective-permute-start | bytes 10616840 | tf_op jit(solution)/shard_map/ppermute | solution.py:51
  114.6 16.9 %collective-permute-start.13 = (f32[2,192,256]{2,1,0:T(8,128)S(1)}, f32[2,192,256]{2,1,0:T(8,128)S(1)}, u32[]{:S(2)}, u32[]{:S(2)}) collective-permute-start(f32[2,192,256]{2,1,0:T(8,128)S(1)} %pad_maximum_fusion.1.refs_0_), channel_id=1, source_target_pairs={{0,2},{1,3},{2,4},{3,5},{4,6},{5,7},{6,0},{7,1},{8,10},{9,11},{10,... | collective-permute-start | bytes 1179656 | tf_op jit(solution)/shard_map/ppermute | solution.py:43
  120.5 10.9 %collective-permute-start.14 = (f32[2,192,256]{2,1,0:T(8,128)S(1)}, f32[2,192,256]{2,1,0:T(8,128)S(1)}, u32[]{:S(2)}, u32[]{:S(2)}) collective-permute-start(f32[2,192,256]{2,1,0:T(8,128)S(1)} %pad_maximum_fusion.1.refs_0_), channel_id=1, source_target_pairs={{0,6},{1,7},{2,0},{3,1},{4,2},{5,3},{6,4},{7,5},{8,14},{9,15},{10,... | collective-permute-start | bytes 1179656 | tf_op jit(solution)/shard_map/ppermute | solution.py:43
  122.1 18.7 %collective-permute-start.11 = (f32[2,192,256]{2,1,0:T(8,128)S(1)}, f32[2,192,256]{2,1,0:T(8,128)S(1)}, u32[]{:S(2)}, u32[]{:S(2)}) collective-permute-start(f32[2,192,256]{2,1,0:T(8,128)S(1)} %pad_maximum_fusion.1.refs_0_), channel_id=1, source_target_pairs={{0,4},{1,5},{2,6},{3,7},{4,0},{5,1},{6,2},{7,3},{8,12},{9,13},{10,... | collective-permute-start | bytes 1179656 | tf_op jit(solution)/shard_map/ppermute | solution.py:43
Sparse Core Ops, SparseCore 0:
  9.7 46.6 all-gather.1

commit v13 on v11

--- a/solution.py
+++ b/solution.py
@@ -274,12 +274,13 @@
 
     got = {}
     for dy in (2, 1, 3, 0):
-        if dy:
-            far, near = rows_of(lax.rem(y + dy, NY), zh, a_high, a_low, gathered)
+        to = lax.rem(y + dy, NY)
+        if dy % 2:
+            far, near = rows_of(to, zh, a_high, a_low, gathered)
         else:
-            far = block_of(2 * y + 1 - zh, a_high, a_low, gathered)
+            far = block_of(2 * to + 1 - zh, a_high, a_low, gathered)
             gathered, far = lax.optimization_barrier((gathered, far))
-            near = block_of(2 * y + zh, a_high, a_low, gathered)
+            near = block_of(2 * to + zh, a_high, a_low, gathered)
         if dy == 2:
             far, near, bands, *columns = lax.optimization_barrier((far, near, bands, *columns))
         if dy == 3:

time: 191 us -> 193 us (1.010)
  Pallas kernels: 59.9 us -> 62.5 us
    pallas_call x2 -> x4, Pallas kernels: 11 us -> 22 us  [block_of(): pl.pallas_call(block_body, grid_spec=pltpu.PrefetchScalarGridSpec(num_sca...]
    pallas_call x3 -> x2, Pallas kernels: 25.3 us -> 16.8 us  [rows_of(): pl.pallas_call(row_body, grid_spec=pltpu.PrefetchScalarGridSpec(num_scala...]
  transfers between devices with their start and end apart: 17 -> 17, of which waited for: 6 -> 6; matrix products, arithmetic and copies ran while one was open for 4% -> 3% of each run, Pallas kernels for 30% -> 31%
where the time goes in v13:
time: 193 us; the launch traced here: 192 us
  Pallas kernels  62.5 us (32%)
  blocking collectives  43.1 us (22%)
  waiting for transfers between devices  33.2 us (17%)
  starting transfers between devices  32.9 us (17%)
  between operations  14.2 us (7%)
  local copies, waits for them, and re-layouts  4.21 us (2%)
  other arithmetic  2.44 us (1%)
    all_to_all x1, blocking collectives, per_device(): pieces = lax.all_to_all(projected, CHIPS, 0, 0, tiled=True)  23.2 us
    pallas_call x4, Pallas kernels, block_of(): pl.pallas_call(block_body, grid_spec=pltpu.PrefetchScalarGridSpec(num_sca...  22 us
    all_to_all x1, blocking collectives, per_device(): blocks = lax.all_to_all(sums, ('c',) + CHIPS + ('y',), 0, 0, tiled=True)  19.8 us
    ppermute x10, waiting for transfers between devices, shift(): return lax.ppermute(value, RING, pairs)  17.9 us
    pallas_call x1, Pallas kernels, split_rows(): pl.pallas_call(split_body, grid=(rows // step,), in_specs=[block], out_sp...  17 us
    pallas_call x2, Pallas kernels, rows_of(): pl.pallas_call(row_body, grid_spec=pltpu.PrefetchScalarGridSpec(num_scala...  16.8 us
    ppermute x10, starting transfers between devices, shift(): return lax.ppermute(value, RING, pairs)  16.6 us
    all_gather x1, waiting for transfers between devices, per_device(): gathered = lax.all_gather(sim_maps, BLK, axis=0, tiled=True)  11.9 us
  transfers between devices with their start and end apart: 17, of which 6 were waited for; matrix products, arithmetic and copies ran while one was open for 3% of the time, Pallas kernels for 31%

profile of v13, /device:TPU:1, one launch (start us, length us, event | category | flops | bytes accessed | tf_op | source)
XLA Modules:
  0.0 192.5 jit_solution(4637441597383434407)
XLA Ops:
  7.9 3.5 %constant_dynamic-slice_fusion.1 = (f32[192,1152]{1,0:T(8,128)}, f32[192,1152]{1,0:T(8,128)}, f32[192,1152]{1,0:T(8,128)S(1)}, f32[192,1152]{1,0:T(8,128)}) fusion(f32[192,4608]{1,0:T(8,128)} %param.6, s32[]{:T(128)S(6)} %select_n.21, s32[]{:T(128)S(6)} %select_n.19, s32[]{:T(128)S(6)} %select_n.18, s32[]{:T(128)S(6)} %select_n.20), kind=kLoop, calls=%fused_computation.5 | loop fusion | bytes 7077904 | tf_op jit(solution)/shard_map/dynamic_slice | solution.py:266
  11.4 2.1 %collective-permute-start = (f32[192,1152]{1,0:T(8,128)}, f32[192,1152]{1,0:T(8,128)S(1)}, u32[]{:S(2)}, u32[]{:S(2)}) collective-permute-start(f32[192,1152]{1,0:T(8,128)} %get-tuple-element.95), channel_id=1, source_target_pairs={{0,2},{2,4},{4,6},{6,0},{1,3},{3,5},{5,7},{7,1},{8,10},{10,12},{12... | collective-permute-start | bytes 2654216 | tf_op jit(solution)/shard_map/ppermute | solution.py:267
  13.6 2.6 %collective-permute-start.1 = (f32[192,1152]{1,0:T(8,128)}, f32[192,1152]{1,0:T(8,128)S(1)}, u32[]{:S(2)}, u32[]{:S(2)}) collective-permute-start(f32[192,1152]{1,0:T(8,128)} %get-tuple-element.97), channel_id=1, source_target_pairs={{0,4},{2,6},{4,0},{6,2},{1,5},{3,7},{5,1},{7,3},{8,12},{10,14},{12... | collective-permute-start | bytes 2654216 | tf_op jit(solution)/shard_map/ppermute | solution.py:267
  17.9 9.0 %all-to-all-start = ((s32[128,1,36]{2,1,0:T(1,128)}), s32[128,1,36]{2,1,0:T(1,128)S(1)}, u32[]{:S(2)}, u32[]{:S(2)}) async-start(s32[128,1,36]{2,1,0:T(1,128)} %broadcast_in_dim.2), calls=%async_computation | async-start | bytes 131072 | tf_op jit(solution)/shard_map/all_to_all | solution.py:269
  26.9 17.0 %shard_map.59 = (bf16[1536,3072]{1,0:T(8,128)(2,1)}, bf16[1536,3072]{1,0:T(8,128)(2,1)}) custom-call(f32[1536,3072]{1,0:T(8,128)} %a.1), custom_call_target="tpu_custom_call" | custom-call | flops 9437184 | bytes 37748736 | tf_op jit(solution)/shard_map/pallas_call | solution.py:62
  44.5 11.9 %all-gather.2.cloned.1.call-done.s = f32[3072,512]{1,0:T(8,128)} async-done(((f32[192,512]{1,0:T(8,128)}), f32[3072,512]{1,0:T(8,128)}) %all-gather.2.cloned.1.call-update) | async-done | bytes 6291472 | tf_op jit(solution)/shard_map/all_gather | solution.py:262
  56.4 5.5 %shard_map.60 = f32[192,512]{1,0:T(8,128)} custom-call(s32[1]{0:T(128)} %bitcast.3.at, bf16[1536,3072]{1,0:T(8,128)(2,1)} %get-tuple-element.70.a_high, bf16[1536,3072]{1,0:T(8,128)(2,1)} %get-tuple-element.52.a_low, f32[3072,512]{1,0:T(8,128)} %all-gather.2.cloned.1.call-done.s), custom_call_target="tpu_custom_call" | custom-call | flops 1811939328 | bytes 8650752 | tf_op jit(solution)/shard_map/pallas_call | solution.py:128
  61.9 5.5 %shard_map.61 = f32[192,512]{1,0:T(8,128)} custom-call(s32[1]{0:T(128)} %bitcast.4.at, bf16[1536,3072]{1,0:T(8,128)(2,1)} %get-tuple-element.70.a_high, bf16[1536,3072]{1,0:T(8,128)(2,1)} %get-tuple-element.52.a_low, f32[3072,512]{1,0:T(8,128)} %all-gather.2.cloned.1.call-done.s), custom_call_target="tpu_custom_call" | custom-call | flops 1811939328 | bytes 8650752 | tf_op jit(solution)/shard_map/pallas_call | solution.py:128
  67.5 5.2 %collective-permute-start.3 = (f32[192,512]{1,0:T(8,128)S(1)}, f32[192,512]{1,0:T(8,128)S(1)}, u32[]{:S(2)}, u32[]{:S(2)}) collective-permute-start(f32[192,512]{1,0:T(8,128)S(1)} %copy-done.1), channel_id=1, source_target_pairs={{0,5},{1,4},{2,7},{3,6},{4,1},{5,0},{6,3},{7,2},{8,13},{9,12},{10,... | collective-permute-start | bytes 1179656 | tf_op jit(solution)/shard_map/ppermute | solution.py:43
  72.9 8.4 %shard_map.62 = (f32[192,512]{1,0:T(8,128)}, f32[192,512]{1,0:T(8,128)}) custom-call(s32[2]{0:T(128)} %get-tuple-element.101.at, bf16[1536,3072]{1,0:T(8,128)(2,1)} %get-tuple-element.70.a_high, bf16[1536,3072]{1,0:T(8,128)(2,1)} %get-tuple-element.52.a_low, f32[3072,512]{1,0:T(8,128)} %all-gather.2.cloned.1.call-done.s), custom_call_target="tpu_custom_call" | custom-call | flops 3623878656 | bytes 11010048 | tf_op jit(solution)/shard_map/pallas_call | solution.py:100
  83.7 8.4 %shard_map.63 = (f32[192,512]{1,0:T(8,128)}, f32[192,512]{1,0:T(8,128)}) custom-call(s32[2]{0:T(128)} %get-tuple-element.100.at, bf16[1536,3072]{1,0:T(8,128)(2,1)} %get-tuple-element.70.a_high, bf16[1536,3072]{1,0:T(8,128)(2,1)} %get-tuple-element.52.a_low, f32[3072,512]{1,0:T(8,128)} %all-gather.2.cloned.1.call-done.s), custom_call_target="tpu_custom_call" | custom-call | flops 3623878656 | bytes 11010048 | tf_op jit(solution)/shard_map/pallas_call | solution.py:100
  92.2 3.9 %collective-permute-start.7 = (f32[192,512]{1,0:T(8,128)}, f32[192,512]{1,0:T(8,128)S(1)}, u32[]{:S(2)}, u32[]{:S(2)}) collective-permute-start(f32[192,512]{1,0:T(8,128)} %get-tuple-element.67), channel_id=1, source_target_pairs={{0,7},{1,6},{2,1},{3,0},{4,3},{5,2},{6,5},{7,4},{8,15},{9,14},{10,... | collective-permute-start | bytes 1179656 | tf_op jit(solution)/shard_map/ppermute | solution.py:43
  96.1 5.5 %shard_map.64 = f32[192,512]{1,0:T(8,128)} custom-call(s32[1]{0:T(128)} %bitcast.6.at, bf16[1536,3072]{1,0:T(8,128)(2,1)} %get-tuple-element.70.a_high, bf16[1536,3072]{1,0:T(8,128)(2,1)} %get-tuple-element.52.a_low, f32[3072,512]{1,0:T(8,128)} %all-gather.2.cloned.1.call-done.s), custom_call_target="tpu_custom_call" | custom-call | flops 1811939328 | bytes 8650752 | tf_op jit(solution)/shard_map/pallas_call | solution.py:128
  102.2 5.5 %shard_map.65 = f32[192,512]{1,0:T(8,128)} custom-call(s32[1]{0:T(128)} %bitcast.7.at, bf16[1536,3072]{1,0:T(8,128)(2,1)} %get-tuple-element.70.a_high, bf16[1536,3072]{1,0:T(8,128)(2,1)} %get-tuple-element.52.a_low, f32[3072,512]{1,0:T(8,128)} %all-gather.2.cloned.1.call-done.s), custom_call_target="tpu_custom_call" | custom-call | flops 1811939328 | bytes 8650752 | tf_op jit(solution)/shard_map/pallas_call | solution.py:128
  107.6 1.4 pad_maximum_fusion.refs_1_.refs_4_
  109.1 6.6 %collective-permute-done.9 = f32[192,512]{1,0:T(8,128)S(1)} collective-permute-done((f32[192,512]{1,0:T(8,128)}, f32[192,512]{1,0:T(8,128)S(1)}, u32[]{:S(2)}, u32[]{:S(2)}) %collective-permute-start.9) | collective-permute-done | bytes 393248 | tf_op jit(solution)/shard_map/ppermute | solution.py:43
  120.0 1.4 collective-permute-start.14
  121.4 1.5 collective-permute-start.11
  123.0 1.6 collective-permute-done.12.refs_2_.refs_5_
  125.8 4.7 %collective-permute-done.13.refs_0_ = f32[2,192,256]{2,1,0:T(8,128)S(1)} collective-permute-done((f32[2,192,256]{2,1,0:T(8,128)S(1)}, f32[2,192,256]{2,1,0:T(8,128)S(1)}, u32[]{:S(2)}, u32[]{:S(2)}) %collective-permute-start.13) | collective-permute-done | bytes 393248 | tf_op jit(solution)/shard_map/ppermute | solution.py:43
  130.5 2.2 %shard_map.67.refs_3_ = f32[16,2,8,1152]{3,2,1,0:T(8,128)S(1)} custom-call(f32[2,192,256]{2,1,0:T(8,128)S(1)} %collective-permute-done.13.refs_0_, f32[4,192,1152]{2,1,0:T(8,128)S(1)} %pad_maximum_fusion.refs_1_.refs_4_, f32[4,192,1152]{2,1,0:T(8,128)S(1)} %collective-permute-done.12.refs_2_.refs_5_, f32[2,192,256]{2,1,0:T(8,128)S(1)} %collective-permute-done.14.refs_3_, ...), custom_call_target="tpu_custom_call" | custom-call | flops 1358954496 | bytes 3538944 | tf_op jit(solution)/shard_map/pallas_call | solution.py:185
  132.7 6.5 %collective-permute-done.11.refs_0_ = f32[2,192,256]{2,1,0:T(8,128)S(1)} collective-permute-done((f32[2,192,256]{2,1,0:T(8,128)S(1)}, f32[2,192,256]{2,1,0:T(8,128)S(1)}, u32[]{:S(2)}, u32[]{:S(2)}) %collective-permute-start.11) | collective-permute-done | bytes 393248 | tf_op jit(solution)/shard_map/ppermute | solution.py:43
  140.5 23.2 %all_to_all.15.pieces = f32[16,2,8,1152]{3,2,1,0:T(8,128)S(1)} all-to-all(f32[16,2,8,1152]{3,2,1,0:T(8,128)S(1)} %shard_map.68), channel_id=1, replica_groups=mesh['x'=4,'zl'=2,'c'=2,'y'=4,'zh'=2] {'x','zh','zl'}, dimensions={0} | all-to-all | bytes 2359296 | tf_op jit(solution)/shard_map/all_to_all | solution.py:308
  164.6 19.8 %all_to_all.16.blocks = f32[128,8,128]{2,1,0:T(8,128)S(1)} all-to-all(f32[128,8,128]{2,1,0:T(8,128)S(1)} %shard_map.69), channel_id=1, replica_groups=mesh['x'=4,'zl'=2,'c'=2,'y'=4,'zh'=2] {'c','x','zh','zl','y'}, dimensions={0} | all-to-all | bytes 1048576 | tf_op jit(solution)/shard_map/all_to_all | solution.py:320
  (40 shorter events, 15.1 us)
Async XLA Ops:
  7.2 49.3 %all-gather.2.cloned.1.call-start = ((), (), s32[]{:S(2)}) async-start(), calls=%async_computation.3 | async-start | bytes 6684672 | tf_op jit(solution)/shard_map/all_gather | solution.py:262
  7.9 9.3 %copy-start.2 = (s32[36]{0:T(128)S(1)}, s32[36]{0:T(128)}, u32[]{:S(2)}) copy-start(s32[36]{0:T(128)} %param.7) | copy-start | bytes 436
  11.4 56.0 %collective-permute-start = (f32[192,1152]{1,0:T(8,128)}, f32[192,1152]{1,0:T(8,128)S(1)}, u32[]{:S(2)}, u32[]{:S(2)}) collective-permute-start(f32[192,1152]{1,0:T(8,128)} %get-tuple-element.95), channel_id=1, source_target_pairs={{0,2},{2,4},{4,6},{6,0},{1,3},{3,5},{5,7},{7,1},{8,10},{10,12},{12... | collective-permute-start | bytes 2654216 | tf_op jit(solution)/shard_map/ppermute | solution.py:267
  13.6 53.9 %collective-permute-start.1 = (f32[192,1152]{1,0:T(8,128)}, f32[192,1152]{1,0:T(8,128)S(1)}, u32[]{:S(2)}, u32[]{:S(2)}) collective-permute-start(f32[192,1152]{1,0:T(8,128)} %get-tuple-element.97), channel_id=1, source_target_pairs={{0,4},{2,6},{4,0},{6,2},{1,5},{3,7},{5,1},{7,3},{8,12},{10,14},{12... | collective-permute-start | bytes 2654216 | tf_op jit(solution)/shard_map/ppermute | solution.py:267
  16.2 51.3 %collective-permute-start.2 = (f32[192,1152]{1,0:T(8,128)}, f32[192,1152]{1,0:T(8,128)}, u32[]{:S(2)}, u32[]{:S(2)}) collective-permute-start(f32[192,1152]{1,0:T(8,128)} %get-tuple-element.94), channel_id=1, source_target_pairs={{0,6},{2,0},{4,2},{6,4},{1,7},{3,1},{5,3},{7,5},{8,14},{10,8},{12,... | collective-permute-start | bytes 2654216 | tf_op jit(solution)/shard_map/ppermute | solution.py:267
  17.9 49.5 %all-to-all-start = ((s32[128,1,36]{2,1,0:T(1,128)}), s32[128,1,36]{2,1,0:T(1,128)S(1)}, u32[]{:S(2)}, u32[]{:S(2)}) async-start(s32[128,1,36]{2,1,0:T(1,128)} %broadcast_in_dim.2), calls=%async_computation | async-start | bytes 131072 | tf_op jit(solution)/shard_map/all_to_all | solution.py:269
  61.9 5.5 %copy-start.1 = (f32[192,512]{1,0:T(8,128)S(1)}, f32[192,512]{1,0:T(8,128)}, u32[]{:S(2)}) copy-start(f32[192,512]{1,0:T(8,128)} %shard_map.60) | copy-start | bytes 1179652
  67.5 24.7 %collective-permute-start.3 = (f32[192,512]{1,0:T(8,128)S(1)}, f32[192,512]{1,0:T(8,128)S(1)}, u32[]{:S(2)}, u32[]{:S(2)}) collective-permute-start(f32[192,512]{1,0:T(8,128)S(1)} %copy-done.1), channel_id=1, source_target_pairs={{0,5},{1,4},{2,7},{3,6},{4,1},{5,0},{6,3},{7,2},{8,13},{9,12},{10,... | collective-permute-start | bytes 1179656 | tf_op jit(solution)/shard_map/ppermute | solution.py:43
  72.6 19.5 %collective-permute-start.4 = (f32[192,512]{1,0:T(8,128)}, f32[192,512]{1,0:T(8,128)S(1)}, u32[]{:S(2)}, u32[]{:S(2)}) collective-permute-start(f32[192,512]{1,0:T(8,128)} %shard_map.61), channel_id=1, source_target_pairs={{0,4},{1,5},{2,6},{3,7},{4,0},{5,1},{6,2},{7,3},{8,12},{9,13},{10,... | collective-permute-start | bytes 1179656 | tf_op jit(solution)/shard_map/ppermute | solution.py:43
  81.3 27.8 %collective-permute-start.5 = (f32[192,512]{1,0:T(8,128)}, f32[192,512]{1,0:T(8,128)S(1)}, u32[]{:S(2)}, u32[]{:S(2)}) collective-permute-start(f32[192,512]{1,0:T(8,128)} %get-tuple-element.58), channel_id=1, source_target_pairs={{0,3},{1,2},{2,5},{3,4},{4,7},{5,6},{6,1},{7,0},{8,11},{9,10},{10,... | collective-permute-start | bytes 1179656 | tf_op jit(solution)/shard_map/ppermute | solution.py:43
  82.5 26.6 %collective-permute-start.6 = (f32[192,512]{1,0:T(8,128)}, f32[192,512]{1,0:T(8,128)S(1)}, u32[]{:S(2)}, u32[]{:S(2)}) collective-permute-start(f32[192,512]{1,0:T(8,128)} %get-tuple-element.66), channel_id=1, source_target_pairs={{0,2},{1,3},{2,4},{3,5},{4,6},{5,7},{6,0},{7,1},{8,10},{9,11},{10,... | collective-permute-start | bytes 1179656 | tf_op jit(solution)/shard_map/ppermute | solution.py:43
  92.2 23.5 %collective-permute-start.7 = (f32[192,512]{1,0:T(8,128)}, f32[192,512]{1,0:T(8,128)S(1)}, u32[]{:S(2)}, u32[]{:S(2)}) collective-permute-start(f32[192,512]{1,0:T(8,128)} %get-tuple-element.67), channel_id=1, source_target_pairs={{0,7},{1,6},{2,1},{3,0},{4,3},{5,2},{6,5},{7,4},{8,15},{9,14},{10,... | collective-permute-start | bytes 1179656 | tf_op jit(solution)/shard_map/ppermute | solution.py:43
  96.1 5.8 %copy-start.3 = (f32[192,512]{1,0:T(8,128)S(1)}, f32[192,512]{1,0:T(8,128)}, u32[]{:S(2)}) copy-start(f32[192,512]{1,0:T(8,128)} %get-tuple-element.68) | copy-start | bytes 1179652
  101.6 14.1 %collective-permute-start.9 = (f32[192,512]{1,0:T(8,128)}, f32[192,512]{1,0:T(8,128)S(1)}, u32[]{:S(2)}, u32[]{:S(2)}) collective-permute-start(f32[192,512]{1,0:T(8,128)} %shard_map.64), channel_id=1, source_target_pairs={{0,1},{1,0},{2,3},{3,2},{4,5},{5,4},{6,7},{7,6},{8,9},{9,8},{10,11... | collective-permute-start | bytes 1179656 | tf_op jit(solution)/shard_map/ppermute | solution.py:43
  101.9 13.8 %collective-permute-start.8 = (f32[192,512]{1,0:T(8,128)S(1)}, f32[192,512]{1,0:T(8,128)S(1)}, u32[]{:S(2)}, u32[]{:S(2)}) collective-permute-start(f32[192,512]{1,0:T(8,128)S(1)} %copy-done.3), channel_id=1, source_target_pairs={{0,6},{1,7},{2,0},{3,1},{4,2},{5,3},{6,4},{7,5},{8,14},{9,15},{10,... | collective-permute-start | bytes 1179656 | tf_op jit(solution)/shard_map/ppermute | solution.py:43
  107.6 8.1 %copy-start = (f32[192,512]{1,0:T(8,128)S(1)}, f32[192,512]{1,0:T(8,128)}, u32[]{:S(2)}) copy-start(f32[192,512]{1,0:T(8,128)} %shard_map.65) | copy-start | bytes 1179652
  116.1 2.1 %collective-permute-start.10 = (f32[192,256]{1,0:T(8,128)S(1)}, f32[192,256]{1,0:T(8,128)S(1)}, u32[]{:S(2)}, u32[]{:S(2)}) collective-permute-start(f32[192,256]{1,0:T(8,128)S(1)} %get-tuple-element.99), channel_id=1, source_target_pairs={{0,8},{8,0},{1,9},{9,1},{2,10},{10,2},{3,11},{11,3},{4,12},{12,4},... | collective-permute-start | bytes 589832 | tf_op jit(solution)/shard_map/ppermute | solution.py:51
  118.3 6.3 %collective-permute-start.12 = (f32[4,192,1152]{2,1,0:T(8,128)S(1)}, f32[4,192,1152]{2,1,0:T(8,128)S(1)}, u32[]{:S(2)}, u32[]{:S(2)}) collective-permute-start(f32[4,192,1152]{2,1,0:T(8,128)S(1)} %pad_maximum_fusion.refs_1_.refs_4_), channel_id=1, source_target_pairs={{0,8},{8,0},{1,9},{9,1},{2,10},{10,2},{3,11},{11,3},{4,12},{12,4},... | collective-permute-start | bytes 10616840 | tf_op jit(solution)/shard_map/ppermute | solution.py:51
  118.7 11.8 %collective-permute-start.13 = (f32[2,192,256]{2,1,0:T(8,128)S(1)}, f32[2,192,256]{2,1,0:T(8,128)S(1)}, u32[]{:S(2)}, u32[]{:S(2)}) collective-permute-start(f32[2,192,256]{2,1,0:T(8,128)S(1)} %pad_maximum_fusion.1.refs_0_), channel_id=1, source_target_pairs={{0,2},{1,3},{2,4},{3,5},{4,6},{5,7},{6,0},{7,1},{8,10},{9,11},{10,... | collective-permute-start | bytes 1179656 | tf_op jit(solution)/shard_map/ppermute | solution.py:43
  120.0 10.5 %collective-permute-start.14 = (f32[2,192,256]{2,1,0:T(8,128)S(1)}, f32[2,192,256]{2,1,0:T(8,128)S(1)}, u32[]{:S(2)}, u32[]{:S(2)}) collective-permute-start(f32[2,192,256]{2,1,0:T(8,128)S(1)} %pad_maximum_fusion.1.refs_0_), channel_id=1, source_target_pairs={{0,6},{1,7},{2,0},{3,1},{4,2},{5,3},{6,4},{7,5},{8,14},{9,15},{10,... | collective-permute-start | bytes 1179656 | tf_op jit(solution)/shard_map/ppermute | solution.py:43
  121.4 17.8 %collective-permute-start.11 = (f32[2,192,256]{2,1,0:T(8,128)S(1)}, f32[2,192,256]{2,1,0:T(8,128)S(1)}, u32[]{:S(2)}, u32[]{:S(2)}) collective-permute-start(f32[2,192,256]{2,1,0:T(8,128)S(1)} %pad_maximum_fusion.1.refs_0_), channel_id=1, source_target_pairs={{0,4},{1,5},{2,6},{3,7},{4,0},{5,1},{6,2},{7,3},{8,12},{9,13},{10,... | collective-permute-start | bytes 1179656 | tf_op jit(solution)/shard_map/ppermute | solution.py:43
Sparse Core Ops, SparseCore 0:
  9.7 46.6 all-gather.1
